TPU v7x, 32 devices: a whole 2x2x4 slice. The times are simulated.
32 devices in a mesh: ctx: 8 (over z, y), head: 4 (over x, core).
Axes of the slice: x: 2, y: 2, z: 4, core: 2. Of those that a mesh axis runs over, the one named last changes fastest.
Arguments:
- queries: bfloat16 [8, 32, 128], P('ctx', 'head'), may hold values from -9 to 9
- k_new: bfloat16 [8, 16, 128], P('ctx', 'head'), may hold values from -9 to 9
- v_new: bfloat16 [8, 16, 128], P('ctx', 'head'), may hold values from -6 to 6
- k_suffix: bfloat16 [8, 256, 16, 128], P('ctx', None, 'head'), may hold values from -9 to 9
- v_suffix: bfloat16 [8, 256, 16, 128], P('ctx', None, 'head'), may hold values from -6 to 6
- lengths: int32 [8], P('ctx'), may hold values from 0 to 256, as said below
- k_prefix: bfloat16 [8192, 16, 128], P('ctx', 'head'), may hold values from -6 to 6
- v_prefix: bfloat16 [8192, 16, 128], P('ctx', 'head'), may hold values from -6 to 6
- w_out: bfloat16 [4096, 5376], P(None, ('ctx', 'head')), may hold values from -0.09375 to 0.09375
- residual: bfloat16 [8, 5376], P(None, ('ctx', 'head')), may hold values from -5 to 5
- norm_gain: float32 [5376], replicated, may hold values from 0.1 to 1.9
- w_gate: bfloat16 [5376, 21504], P(None, ('ctx', 'head')), may hold values from -0.078125 to 0.078125
- w_up: bfloat16 [5376, 21504], P(None, ('ctx', 'head')), may hold values from -0.078125 to 0.078125
- w_down: bfloat16 [21504, 5376], P(('ctx', 'head')), may hold values from -0.078125 to 0.078125
Outputs:
- attention: bfloat16 [8, 32, 128], P('ctx', 'head')
- next_hidden: bfloat16 [8, 5376], P(None, ('ctx', 'head'))
Inputs may be any that keep to these rules, and one draw needn't show every extreme that they name: `lengths`: slots at or past a completion's length hold entries that no key uses.
All inputs are finite; a program needn't handle non-finite values.
Results may differ from a plain program's by a relative error of at most 0.008.
Values may be sent and summed in bfloat16 or wider, within the bound.
No kernel may reach another device: no remote copies, remote signals or barrier semaphores. Data moves between devices by JAX's collectives and lax.ppermute only.
A program may use at most 64 MiB of HBM per device.

v0:
```python
import jax
import jax.numpy as jnp
from jax import lax
from jax.sharding import PartitionSpec as P

BLOCK = 512


score_scale = 168.0 ** (-0.5)
norm_epsilon = 1e-06


def join_parts(first, second):
    first_max, first_sum, first_total = first
    second_max, second_sum, second_total = second
    joint_max = jnp.maximum(first_max, second_max)
    first_factor = jnp.exp(first_max - joint_max)
    second_factor = jnp.exp(second_max - joint_max)
    joint_sum = first_sum * first_factor[..., None] + second_sum * second_factor[..., None]
    joint_total = first_total * first_factor + second_total * second_factor
    return (joint_max, joint_sum, joint_total)


def prefix_partials(queries_all, k_prefix, v_prefix):
    blocks = k_prefix.shape[0] // BLOCK
    kv_heads = k_prefix.shape[1]
    head_width = k_prefix.shape[2]
    key_blocks = k_prefix.reshape(blocks, BLOCK, kv_heads, head_width)
    value_blocks = v_prefix.reshape(blocks, BLOCK, kv_heads, head_width)

    def block_step(running, block):
        key_block, value_block = block
        scores = (
            jnp.einsum("bgrd,pgd->bgrp", queries_all, key_block, preferred_element_type=jnp.float32)
            * score_scale
        )
        block_max = jnp.max(scores, axis=-1)
        weights = jnp.exp(scores - block_max[..., None]).astype(jnp.bfloat16)
        block_total = jnp.sum(weights.astype(jnp.float32), axis=-1)
        block_sum = jnp.einsum(
            "bgrp,pgd->bgrd", weights, value_block, preferred_element_type=jnp.float32
        )
        return (join_parts(running, (block_max, block_sum, block_total)), None)

    start_max = jnp.full(queries_all.shape[:3], -jnp.inf, jnp.float32)
    start_sum = jnp.zeros(queries_all.shape, jnp.float32)
    start_total = jnp.zeros(queries_all.shape[:3], jnp.float32)
    result, unused = lax.scan(
        block_step, (start_max, start_sum, start_total), (key_blocks, value_blocks)
    )
    return result


def suffix_partials(queries_local, k_suffix, v_suffix, k_new, v_new, lengths):
    slot_count = k_suffix.shape[1]
    scores = (
        jnp.einsum("bgrd,bsgd->bgrs", queries_local, k_suffix, preferred_element_type=jnp.float32)
        * score_scale
    )
    new_scores = (
        jnp.einsum("bgrd,bgd->bgr", queries_local, k_new, preferred_element_type=jnp.float32)
        * score_scale
    )
    in_use = (
        lax.broadcasted_iota(jnp.int32, (lengths.shape[0], slot_count), 1) < lengths[:, None]
    )[:, None, None, :]
    suffix_max = jnp.maximum(jnp.max(jnp.where(in_use, scores, -jnp.inf), axis=-1), new_scores)
    weights = jnp.where(in_use, jnp.exp(scores - suffix_max[..., None]), 0.0).astype(jnp.bfloat16)
    new_weight = jnp.exp(new_scores - suffix_max).astype(jnp.bfloat16).astype(jnp.float32)
    suffix_total = jnp.sum(weights.astype(jnp.float32), axis=-1) + new_weight
    suffix_sum = jnp.einsum(
        "bgrs,bsgd->bgrd", weights, v_suffix, preferred_element_type=jnp.float32
    )
    suffix_sum = suffix_sum + new_weight[..., None] * v_new.astype(jnp.float32)[:, :, None, :]
    return (suffix_max, suffix_sum, suffix_total)


def body(
    queries,
    k_new,
    v_new,
    k_suffix,
    v_suffix,
    lengths,
    k_prefix,
    v_prefix,
    w_out,
    residual,
    norm_gain,
    w_gate,
    w_up,
    w_down,
):
    completions, query_heads, head_width = queries.shape
    kv_heads = k_new.shape[1]
    group_size = query_heads // kv_heads
    queries_local = queries.reshape(completions, kv_heads, group_size, head_width)
    gathered = lax.all_gather(queries, "ctx", axis=0, tiled=True)
    queries_all = gathered.reshape(gathered.shape[0], kv_heads, group_size, head_width)
    prefix_max, prefix_sum, prefix_total = prefix_partials(queries_all, k_prefix, v_prefix)
    arrived = (
        lax.all_to_all(prefix_max[:, None], "ctx", split_axis=0, concat_axis=1, tiled=True),
        lax.all_to_all(prefix_sum[:, None], "ctx", split_axis=0, concat_axis=1, tiled=True),
        lax.all_to_all(prefix_total[:, None], "ctx", split_axis=0, concat_axis=1, tiled=True),
    )
    source_max, source_sum, source_total = arrived
    owner_max = jnp.max(source_max, axis=1)
    factor = jnp.exp(source_max - owner_max[:, None])
    owner_sum = jnp.sum(source_sum * factor[..., None], axis=1)
    owner_total = jnp.sum(source_total * factor, axis=1)
    suffix_part = suffix_partials(queries_local, k_suffix, v_suffix, k_new, v_new, lengths)
    combined = join_parts((owner_max, owner_sum, owner_total), suffix_part)
    attention = (combined[1] / combined[2][..., None]).astype(jnp.bfloat16)
    attention = attention.reshape(completions, query_heads, head_width)
    ctx_count = lax.axis_size("ctx")
    head_count = lax.axis_size("head")
    columns = residual.shape[1]
    flat_rows = attention.reshape(completions, query_heads * head_width)
    every_row = lax.all_gather(flat_rows, ("ctx", "head"), axis=0, tiled=True)
    every_row = every_row.reshape(ctx_count, head_count, completions, query_heads * head_width)
    out_blocks = w_out.reshape(head_count, query_heads * head_width, columns)
    projected = jnp.einsum(
        "chjf,hfe->cje", every_row, out_blocks, preferred_element_type=jnp.float32
    )
    projected = projected.reshape(ctx_count * completions, columns)
    hidden_part = (residual.astype(jnp.float32) + projected).astype(jnp.bfloat16)
    hidden_state = lax.all_gather(hidden_part, ("ctx", "head"), axis=1, tiled=True)
    state_float = hidden_state.astype(jnp.float32)
    mean_square = jnp.mean(state_float * state_float, axis=-1, keepdims=True)
    normed = (state_float * lax.rsqrt(mean_square + norm_epsilon) * norm_gain).astype(jnp.bfloat16)
    gate_values = jnp.dot(normed, w_gate, preferred_element_type=jnp.float32)
    up_values = jnp.dot(normed, w_up, preferred_element_type=jnp.float32)
    activated = (jax.nn.gelu(gate_values, approximate=True) * up_values).astype(jnp.bfloat16)
    summed = lax.psum_scatter(
        lax.dot_general(
            w_down, activated, (((0,), (1,)), ((), ())), preferred_element_type=jnp.float32
        ),
        ("ctx", "head"),
        scatter_dimension=0,
        tiled=True,
    )
    next_hidden = (hidden_part.astype(jnp.float32) + summed.T).astype(jnp.bfloat16)
    return (attention, next_hidden)


def solution(mesh):
    placed = (
        P("ctx", "head", None),
        P("ctx", "head", None),
        P("ctx", "head", None),
        P("ctx", None, "head", None),
        P("ctx", None, "head", None),
        P("ctx"),
        P("ctx", "head", None),
        P("ctx", "head", None),
        P(None, ("ctx", "head")),
        P(None, ("ctx", "head")),
        P(),
        P(None, ("ctx", "head")),
        P(None, ("ctx", "head")),
        P(("ctx", "head"), None),
    )
    return jax.shard_map(
        body,
        mesh=mesh,
        in_specs=placed,
        out_specs=(P("ctx", "head", None), P(None, ("ctx", "head"))),
        check_vma=False,
    )
```

profile of v0, /device:TPU:0, one launch (start us, length us, event | category | flops | bytes accessed | tf_op | source)
XLA Modules:
  0.0 290.2 jit_solution(17221662002311175361)
XLA Ops:
  7.2 28.1 %all_gather.9 = bf16[8,8,128]{2,1,0:T(8,128)(2,1)S(1)} all-gather(bf16[1,8,128]{2,1,0:T(8,128)(2,1)} %param.16), channel_id=1, replica_groups=mesh['ctx'=8,'head'=4] {'ctx'}, dimensions={0}, use_global_device_ids=true | all-gather | bytes 18432 | tf_op jit(solution)/shard_map/all_gather | solution.py:98
  35.4 4.9 %while.15 = (s32[]{:T(128)}, f32[8,4,2]{0,2,1:T(2,128)S(1)}, f32[8,4,2,128]{3,0,2,1:T(8,128)S(1)}, f32[8,4,2]{0,2,1:T(2,128)S(1)}, bf16[2,512,4,128]{3,2,1,0:T(4...) while((s32[]{:T(128)}, f32[8,4,2]{0,2,1:T(2,128)S(1)}, ...), condition=%wide.region_3.4_spmd.clone, body=%wide.region_0.3_spmd.clone.sunk | while | flops 17072516 | bytes 3624556 | solution.py:48
  35.4 1.7 constant_dynamic-slice_fusion.3
  37.0 0.3 fusion.72
  37.9 1.6 constant_dynamic-slice_fusion.3
  39.4 0.3 fusion.72
  40.2 0.7 copy.73
  40.9 3.9 %all-to-all-start.1 = ((f32[8,1,4,2]{2,3,1,0:T(2,128)}), f32[8,1,4,2]{2,3,1,0:T(2,128)S(1)}, u32[]{:S(2)}, u32[]{:S(2)}) async-start(f32[8,1,4,2]{2,3,1,0:T(2,128)} %copy.73), calls=%async_computation.1 | async-start | bytes 16384 | tf_op jit(solution)/shard_map/all_to_all | solution.py:102
  45.5 0.3 select_reduce_fusion
  46.4 0.7 copy.85
  47.1 0.6 copy.139
  47.8 3.6 %all-to-all-done.1 = f32[8,1,4,2]{2,3,1,0:T(2,128)S(1)} async-done(((f32[8,1,4,2]{2,3,1,0:T(2,128)}), f32[8,1,4,2]{2,3,1,0:T(2,128)S(1)}, u32[]{:S(2)}, u32[]{:S(2)}) %all-to-all-start.1) | async-done | bytes 288 | tf_op jit(solution)/shard_map/all_to_all | solution.py:102
  51.3 3.3 %all-to-all-start.2 = ((f32[8,1,4,2]{2,3,1,0:T(2,128)}), f32[8,1,4,2]{2,3,1,0:T(2,128)S(1)}, u32[]{:S(2)}, u32[]{:S(2)}) async-start(f32[8,1,4,2]{2,3,1,0:T(2,128)} %copy.85), calls=%async_computation.2 | async-start | bytes 16384 | tf_op jit(solution)/shard_map/all_to_all | solution.py:104
  54.8 6.3 %all-to-all-done.2 = f32[8,1,4,2]{2,3,1,0:T(2,128)S(1)} async-done(((f32[8,1,4,2]{2,3,1,0:T(2,128)}), f32[8,1,4,2]{2,3,1,0:T(2,128)S(1)}, u32[]{:S(2)}, u32[]{:S(2)}) %all-to-all-start.2) | async-done | bytes 288 | tf_op jit(solution)/shard_map/all_to_all | solution.py:104
  61.1 3.3 %all-to-all-start = ((f32[8,1,4,2,128]{4,3,2,1,0:T(2,128)}), f32[8,1,4,2,128]{4,3,2,1,0:T(2,128)S(1)}, u32[]{:S(2)}, u32[]{:S(2)}) async-start(f32[8,1,4,2,128]{4,3,2,1,0:T(2,128)} %bitcast.104), calls=%async_computation | async-start | bytes 65536 | tf_op jit(solution)/shard_map/all_to_all | solution.py:103
  65.2 5.8 %all-to-all-done = f32[8,1,4,2,128]{4,3,2,1,0:T(2,128)S(1)} async-done(((f32[8,1,4,2,128]{4,3,2,1,0:T(2,128)}), f32[8,1,4,2,128]{4,3,2,1,0:T(2,128)S(1)}, u32[]{:S(2)}, u32[]{:S(2)}) %all-to-all-start) | async-done | bytes 32800 | tf_op jit(solution)/shard_map/all_to_all | solution.py:103
  71.4 38.2 %all-gather = bf16[32,1,1024]{2,1,0:T(2,128)(2,1)S(1)} all-gather(bf16[1,1,1024]{2,1,0:T(2,128)(2,1)S(1)} %reshape.216), channel_id=1, replica_groups=mesh['ctx'=8,'head'=4] {'ctx','head'}, dimensions={0}, use_global_device_ids=true | all-gather | bytes 67584 | tf_op jit(solution)/shard_map/all_gather | solution.py:119
  109.6 0.4 reduce.9
  110.0 0.5 fusion.15
  110.5 37.1 %all-gather.1 = bf16[32,168,8]{1,2,0:T(8,128)(2,1)S(1)} all-gather(bf16[1,168,8]{1,2,0:T(8,128)(2,1)S(1)} %bitcast.121), channel_id=1, replica_groups=mesh['ctx'=8,'head'=4] {'ctx','head'}, dimensions={0}, use_global_device_ids=true | all-gather | bytes 88704 | tf_op jit(solution)/shard_map/all_gather | solution.py:127
  148.0 5.0 %fusion.54 = f32[8,672]{1,0:T(8,128)S(1)} fusion(bf16[5376,672]{0,1:T(8,128)(2,1)} %param.27, f32[5376,8]{0,1:T(8,128)S(1)} %reshape.222, f32[5376]{0:T(1024)S(1)} %copy-done.2, f32[8]{0:T(128)S(1)} %add_rsqrt_fusion), kind=kOutput, calls=%fused_computation.83 | convolution fusion | flops 57931776 | bytes 7440416 | tf_op jit(solution)/shard_map/dot_general | solution.py:131
  153.0 9.5 %convolution_bitcast_fusion.1 = f32[5376,8]{0,1:T(8,128)} fusion(bf16[672,5376]{1,0:T(8,128)(2,1)} %param.29, bf16[5376,672]{0,1:T(8,128)(2,1)} %param.28, f32[8,672]{1,0:T(8,128)S(1)} %fusion.54, f32[5376,8]{0,1:T(8,128)S(1)} %reshape.222, f32[5376]{0:T(1024)S(1)} %copy-done.2, f32[8]{0:T(128)S(1)} %add_rsqrt_fusion), kind=kOutput, calls=%fused_computation.18 | convolution fusion | flops 115788288 | bytes 14837792 | tf_op jit(solution)/shard_map/dot_general | solution.py:135
  162.5 119.5 %all-reduce.3.cloned.1.call-done = f32[5376,8]{0,1:T(8,128)} async-done(((f32[5376,8]{0,1:T(8,128)}), f32[5376,8]{0,1:T(8,128)}) %all-reduce.3.cloned.1.call-update) | async-done | bytes 172048
  282.0 1.4 fusion.39
  (58 shorter events, 3.3 us)
Async XLA Ops:
  7.2 38.3 %copy-start = (bf16[1,256,4,128]{3,2,1,0:T(4,128)(2,1)S(1)}, bf16[1,256,4,128]{3,2,1,0:T(4,128)(2,1)}, u32[]{:S(2)}) copy-start(bf16[1,256,4,128]{3,2,1,0:T(4,128)(2,1)} %param.19) | copy-start | bytes 786436
  35.3 10.2 %copy-start.4 = (bf16[1,8,128]{2,1,0:T(8,128)(2,1)S(1)}, bf16[1,8,128]{2,1,0:T(8,128)(2,1)}, u32[]{:S(2)}) copy-start(bf16[1,8,128]{2,1,0:T(8,128)(2,1)} %param.16) | copy-start | bytes 6148
  35.3 10.6 %copy-start.8 = (bf16[1,4,128]{2,1,0:T(4,128)(2,1)S(1)}, bf16[1,4,128]{2,1,0:T(4,128)(2,1)}, u32[]{:S(2)}) copy-start(bf16[1,4,128]{2,1,0:T(4,128)(2,1)} %param.17) | copy-start | bytes 3076
  35.3 11.1 %copy-start.6 = (bf16[1,4,128]{2,1,0:T(4,128)(2,1)S(1)}, bf16[1,4,128]{2,1,0:T(4,128)(2,1)}, u32[]{:S(2)}) copy-start(bf16[1,4,128]{2,1,0:T(4,128)(2,1)} %param.18) | copy-start | bytes 3076
  35.3 35.9 %copy-start.7 = (bf16[1,256,4,128]{3,2,1,0:T(4,128)(2,1)S(1)}, bf16[1,256,4,128]{3,2,1,0:T(4,128)(2,1)}, u32[]{:S(2)}) copy-start(bf16[1,256,4,128]{3,2,1,0:T(4,128)(2,1)} %param.20) | copy-start | bytes 786436
  35.3 74.7 %copy-start.1 = (bf16[4096,168]{0,1:T(8,128)(2,1)S(1)}, bf16[4096,168]{0,1:T(8,128)(2,1)}, u32[]{:S(2)}) copy-start(bf16[4096,168]{0,1:T(8,128)(2,1)} %param.24) | copy-start | bytes 4128772
  35.3 74.7 %copy-start.3 = (bf16[8,168]{1,0:T(8,128)(2,1)S(1)}, bf16[8,168]{1,0:T(8,128)(2,1)}, u32[]{:S(2)}) copy-start(bf16[8,168]{1,0:T(8,128)(2,1)} %param.25) | copy-start | bytes 8068
  35.3 112.6 %copy-start.2 = (f32[5376]{0:T(1024)S(1)}, f32[5376]{0:T(1024)}, u32[]{:S(2)}) copy-start(f32[5376]{0:T(1024)} %param.26) | copy-start | bytes 64516
  40.9 10.4 %all-to-all-start.1 = ((f32[8,1,4,2]{2,3,1,0:T(2,128)}), f32[8,1,4,2]{2,3,1,0:T(2,128)S(1)}, u32[]{:S(2)}, u32[]{:S(2)}) async-start(f32[8,1,4,2]{2,3,1,0:T(2,128)} %copy.73), calls=%async_computation.1 | async-start | bytes 16384 | tf_op jit(solution)/shard_map/all_to_all | solution.py:102
  51.3 9.8 %all-to-all-start.2 = ((f32[8,1,4,2]{2,3,1,0:T(2,128)}), f32[8,1,4,2]{2,3,1,0:T(2,128)S(1)}, u32[]{:S(2)}, u32[]{:S(2)}) async-start(f32[8,1,4,2]{2,3,1,0:T(2,128)} %copy.85), calls=%async_computation.2 | async-start | bytes 16384 | tf_op jit(solution)/shard_map/all_to_all | solution.py:104
  61.1 10.0 %all-to-all-start = ((f32[8,1,4,2,128]{4,3,2,1,0:T(2,128)}), f32[8,1,4,2,128]{4,3,2,1,0:T(2,128)S(1)}, u32[]{:S(2)}, u32[]{:S(2)}) async-start(f32[8,1,4,2,128]{4,3,2,1,0:T(2,128)} %bitcast.104), calls=%async_computation | async-start | bytes 65536 | tf_op jit(solution)/shard_map/all_to_all | solution.py:103
  64.4 217.5 %all-reduce.3.cloned.1.call-start = ((), (), s32[]{:S(2)}) async-start(), calls=%async_computation.3 | async-start | bytes 344064
  71.3 91.2 %copy-start.5 = (bf16[4,2,128]{2,1,0:T(2,128)(2,1)}, bf16[4,2,128]{2,1,0:T(2,128)(2,1)S(1)}, u32[]{:S(2)}) copy-start(bf16[4,2,128]{2,1,0:T(2,128)(2,1)S(1)} %fusion.21) | copy-start | bytes 6148
Sparse Core Ops, SparseCore 0:
  162.6 119.3 all-reduce.2
where the time goes:
time: 292 us; the launch traced here: 290 us
  waiting for transfers between devices  135 us (46%)
  blocking collectives  103 us (35%)
  matrix products  16.7 us (6%)
  between operations  14.9 us (5%)
  starting transfers between devices  10.6 us (4%)
  local copies, waits for them, and re-layouts  6.58 us (2%)
  other arithmetic  2.92 us (1%)
    unnamed x2, waiting for transfers between devices  119 us
    all_gather x1, blocking collectives, body(): every_row = lax.all_gather(flat_rows, ('ctx', 'head'), axis=0, tiled=True)  38.2 us
    all_gather x1, blocking collectives, body(): lax.all_gather(hidden_part, ('ctx', 'head'), axis=1, tiled=True)  37.1 us
    all_gather x1, blocking collectives, body(): gathered = lax.all_gather(queries, 'ctx', axis=0, tiled=True)  28.1 us
    dot_general x1, matrix products, body(): lax.dot_general(w_down, activated, (((0,), (1,)), ((), ())), preferred_el...  9.54 us
    all_to_all x1, waiting for transfers between devices, body(): lax.all_to_all(prefix_total[:, None], 'ctx', split_axis=0, concat_axis=1,...  6.26 us
  transfers between devices with their start and end apart: 4, of which 4 were waited for; matrix products, arithmetic and copies ran while one was open for 1% of the time, Pallas kernels for 0%

commit v1 on v0

v1 whole, which is shorter than its diff:
```python
import functools

import jax
import jax.numpy as jnp
from jax import lax
from jax.experimental import pallas as pl
from jax.experimental.pallas import tpu as pltpu
from jax.sharding import PartitionSpec as P

SCORE_SCALE = 168.0 ** (-0.5)
NORM_EPSILON = 1e-06
MASKED = -1e30
BOTH = ("ctx", "head")


def pack_partial(row_max, row_total, row_sum):
    lane = lax.broadcasted_iota(jnp.int32, row_sum.shape, 1)
    return row_sum, jnp.where(lane == 0, row_max, row_total)


def masked_softmax(scores, keep):
    scores = jnp.where(keep, scores, MASKED)
    row_max = jnp.max(scores, axis=1, keepdims=True)
    weights = jnp.exp(scores - row_max).astype(jnp.bfloat16)
    row_total = jnp.sum(weights.astype(jnp.float32), axis=1, keepdims=True)
    return row_max, row_total, weights


def head_match(shape, heads, kv_heads):
    group = heads // kv_heads
    row = lax.broadcasted_iota(jnp.int32, shape, 0)
    column = lax.broadcasted_iota(jnp.int32, shape, 1)
    return lax.rem(row, heads) // group == lax.rem(column, kv_heads), column // kv_heads


def prefix_kernel(count, me_ref, *refs):
    arrived, (k_ref, v_ref, sum_ref, stat_ref, ordered_ref) = refs[:count], refs[count:]
    heads = arrived[0].shape[1]
    for step, ref in enumerate(arrived):
        owner = lax.rem(me_ref[0] + (count - step), count)
        ordered_ref[owner] = ref[0]
    positions, kv_heads, width = k_ref.shape
    keys = k_ref[...].reshape(positions * kv_heads, width)
    values = v_ref[...].reshape(positions * kv_heads, width)
    queries = ordered_ref[...].reshape(count * heads, width)
    scores = SCORE_SCALE * lax.dot_general(
        queries, keys, (((1,), (1,)), ((), ())), preferred_element_type=jnp.float32
    )
    match, unused = head_match(scores.shape, heads, kv_heads)
    row_max, row_total, weights = masked_softmax(scores, match)
    row_sum = jnp.dot(weights, values, preferred_element_type=jnp.float32)
    sum_ref[...], stat_ref[...] = pack_partial(row_max, row_total, row_sum)


def prefix_partials(me, arrived, k_prefix, v_prefix):
    count = len(arrived)
    unused, heads, width = arrived[0].shape
    shape = jax.ShapeDtypeStruct((count * heads, width), jnp.float32)
    whole = pl.BlockSpec(memory_space=pltpu.VMEM)
    return pl.pallas_call(
        functools.partial(prefix_kernel, count),
        out_shape=(shape, shape),
        in_specs=[pl.BlockSpec(memory_space=pltpu.SMEM)] + [whole] * (count + 2),
        scratch_shapes=[pltpu.VMEM((count, heads, width), jnp.bfloat16)],
        compiler_params=pltpu.CompilerParams(vmem_limit_bytes=24 * 1024 * 1024),
    )(me.astype(jnp.int32)[None], *arrived, k_prefix, v_prefix)


def suffix_kernel(length_ref, q_ref, k_ref, v_ref, k_new_ref, v_new_ref, sum_ref, stat_ref):
    unused, slots, kv_heads, width = k_ref.shape
    heads = q_ref.shape[1]
    keys = k_ref[0].reshape(slots * kv_heads, width)
    values = v_ref[0].reshape(slots * kv_heads, width)
    queries = q_ref[0]
    scores = SCORE_SCALE * lax.dot_general(
        queries, keys, (((1,), (1,)), ((), ())), preferred_element_type=jnp.float32
    )
    new_scores = SCORE_SCALE * lax.dot_general(
        queries, k_new_ref[0], (((1,), (1,)), ((), ())), preferred_element_type=jnp.float32
    )
    match, slot = head_match(scores.shape, heads, kv_heads)
    new_match, unused = head_match(new_scores.shape, heads, kv_heads)
    scores = jnp.where(match & (slot < length_ref[0]), scores, MASKED)
    new_scores = jnp.where(new_match, new_scores, MASKED)
    row_max = jnp.maximum(
        jnp.max(scores, axis=1, keepdims=True), jnp.max(new_scores, axis=1, keepdims=True)
    )
    weights = jnp.exp(scores - row_max).astype(jnp.bfloat16)
    new_weights = jnp.exp(new_scores - row_max).astype(jnp.bfloat16)
    row_total = jnp.sum(weights.astype(jnp.float32), axis=1, keepdims=True) + jnp.sum(
        new_weights.astype(jnp.float32), axis=1, keepdims=True
    )
    row_sum = jnp.dot(weights, values, preferred_element_type=jnp.float32) + jnp.dot(
        new_weights, v_new_ref[0], preferred_element_type=jnp.float32
    )
    sum_ref[...], stat_ref[...] = pack_partial(row_max, row_total, row_sum)


def suffix_partials(lengths, queries, k_suffix, v_suffix, k_new, v_new):
    shape = jax.ShapeDtypeStruct(queries.shape[1:], jnp.float32)
    whole = pl.BlockSpec(memory_space=pltpu.VMEM)
    return pl.pallas_call(
        suffix_kernel,
        out_shape=(shape, shape),
        in_specs=[pl.BlockSpec(memory_space=pltpu.SMEM)] + [whole] * 5,
        compiler_params=pltpu.CompilerParams(vmem_limit_bytes=8 * 1024 * 1024),
    )(lengths, queries, k_suffix, v_suffix, k_new, v_new)


def join_kernel(part_ref, sum_ref, stat_ref, out_ref):
    sources = part_ref.shape[1]
    suffix_max = stat_ref[:, 0:1]
    suffix_total = stat_ref[:, 1:2]
    joint_max = suffix_max
    for source in range(sources):
        joint_max = jnp.maximum(joint_max, part_ref[1, source, :, 0:1])
    factor = jnp.exp(suffix_max - joint_max)
    total = suffix_total * factor
    summed = sum_ref[...] * factor
    for source in range(sources):
        factor = jnp.exp(part_ref[1, source, :, 0:1] - joint_max)
        total = total + part_ref[1, source, :, 1:2] * factor
        summed = summed + part_ref[0, source] * factor
    out_ref[...] = (summed / total).astype(jnp.bfloat16)


def join_partials(parts, suffix_sum, suffix_stat):
    return pl.pallas_call(
        join_kernel,
        out_shape=jax.ShapeDtypeStruct(suffix_sum.shape, jnp.bfloat16),
        compiler_params=pltpu.CompilerParams(vmem_limit_bytes=8 * 1024 * 1024),
    )(parts, suffix_sum, suffix_stat)


def rotate(value, axis, count, steps):
    if steps == 0:
        return value
    return lax.ppermute(value, axis, [(i, (i + steps) % count) for i in range(count)])


def gather_every(value, devices):
    copies = jnp.broadcast_to(value[None], (devices, *value.shape))
    return lax.all_to_all(copies, BOTH, split_axis=0, concat_axis=0, tiled=True)


def body(
    queries,
    k_new,
    v_new,
    k_suffix,
    v_suffix,
    lengths,
    k_prefix,
    v_prefix,
    w_out,
    residual,
    norm_gain,
    w_gate,
    w_up,
    w_down,
):
    ctx_count = lax.axis_size("ctx")
    head_count = lax.axis_size("head")
    devices = ctx_count * head_count
    unused, heads, width = queries.shape
    columns = residual.shape[1]
    completions = residual.shape[0]

    arrived = [rotate(queries, "ctx", ctx_count, step) for step in range(ctx_count)]
    suffix_sum, suffix_stat = suffix_partials(lengths, queries, k_suffix, v_suffix, k_new, v_new)
    prefix_sum, prefix_stat = prefix_partials(lax.axis_index("ctx"), arrived, k_prefix, v_prefix)
    parts = jnp.stack([prefix_sum, prefix_stat], axis=0).reshape(2, ctx_count, heads, width)
    parts = lax.all_to_all(parts, "ctx", split_axis=1, concat_axis=1, tiled=True)
    attention = join_partials(parts, suffix_sum, suffix_stat)

    rows = gather_every(attention, devices).reshape(completions, devices * heads * width // completions)
    projected = jnp.dot(rows, w_out, preferred_element_type=jnp.float32)
    hidden_part = (residual.astype(jnp.float32) + projected).astype(jnp.bfloat16)

    hidden_state = gather_every(hidden_part, devices)
    hidden_state = jnp.swapaxes(hidden_state, 0, 1).reshape(completions, devices * columns)
    state_float = hidden_state.astype(jnp.float32)
    mean_square = jnp.mean(state_float * state_float, axis=-1, keepdims=True)
    normed = (state_float * lax.rsqrt(mean_square + NORM_EPSILON) * norm_gain).astype(jnp.bfloat16)
    gate_values = jnp.dot(normed, w_gate, preferred_element_type=jnp.float32)
    up_values = jnp.dot(normed, w_up, preferred_element_type=jnp.float32)
    activated = (jax.nn.gelu(gate_values, approximate=True) * up_values).astype(jnp.bfloat16)
    share = jnp.dot(activated, w_down, preferred_element_type=jnp.float32).astype(jnp.bfloat16)
    share = jnp.swapaxes(share.reshape(completions, devices, columns), 0, 1)
    shares = lax.all_to_all(share, BOTH, split_axis=0, concat_axis=0, tiled=True)
    summed = jnp.sum(shares.astype(jnp.float32), axis=0)
    next_hidden = (hidden_part.astype(jnp.float32) + summed).astype(jnp.bfloat16)
    return (attention[None], next_hidden)


def solution(mesh):
    placed = (
        P("ctx", "head", None),
        P("ctx", "head", None),
        P("ctx", "head", None),
        P("ctx", None, "head", None),
        P("ctx", None, "head", None),
        P("ctx"),
        P("ctx", "head", None),
        P("ctx", "head", None),
        P(None, BOTH),
        P(None, BOTH),
        P(),
        P(None, BOTH),
        P(None, BOTH),
        P(BOTH, None),
    )
    return jax.shard_map(
        body,
        mesh=mesh,
        in_specs=placed,
        out_specs=(P("ctx", "head", None), P(None, BOTH)),
        check_vma=False,
    )
```

time: 292 us -> 83.5 us (0.29)
  waiting for transfers between devices: 135 us -> 7.2 us
  blocking collectives: 103 us -> 31.2 us
  between operations: 14.9 us -> 1.39 us
  starting transfers between devices: 10.6 us -> 15.8 us
    unnamed x2 -> x0, waiting for transfers between devices: 119 us -> none
    all_gather x3 -> x0, blocking collectives: 103 us -> none  [the longest x1 38.2 us: body(): every_row = lax.all_gather(flat_rows, ('ctx', 'head'), axis=0, tiled=True)]
    all_to_all x0 -> x3, blocking collectives: none -> 31.2 us  [the longest x2 21.3 us: gather_every(): return lax.all_to_all(copies, BOTH, split_axis=0, concat_axis=0, tiled=True)]
    all_to_all x3 -> x1, waiting for transfers between devices: 15.7 us -> 1.84 us  [body(): lax.all_to_all(parts, 'ctx', split_axis=1, concat_axis=1, tiled=True)]
    ppermute x0 -> x7, starting transfers between devices: none -> 12.5 us  [rotate(): lax.ppermute(value, axis, [(i, (i + steps) % count) for i in range(count)])]
    all_to_all x3 -> x1, starting transfers between devices: 10.5 us -> 3.35 us  [body(): lax.all_to_all(parts, 'ctx', split_axis=1, concat_axis=1, tiled=True)]
    unnamed x20, local copies, waits for them, and re-layouts: 0.07 us -> 7.08 us
    ppermute x0 -> x7, waiting for transfers between devices: none -> 5.37 us  [rotate(): lax.ppermute(value, axis, [(i, (i + steps) % count) for i in range(count)])]
  transfers between devices with their start and end apart: 4 -> 8, of which waited for: 4 -> 4; matrix products, arithmetic and copies ran while one was open for 1% -> 0% of each run, Pallas kernels for 0% -> 0%
where the time goes in v1:
time: 83.5 us; the launch traced here: 83 us
  blocking collectives  31.2 us (37%)
  starting transfers between devices  15.8 us (19%)
  matrix products  15 us (18%)
  local copies, waits for them, and re-layouts  8.56 us (10%)
  waiting for transfers between devices  7.2 us (9%)
  Pallas kernels  2.29 us (3%)
  other arithmetic  1.47 us (2%)
  between operations  1.39 us (2%)
    all_to_all x2, blocking collectives, gather_every(): return lax.all_to_all(copies, BOTH, split_axis=0, concat_axis=0, tiled=True)  21.3 us
    ppermute x7, starting transfers between devices, rotate(): lax.ppermute(value, axis, [(i, (i + steps) % count) for i in range(count)])  12.5 us
    all_to_all x1, blocking collectives, body(): lax.all_to_all(share, BOTH, split_axis=0, concat_axis=0, tiled=True)  9.93 us
    dot_general x1, matrix products, body(): jnp.dot(activated, w_down, preferred_element_type=jnp.float32)  8.86 us
    unnamed x20, local copies, waits for them, and re-layouts  7.08 us
    ppermute x7, waiting for transfers between devices, rotate(): lax.ppermute(value, axis, [(i, (i + steps) % count) for i in range(count)])  5.37 us
    dot_general x1, matrix products, body(): gate_values = jnp.dot(normed, w_gate, preferred_element_type=jnp.float32)  5.02 us
    all_to_all x1, starting transfers between devices, body(): lax.all_to_all(parts, 'ctx', split_axis=1, concat_axis=1, tiled=True)  3.35 us
  transfers between devices with their start and end apart: 8, of which 4 were waited for; matrix products, arithmetic and copies ran while one was open for 0% of the time, Pallas kernels for 0%

profile of v1, /device:TPU:0, one launch (start us, length us, event | category | flops | bytes accessed | tf_op | source)
XLA Modules:
  0.0 83.0 jit_solution(6002112134471898154)
XLA Ops:
  0.6 6.1 %collective-permute-start.6 = (bf16[1,8,128]{2,1,0:T(8,128)(2,1)}, bf16[1,8,128]{2,1,0:T(8,128)(2,1)S(1)}, u32[]{:S(2)}, u32[]{:S(2)}) collective-permute-start(bf16[1,8,128]{2,1,0:T(8,128)(2,1)} %q_ref.1), channel_id=1, source_target_pairs={{0,28},{4,0},{8,4},{12,8},{16,12},{20,16},{24,20},{28,24},{1,29},{... | collective-permute-start | bytes 6152 | tf_op jit(solution)/shard_map/ppermute | solution.py:138
  7.2 3.0 %collective-permute-start.3 = (bf16[1,8,128]{2,1,0:T(8,128)(2,1)}, bf16[1,8,128]{2,1,0:T(8,128)(2,1)S(1)}, u32[]{:S(2)}, u32[]{:S(2)}) collective-permute-start(bf16[1,8,128]{2,1,0:T(8,128)(2,1)} %q_ref.1), channel_id=1, source_target_pairs={{0,16},{4,20},{8,24},{12,28},{16,0},{20,4},{24,8},{28,12},{1,17},{... | collective-permute-start | bytes 6152 | tf_op jit(solution)/shard_map/ppermute | solution.py:138
  10.1 1.9 %collective-permute-start.1 = (bf16[1,8,128]{2,1,0:T(8,128)(2,1)}, bf16[1,8,128]{2,1,0:T(8,128)(2,1)S(1)}, u32[]{:S(2)}, u32[]{:S(2)}) collective-permute-start(bf16[1,8,128]{2,1,0:T(8,128)(2,1)} %q_ref.1), channel_id=1, source_target_pairs={{0,8},{4,12},{8,16},{12,20},{16,24},{20,28},{24,0},{28,4},{1,9},{5... | collective-permute-start | bytes 6152 | tf_op jit(solution)/shard_map/ppermute | solution.py:138
  12.0 1.1 %collective-permute-start = (bf16[1,8,128]{2,1,0:T(8,128)(2,1)}, bf16[1,8,128]{2,1,0:T(8,128)(2,1)S(1)}, u32[]{:S(2)}, u32[]{:S(2)}) collective-permute-start(bf16[1,8,128]{2,1,0:T(8,128)(2,1)} %q_ref.1), channel_id=1, source_target_pairs={{0,4},{4,8},{8,12},{12,16},{16,20},{20,24},{24,28},{28,0},{1,5},{5... | collective-permute-start | bytes 6152 | tf_op jit(solution)/shard_map/ppermute | solution.py:138
  13.1 2.6 %collective-permute-done.2.refs_3_ = bf16[1,8,128]{2,1,0:T(8,128)(2,1)S(1)} collective-permute-done((bf16[1,8,128]{2,1,0:T(8,128)(2,1)}, bf16[1,8,128]{2,1,0:T(8,128)(2,1)S(1)}, u32[]{:S(2)}, u32[]{:S(2)}) %collective-permute-start.2) | collective-permute-done | bytes 2080 | tf_op jit(solution)/shard_map/ppermute | solution.py:138
  15.7 1.0 %collective-permute-done.1.refs_2_ = bf16[1,8,128]{2,1,0:T(8,128)(2,1)S(1)} collective-permute-done((bf16[1,8,128]{2,1,0:T(8,128)(2,1)}, bf16[1,8,128]{2,1,0:T(8,128)(2,1)S(1)}, u32[]{:S(2)}, u32[]{:S(2)}) %collective-permute-start.1) | collective-permute-done | bytes 2080 | tf_op jit(solution)/shard_map/ppermute | solution.py:138
  16.7 1.8 %collective-permute-done.refs_1_ = bf16[1,8,128]{2,1,0:T(8,128)(2,1)S(1)} collective-permute-done((bf16[1,8,128]{2,1,0:T(8,128)(2,1)}, bf16[1,8,128]{2,1,0:T(8,128)(2,1)S(1)}, u32[]{:S(2)}, u32[]{:S(2)}) %collective-permute-start) | collective-permute-done | bytes 2080 | tf_op jit(solution)/shard_map/ppermute | solution.py:138
  18.5 1.2 %copy-done.1 = bf16[1024,4,128]{2,1,0:T(4,128)(2,1)S(1)} copy-done((bf16[1024,4,128]{2,1,0:T(4,128)(2,1)S(1)}, bf16[1024,4,128]{2,1,0:T(4,128)(2,1)}, u32[]{:S(2)}) %copy-start.1) | copy-done | bytes 1048600
  19.7 1.2 %copy-done.2 = bf16[1024,4,128]{2,1,0:T(4,128)(2,1)S(1)} copy-done((bf16[1024,4,128]{2,1,0:T(4,128)(2,1)S(1)}, bf16[1024,4,128]{2,1,0:T(4,128)(2,1)}, u32[]{:S(2)}) %copy-start.2) | copy-done | bytes 1048600
  20.9 0.7 copy-done.5
  21.6 1.1 %shard_map.149 = (f32[64,128]{1,0:T(8,128)S(1)}, f32[64,128]{1,0:T(8,128)S(1)}) custom-call(s32[1]{0:T(128)} %bitcast.me_ref, bf16[1,8,128]{2,1,0:T(8,128)(2,1)S(1)} %copy-done.5, bf16[1,8,128]{2,1,0:T(8,128)(2,1)S(1)} %collective-permute-done.refs_1_, bf16[1,8,128]{2,1,0:T(8,128)(2,1)S(1)} %collective-permute-done.1.refs_2_, ...), custom_call_target="tpu_custom_call" | custom-call | tf_op jit(solution)/shard_map/pallas_call | solution.py:60
  23.4 3.3 %all-to-all-start = ((f32[2,8,8,128]{3,2,0,1:T(8,128)}), f32[2,8,8,128]{3,2,0,1:T(8,128)S(1)}, u32[]{:S(2)}, u32[]{:S(2)}) async-start(f32[2,8,8,128]{3,2,0,1:T(8,128)} %pad_maximum_fusion), calls=%async_computation | async-start | bytes 131072 | tf_op jit(solution)/shard_map/all_to_all | solution.py:173
  27.4 0.9 %copy-done.3 = bf16[1,256,4,128]{3,2,1,0:T(4,128)(2,1)S(1)} copy-done((bf16[1,256,4,128]{3,2,1,0:T(4,128)(2,1)S(1)}, bf16[1,256,4,128]{3,2,1,0:T(4,128)(2,1)}, u32[]{:S(2)}) %copy-start.3) | copy-done | bytes 262168
  28.3 0.9 %copy-done.4 = bf16[1,256,4,128]{3,2,1,0:T(4,128)(2,1)S(1)} copy-done((bf16[1,256,4,128]{3,2,1,0:T(4,128)(2,1)S(1)}, bf16[1,256,4,128]{3,2,1,0:T(4,128)(2,1)}, u32[]{:S(2)}) %copy-start.4) | copy-done | bytes 262168
  29.3 0.7 copy-done.6
  31.7 1.8 %all-to-all-done = f32[2,8,8,128]{3,2,0,1:T(8,128)S(1)} async-done(((f32[2,8,8,128]{3,2,0,1:T(8,128)}), f32[2,8,8,128]{3,2,0,1:T(8,128)S(1)}, u32[]{:S(2)}, u32[]{:S(2)}) %all-to-all-start) | async-done | bytes 65568 | tf_op jit(solution)/shard_map/all_to_all | solution.py:173
  33.6 0.8 shard_map.151
  34.3 0.7 broadcast_in_dim.10
  35.0 11.4 %all_to_all.20 = bf16[32,8,128]{2,1,0:T(8,128)(2,1)S(1)} all-to-all(bf16[32,8,128]{2,1,0:T(8,128)(2,1)S(1)} %broadcast_in_dim.10), channel_id=1, replica_groups=mesh['ctx'=8,'head'=4] {'ctx','head'}, dimensions={0} | all-to-all | bytes 131072 | tf_op jit(solution)/shard_map/all_to_all | solution.py:143
  46.4 1.1 %fusion.1 = bf16[8,168]{1,0:T(8,128)(2,1)S(1)} fusion(bf16[8,4096]{1,0:T(8,128)(2,1)S(1)} %reshape.29, bf16[4096,168]{0,1:T(8,128)(2,1)S(1)} %copy-done, bf16[8,168]{1,0:T(8,128)(2,1)} %param.23), kind=kOutput, calls=%fused_computation.4 | convolution fusion | flops 11014080 | bytes 1447168 | tf_op jit(solution)/shard_map/dot_general | solution.py:177
  47.6 9.9 %all_to_all.21 = bf16[32,8,168]{2,1,0:T(8,128)(2,1)S(1)} all-to-all(bf16[32,8,168]{2,1,0:T(8,128)(2,1)S(1)} %broadcast_in_dim.11), channel_id=1, replica_groups=mesh['ctx'=8,'head'=4] {'ctx','head'}, dimensions={0} | all-to-all | bytes 172032 | tf_op jit(solution)/shard_map/all_to_all | solution.py:143
  58.0 5.0 %fusion.19 = f32[8,672]{1,0:T(8,128)S(1)} fusion(bf16[5376,672]{0,1:T(8,128)(2,1)} %param.25, f32[8,5376]{1,0:T(8,128)S(1)} %reshape.31, f32[5376]{0:T(1024)} %param.24, f32[8]{0:T(128)S(1)} %add_rsqrt_fusion), kind=kOutput, calls=%fused_computation.30 | convolution fusion | flops 57931776 | bytes 7440416 | tf_op jit(solution)/shard_map/dot_general | solution.py:185
  63.1 8.9 %convolution_convert_fusion = bf16[8,5376]{1,0:T(8,128)(2,1)S(1)} fusion(bf16[672,5376]{1,0:T(8,128)(2,1)} %param.27, bf16[5376,672]{0,1:T(8,128)(2,1)} %param.26, f32[8,672]{1,0:T(8,128)S(1)} %fusion.19, f32[8,5376]{1,0:T(8,128)S(1)} %reshape.31, f32[5376]{0:T(1024)S(1)} %copy-done.9, f32[8]{0:T(128)S(1)} %add_rsqrt_fusion), kind=kOutput, calls=%fused_computation | convolution fusion | flops 115831296 | bytes 14751776 | tf_op jit(solution)/shard_map/dot_general | solution.py:188
  72.4 9.9 %all_to_all.22 = bf16[32,8,168]{2,1,0:T(8,128)(2,1)S(1)} all-to-all(bf16[32,8,168]{2,1,0:T(8,128)(2,1)S(1)} %bitcast.20), channel_id=1, replica_groups=mesh['ctx'=8,'head'=4] {'ctx','head'}, dimensions={0} | all-to-all | bytes 172032 | tf_op jit(solution)/shard_map/all_to_all | solution.py:190
  (35 shorter events, 4.5 us)
Async XLA Ops:
  0.6 45.8 %copy-start = (bf16[4096,168]{0,1:T(8,128)(2,1)S(1)}, bf16[4096,168]{0,1:T(8,128)(2,1)}, u32[]{:S(2)}) copy-start(bf16[4096,168]{0,1:T(8,128)(2,1)} %param.22) | copy-start | bytes 4128772
  0.6 9.5 %collective-permute-start.6 = (bf16[1,8,128]{2,1,0:T(8,128)(2,1)}, bf16[1,8,128]{2,1,0:T(8,128)(2,1)S(1)}, u32[]{:S(2)}, u32[]{:S(2)}) collective-permute-start(bf16[1,8,128]{2,1,0:T(8,128)(2,1)} %q_ref.1), channel_id=1, source_target_pairs={{0,28},{4,0},{8,4},{12,8},{16,12},{20,16},{24,20},{28,24},{1,29},{... | collective-permute-start | bytes 6152 | tf_op jit(solution)/shard_map/ppermute | solution.py:138
  6.7 5.3 %collective-permute-start.5 = (bf16[1,8,128]{2,1,0:T(8,128)(2,1)}, bf16[1,8,128]{2,1,0:T(8,128)(2,1)S(1)}, u32[]{:S(2)}, u32[]{:S(2)}) collective-permute-start(bf16[1,8,128]{2,1,0:T(8,128)(2,1)} %q_ref.1), channel_id=1, source_target_pairs={{0,24},{4,28},{8,0},{12,4},{16,8},{20,12},{24,16},{28,20},{1,25},{... | collective-permute-start | bytes 6152 | tf_op jit(solution)/shard_map/ppermute | solution.py:138
  7.2 6.0 %collective-permute-start.4 = (bf16[1,8,128]{2,1,0:T(8,128)(2,1)}, bf16[1,8,128]{2,1,0:T(8,128)(2,1)S(1)}, u32[]{:S(2)}, u32[]{:S(2)}) collective-permute-start(bf16[1,8,128]{2,1,0:T(8,128)(2,1)} %q_ref.1), channel_id=1, source_target_pairs={{0,20},{4,24},{8,28},{12,0},{16,4},{20,8},{24,12},{28,16},{1,21},{... | collective-permute-start | bytes 6152 | tf_op jit(solution)/shard_map/ppermute | solution.py:138
  7.2 6.0 %collective-permute-start.3 = (bf16[1,8,128]{2,1,0:T(8,128)(2,1)}, bf16[1,8,128]{2,1,0:T(8,128)(2,1)S(1)}, u32[]{:S(2)}, u32[]{:S(2)}) collective-permute-start(bf16[1,8,128]{2,1,0:T(8,128)(2,1)} %q_ref.1), channel_id=1, source_target_pairs={{0,16},{4,20},{8,24},{12,28},{16,0},{20,4},{24,8},{28,12},{1,17},{... | collective-permute-start | bytes 6152 | tf_op jit(solution)/shard_map/ppermute | solution.py:138
  10.1 5.6 %collective-permute-start.2 = (bf16[1,8,128]{2,1,0:T(8,128)(2,1)}, bf16[1,8,128]{2,1,0:T(8,128)(2,1)S(1)}, u32[]{:S(2)}, u32[]{:S(2)}) collective-permute-start(bf16[1,8,128]{2,1,0:T(8,128)(2,1)} %q_ref.1), channel_id=1, source_target_pairs={{0,12},{4,16},{8,20},{12,24},{16,28},{20,0},{24,4},{28,8},{1,13},{... | collective-permute-start | bytes 6152 | tf_op jit(solution)/shard_map/ppermute | solution.py:138
  10.1 6.6 %collective-permute-start.1 = (bf16[1,8,128]{2,1,0:T(8,128)(2,1)}, bf16[1,8,128]{2,1,0:T(8,128)(2,1)S(1)}, u32[]{:S(2)}, u32[]{:S(2)}) collective-permute-start(bf16[1,8,128]{2,1,0:T(8,128)(2,1)} %q_ref.1), channel_id=1, source_target_pairs={{0,8},{4,12},{8,16},{12,20},{16,24},{20,28},{24,0},{28,4},{1,9},{5... | collective-permute-start | bytes 6152 | tf_op jit(solution)/shard_map/ppermute | solution.py:138
  12.0 6.5 %collective-permute-start = (bf16[1,8,128]{2,1,0:T(8,128)(2,1)}, bf16[1,8,128]{2,1,0:T(8,128)(2,1)S(1)}, u32[]{:S(2)}, u32[]{:S(2)}) collective-permute-start(bf16[1,8,128]{2,1,0:T(8,128)(2,1)} %q_ref.1), channel_id=1, source_target_pairs={{0,4},{4,8},{8,12},{12,16},{16,20},{20,24},{24,28},{28,0},{1,5},{5... | collective-permute-start | bytes 6152 | tf_op jit(solution)/shard_map/ppermute | solution.py:138
  18.5 1.2 %copy-start.1 = (bf16[1024,4,128]{2,1,0:T(4,128)(2,1)S(1)}, bf16[1024,4,128]{2,1,0:T(4,128)(2,1)}, u32[]{:S(2)}) copy-start(bf16[1024,4,128]{2,1,0:T(4,128)(2,1)} %refs_8_.1) | copy-start | bytes 3145732
  19.7 1.2 %copy-start.2 = (bf16[1024,4,128]{2,1,0:T(4,128)(2,1)S(1)}, bf16[1024,4,128]{2,1,0:T(4,128)(2,1)}, u32[]{:S(2)}) copy-start(bf16[1024,4,128]{2,1,0:T(4,128)(2,1)} %refs_9_.1) | copy-start | bytes 3145732
  20.9 0.7 copy-start.5
  21.6 41.4 %copy-start.9 = (f32[5376]{0:T(1024)S(1)}, f32[5376]{0:T(1024)}, u32[]{:S(2)}) copy-start(f32[5376]{0:T(1024)} %param.24) | copy-start | bytes 64516
  23.4 10.2 %all-to-all-start = ((f32[2,8,8,128]{3,2,0,1:T(8,128)}), f32[2,8,8,128]{3,2,0,1:T(8,128)S(1)}, u32[]{:S(2)}, u32[]{:S(2)}) async-start(f32[2,8,8,128]{3,2,0,1:T(8,128)} %pad_maximum_fusion), calls=%async_computation | async-start | bytes 131072 | tf_op jit(solution)/shard_map/all_to_all | solution.py:173
  27.4 1.0 %copy-start.3 = (bf16[1,256,4,128]{3,2,1,0:T(4,128)(2,1)S(1)}, bf16[1,256,4,128]{3,2,1,0:T(4,128)(2,1)}, u32[]{:S(2)}) copy-start(bf16[1,256,4,128]{3,2,1,0:T(4,128)(2,1)} %k_ref.1) | copy-start | bytes 786436
  28.3 0.9 %copy-start.4 = (bf16[1,256,4,128]{3,2,1,0:T(4,128)(2,1)S(1)}, bf16[1,256,4,128]{3,2,1,0:T(4,128)(2,1)}, u32[]{:S(2)}) copy-start(bf16[1,256,4,128]{3,2,1,0:T(4,128)(2,1)} %v_ref.1) | copy-start | bytes 786436
  29.3 0.7 copy-start.6
  30.0 0.7 copy-start.7
  30.6 0.7 copy-start.8

commit v2 on v1

v2 whole, which is shorter than its diff:
```python
import functools

import jax
import jax.numpy as jnp
from jax import lax
from jax.experimental import pallas as pl
from jax.experimental.pallas import tpu as pltpu
from jax.sharding import PartitionSpec as P

SCORE_SCALE = 168.0 ** (-0.5)
NORM_EPSILON = 1e-06
MASKED = -1e30
MIB = 1024 * 1024
GRANT = 60 * MIB
LOADS = 4
FORWARD_LOADS = 6
BOTH = ("ctx", "head")


def head_match(shape, heads, kv_heads):
    group = heads // kv_heads
    row = lax.broadcasted_iota(jnp.int32, shape, 0)
    column = lax.broadcasted_iota(jnp.int32, shape, 1)
    return lax.rem(row, heads) // group == lax.rem(column, kv_heads), column // kv_heads


def dot_rows(left, right):
    return lax.dot_general(left, right, (((1,), (1,)), ((), ())), preferred_element_type=jnp.float32)


def stat_rows(row_max, row_total, shape):
    lane = lax.broadcasted_iota(jnp.int32, shape, 1)
    return jnp.where(lane == 0, row_max, row_total)


def row_chunks(rows, most):
    for count in range(most, 1, -1):
        if rows % (16 * count) == 0:
            return count
    return 1


def start_chunks(source, target, sems, first, most):
    count = row_chunks(source.shape[0], most)
    size = source.shape[0] // count
    copies = []
    for chunk in range(count):
        rows = pl.ds(chunk * size, size)
        copies.append(pltpu.make_async_copy(source.at[rows], target.at[rows], sems.at[first + chunk]))
    for copy in copies:
        copy.start()
    return copies


def suffix_kernel(
    length_ref, q_hbm, kn_hbm, vn_hbm, ks_hbm, vs_hbm, part_ref, q_ref, kn_ref, vn_ref, ks_ref, vs_ref, sems
):
    copies = [
        pltpu.make_async_copy(source, target, sems.at[place])
        for place, (source, target) in enumerate(
            ((q_hbm, q_ref), (kn_hbm, kn_ref), (ks_hbm, ks_ref), (vn_hbm, vn_ref), (vs_hbm, vs_ref))
        )
    ]
    for copy in copies:
        copy.start()
    unused, slots, kv_heads, width = ks_ref.shape
    heads = q_ref.shape[1]
    for copy in copies[:3]:
        copy.wait()
    queries = q_ref[0]
    scores = SCORE_SCALE * dot_rows(queries, ks_ref[0].reshape(slots * kv_heads, width))
    new_scores = SCORE_SCALE * dot_rows(queries, kn_ref[0])
    match, slot = head_match(scores.shape, heads, kv_heads)
    new_match, unused = head_match(new_scores.shape, heads, kv_heads)
    scores = jnp.where(match & (slot < length_ref[0]), scores, MASKED)
    new_scores = jnp.where(new_match, new_scores, MASKED)
    row_max = jnp.maximum(
        jnp.max(scores, axis=1, keepdims=True), jnp.max(new_scores, axis=1, keepdims=True)
    )
    weights = jnp.exp(scores - row_max).astype(jnp.bfloat16)
    new_weights = jnp.exp(new_scores - row_max).astype(jnp.bfloat16)
    row_total = jnp.sum(weights.astype(jnp.float32), axis=1, keepdims=True) + jnp.sum(
        new_weights.astype(jnp.float32), axis=1, keepdims=True
    )
    for copy in copies[3:]:
        copy.wait()
    row_sum = jnp.dot(
        weights, vs_ref[0].reshape(slots * kv_heads, width), preferred_element_type=jnp.float32
    ) + jnp.dot(new_weights, vn_ref[0], preferred_element_type=jnp.float32)
    part_ref[0] = row_sum
    part_ref[1] = stat_rows(row_max, row_total, row_sum.shape)


def suffix_partials(lengths, *operands):
    return pl.pallas_call(
        suffix_kernel,
        out_shape=jax.ShapeDtypeStruct((2, *operands[0].shape[1:]), jnp.float32),
        in_specs=[pl.BlockSpec(memory_space=pltpu.SMEM)] + [pl.BlockSpec(memory_space=pl.ANY)] * 5,
        scratch_shapes=[pltpu.VMEM(operand.shape, operand.dtype) for operand in operands]
        + [pltpu.SemaphoreType.DMA((5,))],
        compiler_params=pltpu.CompilerParams(vmem_limit_bytes=GRANT),
        cost_estimate=pl.CostEstimate(flops=10**7, bytes_accessed=2 * MIB, transcendentals=10**4),
    )(lengths, *operands)


def prefix_kernel(me_ref, *refs):
    arrived, (k_hbm, v_hbm, part_ref, ordered_ref, k_ref, v_ref, sems) = refs[:-7], refs[-7:]
    key_copies = start_chunks(k_hbm, k_ref, sems, 0, LOADS)
    value_copies = start_chunks(v_hbm, v_ref, sems, LOADS, LOADS)
    place = 0
    for ref in arrived:
        for source in range(ref.shape[0]):
            ordered_ref[lax.bitwise_xor(me_ref[0], place)] = ref[source]
            place += 1
    count, heads, width = ordered_ref.shape
    positions, kv_heads, unused = k_ref.shape
    size = positions // len(key_copies)
    queries = ordered_ref[...].reshape(count * heads, width)
    chunks = []
    for chunk, copy in enumerate(key_copies):
        copy.wait()
        keys = k_ref[chunk * size : (chunk + 1) * size].reshape(size * kv_heads, width)
        scores = SCORE_SCALE * dot_rows(queries, keys)
        match, unused = head_match(scores.shape, heads, kv_heads)
        chunks.append(jnp.where(match, scores, MASKED))
    row_max = functools.reduce(
        jnp.maximum, [jnp.max(scores, axis=1, keepdims=True) for scores in chunks]
    )
    row_total = jnp.zeros_like(row_max)
    row_sum = jnp.zeros((count * heads, width), jnp.float32)
    for chunk, copy in enumerate(value_copies):
        weights = jnp.exp(chunks[chunk] - row_max).astype(jnp.bfloat16)
        row_total += jnp.sum(weights.astype(jnp.float32), axis=1, keepdims=True)
        copy.wait()
        values = v_ref[chunk * size : (chunk + 1) * size].reshape(size * kv_heads, width)
        row_sum += jnp.dot(weights, values, preferred_element_type=jnp.float32)
    stats = stat_rows(row_max, row_total, row_sum.shape)
    part_ref[:, 0] = row_sum.reshape(count, heads, width)
    part_ref[:, 1] = stats.reshape(count, heads, width)


def prefix_partials(me, arrived, k_prefix, v_prefix):
    whole = pl.BlockSpec(memory_space=pltpu.VMEM)
    unused, heads, width = arrived[0].shape
    count = sum(piece.shape[0] for piece in arrived)
    return pl.pallas_call(
        prefix_kernel,
        out_shape=jax.ShapeDtypeStruct((count, 2, heads, width), jnp.float32),
        in_specs=[pl.BlockSpec(memory_space=pltpu.SMEM)]
        + [whole] * len(arrived)
        + [pl.BlockSpec(memory_space=pl.ANY)] * 2,
        scratch_shapes=[
            pltpu.VMEM((count, heads, width), jnp.bfloat16),
            pltpu.VMEM(k_prefix.shape, k_prefix.dtype),
            pltpu.VMEM(v_prefix.shape, v_prefix.dtype),
            pltpu.SemaphoreType.DMA((2 * LOADS,)),
        ],
        compiler_params=pltpu.CompilerParams(vmem_limit_bytes=GRANT),
    )(me.astype(jnp.int32)[None], *arrived, k_prefix, v_prefix)


def join_kernel(part_ref, suffix_ref, out_ref, copies_ref):
    sources = part_ref.shape[0]
    suffix_max = suffix_ref[1, :, 0:1]
    joint_max = suffix_max
    for source in range(sources):
        joint_max = jnp.maximum(joint_max, part_ref[source, 1, :, 0:1])
    factor = jnp.exp(suffix_max - joint_max)
    total = suffix_ref[1, :, 1:2] * factor
    summed = suffix_ref[0] * factor
    for source in range(sources):
        factor = jnp.exp(part_ref[source, 1, :, 0:1] - joint_max)
        total = total + part_ref[source, 1, :, 1:2] * factor
        summed = summed + part_ref[source, 0] * factor
    attention = (summed / total).astype(jnp.bfloat16)
    out_ref[...] = attention
    for place in range(copies_ref.shape[0]):
        copies_ref[place] = attention


def join_partials(parts, suffix_part, devices):
    shape = suffix_part.shape[1:]
    return pl.pallas_call(
        join_kernel,
        out_shape=(
            jax.ShapeDtypeStruct(shape, jnp.bfloat16),
            jax.ShapeDtypeStruct((devices, *shape), jnp.bfloat16),
        ),
        compiler_params=pltpu.CompilerParams(vmem_limit_bytes=8 * MIB),
    )(parts, suffix_part)


def project_kernel(rows_ref, w_ref, residual_ref, out_ref, copies_ref):
    projected = dot_rows(rows_ref[...], w_ref[...])
    hidden = (residual_ref[...].astype(jnp.float32) + projected).astype(jnp.bfloat16)
    out_ref[...] = hidden
    for place in range(copies_ref.shape[0]):
        copies_ref[place] = hidden


def project(rows, w_out, residual, devices):
    return pl.pallas_call(
        project_kernel,
        out_shape=(
            jax.ShapeDtypeStruct(residual.shape, jnp.bfloat16),
            jax.ShapeDtypeStruct((devices, *residual.shape), jnp.bfloat16),
        ),
        compiler_params=pltpu.CompilerParams(vmem_limit_bytes=12 * MIB),
    )(rows, w_out, residual)


def forward_kernel(
    state_ref, gain_ref, gate_hbm, up_hbm, down_hbm, out_ref, gate_ref, up_ref, down_ref, sems
):
    units = gate_ref.shape[0]
    count = row_chunks(units, FORWARD_LOADS)
    size = units // count
    copies = []
    for chunk in range(count):
        rows = pl.ds(chunk * size, size)
        for place, (source, target) in enumerate(
            ((gate_hbm, gate_ref), (up_hbm, up_ref), (down_hbm, down_ref))
        ):
            copies.append(
                pltpu.make_async_copy(source.at[rows], target.at[rows], sems.at[3 * chunk + place])
            )
            copies[-1].start()
    state = state_ref[...].astype(jnp.float32)
    mean_square = jnp.mean(state * state, axis=-1, keepdims=True)
    normed = (state * lax.rsqrt(mean_square + NORM_EPSILON) * gain_ref[...]).astype(jnp.bfloat16)
    total = jnp.zeros(out_ref.shape, jnp.float32)
    for chunk in range(count):
        rows = slice(chunk * size, (chunk + 1) * size)
        copies[3 * chunk].wait()
        gate_values = dot_rows(normed, gate_ref[rows])
        copies[3 * chunk + 1].wait()
        up_values = dot_rows(normed, up_ref[rows])
        activated = (jax.nn.gelu(gate_values, approximate=True) * up_values).astype(jnp.bfloat16)
        copies[3 * chunk + 2].wait()
        total += jnp.dot(activated, down_ref[rows], preferred_element_type=jnp.float32)
    out_ref[...] = total.astype(jnp.bfloat16)


def forward(state, gain, w_gate, w_up, w_down):
    whole = pl.BlockSpec(memory_space=pltpu.VMEM)
    return pl.pallas_call(
        forward_kernel,
        out_shape=jax.ShapeDtypeStruct(state.shape, jnp.bfloat16),
        in_specs=[whole, whole] + [pl.BlockSpec(memory_space=pl.ANY)] * 3,
        scratch_shapes=[pltpu.VMEM(w.shape, w.dtype) for w in (w_gate, w_up, w_down)]
        + [pltpu.SemaphoreType.DMA((3 * FORWARD_LOADS,))],
        compiler_params=pltpu.CompilerParams(vmem_limit_bytes=56 * MIB),
    )(state, gain, w_gate, w_up, w_down)


def gather_by_xor(value, axis):
    count = lax.axis_size(axis)
    pieces = [value]
    step = 1
    while step < count:
        partners = [(i, i ^ step) for i in range(count)]
        pieces.append(lax.ppermute(jnp.concatenate(pieces, axis=0), axis, partners))
        step *= 2
    return pieces


def exchange(copies):
    return lax.all_to_all(copies, BOTH, split_axis=0, concat_axis=0, tiled=True)


def body(
    queries,
    k_new,
    v_new,
    k_suffix,
    v_suffix,
    lengths,
    k_prefix,
    v_prefix,
    w_out,
    residual,
    norm_gain,
    w_gate,
    w_up,
    w_down,
):
    devices = lax.axis_size("ctx") * lax.axis_size("head")
    completions, columns = residual.shape

    arrived = gather_by_xor(queries, "ctx")
    suffix_part = suffix_partials(lengths, queries, k_new, v_new, k_suffix, v_suffix)
    parts = prefix_partials(lax.axis_index("ctx"), arrived, k_prefix, v_prefix)
    parts = lax.all_to_all(parts, "ctx", split_axis=0, concat_axis=0, tiled=True)
    attention, copies = join_partials(parts, suffix_part, devices)

    rows = exchange(copies).reshape(completions, w_out.shape[0])
    hidden_part, copies = project(rows, w_out.T, residual, devices)

    hidden_state = jnp.swapaxes(exchange(copies), 0, 1).reshape(completions, devices * columns)
    share = forward(hidden_state, norm_gain[None], w_gate.T, w_up.T, w_down)
    share = jnp.swapaxes(share.reshape(completions, devices, columns), 0, 1)
    summed = jnp.sum(exchange(share).astype(jnp.float32), axis=0)
    next_hidden = (hidden_part.astype(jnp.float32) + summed).astype(jnp.bfloat16)
    return (attention[None], next_hidden)


def solution(mesh):
    placed = (
        P("ctx", "head", None),
        P("ctx", "head", None),
        P("ctx", "head", None),
        P("ctx", None, "head", None),
        P("ctx", None, "head", None),
        P("ctx"),
        P("ctx", "head", None),
        P("ctx", "head", None),
        P(None, BOTH),
        P(None, BOTH),
        P(),
        P(None, BOTH),
        P(None, BOTH),
        P(BOTH, None),
    )
    return jax.shard_map(
        body,
        mesh=mesh,
        in_specs=placed,
        out_specs=(P("ctx", "head", None), P(None, BOTH)),
        check_vma=False,
    )
```

time: 83.5 us -> 84.3 us (level)
  Pallas kernels: 2.29 us -> 21.2 us
  matrix products: 15 us -> 0 us
  blocking collectives: 31.2 us -> 19.3 us
  waiting for transfers between devices: 7.2 us -> 15.9 us
  local copies, waits for them, and re-layouts: 8.56 us -> 6.89 us
  starting transfers between devices: 15.8 us -> 16.9 us
    pallas_call x3 -> x5, Pallas kernels: 2.29 us -> 21.2 us  [the longest x1 12.9 us: forward(): pl.pallas_call(forward_kernel, out_shape=jax.ShapeDtypeStruct(state.shape...]
    dot_general x3 -> x0, matrix products: 15 us -> none  [the longest x1 8.86 us: body(): jnp.dot(activated, w_down, preferred_element_type=jnp.float32)]
    all_to_all x3 -> x2, blocking collectives: 31.2 us -> 19.3 us  [exchange(): return lax.all_to_all(copies, BOTH, split_axis=0, concat_axis=0, tiled=True)]
    all_to_all x1 -> x2, waiting for transfers between devices: 1.84 us -> 11 us  [the longest x1 6.87 us: exchange(): return lax.all_to_all(copies, BOTH, split_axis=0, concat_axis=0, tiled=True)]
    all_to_all x1 -> x2, starting transfers between devices: 3.35 us -> 8.75 us  [the longest x1 6.18 us: body(): lax.all_to_all(parts, 'ctx', split_axis=0, concat_axis=0, tiled=True)]
    ppermute x7 -> x3, starting transfers between devices: 12.5 us -> 8.14 us  [gather_by_xor(): pieces.append(lax.ppermute(jnp.concatenate(pieces, axis=0), axis, partners))]
    unnamed x20 -> x12, local copies, waits for them, and re-layouts: 7.08 us -> 3.31 us
    concatenate x0 -> x2, other arithmetic: none -> 1.38 us  [gather_by_xor(): pieces.append(lax.ppermute(jnp.concatenate(pieces, axis=0), axis, partners))]
  transfers between devices with their start and end apart: 8 -> 5, of which waited for: 4 -> 5; matrix products, arithmetic and copies ran while one was open for 0% -> 2% of each run, Pallas kernels for 0% -> 3%
where the time goes in v2:
time: 84.3 us; the launch traced here: 83.6 us
  Pallas kernels  21.2 us (25%)
  blocking collectives  19.3 us (23%)
  starting transfers between devices  16.9 us (20%)
  waiting for transfers between devices  15.9 us (19%)
  local copies, waits for them, and re-layouts  6.89 us (8%)
  other arithmetic  2.02 us (2%)
  between operations  1.36 us (2%)
    all_to_all x2, blocking collectives, exchange(): return lax.all_to_all(copies, BOTH, split_axis=0, concat_axis=0, tiled=True)  19.3 us
    pallas_call x1, Pallas kernels, forward(): pl.pallas_call(forward_kernel, out_shape=jax.ShapeDtypeStruct(state.shape...  12.9 us
    ppermute x3, starting transfers between devices, gather_by_xor(): pieces.append(lax.ppermute(jnp.concatenate(pieces, axis=0), axis, partners))  8.14 us
    all_to_all x1, waiting for transfers between devices, exchange(): return lax.all_to_all(copies, BOTH, split_axis=0, concat_axis=0, tiled=True)  6.87 us
    all_to_all x1, starting transfers between devices, body(): lax.all_to_all(parts, 'ctx', split_axis=0, concat_axis=0, tiled=True)  6.18 us
    ppermute x3, waiting for transfers between devices, gather_by_xor(): pieces.append(lax.ppermute(jnp.concatenate(pieces, axis=0), axis, partners))  4.99 us
    pallas_call x1, Pallas kernels, prefix_partials(): pl.pallas_call(prefix_kernel, out_shape=jax.ShapeDtypeStruct((count, 2, h...  4.26 us
    all_to_all x1, waiting for transfers between devices, body(): lax.all_to_all(parts, 'ctx', split_axis=0, concat_axis=0, tiled=True)  4.09 us
  transfers between devices with their start and end apart: 5, of which 5 were waited for; matrix products, arithmetic and copies ran while one was open for 2% of the time, Pallas kernels for 3%

profile of v2, /device:TPU:0, one launch (start us, length us, event | category | flops | bytes accessed | tf_op | source)
XLA Modules:
  0.0 83.6 jit_solution(2185683635400806060)
XLA Ops:
  0.6 3.0 %collective-permute-start = (bf16[1,8,128]{2,1,0:T(8,128)(2,1)}, bf16[1,8,128]{2,1,0:T(8,128)(2,1)S(1)}, u32[]{:S(2)}, u32[]{:S(2)}) collective-permute-start(bf16[1,8,128]{2,1,0:T(8,128)(2,1)} %q_hbm.1), channel_id=1, source_target_pairs={{0,4},{4,0},{8,12},{12,8},{16,20},{20,16},{24,28},{28,24},{1,5},{5... | collective-permute-start | bytes 6152 | tf_op jit(solution)/shard_map/ppermute | solution.py:262
  3.7 1.8 %collective-permute-done.refs_1_ = bf16[1,8,128]{2,1,0:T(8,128)(2,1)S(1)} collective-permute-done((bf16[1,8,128]{2,1,0:T(8,128)(2,1)}, bf16[1,8,128]{2,1,0:T(8,128)(2,1)S(1)}, u32[]{:S(2)}, u32[]{:S(2)}) %collective-permute-start) | collective-permute-done | bytes 2080 | tf_op jit(solution)/shard_map/ppermute | solution.py:262
  5.4 0.7 pad_maximum_fusion.1
  6.1 2.1 %collective-permute-start.1 = (bf16[2,8,128]{2,1,0:T(8,128)(2,1)S(1)}, bf16[2,8,128]{2,1,0:T(8,128)(2,1)S(1)}, u32[]{:S(2)}, u32[]{:S(2)}) collective-permute-start(bf16[2,8,128]{2,1,0:T(8,128)(2,1)S(1)} %pad_maximum_fusion.1), channel_id=1, source_target_pairs={{0,8},{4,12},{8,0},{12,4},{16,24},{20,28},{24,16},{28,20},{1,9},{5... | collective-permute-start | bytes 12296 | tf_op jit(solution)/shard_map/ppermute | solution.py:262
  8.2 1.6 %collective-permute-done.1.refs_2_ = bf16[2,8,128]{2,1,0:T(8,128)(2,1)S(1)} collective-permute-done((bf16[2,8,128]{2,1,0:T(8,128)(2,1)S(1)}, bf16[2,8,128]{2,1,0:T(8,128)(2,1)S(1)}, u32[]{:S(2)}, u32[]{:S(2)}) %collective-permute-start.1) | collective-permute-done | bytes 4128 | tf_op jit(solution)/shard_map/ppermute | solution.py:262
  9.8 0.7 pad_maximum_fusion
  10.5 3.0 %collective-permute-start.2 = (bf16[4,8,128]{2,1,0:T(8,128)(2,1)S(1)}, bf16[4,8,128]{2,1,0:T(8,128)(2,1)S(1)}, u32[]{:S(2)}, u32[]{:S(2)}) collective-permute-start(bf16[4,8,128]{2,1,0:T(8,128)(2,1)S(1)} %pad_maximum_fusion), channel_id=1, source_target_pairs={{0,16},{4,20},{8,24},{12,28},{16,0},{20,4},{24,8},{28,12},{1,17},{... | collective-permute-start | bytes 24584 | tf_op jit(solution)/shard_map/ppermute | solution.py:262
  13.5 1.6 %collective-permute-done.2.refs_3_ = bf16[4,8,128]{2,1,0:T(8,128)(2,1)S(1)} collective-permute-done((bf16[4,8,128]{2,1,0:T(8,128)(2,1)S(1)}, bf16[4,8,128]{2,1,0:T(8,128)(2,1)S(1)}, u32[]{:S(2)}, u32[]{:S(2)}) %collective-permute-start.2) | collective-permute-done | bytes 8224 | tf_op jit(solution)/shard_map/ppermute | solution.py:262
  15.7 4.3 %shard_map.149 = f32[8,2,8,128]{3,2,1,0:T(8,128)} custom-call(s32[1]{0:T(128)} %bitcast.me_ref, bf16[1,8,128]{2,1,0:T(8,128)(2,1)} %q_hbm.1, bf16[1,8,128]{2,1,0:T(8,128)(2,1)} %copy-done.3, bf16[2,8,128]{2,1,0:T(8,128)(2,1)} %copy-done.4, bf16[4,8,128]{2,1,0:T(8,128)(2,1)} %copy-done.5, bf16[1024,4,128]{2,1,0:T(4,128)(2,1)} %refs_4_.1, ...), custom_call_target="tpu_custom_call" | custom-call | tf_op jit(solution)/shard_map/pallas_call | solution.py:146
  20.0 6.2 %all-to-all-start = ((f32[8,2,8,128]{3,2,1,0:T(8,128)}), f32[8,2,8,128]{3,2,1,0:T(8,128)S(1)}, u32[]{:S(2)}, u32[]{:S(2)}) async-start(f32[8,2,8,128]{3,2,1,0:T(8,128)} %shard_map.149), calls=%async_computation | async-start | bytes 131072 | tf_op jit(solution)/shard_map/all_to_all | solution.py:293
  26.8 2.2 %shard_map.150.suffix_ref = f32[2,8,128]{2,1,0:T(8,128)} custom-call(s32[1]{0:T(128)S(6)} %copy.21.length_ref, bf16[1,8,128]{2,1,0:T(8,128)(2,1)} %q_hbm.1, bf16[1,4,128]{2,1,0:T(4,128)(2,1)} %kn_hbm.1, bf16[1,4,128]{2,1,0:T(4,128)(2,1)} %vn_hbm.1, bf16[1,256,4,128]{3,2,1,0:T(4,128)(2,1)} %ks_hbm.1, bf16[1,256,4,128]{3,2,1,0:T(4,128)(2,1)} %vs_hbm.1), custom_call_target="tpu_custom_call" | custom-call | flops 10000000 | bytes 2097152 | tf_op jit(solution)/shard_map/pallas_call | solution.py:95
  29.0 4.1 %all-to-all-done.part_ref = f32[8,2,8,128]{3,2,1,0:T(8,128)S(1)} async-done(((f32[8,2,8,128]{3,2,1,0:T(8,128)}), f32[8,2,8,128]{3,2,1,0:T(8,128)S(1)}, u32[]{:S(2)}, u32[]{:S(2)}) %all-to-all-start) | async-done | bytes 65568 | tf_op jit(solution)/shard_map/all_to_all | solution.py:293
  33.1 0.7 copy-done.1
  33.8 0.8 shard_map.151
  34.5 9.3 %all_to_all.20 = bf16[32,8,128]{2,1,0:T(8,128)(2,1)S(1)} all-to-all(bf16[32,8,128]{2,1,0:T(8,128)(2,1)S(1)} %get-tuple-element.7), channel_id=1, replica_groups=mesh['ctx'=8,'head'=4] {'ctx','head'}, dimensions={0} | all-to-all | bytes 131072 | tf_op jit(solution)/shard_map/all_to_all | solution.py:268
  43.9 1.3 %copy-done = bf16[4096,168]{0,1:T(8,128)(2,1)S(1)} copy-done((bf16[4096,168]{0,1:T(8,128)(2,1)S(1)}, bf16[4096,168]{0,1:T(8,128)(2,1)}, u32[]{:S(2)}) %copy-start) | copy-done | bytes 1376280
  45.9 1.2 %shard_map.152 = (bf16[8,168]{1,0:T(8,128)(2,1)S(1)}, bf16[32,8,168]{2,1,0:T(8,128)(2,1)}) custom-call(bf16[8,4096]{1,0:T(8,128)(2,1)S(1)} %reshape.13.rows_ref, bf16[168,4096]{1,0:T(8,128)(2,1)S(1)} %bitcast.9, bf16[8,168]{1,0:T(8,128)(2,1)S(1)} %copy-done.2), custom_call_target="tpu_custom_call" | custom-call | tf_op jit(solution)/shard_map/pallas_call | solution.py:202
  47.1 2.6 %all-to-all-start.2 = ((bf16[32,8,168]{2,1,0:T(8,128)(2,1)}), bf16[32,8,168]{2,1,0:T(8,128)(2,1)S(1)}, u32[]{:S(2)}, u32[]{:S(2)}) async-start(bf16[32,8,168]{2,1,0:T(8,128)(2,1)} %get-tuple-element.9), calls=%async_computation.2 | async-start | bytes 262144 | tf_op jit(solution)/shard_map/all_to_all | solution.py:268
  49.7 1.4 %broadcast_in_dim.11.gain_ref = f32[1,5376]{1,0:T(1,128)} reshape(f32[5376]{0:T(1024)} %param.24) | data formatting | bytes 43008 | tf_op jit(solution)/shard_map/broadcast_in_dim | solution.py:300
  51.0 6.9 %all-to-all-done.2 = bf16[32,8,168]{2,1,0:T(8,128)(2,1)S(1)} async-done(((bf16[32,8,168]{2,1,0:T(8,128)(2,1)}), bf16[32,8,168]{2,1,0:T(8,128)(2,1)S(1)}, u32[]{:S(2)}, u32[]{:S(2)}) %all-to-all-start.2) | async-done | bytes 86048 | tf_op jit(solution)/shard_map/all_to_all | solution.py:268
  57.9 0.8 reshape.14.state_ref
  58.7 12.9 %shard_map.153 = bf16[8,5376]{1,0:T(8,128)(2,1)} custom-call(bf16[8,5376]{1,0:T(8,128)(2,1)} %reshape.14.state_ref, f32[1,5376]{1,0:T(1,128)} %broadcast_in_dim.11.gain_ref, bf16[672,5376]{1,0:T(8,128)(2,1)} %bitcast.10, bf16[672,5376]{1,0:T(8,128)(2,1)} %bitcast.11, bf16[672,5376]{1,0:T(8,128)(2,1)} %down_hbm.1), custom_call_target="tpu_custom_call" | custom-call | tf_op jit(solution)/shard_map/pallas_call | solution.py:246
  71.7 1.3 %reshape.15 = bf16[8,32,168]{2,1,0:T(8,128)(2,1)S(1)} reshape(bf16[8,5376]{1,0:T(8,128)(2,1)} %shard_map.153) | data formatting | bytes 172032 | tf_op jit(solution)/shard_map/reshape | solution.py:301
  73.0 9.9 %all_to_all.21 = bf16[32,8,168]{2,1,0:T(8,128)(2,1)S(1)} all-to-all(bf16[32,8,168]{2,1,0:T(8,128)(2,1)S(1)} %bitcast.13), channel_id=1, replica_groups=mesh['ctx'=8,'head'=4] {'ctx','head'}, dimensions={0} | all-to-all | bytes 172032 | tf_op jit(solution)/shard_map/all_to_all | solution.py:268
  (15 shorter events, 2.1 us)
Async XLA Ops:
  0.6 4.8 %collective-permute-start = (bf16[1,8,128]{2,1,0:T(8,128)(2,1)}, bf16[1,8,128]{2,1,0:T(8,128)(2,1)S(1)}, u32[]{:S(2)}, u32[]{:S(2)}) collective-permute-start(bf16[1,8,128]{2,1,0:T(8,128)(2,1)} %q_hbm.1), channel_id=1, source_target_pairs={{0,4},{4,0},{8,12},{12,8},{16,20},{20,16},{24,28},{28,24},{1,5},{5... | collective-permute-start | bytes 6152 | tf_op jit(solution)/shard_map/ppermute | solution.py:262
  5.4 9.7 %copy-start.3 = (bf16[1,8,128]{2,1,0:T(8,128)(2,1)}, bf16[1,8,128]{2,1,0:T(8,128)(2,1)S(1)}, u32[]{:S(2)}) copy-start(bf16[1,8,128]{2,1,0:T(8,128)(2,1)S(1)} %collective-permute-done.refs_1_) | copy-start | bytes 6148
  6.1 3.7 %collective-permute-start.1 = (bf16[2,8,128]{2,1,0:T(8,128)(2,1)S(1)}, bf16[2,8,128]{2,1,0:T(8,128)(2,1)S(1)}, u32[]{:S(2)}, u32[]{:S(2)}) collective-permute-start(bf16[2,8,128]{2,1,0:T(8,128)(2,1)S(1)} %pad_maximum_fusion.1), channel_id=1, source_target_pairs={{0,8},{4,12},{8,0},{12,4},{16,24},{20,28},{24,16},{28,20},{1,9},{5... | collective-permute-start | bytes 12296 | tf_op jit(solution)/shard_map/ppermute | solution.py:262
  9.8 5.4 %copy-start.4 = (bf16[2,8,128]{2,1,0:T(8,128)(2,1)}, bf16[2,8,128]{2,1,0:T(8,128)(2,1)S(1)}, u32[]{:S(2)}) copy-start(bf16[2,8,128]{2,1,0:T(8,128)(2,1)S(1)} %collective-permute-done.1.refs_2_) | copy-start | bytes 12292
  10.5 4.7 %collective-permute-start.2 = (bf16[4,8,128]{2,1,0:T(8,128)(2,1)S(1)}, bf16[4,8,128]{2,1,0:T(8,128)(2,1)S(1)}, u32[]{:S(2)}, u32[]{:S(2)}) collective-permute-start(bf16[4,8,128]{2,1,0:T(8,128)(2,1)S(1)} %pad_maximum_fusion), channel_id=1, source_target_pairs={{0,16},{4,20},{8,24},{12,28},{16,0},{20,4},{24,8},{28,12},{1,17},{... | collective-permute-start | bytes 24584 | tf_op jit(solution)/shard_map/ppermute | solution.py:262
  15.1 0.6 copy-start.5
  20.0 13.1 %all-to-all-start = ((f32[8,2,8,128]{3,2,1,0:T(8,128)}), f32[8,2,8,128]{3,2,1,0:T(8,128)S(1)}, u32[]{:S(2)}, u32[]{:S(2)}) async-start(f32[8,2,8,128]{3,2,1,0:T(8,128)} %shard_map.149), calls=%async_computation | async-start | bytes 131072 | tf_op jit(solution)/shard_map/all_to_all | solution.py:293
  33.1 0.7 copy-start.1
  43.9 1.3 %copy-start = (bf16[4096,168]{0,1:T(8,128)(2,1)S(1)}, bf16[4096,168]{0,1:T(8,128)(2,1)}, u32[]{:S(2)}) copy-start(bf16[4096,168]{0,1:T(8,128)(2,1)} %param.22) | copy-start | bytes 4128772
  45.2 0.7 copy-start.2
  47.1 10.8 %all-to-all-start.2 = ((bf16[32,8,168]{2,1,0:T(8,128)(2,1)}), bf16[32,8,168]{2,1,0:T(8,128)(2,1)S(1)}, u32[]{:S(2)}, u32[]{:S(2)}) async-start(bf16[32,8,168]{2,1,0:T(8,128)(2,1)} %get-tuple-element.9), calls=%async_computation.2 | async-start | bytes 262144 | tf_op jit(solution)/shard_map/all_to_all | solution.py:268

commit v3 on v2

v3 whole, which is shorter than its diff:
```python
import functools

import jax
import jax.numpy as jnp
from jax import lax
from jax.experimental import pallas as pl
from jax.experimental.pallas import tpu as pltpu
from jax.sharding import PartitionSpec as P

SCORE_SCALE = 168.0 ** (-0.5)
NORM_EPSILON = 1e-06
MASKED = -1e30
MIB = 1024 * 1024
LOADS = 6
COST = pl.CostEstimate(flops=10**9, bytes_accessed=32 * MIB, transcendentals=10**6)
BOTH = ("ctx", "head")


def head_bias(rows, columns, heads, kv_heads):
    group = heads // kv_heads
    tile = (heads, 128)
    row = lax.broadcasted_iota(jnp.int32, tile, 0)
    column = lax.broadcasted_iota(jnp.int32, tile, 1)
    bias = jnp.where(row // group == lax.rem(column, kv_heads), 0.0, MASKED)
    return jnp.tile(bias, (rows // heads, columns // 128))


def dot_rows(left, right):
    return lax.dot_general(left, right, (((1,), (1,)), ((), ())), preferred_element_type=jnp.float32)


def stat_rows(row_max, row_total, shape):
    lane = lax.broadcasted_iota(jnp.int32, shape, 1)
    return jnp.where(lane == 0, row_max, row_total)


def attention_kernel(
    length_ref, arrived_ref, q_hbm, kn_hbm, vn_hbm, ks_hbm, vs_hbm, kp_hbm, vp_hbm,
    part_ref,
    q_ref, kn_ref, vn_ref, ks_ref, vs_ref, kp_ref, vp_ref, sems,
):
    pairs = (
        (kp_hbm, kp_ref), (q_hbm, q_ref), (ks_hbm, ks_ref), (kn_hbm, kn_ref),
        (vs_hbm, vs_ref), (vn_hbm, vn_ref), (vp_hbm, vp_ref),
    )
    copies = [
        pltpu.make_async_copy(source, target, sems.at[place])
        for place, (source, target) in enumerate(pairs)
    ]
    for copy in copies:
        copy.start()
    count, heads, width = arrived_ref.shape
    kv_heads = kn_ref.shape[1]
    queries = arrived_ref[...].reshape(count * heads, width)
    copies[0].wait()
    scores = SCORE_SCALE * dot_rows(queries, kp_ref[...])
    scores = scores + head_bias(*scores.shape, heads, kv_heads)
    row_max = jnp.max(scores, axis=1, keepdims=True)
    weights = jnp.exp(scores - row_max).astype(jnp.bfloat16)
    row_total = jnp.sum(weights.astype(jnp.float32), axis=1, keepdims=True)
    for copy in copies[1:6]:
        copy.wait()
    own = q_ref[0]
    own_scores = SCORE_SCALE * dot_rows(own, ks_ref[...])
    new_scores = SCORE_SCALE * dot_rows(own, kn_ref[0])
    slot = lax.broadcasted_iota(jnp.int32, own_scores.shape, 1) // kv_heads
    own_scores = own_scores + head_bias(*own_scores.shape, heads, kv_heads)
    own_scores = jnp.where(slot < length_ref[0], own_scores, MASKED)
    new_scores = new_scores + head_bias(heads, 128, heads, kv_heads)[:, :kv_heads]
    suffix_max = jnp.maximum(
        jnp.max(own_scores, axis=1, keepdims=True), jnp.max(new_scores, axis=1, keepdims=True)
    )
    own_weights = jnp.exp(own_scores - suffix_max).astype(jnp.bfloat16)
    new_weights = jnp.exp(new_scores - suffix_max).astype(jnp.bfloat16)
    suffix_total = jnp.sum(own_weights.astype(jnp.float32), axis=1, keepdims=True) + jnp.sum(
        new_weights.astype(jnp.float32), axis=1, keepdims=True
    )
    suffix_sum = jnp.dot(own_weights, vs_ref[...], preferred_element_type=jnp.float32) + jnp.dot(
        new_weights, vn_ref[0], preferred_element_type=jnp.float32
    )
    copies[6].wait()
    row_sum = jnp.dot(weights, vp_ref[...], preferred_element_type=jnp.float32)
    part_ref[:, 0] = row_sum.reshape(count, heads, width)
    part_ref[:, 1] = stat_rows(row_max, row_total, row_sum.shape).reshape(count, heads, width)
    me = lax.axis_index("ctx")
    prefix_stat = part_ref[me, 1]
    prefix_max = prefix_stat[:, 0:1]
    joint_max = jnp.maximum(prefix_max, suffix_max)
    prefix_factor = jnp.exp(prefix_max - joint_max)
    suffix_factor = jnp.exp(suffix_max - joint_max)
    joint_total = prefix_stat[:, 1:2] * prefix_factor + suffix_total * suffix_factor
    joint_sum = part_ref[me, 0] * prefix_factor + suffix_sum * suffix_factor
    part_ref[me, 0] = joint_sum
    part_ref[me, 1] = stat_rows(joint_max, joint_total, joint_sum.shape)


def attend(lengths, arrived, *operands):
    count, heads, width = arrived.shape
    return pl.pallas_call(
        attention_kernel,
        out_shape=jax.ShapeDtypeStruct((count, 2, heads, width), jnp.float32),
        in_specs=[pl.BlockSpec(memory_space=pltpu.SMEM), pl.BlockSpec(memory_space=pltpu.VMEM)]
        + [pl.BlockSpec(memory_space=pl.ANY)] * len(operands),
        scratch_shapes=[pltpu.VMEM(operand.shape, operand.dtype) for operand in operands]
        + [pltpu.SemaphoreType.DMA((len(operands),))],
        compiler_params=pltpu.CompilerParams(vmem_limit_bytes=60 * MIB),
        cost_estimate=COST,
    )(lengths, arrived, *operands)


def join_kernel(part_ref, out_ref, copies_ref):
    sources = part_ref.shape[0]
    joint_max = functools.reduce(
        jnp.maximum, [part_ref[source, 1, :, 0:1] for source in range(sources)]
    )
    total = jnp.zeros_like(joint_max)
    summed = jnp.zeros(out_ref.shape, jnp.float32)
    for source in range(sources):
        factor = jnp.exp(part_ref[source, 1, :, 0:1] - joint_max)
        total = total + part_ref[source, 1, :, 1:2] * factor
        summed = summed + part_ref[source, 0] * factor
    attention = (summed / total).astype(jnp.bfloat16)
    out_ref[...] = attention
    for place in range(copies_ref.shape[0]):
        copies_ref[place] = attention


def join_partials(parts, devices):
    shape = parts.shape[2:]
    return pl.pallas_call(
        join_kernel,
        out_shape=(
            jax.ShapeDtypeStruct(shape, jnp.bfloat16),
            jax.ShapeDtypeStruct((devices, *shape), jnp.bfloat16),
        ),
        compiler_params=pltpu.CompilerParams(vmem_limit_bytes=8 * MIB),
        cost_estimate=COST,
    )(parts)


def project_kernel(rows_ref, w_ref, residual_ref, out_ref, copies_ref, wide_ref):
    devices, heads, width = rows_ref.shape
    completions = residual_ref.shape[0]
    all_heads = devices * heads // completions
    wide_ref[...] = rows_ref[...].reshape(devices * heads, width).astype(jnp.float32)
    rows = [wide_ref[pl.ds(head, completions, stride=all_heads), :] for head in range(all_heads)]
    rows = jnp.concatenate([row.astype(jnp.bfloat16) for row in rows], axis=1)
    hidden = (residual_ref[...].astype(jnp.float32) + dot_rows(rows, w_ref[...])).astype(jnp.bfloat16)
    out_ref[...] = hidden
    for place in range(copies_ref.shape[0]):
        copies_ref[place] = hidden


def project(rows, w_out, residual):
    devices, heads, width = rows.shape
    return pl.pallas_call(
        project_kernel,
        out_shape=(
            jax.ShapeDtypeStruct(residual.shape, jnp.bfloat16),
            jax.ShapeDtypeStruct((devices, *residual.shape), jnp.bfloat16),
        ),
        scratch_shapes=[pltpu.VMEM((devices * heads, width), jnp.float32)],
        compiler_params=pltpu.CompilerParams(vmem_limit_bytes=12 * MIB),
        cost_estimate=COST,
    )(rows, w_out, residual)


def row_chunks(rows, most):
    for count in range(most, 1, -1):
        if rows % (16 * count) == 0:
            return count
    return 1


def forward_kernel(
    pieces_ref, gain_ref, gate_hbm, up_hbm, down_hbm, out_ref, state_ref, gate_ref, up_ref, down_ref, sems
):
    units = gate_ref.shape[0]
    count = row_chunks(units, LOADS)
    size = units // count
    copies = []
    for chunk in range(count):
        rows = pl.ds(chunk * size, size)
        for place, (source, target) in enumerate(
            ((gate_hbm, gate_ref), (up_hbm, up_ref), (down_hbm, down_ref))
        ):
            copies.append(
                pltpu.make_async_copy(source.at[rows], target.at[rows], sems.at[3 * chunk + place])
            )
            copies[-1].start()
    devices, completions, columns = pieces_ref.shape
    for place in range(devices):
        state_ref[:, place * columns : (place + 1) * columns] = pieces_ref[place].astype(jnp.float32)
    state = state_ref[...]
    mean_square = jnp.mean(state * state, axis=-1, keepdims=True)
    gain = gain_ref[...].reshape(1, devices * columns)
    normed = (state * lax.rsqrt(mean_square + NORM_EPSILON) * gain).astype(jnp.bfloat16)
    share = jnp.zeros(state.shape, jnp.float32)
    for chunk in range(count):
        rows = slice(chunk * size, (chunk + 1) * size)
        copies[3 * chunk].wait()
        gate_values = dot_rows(gate_ref[rows], normed)
        copies[3 * chunk + 1].wait()
        up_values = dot_rows(up_ref[rows], normed)
        activated = jax.nn.gelu(gate_values, approximate=True) * up_values
        copies[3 * chunk + 2].wait()
        share += jnp.dot(
            activated.T.astype(jnp.bfloat16), down_ref[rows], preferred_element_type=jnp.float32
        )
    for place in range(devices):
        out_ref[place] = share[:, place * columns : (place + 1) * columns].astype(jnp.bfloat16)


def forward(pieces, gain, *weights):
    devices, completions, columns = pieces.shape
    whole = pl.BlockSpec(memory_space=pltpu.VMEM)
    return pl.pallas_call(
        forward_kernel,
        out_shape=jax.ShapeDtypeStruct(pieces.shape, jnp.bfloat16),
        in_specs=[whole, whole] + [pl.BlockSpec(memory_space=pl.ANY)] * 3,
        scratch_shapes=[pltpu.VMEM((completions, devices * columns), jnp.float32)]
        + [pltpu.VMEM(w.shape, w.dtype) for w in weights]
        + [pltpu.SemaphoreType.DMA((3 * LOADS,))],
        compiler_params=pltpu.CompilerParams(vmem_limit_bytes=56 * MIB),
        cost_estimate=COST,
    )(pieces, gain, *weights)


def exchange(copies, axes=BOTH):
    return lax.all_to_all(copies, axes, split_axis=0, concat_axis=0, tiled=True)


def body(
    queries,
    k_new,
    v_new,
    k_suffix,
    v_suffix,
    lengths,
    k_prefix,
    v_prefix,
    w_out,
    residual,
    norm_gain,
    w_gate,
    w_up,
    w_down,
):
    ctx_count = lax.axis_size("ctx")
    devices = ctx_count * lax.axis_size("head")
    arrived = exchange(jnp.broadcast_to(queries, (ctx_count, *queries.shape[1:])), "ctx")
    rows_of = lambda values: values.reshape(-1, values.shape[-1])
    parts = attend(
        lengths, arrived, queries, k_new, v_new, *map(rows_of, (k_suffix, v_suffix, k_prefix, v_prefix))
    )
    attention, copies = join_partials(exchange(parts, "ctx"), devices)
    hidden_part, copies = project(exchange(copies), w_out.T, residual)
    shares = forward(exchange(copies), norm_gain, w_gate.T, w_up.T, w_down)
    summed = jnp.sum(exchange(shares).astype(jnp.float32), axis=0)
    next_hidden = (hidden_part.astype(jnp.float32) + summed).astype(jnp.bfloat16)
    return (attention[None], next_hidden)


def solution(mesh):
    placed = (
        P("ctx", "head", None),
        P("ctx", "head", None),
        P("ctx", "head", None),
        P("ctx", None, "head", None),
        P("ctx", None, "head", None),
        P("ctx"),
        P("ctx", "head", None),
        P("ctx", "head", None),
        P(None, BOTH),
        P(None, BOTH),
        P(),
        P(None, BOTH),
        P(None, BOTH),
        P(BOTH, None),
    )
    return jax.shard_map(
        body,
        mesh=mesh,
        in_specs=placed,
        out_specs=(P("ctx", "head", None), P(None, BOTH)),
        check_vma=False,
    )
```

time: 84.3 us -> 77.5 us (0.919)
  blocking collectives: 19.3 us -> 40.9 us
  waiting for transfers between devices: 15.9 us -> 5.92 us
  starting transfers between devices: 16.9 us -> 7.28 us
  local copies, waits for them, and re-layouts: 6.89 us -> 1.99 us
  Pallas kernels: 21.2 us -> 18.9 us
  other arithmetic: 2.02 us -> 0.64 us
    all_to_all x2 -> x4, blocking collectives: 19.3 us -> 40.9 us  [exchange(): return lax.all_to_all(copies, axes, split_axis=0, concat_axis=0, tiled=True)]
    ppermute x3 -> x0, starting transfers between devices: 8.14 us -> none  [gather_by_xor(): pieces.append(lax.ppermute(jnp.concatenate(pieces, axis=0), axis, partners))]
    all_to_all x2 -> x1, waiting for transfers between devices: 11 us -> 5.92 us  [exchange(): return lax.all_to_all(copies, axes, split_axis=0, concat_axis=0, tiled=True)]
    ppermute x3 -> x0, waiting for transfers between devices: 4.99 us -> none  [gather_by_xor(): pieces.append(lax.ppermute(jnp.concatenate(pieces, axis=0), axis, partners))]
    unnamed x12 -> x6, local copies, waits for them, and re-layouts: 3.31 us -> 0.6 us
    reshape x4 -> x0, local copies, waits for them, and re-layouts: 2.2 us -> none  [the longest x2 1.34 us: body(): share = jnp.swapaxes(share.reshape(completions, devices, columns), 0, 1)]
    pallas_call x3 -> x2, Pallas kernels: 19.3 us -> 17.6 us  [the longest x1 13.3 us: forward(): pl.pallas_call(forward_kernel, out_shape=jax.ShapeDtypeStruct(pieces.shap...]
    all_to_all x2 -> x1, starting transfers between devices: 8.75 us -> 7.28 us  [exchange(): return lax.all_to_all(copies, axes, split_axis=0, concat_axis=0, tiled=True)]
  transfers between devices with their start and end apart: 5 -> 1, of which waited for: 5 -> 1; matrix products, arithmetic and copies ran while one was open for 2% -> 0% of each run, Pallas kernels for 3% -> 0%
where the time goes in v3:
time: 77.5 us; the launch traced here: 77 us
  blocking collectives  40.9 us (53%)
  Pallas kernels  18.9 us (24%)
  starting transfers between devices  7.28 us (9%)
  waiting for transfers between devices  5.92 us (8%)
  local copies, waits for them, and re-layouts  1.99 us (3%)
  between operations  1.33 us (2%)
    all_to_all x4, blocking collectives, exchange(): return lax.all_to_all(copies, axes, split_axis=0, concat_axis=0, tiled=True)  40.9 us
    pallas_call x1, Pallas kernels, forward(): pl.pallas_call(forward_kernel, out_shape=jax.ShapeDtypeStruct(pieces.shap...  13.3 us
    all_to_all x1, starting transfers between devices, exchange(): return lax.all_to_all(copies, axes, split_axis=0, concat_axis=0, tiled=True)  7.28 us
    all_to_all x1, waiting for transfers between devices, exchange(): return lax.all_to_all(copies, axes, split_axis=0, concat_axis=0, tiled=True)  5.92 us
    pallas_call x1, Pallas kernels, attend(): pl.pallas_call(attention_kernel, out_shape=jax.ShapeDtypeStruct((count, 2...  4.33 us
  transfers between devices with their start and end apart: 1, of which 1 were waited for; matrix products, arithmetic and copies ran while one was open for 0% of the time, Pallas kernels for 0%

profile of v3, /device:TPU:0, one launch (start us, length us, event | category | flops | bytes accessed | tf_op | source)
XLA Modules:
  0.0 77.0 jit_solution(13968416097662336480)
XLA Ops:
  0.6 0.0 copy-start.1
  0.6 0.0 copy-start
  0.6 1.4 %broadcast_in_dim.11 = bf16[8,8,128]{2,1,0:T(8,128)(2,1)} broadcast(bf16[8,128]{1,0:T(8,128)(2,1)} %bitcast.12), dimensions={1,2} | broadcast | bytes 18432 | tf_op jit(solution)/shard_map/broadcast_in_dim | solution.py:251
  2.0 7.3 %all-to-all-start = ((bf16[8,8,128]{2,1,0:T(8,128)(2,1)}), bf16[8,8,128]{2,1,0:T(8,128)(2,1)S(1)}, u32[]{:S(2)}, u32[]{:S(2)}) async-start(bf16[8,8,128]{2,1,0:T(8,128)(2,1)} %broadcast_in_dim.11), calls=%async_computation | async-start | bytes 32768 | tf_op jit(solution)/shard_map/all_to_all | solution.py:230
  10.0 5.9 %all-to-all-done.arrived_ref = bf16[8,8,128]{2,1,0:T(8,128)(2,1)S(1)} async-done(((bf16[8,8,128]{2,1,0:T(8,128)(2,1)}), bf16[8,8,128]{2,1,0:T(8,128)(2,1)S(1)}, u32[]{:S(2)}, u32[]{:S(2)}) %all-to-all-start) | async-done | bytes 16416 | tf_op jit(solution)/shard_map/all_to_all | solution.py:230
  15.9 0.0 copy-start.2
  15.9 0.6 copy-done.2
  16.5 4.3 %shard_map.149 = f32[8,2,8,128]{3,2,1,0:T(8,128)} custom-call(s32[1]{0:T(128)S(6)} %copy.16.length_ref, bf16[8,8,128]{2,1,0:T(8,128)(2,1)} %copy-done.2, bf16[1,8,128]{2,1,0:T(8,128)(2,1)} %q_hbm.1, bf16[1,4,128]{2,1,0:T(4,128)(2,1)} %kn_hbm.1, bf16[1,4,128]{2,1,0:T(4,128)(2,1)} %vn_hbm.1, bf16[1024,128]{1,0:T(8,128)(2,1)} %bitcast.15, ...), custom_call_target="tpu_custom_call" | custom-call | flops 1000000000 | bytes 33554432 | tf_op jit(solution)/shard_map/pallas_call | solution.py:99
  20.8 10.2 %all_to_all.25.part_ref = f32[8,2,8,128]{3,2,1,0:T(8,128)S(1)} all-to-all(f32[8,2,8,128]{3,2,1,0:T(8,128)} %shard_map.149), channel_id=1, replica_groups=mesh['ctx'=8,'head'=4] {'ctx'}, dimensions={0} | all-to-all | bytes 131072 | tf_op jit(solution)/shard_map/all_to_all | solution.py:230
  31.0 0.8 shard_map.150
  31.8 9.3 %all_to_all.26.rows_ref = bf16[32,8,128]{2,1,0:T(8,128)(2,1)S(1)} all-to-all(bf16[32,8,128]{2,1,0:T(8,128)(2,1)S(1)} %get-tuple-element.7), channel_id=1, replica_groups=mesh['ctx'=8,'head'=4] {'ctx','head'}, dimensions={0} | all-to-all | bytes 131072 | tf_op jit(solution)/shard_map/all_to_all | solution.py:230
  41.1 0.0 copy-done.1
  41.1 0.0 copy-done
  41.1 0.5 shard_map.151
  41.6 10.6 %all_to_all.27.pieces_ref = bf16[32,8,168]{2,1,0:T(8,128)(2,1)} all-to-all(bf16[32,8,168]{2,1,0:T(8,128)(2,1)S(1)} %get-tuple-element.9), channel_id=1, replica_groups=mesh['ctx'=8,'head'=4] {'ctx','head'}, dimensions={0} | all-to-all | bytes 172032 | tf_op jit(solution)/shard_map/all_to_all | solution.py:230
  52.2 13.3 %shard_map.152 = bf16[32,8,168]{2,1,0:T(8,128)(2,1)} custom-call(bf16[32,8,168]{2,1,0:T(8,128)(2,1)} %all_to_all.27.pieces_ref, f32[5376]{0:T(1024)} %gain_ref.1, bf16[672,5376]{1,0:T(8,128)(2,1)} %bitcast.10, bf16[672,5376]{1,0:T(8,128)(2,1)} %bitcast.11, bf16[672,5376]{1,0:T(8,128)(2,1)} %down_hbm.1), custom_call_target="tpu_custom_call" | custom-call | flops 1000000000 | bytes 33554432 | tf_op jit(solution)/shard_map/pallas_call | solution.py:217
  65.5 10.8 %all_to_all.28 = bf16[32,8,168]{2,1,0:T(8,128)(2,1)S(1)} all-to-all(bf16[32,8,168]{2,1,0:T(8,128)(2,1)} %shard_map.152), channel_id=1, replica_groups=mesh['ctx'=8,'head'=4] {'ctx','head'}, dimensions={0} | all-to-all | bytes 172032 | tf_op jit(solution)/shard_map/all_to_all | solution.py:230
  76.4 0.6 add_convert_fusion
  (1 shorter events, 0.0 us)
Async XLA Ops:
  0.6 40.4 %copy-start.1 = (bf16[8,168]{1,0:T(8,128)(2,1)S(1)}, bf16[8,168]{1,0:T(8,128)(2,1)}, u32[]{:S(2)}) copy-start(bf16[8,168]{1,0:T(8,128)(2,1)} %residual_ref.1) | copy-start | bytes 8068
  0.6 40.4 %copy-start = (bf16[4096,168]{0,1:T(8,128)(2,1)S(1)}, bf16[4096,168]{0,1:T(8,128)(2,1)}, u32[]{:S(2)}) copy-start(bf16[4096,168]{0,1:T(8,128)(2,1)} %param.22) | copy-start | bytes 4128772
  2.0 13.9 %all-to-all-start = ((bf16[8,8,128]{2,1,0:T(8,128)(2,1)}), bf16[8,8,128]{2,1,0:T(8,128)(2,1)S(1)}, u32[]{:S(2)}, u32[]{:S(2)}) async-start(bf16[8,8,128]{2,1,0:T(8,128)(2,1)} %broadcast_in_dim.11), calls=%async_computation | async-start | bytes 32768 | tf_op jit(solution)/shard_map/all_to_all | solution.py:230
  15.9 0.6 copy-start.2

commit v4 on v3

--- a/solution.py
+++ b/solution.py
@@ -11,7 +11,7 @@
 NORM_EPSILON = 1e-06
 MASKED = -1e30
 MIB = 1024 * 1024
-LOADS = 6
+LOADS = 3
 COST = pl.CostEstimate(flops=10**9, bytes_accessed=32 * MIB, transcendentals=10**6)
 BOTH = ("ctx", "head")
 
@@ -25,6 +25,10 @@
     return jnp.tile(bias, (rows // heads, columns // 128))
 
 
+def in_hbm(operand):
+    return pltpu.with_memory_space_constraint(operand, pltpu.HBM)
+
+
 def dot_rows(left, right):
     return lax.dot_general(left, right, (((1,), (1,)), ((), ())), preferred_element_type=jnp.float32)
 
@@ -32,6 +36,27 @@
 def stat_rows(row_max, row_total, shape):
     lane = lax.broadcasted_iota(jnp.int32, shape, 1)
     return jnp.where(lane == 0, row_max, row_total)
+
+
+def spread_kernel(source_ref, copies_ref, sems):
+    copies = [
+        pltpu.make_async_copy(source_ref, copies_ref.at[pl.ds(place, 1)], sems.at[place])
+        for place in range(copies_ref.shape[0])
+    ]
+    for copy in copies:
+        copy.start()
+    for copy in copies:
+        copy.wait()
+
+
+def spread(value, count):
+    return pl.pallas_call(
+        spread_kernel,
+        out_shape=jax.ShapeDtypeStruct((count, *value.shape[1:]), value.dtype),
+        in_specs=[pl.BlockSpec(memory_space=pl.ANY)],
+        scratch_shapes=[pltpu.SemaphoreType.DMA((count,))],
+        compiler_params=pltpu.CompilerParams(vmem_limit_bytes=4 * MIB),
+    )(in_hbm(value))
 
 
 def attention_kernel(
@@ -47,12 +72,13 @@
         pltpu.make_async_copy(source, target, sems.at[place])
         for place, (source, target) in enumerate(pairs)
     ]
-    for copy in copies:
-        copy.start()
+    copies[0].start()
     count, heads, width = arrived_ref.shape
     kv_heads = kn_ref.shape[1]
     queries = arrived_ref[...].reshape(count * heads, width)
     copies[0].wait()
+    for copy in copies[1:]:
+        copy.start()
     scores = SCORE_SCALE * dot_rows(queries, kp_ref[...])
     scores = scores + head_bias(*scores.shape, heads, kv_heads)
     row_max = jnp.max(scores, axis=1, keepdims=True)
@@ -103,9 +129,9 @@
         + [pl.BlockSpec(memory_space=pl.ANY)] * len(operands),
         scratch_shapes=[pltpu.VMEM(operand.shape, operand.dtype) for operand in operands]
         + [pltpu.SemaphoreType.DMA((len(operands),))],
-        compiler_params=pltpu.CompilerParams(vmem_limit_bytes=60 * MIB),
+        compiler_params=pltpu.CompilerParams(vmem_limit_bytes=24 * MIB),
         cost_estimate=COST,
-    )(lengths, arrived, *operands)
+    )(lengths, arrived, *map(in_hbm, operands))
 
 
 def join_kernel(part_ref, out_ref, copies_ref):
@@ -199,14 +225,12 @@
     for chunk in range(count):
         rows = slice(chunk * size, (chunk + 1) * size)
         copies[3 * chunk].wait()
-        gate_values = dot_rows(gate_ref[rows], normed)
+        gate_values = dot_rows(normed, gate_ref[rows])
         copies[3 * chunk + 1].wait()
-        up_values = dot_rows(up_ref[rows], normed)
-        activated = jax.nn.gelu(gate_values, approximate=True) * up_values
+        up_values = dot_rows(normed, up_ref[rows])
+        activated = (jax.nn.gelu(gate_values, approximate=True) * up_values).astype(jnp.bfloat16)
         copies[3 * chunk + 2].wait()
-        share += jnp.dot(
-            activated.T.astype(jnp.bfloat16), down_ref[rows], preferred_element_type=jnp.float32
-        )
+        share += jnp.dot(activated, down_ref[rows], preferred_element_type=jnp.float32)
     for place in range(devices):
         out_ref[place] = share[:, place * columns : (place + 1) * columns].astype(jnp.bfloat16)
 
@@ -221,9 +245,9 @@
         scratch_shapes=[pltpu.VMEM((completions, devices * columns), jnp.float32)]
         + [pltpu.VMEM(w.shape, w.dtype) for w in weights]
         + [pltpu.SemaphoreType.DMA((3 * LOADS,))],
-        compiler_params=pltpu.CompilerParams(vmem_limit_bytes=56 * MIB),
+        compiler_params=pltpu.CompilerParams(vmem_limit_bytes=30 * MIB),
         cost_estimate=COST,
-    )(pieces, gain, *weights)
+    )(pieces, gain, *map(in_hbm, weights))
 
 
 def exchange(copies, axes=BOTH):
@@ -248,7 +272,7 @@
 ):
     ctx_count = lax.axis_size("ctx")
     devices = ctx_count * lax.axis_size("head")
-    arrived = exchange(jnp.broadcast_to(queries, (ctx_count, *queries.shape[1:])), "ctx")
+    arrived = exchange(spread(queries, ctx_count), "ctx")
     rows_of = lambda values: values.reshape(-1, values.shape[-1])
     parts = attend(
         lengths, arrived, queries, k_new, v_new, *map(rows_of, (k_suffix, v_suffix, k_prefix, v_prefix))

time: 77.5 us -> 71.3 us (0.920)
  blocking collectives: 40.9 us -> 38.5 us
  local copies, waits for them, and re-layouts: 1.99 us -> 0.01 us
  Pallas kernels: 18.9 us -> 17.3 us
    all_to_all x4, blocking collectives: 40.9 us -> 38.5 us  [exchange(): return lax.all_to_all(copies, axes, split_axis=0, concat_axis=0, tiled=True)]
    pallas_call x1, Pallas kernels: 13.3 us -> 11.2 us  [forward(): pl.pallas_call(forward_kernel, out_shape=jax.ShapeDtypeStruct(pieces.shap...]
    pallas_call x0 -> x1, Pallas kernels: none -> 1.64 us  [spread(): pl.pallas_call(spread_kernel, out_shape=jax.ShapeDtypeStruct((count, *val...]
    broadcast_in_dim x1 -> x0, local copies, waits for them, and re-layouts: 1.39 us -> none  [body(): jnp.broadcast_to(queries, (ctx_count, *queries.shape[1:]))]
    pallas_call x1, Pallas kernels: 4.33 us -> 3.22 us  [attend(): pl.pallas_call(attention_kernel, out_shape=jax.ShapeDtypeStruct((count, 2...]
where the time goes in v4:
time: 71.3 us; the launch traced here: 71 us
  blocking collectives  38.5 us (54%)
  Pallas kernels  17.3 us (24%)
  starting transfers between devices  7.29 us (10%)
  waiting for transfers between devices  5.92 us (8%)
  between operations  1.35 us (2%)
    all_to_all x4, blocking collectives, exchange(): return lax.all_to_all(copies, axes, split_axis=0, concat_axis=0, tiled=True)  38.5 us
    pallas_call x1, Pallas kernels, forward(): pl.pallas_call(forward_kernel, out_shape=jax.ShapeDtypeStruct(pieces.shap...  11.2 us
    all_to_all x1, starting transfers between devices, exchange(): return lax.all_to_all(copies, axes, split_axis=0, concat_axis=0, tiled=True)  7.29 us
    all_to_all x1, waiting for transfers between devices, exchange(): return lax.all_to_all(copies, axes, split_axis=0, concat_axis=0, tiled=True)  5.92 us
    pallas_call x1, Pallas kernels, attend(): pl.pallas_call(attention_kernel, out_shape=jax.ShapeDtypeStruct((count, 2...  3.22 us
    pallas_call x1, Pallas kernels, spread(): pl.pallas_call(spread_kernel, out_shape=jax.ShapeDtypeStruct((count, *val...  1.64 us
  transfers between devices with their start and end apart: 1, of which 1 were waited for; matrix products, arithmetic and copies ran while one was open for 0% of the time, Pallas kernels for 0%

profile of v4, /device:TPU:0, one launch (start us, length us, event | category | flops | bytes accessed | tf_op | source)
XLA Modules:
  0.0 71.0 jit_solution(15947144542074222253)
XLA Ops:
  0.6 0.0 copy-start.2
  0.6 0.0 copy-start.1
  0.7 0.0 copy-start
  0.7 1.6 %shard_map.149 = bf16[8,8,128]{2,1,0:T(8,128)(2,1)} custom-call(bf16[1,8,128]{2,1,0:T(8,128)(2,1)} %q_hbm.1), custom_call_target="tpu_custom_call" | custom-call | tf_op jit(solution)/shard_map/pallas_call | solution.py:53
  2.3 7.3 %all-to-all-start = ((bf16[8,8,128]{2,1,0:T(8,128)(2,1)}), bf16[8,8,128]{2,1,0:T(8,128)(2,1)S(1)}, u32[]{:S(2)}, u32[]{:S(2)}) async-start(bf16[8,8,128]{2,1,0:T(8,128)(2,1)} %shard_map.149), calls=%async_computation | async-start | bytes 32768 | tf_op jit(solution)/shard_map/all_to_all | solution.py:254
  10.3 5.9 %all-to-all-done.arrived_ref = bf16[8,8,128]{2,1,0:T(8,128)(2,1)S(1)} async-done(((bf16[8,8,128]{2,1,0:T(8,128)(2,1)}), bf16[8,8,128]{2,1,0:T(8,128)(2,1)S(1)}, u32[]{:S(2)}, u32[]{:S(2)}) %all-to-all-start) | async-done | bytes 16416 | tf_op jit(solution)/shard_map/all_to_all | solution.py:254
  16.2 3.2 %shard_map.150 = f32[8,2,8,128]{3,2,1,0:T(8,128)S(1)} custom-call(s32[1]{0:T(128)S(6)} %copy.16.length_ref, bf16[8,8,128]{2,1,0:T(8,128)(2,1)S(1)} %all-to-all-done.arrived_ref, bf16[1,8,128]{2,1,0:T(8,128)(2,1)} %q_hbm.1, bf16[1,4,128]{2,1,0:T(4,128)(2,1)} %kn_hbm.1, bf16[1,4,128]{2,1,0:T(4,128)(2,1)} %vn_hbm.1, bf16[1024,128]{1,0:T(8,128)(2,1)} %bitcast.13, ...), custom_call_target="tpu_custom_call" | custom-call | flops 1000000000 | bytes 33554432 | tf_op jit(solution)/shard_map/pallas_call | solution.py:125
  19.4 9.3 %all_to_all.25.part_ref = f32[8,2,8,128]{3,2,1,0:T(8,128)S(1)} all-to-all(f32[8,2,8,128]{3,2,1,0:T(8,128)S(1)} %shard_map.150), channel_id=1, replica_groups=mesh['ctx'=8,'head'=4] {'ctx'}, dimensions={0} | all-to-all | bytes 131072 | tf_op jit(solution)/shard_map/all_to_all | solution.py:254
  28.7 0.8 %shard_map.151 = (bf16[8,128]{1,0:T(8,128)(2,1)}, bf16[32,8,128]{2,1,0:T(8,128)(2,1)S(1)}) custom-call(f32[8,2,8,128]{3,2,1,0:T(8,128)S(1)} %all_to_all.25.part_ref), custom_call_target="tpu_custom_call" | custom-call | flops 1000000000 | bytes 33554432 | tf_op jit(solution)/shard_map/pallas_call | solution.py:156
  29.4 9.3 %all_to_all.26.rows_ref = bf16[32,8,128]{2,1,0:T(8,128)(2,1)S(1)} all-to-all(bf16[32,8,128]{2,1,0:T(8,128)(2,1)S(1)} %get-tuple-element.7), channel_id=1, replica_groups=mesh['ctx'=8,'head'=4] {'ctx','head'}, dimensions={0} | all-to-all | bytes 131072 | tf_op jit(solution)/shard_map/all_to_all | solution.py:254
  38.7 0.0 copy-done.2
  38.8 0.0 copy-done.1
  38.8 0.5 shard_map.152
  39.3 9.9 %all_to_all.27.pieces_ref = bf16[32,8,168]{2,1,0:T(8,128)(2,1)S(1)} all-to-all(bf16[32,8,168]{2,1,0:T(8,128)(2,1)S(1)} %get-tuple-element.9), channel_id=1, replica_groups=mesh['ctx'=8,'head'=4] {'ctx','head'}, dimensions={0} | all-to-all | bytes 172032 | tf_op jit(solution)/shard_map/all_to_all | solution.py:254
  49.2 0.0 copy-done
  49.2 11.2 %shard_map.153 = bf16[32,8,168]{2,1,0:T(8,128)(2,1)S(1)} custom-call(bf16[32,8,168]{2,1,0:T(8,128)(2,1)S(1)} %all_to_all.27.pieces_ref, f32[5376]{0:T(1024)S(1)} %copy-done, bf16[672,5376]{1,0:T(8,128)(2,1)} %bitcast.9, bf16[672,5376]{1,0:T(8,128)(2,1)} %bitcast.10, bf16[672,5376]{1,0:T(8,128)(2,1)} %down_hbm.1), custom_call_target="tpu_custom_call" | custom-call | flops 1000000000 | bytes 33554432 | tf_op jit(solution)/shard_map/pallas_call | solution.py:241
  60.4 9.9 %all_to_all.28 = bf16[32,8,168]{2,1,0:T(8,128)(2,1)S(1)} all-to-all(bf16[32,8,168]{2,1,0:T(8,128)(2,1)S(1)} %shard_map.153), channel_id=1, replica_groups=mesh['ctx'=8,'head'=4] {'ctx','head'}, dimensions={0} | all-to-all | bytes 172032 | tf_op jit(solution)/shard_map/all_to_all | solution.py:254
  70.4 0.6 add_convert_fusion
  (1 shorter events, 0.0 us)
Async XLA Ops:
  0.6 38.1 %copy-start.2 = (bf16[8,168]{1,0:T(8,128)(2,1)S(1)}, bf16[8,168]{1,0:T(8,128)(2,1)}, u32[]{:S(2)}) copy-start(bf16[8,168]{1,0:T(8,128)(2,1)} %residual_ref.1) | copy-start | bytes 8068
  0.6 38.1 %copy-start.1 = (bf16[4096,168]{0,1:T(8,128)(2,1)S(1)}, bf16[4096,168]{0,1:T(8,128)(2,1)}, u32[]{:S(2)}) copy-start(bf16[4096,168]{0,1:T(8,128)(2,1)} %param.22) | copy-start | bytes 4128772
  0.7 48.6 %copy-start = (f32[5376]{0:T(1024)S(1)}, f32[5376]{0:T(1024)}, u32[]{:S(2)}) copy-start(f32[5376]{0:T(1024)} %gain_ref.1) | copy-start | bytes 64516
  2.3 13.9 %all-to-all-start = ((bf16[8,8,128]{2,1,0:T(8,128)(2,1)}), bf16[8,8,128]{2,1,0:T(8,128)(2,1)S(1)}, u32[]{:S(2)}, u32[]{:S(2)}) async-start(bf16[8,8,128]{2,1,0:T(8,128)(2,1)} %shard_map.149), calls=%async_computation | async-start | bytes 32768 | tf_op jit(solution)/shard_map/all_to_all | solution.py:254

commit v5 on v4

--- a/solution.py
+++ b/solution.py
@@ -11,7 +11,9 @@
 NORM_EPSILON = 1e-06
 MASKED = -1e30
 MIB = 1024 * 1024
-LOADS = 3
+CHUNKS = 3
+SPLIT = 2
+AHEAD = 5
 COST = pl.CostEstimate(flops=10**9, bytes_accessed=32 * MIB, transcendentals=10**6)
 BOTH = ("ctx", "head")
 
@@ -54,6 +56,7 @@
         spread_kernel,
         out_shape=jax.ShapeDtypeStruct((count, *value.shape[1:]), value.dtype),
         in_specs=[pl.BlockSpec(memory_space=pl.ANY)],
+        out_specs=pl.BlockSpec(memory_space=pl.ANY),
         scratch_shapes=[pltpu.SemaphoreType.DMA((count,))],
         compiler_params=pltpu.CompilerParams(vmem_limit_bytes=4 * MIB),
     )(in_hbm(value))
@@ -134,19 +137,18 @@
     )(lengths, arrived, *map(in_hbm, operands))
 
 
-def join_kernel(part_ref, out_ref, copies_ref):
+def join_kernel(part_ref, copies_ref):
     sources = part_ref.shape[0]
     joint_max = functools.reduce(
         jnp.maximum, [part_ref[source, 1, :, 0:1] for source in range(sources)]
     )
     total = jnp.zeros_like(joint_max)
-    summed = jnp.zeros(out_ref.shape, jnp.float32)
+    summed = jnp.zeros(part_ref.shape[2:], jnp.float32)
     for source in range(sources):
         factor = jnp.exp(part_ref[source, 1, :, 0:1] - joint_max)
         total = total + part_ref[source, 1, :, 1:2] * factor
         summed = summed + part_ref[source, 0] * factor
     attention = (summed / total).astype(jnp.bfloat16)
-    out_ref[...] = attention
     for place in range(copies_ref.shape[0]):
         copies_ref[place] = attention
 
@@ -155,10 +157,7 @@
     shape = parts.shape[2:]
     return pl.pallas_call(
         join_kernel,
-        out_shape=(
-            jax.ShapeDtypeStruct(shape, jnp.bfloat16),
-            jax.ShapeDtypeStruct((devices, *shape), jnp.bfloat16),
-        ),
+        out_shape=jax.ShapeDtypeStruct((devices, *shape), jnp.bfloat16),
         compiler_params=pltpu.CompilerParams(vmem_limit_bytes=8 * MIB),
         cost_estimate=COST,
     )(parts)
@@ -199,21 +198,35 @@
 
 
 def forward_kernel(
-    pieces_ref, gain_ref, gate_hbm, up_hbm, down_hbm, out_ref, state_ref, gate_ref, up_ref, down_ref, sems
+    pieces_ref, gain_ref, copies_ref, gate_hbm, up_hbm, down_hbm, out_ref, attention_hbm,
+    state_ref, gate_ref, up_ref, down_ref, sems,
 ):
     units = gate_ref.shape[0]
-    count = row_chunks(units, LOADS)
+    count = row_chunks(units, CHUNKS)
     size = units // count
-    copies = []
+    split = row_chunks(size, SPLIT)
+    matrices = ((gate_hbm, gate_ref), (up_hbm, up_ref), (down_hbm, down_ref))
+    loads = []
     for chunk in range(count):
-        rows = pl.ds(chunk * size, size)
-        for place, (source, target) in enumerate(
-            ((gate_hbm, gate_ref), (up_hbm, up_ref), (down_hbm, down_ref))
-        ):
-            copies.append(
-                pltpu.make_async_copy(source.at[rows], target.at[rows], sems.at[3 * chunk + place])
-            )
-            copies[-1].start()
+        for source, target in matrices:
+            for piece in range(split):
+                rows = pl.ds(chunk * size + piece * (size // split), size // split)
+                loads.append(
+                    pltpu.make_async_copy(source.at[rows], target.at[rows], sems.at[len(loads)])
+                )
+    for load in loads[:AHEAD]:
+        load.start()
+    keep = pltpu.make_async_copy(copies_ref.at[0], attention_hbm, sems.at[len(loads)])
+    keep.start()
+
+    def arrived(place, chunk):
+        first = (3 * chunk + place) * split
+        for load in range(first, first + split):
+            loads[load].wait()
+            if load + AHEAD < len(loads):
+                loads[load + AHEAD].start()
+        return matrices[place][1][chunk * size : (chunk + 1) * size]
+
     devices, completions, columns = pieces_ref.shape
     for place in range(devices):
         state_ref[:, place * columns : (place + 1) * columns] = pieces_ref[place].astype(jnp.float32)
@@ -223,31 +236,33 @@
     normed = (state * lax.rsqrt(mean_square + NORM_EPSILON) * gain).astype(jnp.bfloat16)
     share = jnp.zeros(state.shape, jnp.float32)
     for chunk in range(count):
-        rows = slice(chunk * size, (chunk + 1) * size)
-        copies[3 * chunk].wait()
-        gate_values = dot_rows(normed, gate_ref[rows])
-        copies[3 * chunk + 1].wait()
-        up_values = dot_rows(normed, up_ref[rows])
+        gate_values = dot_rows(normed, arrived(0, chunk))
+        up_values = dot_rows(normed, arrived(1, chunk))
         activated = (jax.nn.gelu(gate_values, approximate=True) * up_values).astype(jnp.bfloat16)
-        copies[3 * chunk + 2].wait()
-        share += jnp.dot(activated, down_ref[rows], preferred_element_type=jnp.float32)
+        share += jnp.dot(activated, arrived(2, chunk), preferred_element_type=jnp.float32)
     for place in range(devices):
         out_ref[place] = share[:, place * columns : (place + 1) * columns].astype(jnp.bfloat16)
-
-
-def forward(pieces, gain, *weights):
+    keep.wait()
+
+
+def forward(pieces, gain, copies, *weights):
     devices, completions, columns = pieces.shape
     whole = pl.BlockSpec(memory_space=pltpu.VMEM)
+    far = pl.BlockSpec(memory_space=pl.ANY)
     return pl.pallas_call(
         forward_kernel,
-        out_shape=jax.ShapeDtypeStruct(pieces.shape, jnp.bfloat16),
-        in_specs=[whole, whole] + [pl.BlockSpec(memory_space=pl.ANY)] * 3,
+        out_shape=(
+            jax.ShapeDtypeStruct(pieces.shape, jnp.bfloat16),
+            jax.ShapeDtypeStruct(copies.shape[1:], jnp.bfloat16),
+        ),
+        in_specs=[whole, whole, whole, far, far, far],
+        out_specs=(whole, far),
         scratch_shapes=[pltpu.VMEM((completions, devices * columns), jnp.float32)]
         + [pltpu.VMEM(w.shape, w.dtype) for w in weights]
-        + [pltpu.SemaphoreType.DMA((3 * LOADS,))],
+        + [pltpu.SemaphoreType.DMA((3 * CHUNKS * SPLIT + 1,))],
         compiler_params=pltpu.CompilerParams(vmem_limit_bytes=30 * MIB),
         cost_estimate=COST,
-    )(pieces, gain, *map(in_hbm, weights))
+    )(pieces, gain, copies, *map(in_hbm, weights))
 
 
 def exchange(copies, axes=BOTH):
@@ -277,9 +292,11 @@
     parts = attend(
         lengths, arrived, queries, k_new, v_new, *map(rows_of, (k_suffix, v_suffix, k_prefix, v_prefix))
     )
-    attention, copies = join_partials(exchange(parts, "ctx"), devices)
-    hidden_part, copies = project(exchange(copies), w_out.T, residual)
-    shares = forward(exchange(copies), norm_gain, w_gate.T, w_up.T, w_down)
+    copies = join_partials(exchange(parts, "ctx"), devices)
+    hidden_part, hidden_copies = project(exchange(copies), w_out.T, residual)
+    shares, attention = forward(
+        exchange(hidden_copies), norm_gain, copies, w_gate.T, w_up.T, w_down
+    )
     summed = jnp.sum(exchange(shares).astype(jnp.float32), axis=0)
     next_hidden = (hidden_part.astype(jnp.float32) + summed).astype(jnp.bfloat16)
     return (attention[None], next_hidden)

time: 71.3 us -> 70.8 us (level)
  no operation moved by 1% of the time
where the time goes in v5:
time: 70.8 us; the launch traced here: 70.5 us
  blocking collectives  38.5 us (54%)
  Pallas kernels  16.8 us (24%)
  starting transfers between devices  7.29 us (10%)
  waiting for transfers between devices  5.92 us (8%)
  between operations  1.35 us (2%)
    all_to_all x4, blocking collectives, exchange(): return lax.all_to_all(copies, axes, split_axis=0, concat_axis=0, tiled=True)  38.5 us
    pallas_call x1, Pallas kernels, forward(): pl.pallas_call(forward_kernel, out_shape=(jax.ShapeDtypeStruct(pieces.sha...  11.2 us
    all_to_all x1, starting transfers between devices, exchange(): return lax.all_to_all(copies, axes, split_axis=0, concat_axis=0, tiled=True)  7.29 us
    all_to_all x1, waiting for transfers between devices, exchange(): return lax.all_to_all(copies, axes, split_axis=0, concat_axis=0, tiled=True)  5.92 us
    pallas_call x1, Pallas kernels, attend(): pl.pallas_call(attention_kernel, out_shape=jax.ShapeDtypeStruct((count, 2...  3.22 us
    pallas_call x1, Pallas kernels, spread(): pl.pallas_call(spread_kernel, out_shape=jax.ShapeDtypeStruct((count, *val...  1.67 us
  transfers between devices with their start and end apart: 1, of which 1 were waited for; matrix products, arithmetic and copies ran while one was open for 0% of the time, Pallas kernels for 0%

profile of v5, /device:TPU:0, one launch (start us, length us, event | category | flops | bytes accessed | tf_op | source)
XLA Modules:
  0.0 70.5 jit_solution(1096303902566393774)
XLA Ops:
  0.6 0.0 copy-start.2
  0.6 0.0 copy-start.1
  0.7 0.0 copy-start
  0.7 1.7 %shard_map.149 = bf16[8,8,128]{2,1,0:T(8,128)(2,1)} custom-call(bf16[1,8,128]{2,1,0:T(8,128)(2,1)} %q_hbm.1), custom_call_target="tpu_custom_call" | custom-call | tf_op jit(solution)/shard_map/pallas_call | solution.py:55
  2.3 7.3 %all-to-all-start = ((bf16[8,8,128]{2,1,0:T(8,128)(2,1)}), bf16[8,8,128]{2,1,0:T(8,128)(2,1)S(1)}, u32[]{:S(2)}, u32[]{:S(2)}) async-start(bf16[8,8,128]{2,1,0:T(8,128)(2,1)} %shard_map.149), calls=%async_computation | async-start | bytes 32768 | tf_op jit(solution)/shard_map/all_to_all | solution.py:269
  10.3 5.9 %all-to-all-done.arrived_ref = bf16[8,8,128]{2,1,0:T(8,128)(2,1)S(1)} async-done(((bf16[8,8,128]{2,1,0:T(8,128)(2,1)}), bf16[8,8,128]{2,1,0:T(8,128)(2,1)S(1)}, u32[]{:S(2)}, u32[]{:S(2)}) %all-to-all-start) | async-done | bytes 16416 | tf_op jit(solution)/shard_map/all_to_all | solution.py:269
  16.2 3.2 %shard_map.150 = f32[8,2,8,128]{3,2,1,0:T(8,128)S(1)} custom-call(s32[1]{0:T(128)S(6)} %copy.16.length_ref, bf16[8,8,128]{2,1,0:T(8,128)(2,1)S(1)} %all-to-all-done.arrived_ref, bf16[1,8,128]{2,1,0:T(8,128)(2,1)} %q_hbm.1, bf16[1,4,128]{2,1,0:T(4,128)(2,1)} %kn_hbm.1, bf16[1,4,128]{2,1,0:T(4,128)(2,1)} %vn_hbm.1, bf16[1024,128]{1,0:T(8,128)(2,1)} %bitcast.13, ...), custom_call_target="tpu_custom_call" | custom-call | flops 1000000000 | bytes 33554432 | tf_op jit(solution)/shard_map/pallas_call | solution.py:128
  19.4 9.3 %all_to_all.25.part_ref = f32[8,2,8,128]{3,2,1,0:T(8,128)S(1)} all-to-all(f32[8,2,8,128]{3,2,1,0:T(8,128)S(1)} %shard_map.150), channel_id=1, replica_groups=mesh['ctx'=8,'head'=4] {'ctx'}, dimensions={0} | all-to-all | bytes 131072 | tf_op jit(solution)/shard_map/all_to_all | solution.py:269
  28.7 0.2 shard_map.151.copies_ref
  28.9 9.3 %all_to_all.26.rows_ref = bf16[32,8,128]{2,1,0:T(8,128)(2,1)S(1)} all-to-all(bf16[32,8,128]{2,1,0:T(8,128)(2,1)S(1)} %shard_map.151.copies_ref), channel_id=1, replica_groups=mesh['ctx'=8,'head'=4] {'ctx','head'}, dimensions={0} | all-to-all | bytes 131072 | tf_op jit(solution)/shard_map/all_to_all | solution.py:269
  38.2 0.0 copy-done.2
  38.2 0.0 copy-done.1
  38.2 0.5 shard_map.152
  38.7 9.9 %all_to_all.27.pieces_ref = bf16[32,8,168]{2,1,0:T(8,128)(2,1)S(1)} all-to-all(bf16[32,8,168]{2,1,0:T(8,128)(2,1)S(1)} %get-tuple-element.6), channel_id=1, replica_groups=mesh['ctx'=8,'head'=4] {'ctx','head'}, dimensions={0} | all-to-all | bytes 172032 | tf_op jit(solution)/shard_map/all_to_all | solution.py:269
  48.7 0.0 copy-done
  48.7 11.2 %shard_map.153 = (bf16[32,8,168]{2,1,0:T(8,128)(2,1)S(1)}, bf16[8,128]{1,0:T(8,128)(2,1)}) custom-call(bf16[32,8,168]{2,1,0:T(8,128)(2,1)S(1)} %all_to_all.27.pieces_ref, f32[5376]{0:T(1024)S(1)} %copy-done, bf16[32,8,128]{2,1,0:T(8,128)(2,1)S(1)} %shard_map.151.copies_ref, bf16[672,5376]{1,0:T(8,128)(2,1)} %bitcast.9, bf16[672,5376]{1,0:T(8,128)(2,1)} %bitcast.10, ...), custom_call_target="tpu_custom_call" | custom-call | flops 1000000000 | bytes 33554432 | tf_op jit(solution)/shard_map/pallas_call | solution.py:252
  59.9 9.9 %all_to_all.28 = bf16[32,8,168]{2,1,0:T(8,128)(2,1)S(1)} all-to-all(bf16[32,8,168]{2,1,0:T(8,128)(2,1)S(1)} %get-tuple-element.9), channel_id=1, replica_groups=mesh['ctx'=8,'head'=4] {'ctx','head'}, dimensions={0} | all-to-all | bytes 172032 | tf_op jit(solution)/shard_map/all_to_all | solution.py:269
  69.9 0.6 add_convert_fusion
  (1 shorter events, 0.0 us)
Async XLA Ops:
  0.6 37.6 %copy-start.2 = (bf16[8,168]{1,0:T(8,128)(2,1)S(1)}, bf16[8,168]{1,0:T(8,128)(2,1)}, u32[]{:S(2)}) copy-start(bf16[8,168]{1,0:T(8,128)(2,1)} %residual_ref.1) | copy-start | bytes 8068
  0.6 37.6 %copy-start.1 = (bf16[4096,168]{0,1:T(8,128)(2,1)S(1)}, bf16[4096,168]{0,1:T(8,128)(2,1)}, u32[]{:S(2)}) copy-start(bf16[4096,168]{0,1:T(8,128)(2,1)} %param.22) | copy-start | bytes 4128772
  0.7 48.0 %copy-start = (f32[5376]{0:T(1024)S(1)}, f32[5376]{0:T(1024)}, u32[]{:S(2)}) copy-start(f32[5376]{0:T(1024)} %gain_ref.1) | copy-start | bytes 64516
  2.3 13.9 %all-to-all-start = ((bf16[8,8,128]{2,1,0:T(8,128)(2,1)}), bf16[8,8,128]{2,1,0:T(8,128)(2,1)S(1)}, u32[]{:S(2)}, u32[]{:S(2)}) async-start(bf16[8,8,128]{2,1,0:T(8,128)(2,1)} %shard_map.149), calls=%async_computation | async-start | bytes 32768 | tf_op jit(solution)/shard_map/all_to_all | solution.py:269

commit v6 on v5

--- a/solution.py
+++ b/solution.py
@@ -11,10 +11,7 @@
 NORM_EPSILON = 1e-06
 MASKED = -1e30
 MIB = 1024 * 1024
-CHUNKS = 3
-SPLIT = 2
-AHEAD = 5
-COST = pl.CostEstimate(flops=10**9, bytes_accessed=32 * MIB, transcendentals=10**6)
+COST = pl.CostEstimate(flops=10**10, bytes_accessed=MIB, transcendentals=10**6)
 BOTH = ("ctx", "head")
 
 
@@ -40,61 +37,46 @@
     return jnp.where(lane == 0, row_max, row_total)
 
 
-def spread_kernel(source_ref, copies_ref, sems):
-    copies = [
-        pltpu.make_async_copy(source_ref, copies_ref.at[pl.ds(place, 1)], sems.at[place])
-        for place in range(copies_ref.shape[0])
-    ]
-    for copy in copies:
-        copy.start()
-    for copy in copies:
-        copy.wait()
-
-
-def spread(value, count):
+def spread_kernel(length_ref, source_hbm, copies_ref, lengths_ref, source_ref, sem):
+    load = pltpu.make_async_copy(source_hbm, source_ref, sem)
+    load.start()
+    lengths_ref[...] = jnp.full(lengths_ref.shape, length_ref[0], jnp.int32)
+    load.wait()
+    for place in range(copies_ref.shape[0]):
+        copies_ref[place] = source_ref[0]
+
+
+def spread(lengths, value, count):
     return pl.pallas_call(
         spread_kernel,
-        out_shape=jax.ShapeDtypeStruct((count, *value.shape[1:]), value.dtype),
-        in_specs=[pl.BlockSpec(memory_space=pl.ANY)],
-        out_specs=pl.BlockSpec(memory_space=pl.ANY),
-        scratch_shapes=[pltpu.SemaphoreType.DMA((count,))],
+        out_shape=(
+            jax.ShapeDtypeStruct((count, *value.shape[1:]), value.dtype),
+            jax.ShapeDtypeStruct(value.shape[1:], jnp.int32),
+        ),
+        in_specs=[pl.BlockSpec(memory_space=pltpu.SMEM), pl.BlockSpec(memory_space=pl.ANY)],
+        scratch_shapes=[pltpu.VMEM(value.shape, value.dtype), pltpu.SemaphoreType.DMA],
         compiler_params=pltpu.CompilerParams(vmem_limit_bytes=4 * MIB),
-    )(in_hbm(value))
+        cost_estimate=COST,
+    )(lengths, in_hbm(value))
 
 
 def attention_kernel(
-    length_ref, arrived_ref, q_hbm, kn_hbm, vn_hbm, ks_hbm, vs_hbm, kp_hbm, vp_hbm,
-    part_ref,
-    q_ref, kn_ref, vn_ref, ks_ref, vs_ref, kp_ref, vp_ref, sems,
+    length_ref, arrived_ref, q_ref, kn_ref, vn_ref, ks_ref, vs_ref, kp_ref, vp_ref, part_ref
 ):
-    pairs = (
-        (kp_hbm, kp_ref), (q_hbm, q_ref), (ks_hbm, ks_ref), (kn_hbm, kn_ref),
-        (vs_hbm, vs_ref), (vn_hbm, vn_ref), (vp_hbm, vp_ref),
-    )
-    copies = [
-        pltpu.make_async_copy(source, target, sems.at[place])
-        for place, (source, target) in enumerate(pairs)
-    ]
-    copies[0].start()
     count, heads, width = arrived_ref.shape
     kv_heads = kn_ref.shape[1]
     queries = arrived_ref[...].reshape(count * heads, width)
-    copies[0].wait()
-    for copy in copies[1:]:
-        copy.start()
     scores = SCORE_SCALE * dot_rows(queries, kp_ref[...])
     scores = scores + head_bias(*scores.shape, heads, kv_heads)
     row_max = jnp.max(scores, axis=1, keepdims=True)
     weights = jnp.exp(scores - row_max).astype(jnp.bfloat16)
     row_total = jnp.sum(weights.astype(jnp.float32), axis=1, keepdims=True)
-    for copy in copies[1:6]:
-        copy.wait()
     own = q_ref[0]
     own_scores = SCORE_SCALE * dot_rows(own, ks_ref[...])
     new_scores = SCORE_SCALE * dot_rows(own, kn_ref[0])
     slot = lax.broadcasted_iota(jnp.int32, own_scores.shape, 1) // kv_heads
     own_scores = own_scores + head_bias(*own_scores.shape, heads, kv_heads)
-    own_scores = jnp.where(slot < length_ref[0], own_scores, MASKED)
+    own_scores = jnp.where(slot < length_ref[:, 0:1], own_scores, MASKED)
     new_scores = new_scores + head_bias(heads, 128, heads, kv_heads)[:, :kv_heads]
     suffix_max = jnp.maximum(
         jnp.max(own_scores, axis=1, keepdims=True), jnp.max(new_scores, axis=1, keepdims=True)
@@ -107,7 +89,6 @@
     suffix_sum = jnp.dot(own_weights, vs_ref[...], preferred_element_type=jnp.float32) + jnp.dot(
         new_weights, vn_ref[0], preferred_element_type=jnp.float32
     )
-    copies[6].wait()
     row_sum = jnp.dot(weights, vp_ref[...], preferred_element_type=jnp.float32)
     part_ref[:, 0] = row_sum.reshape(count, heads, width)
     part_ref[:, 1] = stat_rows(row_max, row_total, row_sum.shape).reshape(count, heads, width)
@@ -124,17 +105,12 @@
 
 
 def attend(lengths, arrived, *operands):
-    count, heads, width = arrived.shape
     return pl.pallas_call(
         attention_kernel,
-        out_shape=jax.ShapeDtypeStruct((count, 2, heads, width), jnp.float32),
-        in_specs=[pl.BlockSpec(memory_space=pltpu.SMEM), pl.BlockSpec(memory_space=pltpu.VMEM)]
-        + [pl.BlockSpec(memory_space=pl.ANY)] * len(operands),
-        scratch_shapes=[pltpu.VMEM(operand.shape, operand.dtype) for operand in operands]
-        + [pltpu.SemaphoreType.DMA((len(operands),))],
+        out_shape=jax.ShapeDtypeStruct((arrived.shape[0], 2, *arrived.shape[1:]), jnp.float32),
         compiler_params=pltpu.CompilerParams(vmem_limit_bytes=24 * MIB),
         cost_estimate=COST,
-    )(lengths, arrived, *map(in_hbm, operands))
+    )(lengths, arrived, *operands)
 
 
 def join_kernel(part_ref, copies_ref):
@@ -190,43 +166,11 @@
     )(rows, w_out, residual)
 
 
-def row_chunks(rows, most):
-    for count in range(most, 1, -1):
-        if rows % (16 * count) == 0:
-            return count
-    return 1
-
-
 def forward_kernel(
-    pieces_ref, gain_ref, copies_ref, gate_hbm, up_hbm, down_hbm, out_ref, attention_hbm,
-    state_ref, gate_ref, up_ref, down_ref, sems,
+    pieces_ref, gain_ref, copies_ref, gate_ref, up_ref, down_ref, out_ref, attention_hbm, state_ref, sem
 ):
-    units = gate_ref.shape[0]
-    count = row_chunks(units, CHUNKS)
-    size = units // count
-    split = row_chunks(size, SPLIT)
-    matrices = ((gate_hbm, gate_ref), (up_hbm, up_ref), (down_hbm, down_ref))
-    loads = []
-    for chunk in range(count):
-        for source, target in matrices:
-            for piece in range(split):
-                rows = pl.ds(chunk * size + piece * (size // split), size // split)
-                loads.append(
-                    pltpu.make_async_copy(source.at[rows], target.at[rows], sems.at[len(loads)])
-                )
-    for load in loads[:AHEAD]:
-        load.start()
-    keep = pltpu.make_async_copy(copies_ref.at[0], attention_hbm, sems.at[len(loads)])
+    keep = pltpu.make_async_copy(copies_ref.at[0], attention_hbm, sem)
     keep.start()
-
-    def arrived(place, chunk):
-        first = (3 * chunk + place) * split
-        for load in range(first, first + split):
-            loads[load].wait()
-            if load + AHEAD < len(loads):
-                loads[load + AHEAD].start()
-        return matrices[place][1][chunk * size : (chunk + 1) * size]
-
     devices, completions, columns = pieces_ref.shape
     for place in range(devices):
         state_ref[:, place * columns : (place + 1) * columns] = pieces_ref[place].astype(jnp.float32)
@@ -234,12 +178,10 @@
     mean_square = jnp.mean(state * state, axis=-1, keepdims=True)
     gain = gain_ref[...].reshape(1, devices * columns)
     normed = (state * lax.rsqrt(mean_square + NORM_EPSILON) * gain).astype(jnp.bfloat16)
-    share = jnp.zeros(state.shape, jnp.float32)
-    for chunk in range(count):
-        gate_values = dot_rows(normed, arrived(0, chunk))
-        up_values = dot_rows(normed, arrived(1, chunk))
-        activated = (jax.nn.gelu(gate_values, approximate=True) * up_values).astype(jnp.bfloat16)
-        share += jnp.dot(activated, arrived(2, chunk), preferred_element_type=jnp.float32)
+    gate_values = dot_rows(normed, gate_ref[...])
+    up_values = dot_rows(normed, up_ref[...])
+    activated = (jax.nn.gelu(gate_values, approximate=True) * up_values).astype(jnp.bfloat16)
+    share = jnp.dot(activated, down_ref[...], preferred_element_type=jnp.float32)
     for place in range(devices):
         out_ref[place] = share[:, place * columns : (place + 1) * columns].astype(jnp.bfloat16)
     keep.wait()
@@ -247,22 +189,20 @@
 
 def forward(pieces, gain, copies, *weights):
     devices, completions, columns = pieces.shape
-    whole = pl.BlockSpec(memory_space=pltpu.VMEM)
-    far = pl.BlockSpec(memory_space=pl.ANY)
     return pl.pallas_call(
         forward_kernel,
         out_shape=(
             jax.ShapeDtypeStruct(pieces.shape, jnp.bfloat16),
             jax.ShapeDtypeStruct(copies.shape[1:], jnp.bfloat16),
         ),
-        in_specs=[whole, whole, whole, far, far, far],
-        out_specs=(whole, far),
-        scratch_shapes=[pltpu.VMEM((completions, devices * columns), jnp.float32)]
-        + [pltpu.VMEM(w.shape, w.dtype) for w in weights]
-        + [pltpu.SemaphoreType.DMA((3 * CHUNKS * SPLIT + 1,))],
-        compiler_params=pltpu.CompilerParams(vmem_limit_bytes=30 * MIB),
-        cost_estimate=COST,
-    )(pieces, gain, copies, *map(in_hbm, weights))
+        out_specs=(pl.BlockSpec(memory_space=pltpu.VMEM), pl.BlockSpec(memory_space=pl.ANY)),
+        scratch_shapes=[
+            pltpu.VMEM((completions, devices * columns), jnp.float32),
+            pltpu.SemaphoreType.DMA,
+        ],
+        compiler_params=pltpu.CompilerParams(vmem_limit_bytes=8 * MIB),
+        cost_estimate=COST,
+    )(pieces, gain, copies, *weights)
 
 
 def exchange(copies, axes=BOTH):
@@ -287,10 +227,11 @@
 ):
     ctx_count = lax.axis_size("ctx")
     devices = ctx_count * lax.axis_size("head")
-    arrived = exchange(spread(queries, ctx_count), "ctx")
+    copies, own_length = spread(lengths, queries, ctx_count)
+    arrived = exchange(copies, "ctx")
     rows_of = lambda values: values.reshape(-1, values.shape[-1])
     parts = attend(
-        lengths, arrived, queries, k_new, v_new, *map(rows_of, (k_suffix, v_suffix, k_prefix, v_prefix))
+        own_length, arrived, queries, k_new, v_new, *map(rows_of, (k_suffix, v_suffix, k_prefix, v_prefix))
     )
     copies = join_partials(exchange(parts, "ctx"), devices)
     hidden_part, hidden_copies = project(exchange(copies), w_out.T, residual)

time: 70.8 us -> 63 us (0.89)
  blocking collectives: 38.5 us -> 52.4 us
  Pallas kernels: 16.8 us -> 8 us
  starting transfers between devices: 7.29 us -> 0 us
  waiting for transfers between devices: 5.92 us -> 0 us
    all_to_all x4 -> x5, blocking collectives: 38.5 us -> 52.4 us  [exchange(): return lax.all_to_all(copies, axes, split_axis=0, concat_axis=0, tiled=True)]
    all_to_all x1 -> x0, starting transfers between devices: 7.29 us -> none  [exchange(): return lax.all_to_all(copies, axes, split_axis=0, concat_axis=0, tiled=True)]
    pallas_call x1, Pallas kernels: 11.2 us -> 5.28 us  [forward(): pl.pallas_call(forward_kernel, out_shape=(jax.ShapeDtypeStruct(pieces.sha...]
    all_to_all x1 -> x0, waiting for transfers between devices: 5.92 us -> none  [exchange(): return lax.all_to_all(copies, axes, split_axis=0, concat_axis=0, tiled=True)]
    pallas_call x2, Pallas kernels: 4.89 us -> 2.05 us  [the longest x1 1.21 us: attend(): pl.pallas_call(attention_kernel, out_shape=jax.ShapeDtypeStruct((arrived....]
  transfers between devices with their start and end apart: 1 -> 0, of which waited for: 1 -> 0; matrix products, arithmetic and copies ran while one was open for 0% -> 0% of each run, Pallas kernels for 0% -> 0%
where the time goes in v6:
time: 63 us; the launch traced here: 62.7 us
  blocking collectives  52.4 us (83%)
  Pallas kernels  8 us (13%)
  between operations  1.5 us (2%)
  other arithmetic  0.64 us (1%)
    all_to_all x5, blocking collectives, exchange(): return lax.all_to_all(copies, axes, split_axis=0, concat_axis=0, tiled=True)  52.4 us
    pallas_call x1, Pallas kernels, forward(): pl.pallas_call(forward_kernel, out_shape=(jax.ShapeDtypeStruct(pieces.sha...  5.28 us

profile of v6, /device:TPU:0, one launch (start us, length us, event | category | flops | bytes accessed | tf_op | source)
XLA Modules:
  0.0 62.7 jit_solution(7473916502691574956)
XLA Ops:
  1.3 0.0 copy-start.1
  1.3 0.8 %shard_map.149 = (bf16[8,8,128]{2,1,0:T(8,128)(2,1)S(1)}, s32[8,128]{1,0:T(8,128)S(1)}) custom-call(s32[1]{0:T(128)S(6)} %copy.16.length_ref, bf16[1,8,128]{2,1,0:T(8,128)(2,1)} %q_ref.1), custom_call_target="tpu_custom_call" | custom-call | flops 10000000000 | bytes 1048576 | tf_op jit(solution)/shard_map/pallas_call | solution.py:50
  2.2 13.7 %all_to_all.25.arrived_ref = bf16[8,8,128]{2,1,0:T(8,128)(2,1)S(1)} all-to-all(bf16[8,8,128]{2,1,0:T(8,128)(2,1)S(1)} %get-tuple-element.9), channel_id=1, replica_groups=mesh['ctx'=8,'head'=4] {'ctx'}, dimensions={0} | all-to-all | bytes 32768 | tf_op jit(solution)/shard_map/all_to_all | solution.py:209
  15.9 0.0 copy-done.3
  15.9 0.0 copy-done.4
  15.9 0.0 copy-done.7
  15.9 0.0 copy-done.8
  15.9 0.0 copy-done.9
  15.9 1.2 %shard_map.150 = f32[8,2,8,128]{3,2,1,0:T(8,128)S(1)} custom-call(s32[8,128]{1,0:T(8,128)S(1)} %get-tuple-element.8.length_ref, bf16[8,8,128]{2,1,0:T(8,128)(2,1)S(1)} %all_to_all.25.arrived_ref, bf16[1,8,128]{2,1,0:T(8,128)(2,1)S(1)} %copy-done.7, bf16[1,4,128]{2,1,0:T(4,128)(2,1)S(1)} %copy-done.8, bf16[1,4,128]{2,1,0:T(4,128)(2,1)S(1)} %copy-done.9, ...), custom_call_target="tpu_custom_call" | custom-call | flops 10000000000 | bytes 1048576 | tf_op jit(solution)/shard_map/pallas_call | solution.py:108
  17.1 9.3 %all_to_all.26.part_ref = f32[8,2,8,128]{3,2,1,0:T(8,128)S(1)} all-to-all(f32[8,2,8,128]{3,2,1,0:T(8,128)S(1)} %shard_map.150), channel_id=1, replica_groups=mesh['ctx'=8,'head'=4] {'ctx'}, dimensions={0} | all-to-all | bytes 131072 | tf_op jit(solution)/shard_map/all_to_all | solution.py:209
  26.4 0.0 slice-start.4
  26.4 0.2 shard_map.151.copies_ref
  26.6 9.4 %all_to_all.27.rows_ref = bf16[32,8,128]{2,1,0:T(8,128)(2,1)S(1)} all-to-all(bf16[32,8,128]{2,1,0:T(8,128)(2,1)S(1)} %shard_map.151.copies_ref), channel_id=1, replica_groups=mesh['ctx'=8,'head'=4] {'ctx','head'}, dimensions={0} | all-to-all | bytes 131072 | tf_op jit(solution)/shard_map/all_to_all | solution.py:209
  36.0 0.0 slice-start.5
  36.0 0.0 copy-start.5
  36.0 0.5 shard_map.152
  36.5 10.2 %all_to_all.28.pieces_ref = bf16[32,8,168]{2,1,0:T(8,128)(2,1)S(1)} all-to-all(bf16[32,8,168]{2,1,0:T(8,128)(2,1)S(1)} %get-tuple-element.10), channel_id=1, replica_groups=mesh['ctx'=8,'head'=4] {'ctx','head'}, dimensions={0} | all-to-all | bytes 172032 | tf_op jit(solution)/shard_map/all_to_all | solution.py:209
  46.7 0.0 slice-done.1
  46.7 0.0 slice-done.3
  46.7 0.0 slice-done.5
  46.8 0.0 copy-done.5
  46.8 5.3 %shard_map.153 = (bf16[32,8,168]{2,1,0:T(8,128)(2,1)S(1)}, bf16[8,128]{1,0:T(8,128)(2,1)}) custom-call(bf16[32,8,168]{2,1,0:T(8,128)(2,1)S(1)} %all_to_all.28.pieces_ref, f32[5376]{0:T(1024)S(1)} %copy-done.5, bf16[32,8,128]{2,1,0:T(8,128)(2,1)S(1)} %shard_map.151.copies_ref, bf16[672,5376]{1,0:T(8,128)(2,1)S(1)} %bitcast.10, ...), custom_call_target="tpu_custom_call" | custom-call | flops 10000000000 | bytes 1048576 | tf_op jit(solution)/shard_map/pallas_call | solution.py:192
  52.1 9.9 %all_to_all.29 = bf16[32,8,168]{2,1,0:T(8,128)(2,1)S(1)} all-to-all(bf16[32,8,168]{2,1,0:T(8,128)(2,1)S(1)} %get-tuple-element.13), channel_id=1, replica_groups=mesh['ctx'=8,'head'=4] {'ctx','head'}, dimensions={0} | all-to-all | bytes 172032 | tf_op jit(solution)/shard_map/all_to_all | solution.py:209
  62.1 0.6 add_convert_fusion
  (23 shorter events, 0.1 us)
Async XLA Ops:
  1.3 14.6 %copy-start.1 = (bf16[1024,4,128]{2,1,0:T(4,128)(2,1)S(1)}, bf16[1024,4,128]{2,1,0:T(4,128)(2,1)}, u32[]{:S(2)}) copy-start(bf16[1024,4,128]{2,1,0:T(4,128)(2,1)} %param.20) | copy-start | bytes 3145732
  1.3 14.6 %copy-start.2 = (bf16[1024,4,128]{2,1,0:T(4,128)(2,1)S(1)}, bf16[1024,4,128]{2,1,0:T(4,128)(2,1)}, u32[]{:S(2)}) copy-start(bf16[1024,4,128]{2,1,0:T(4,128)(2,1)} %param.21) | copy-start | bytes 3145732
  1.3 14.6 %copy-start.3 = (bf16[1,256,4,128]{3,2,1,0:T(4,128)(2,1)S(1)}, bf16[1,256,4,128]{3,2,1,0:T(4,128)(2,1)}, u32[]{:S(2)}) copy-start(bf16[1,256,4,128]{3,2,1,0:T(4,128)(2,1)} %param.17) | copy-start | bytes 786436
  1.3 14.6 %copy-start.4 = (bf16[1,256,4,128]{3,2,1,0:T(4,128)(2,1)S(1)}, bf16[1,256,4,128]{3,2,1,0:T(4,128)(2,1)}, u32[]{:S(2)}) copy-start(bf16[1,256,4,128]{3,2,1,0:T(4,128)(2,1)} %param.18) | copy-start | bytes 786436
  1.3 14.6 %copy-start.7 = (bf16[1,8,128]{2,1,0:T(8,128)(2,1)S(1)}, bf16[1,8,128]{2,1,0:T(8,128)(2,1)}, u32[]{:S(2)}) copy-start(bf16[1,8,128]{2,1,0:T(8,128)(2,1)} %q_ref.1) | copy-start | bytes 6148
  1.3 14.6 %copy-start.8 = (bf16[1,4,128]{2,1,0:T(4,128)(2,1)S(1)}, bf16[1,4,128]{2,1,0:T(4,128)(2,1)}, u32[]{:S(2)}) copy-start(bf16[1,4,128]{2,1,0:T(4,128)(2,1)} %kn_ref.1) | copy-start | bytes 3076
  1.3 14.6 %copy-start.9 = (bf16[1,4,128]{2,1,0:T(4,128)(2,1)S(1)}, bf16[1,4,128]{2,1,0:T(4,128)(2,1)}, u32[]{:S(2)}) copy-start(bf16[1,4,128]{2,1,0:T(4,128)(2,1)} %vn_ref.1) | copy-start | bytes 3076
  26.4 9.6 %copy-start = (bf16[4096,168]{0,1:T(8,128)(2,1)S(1)}, bf16[4096,168]{0,1:T(8,128)(2,1)}, u32[]{:S(2)}) copy-start(bf16[4096,168]{0,1:T(8,128)(2,1)} %param.22) | copy-start | bytes 4128772
  26.4 9.6 %copy-start.6 = (bf16[8,168]{1,0:T(8,128)(2,1)S(1)}, bf16[8,168]{1,0:T(8,128)(2,1)}, u32[]{:S(2)}) copy-start(bf16[8,168]{1,0:T(8,128)(2,1)} %residual_ref.1) | copy-start | bytes 8068
  26.4 20.3 %slice-start = ((s8[7225344]{0:T(1024)(128)(4,1)}), s8[4194304]{0:T(1024)(128)(4,1)S(1)}, s32[]{:S(2)}) async-start(s8[7225344]{0:T(1024)(128)(4,1)} %bitcast.8), calls=%async_computation.5 | async-start | bytes 8388608
  26.4 20.3 %slice-start.2 = ((s8[7225344]{0:T(1024)(128)(4,1)}), s8[4194304]{0:T(1024)(128)(4,1)S(1)}, s32[]{:S(2)}) async-start(s8[7225344]{0:T(1024)(128)(4,1)} %bitcast.11), calls=%async_computation.7 | async-start | bytes 8388608
  26.4 20.3 %slice-start.4 = ((s8[7225344]{0:T(1024)(128)(4,1)}), s8[4194304]{0:T(1024)(128)(4,1)S(1)}, s32[]{:S(2)}) async-start(s8[7225344]{0:T(1024)(128)(4,1)} %bitcast.14), calls=%async_computation.9 | async-start | bytes 8388608
  36.0 10.8 %slice-start.1 = ((s8[7225344]{0:T(1024)(128)(4,1)}), s8[3031040]{0:T(1024)(128)(4,1)S(1)}, s32[]{:S(2)}) async-start(s8[7225344]{0:T(1024)(128)(4,1)} %bitcast.8), calls=%async_computation.6 | async-start | bytes 6062080
  36.0 10.8 %slice-start.3 = ((s8[7225344]{0:T(1024)(128)(4,1)}), s8[3031040]{0:T(1024)(128)(4,1)S(1)}, s32[]{:S(2)}) async-start(s8[7225344]{0:T(1024)(128)(4,1)} %bitcast.11), calls=%async_computation.8 | async-start | bytes 6062080
  36.0 10.8 %slice-start.5 = ((s8[7225344]{0:T(1024)(128)(4,1)}), s8[3031040]{0:T(1024)(128)(4,1)S(1)}, s32[]{:S(2)}) async-start(s8[7225344]{0:T(1024)(128)(4,1)} %bitcast.14), calls=%async_computation.10 | async-start | bytes 6062080
  36.0 10.8 %copy-start.5 = (f32[5376]{0:T(1024)S(1)}, f32[5376]{0:T(1024)}, u32[]{:S(2)}) copy-start(f32[5376]{0:T(1024)} %gain_ref.1) | copy-start | bytes 64516

commit v7 on v6

--- a/solution.py
+++ b/solution.py
@@ -61,11 +61,13 @@
 
 
 def attention_kernel(
-    length_ref, arrived_ref, q_ref, kn_ref, vn_ref, ks_ref, vs_ref, kp_ref, vp_ref, part_ref
+    groups, length_ref, arrived_ref, q_ref, kn_ref, vn_ref, ks_ref, vs_ref, kp_ref, vp_ref,
+    part_ref, sum_ref, stat_ref,
 ):
-    count, heads, width = arrived_ref.shape
+    count, heads, width = sum_ref.shape
+    me, group = lax.axis_index("ctx"), lax.axis_index("head")
     kv_heads = kn_ref.shape[1]
-    queries = arrived_ref[...].reshape(count * heads, width)
+    queries = jnp.concatenate([arrived_ref[place * groups + group] for place in range(count)], axis=0)
     scores = SCORE_SCALE * dot_rows(queries, kp_ref[...])
     scores = scores + head_bias(*scores.shape, heads, kv_heads)
     row_max = jnp.max(scores, axis=1, keepdims=True)
@@ -90,75 +92,100 @@
         new_weights, vn_ref[0], preferred_element_type=jnp.float32
     )
     row_sum = jnp.dot(weights, vp_ref[...], preferred_element_type=jnp.float32)
-    part_ref[:, 0] = row_sum.reshape(count, heads, width)
-    part_ref[:, 1] = stat_rows(row_max, row_total, row_sum.shape).reshape(count, heads, width)
-    me = lax.axis_index("ctx")
-    prefix_stat = part_ref[me, 1]
+    sum_ref[...] = row_sum.reshape(count, heads, width)
+    stat_ref[...] = stat_rows(row_max, row_total, row_sum.shape).reshape(count, heads, width)
+    prefix_stat = stat_ref[me]
     prefix_max = prefix_stat[:, 0:1]
     joint_max = jnp.maximum(prefix_max, suffix_max)
     prefix_factor = jnp.exp(prefix_max - joint_max)
     suffix_factor = jnp.exp(suffix_max - joint_max)
     joint_total = prefix_stat[:, 1:2] * prefix_factor + suffix_total * suffix_factor
-    joint_sum = part_ref[me, 0] * prefix_factor + suffix_sum * suffix_factor
-    part_ref[me, 0] = joint_sum
-    part_ref[me, 1] = stat_rows(joint_max, joint_total, joint_sum.shape)
-
-
-def attend(lengths, arrived, *operands):
-    return pl.pallas_call(
-        attention_kernel,
-        out_shape=jax.ShapeDtypeStruct((arrived.shape[0], 2, *arrived.shape[1:]), jnp.float32),
+    joint_sum = sum_ref[me] * prefix_factor + suffix_sum * suffix_factor
+    sum_ref[me] = joint_sum
+    stat_ref[me] = stat_rows(joint_max, joint_total, joint_sum.shape)
+    share = heads // groups
+    for place in range(count):
+        for taker in range(groups):
+            rows = slice(taker * share, (taker + 1) * share)
+            part_ref[place * groups + taker, :share] = sum_ref[place, rows]
+            part_ref[place * groups + taker, share:] = stat_ref[place, rows]
+
+
+def attend(groups, lengths, arrived, *operands):
+    devices, heads, width = arrived.shape
+    count = devices // groups
+    return pl.pallas_call(
+        functools.partial(attention_kernel, groups),
+        out_shape=jax.ShapeDtypeStruct((devices, 2 * (heads // groups), width), jnp.float32),
+        scratch_shapes=[pltpu.VMEM((count, heads, width), jnp.float32)] * 2,
         compiler_params=pltpu.CompilerParams(vmem_limit_bytes=24 * MIB),
         cost_estimate=COST,
     )(lengths, arrived, *operands)
 
 
-def join_kernel(part_ref, copies_ref):
-    sources = part_ref.shape[0]
-    joint_max = functools.reduce(
-        jnp.maximum, [part_ref[source, 1, :, 0:1] for source in range(sources)]
-    )
-    total = jnp.zeros_like(joint_max)
-    summed = jnp.zeros(part_ref.shape[2:], jnp.float32)
-    for source in range(sources):
-        factor = jnp.exp(part_ref[source, 1, :, 0:1] - joint_max)
-        total = total + part_ref[source, 1, :, 1:2] * factor
-        summed = summed + part_ref[source, 0] * factor
+def join_kernel(groups, part_ref, copies_ref):
+    devices, rows, width = part_ref.shape
+    share = rows // 2
+    sums, stats = [], []
+    for source in range(0, devices, groups):
+        pieces = [part_ref[source + group] for group in range(groups)]
+        sums.append(jnp.concatenate([piece[:share] for piece in pieces], axis=0))
+        stats.append(jnp.concatenate([piece[share:] for piece in pieces], axis=0))
+    joint_max = functools.reduce(jnp.maximum, [stat[:, 0:1] for stat in stats])
+    factors = [jnp.exp(stat[:, 0:1] - joint_max) for stat in stats]
+    total = sum(stat[:, 1:2] * factor for stat, factor in zip(stats, factors))
+    summed = sum(part * factor for part, factor in zip(sums, factors))
     attention = (summed / total).astype(jnp.bfloat16)
     for place in range(copies_ref.shape[0]):
         copies_ref[place] = attention
 
 
-def join_partials(parts, devices):
-    shape = parts.shape[2:]
-    return pl.pallas_call(
-        join_kernel,
-        out_shape=jax.ShapeDtypeStruct((devices, *shape), jnp.bfloat16),
+def join_partials(groups, parts):
+    devices, rows, width = parts.shape
+    return pl.pallas_call(
+        functools.partial(join_kernel, groups),
+        out_shape=jax.ShapeDtypeStruct((devices, groups * rows // 2, width), jnp.bfloat16),
         compiler_params=pltpu.CompilerParams(vmem_limit_bytes=8 * MIB),
         cost_estimate=COST,
     )(parts)
 
 
-def project_kernel(rows_ref, w_ref, residual_ref, out_ref, copies_ref, wide_ref):
+def project_kernel(groups, rows_ref, w_ref, residual_ref, out_ref, copies_ref, attention_ref, wide_ref):
     devices, heads, width = rows_ref.shape
     completions = residual_ref.shape[0]
     all_heads = devices * heads // completions
+    share = heads // groups
     wide_ref[...] = rows_ref[...].reshape(devices * heads, width).astype(jnp.float32)
-    rows = [wide_ref[pl.ds(head, completions, stride=all_heads), :] for head in range(all_heads)]
-    rows = jnp.concatenate([row.astype(jnp.bfloat16) for row in rows], axis=1)
-    hidden = (residual_ref[...].astype(jnp.float32) + dot_rows(rows, w_ref[...])).astype(jnp.bfloat16)
+    rows = []
+    for group in range(groups):
+        for taker in range(groups):
+            for head in range(share):
+                place = (taker * groups + group) * share + head
+                row = wide_ref[pl.ds(place, completions, stride=all_heads), :]
+                rows.append(row.astype(jnp.bfloat16))
+    projected = dot_rows(jnp.concatenate(rows, axis=1), w_ref[...])
+    hidden = (residual_ref[...].astype(jnp.float32) + projected).astype(jnp.bfloat16)
     out_ref[...] = hidden
     for place in range(copies_ref.shape[0]):
         copies_ref[place] = hidden
-
-
-def project(rows, w_out, residual):
+    me, mine = lax.axis_index("ctx"), lax.axis_index("head")
+    own = [wide_ref[pl.ds((me * groups + taker) * heads, heads), :] for taker in range(groups)]
+    attention = jnp.zeros((heads, width), jnp.float32)
+    for group in range(groups):
+        rows = slice(group * share, (group + 1) * share)
+        candidate = jnp.concatenate([piece[rows] for piece in own], axis=0)
+        attention = jnp.where(mine == group, candidate, attention)
+    attention_ref[...] = attention.astype(jnp.bfloat16)
+
+
+def project(groups, rows, w_out, residual):
     devices, heads, width = rows.shape
     return pl.pallas_call(
-        project_kernel,
+        functools.partial(project_kernel, groups),
         out_shape=(
             jax.ShapeDtypeStruct(residual.shape, jnp.bfloat16),
             jax.ShapeDtypeStruct((devices, *residual.shape), jnp.bfloat16),
+            jax.ShapeDtypeStruct((heads, width), jnp.bfloat16),
         ),
         scratch_shapes=[pltpu.VMEM((devices * heads, width), jnp.float32)],
         compiler_params=pltpu.CompilerParams(vmem_limit_bytes=12 * MIB),
@@ -167,9 +194,9 @@
 
 
 def forward_kernel(
-    pieces_ref, gain_ref, copies_ref, gate_ref, up_ref, down_ref, out_ref, attention_hbm, state_ref, sem
+    pieces_ref, gain_ref, attention_ref, gate_ref, up_ref, down_ref, out_ref, attention_hbm, state_ref, sem
 ):
-    keep = pltpu.make_async_copy(copies_ref.at[0], attention_hbm, sem)
+    keep = pltpu.make_async_copy(attention_ref, attention_hbm, sem)
     keep.start()
     devices, completions, columns = pieces_ref.shape
     for place in range(devices):
@@ -187,13 +214,13 @@
     keep.wait()
 
 
-def forward(pieces, gain, copies, *weights):
+def forward(pieces, gain, attention, *weights):
     devices, completions, columns = pieces.shape
     return pl.pallas_call(
         forward_kernel,
         out_shape=(
             jax.ShapeDtypeStruct(pieces.shape, jnp.bfloat16),
-            jax.ShapeDtypeStruct(copies.shape[1:], jnp.bfloat16),
+            jax.ShapeDtypeStruct(attention.shape, jnp.bfloat16),
         ),
         out_specs=(pl.BlockSpec(memory_space=pltpu.VMEM), pl.BlockSpec(memory_space=pl.ANY)),
         scratch_shapes=[
@@ -202,11 +229,11 @@
         ],
         compiler_params=pltpu.CompilerParams(vmem_limit_bytes=8 * MIB),
         cost_estimate=COST,
-    )(pieces, gain, copies, *weights)
-
-
-def exchange(copies, axes=BOTH):
-    return lax.all_to_all(copies, axes, split_axis=0, concat_axis=0, tiled=True)
+    )(pieces, gain, attention, *weights)
+
+
+def exchange(copies):
+    return lax.all_to_all(copies, BOTH, split_axis=0, concat_axis=0, tiled=True)
 
 
 def body(
@@ -225,19 +252,15 @@
     w_up,
     w_down,
 ):
-    ctx_count = lax.axis_size("ctx")
-    devices = ctx_count * lax.axis_size("head")
-    copies, own_length = spread(lengths, queries, ctx_count)
-    arrived = exchange(copies, "ctx")
+    groups = lax.axis_size("head")
+    devices = lax.axis_size("ctx") * groups
+    copies, own_length = spread(lengths, queries, devices)
     rows_of = lambda values: values.reshape(-1, values.shape[-1])
-    parts = attend(
-        own_length, arrived, queries, k_new, v_new, *map(rows_of, (k_suffix, v_suffix, k_prefix, v_prefix))
-    )
-    copies = join_partials(exchange(parts, "ctx"), devices)
-    hidden_part, hidden_copies = project(exchange(copies), w_out.T, residual)
-    shares, attention = forward(
-        exchange(hidden_copies), norm_gain, copies, w_gate.T, w_up.T, w_down
-    )
+    cached = map(rows_of, (k_suffix, v_suffix, k_prefix, v_prefix))
+    parts = attend(groups, own_length, exchange(copies), queries, k_new, v_new, *cached)
+    copies = join_partials(groups, exchange(parts))
+    hidden_part, copies, attention = project(groups, exchange(copies), w_out.T, residual)
+    shares, attention = forward(exchange(copies), norm_gain, attention, w_gate.T, w_up.T, w_down)
     summed = jnp.sum(exchange(shares).astype(jnp.float32), axis=0)
     next_hidden = (hidden_part.astype(jnp.float32) + summed).astype(jnp.bfloat16)
     return (attention[None], next_hidden)

time: 63 us -> 63.5 us (level)
  blocking collectives: 52.4 us -> 53.1 us
    all_to_all x5, blocking collectives: 52.4 us -> 53.1 us  [exchange(): return lax.all_to_all(copies, BOTH, split_axis=0, concat_axis=0, tiled=True)]
where the time goes in v7:
time: 63.5 us; the launch traced here: 63.2 us
  blocking collectives  53.1 us (84%)
  Pallas kernels  7.92 us (12%)
  between operations  1.51 us (2%)
  other arithmetic  0.64 us (1%)
    all_to_all x5, blocking collectives, exchange(): return lax.all_to_all(copies, BOTH, split_axis=0, concat_axis=0, tiled=True)  53.1 us
    pallas_call x1, Pallas kernels, forward(): pl.pallas_call(forward_kernel, out_shape=(jax.ShapeDtypeStruct(pieces.sha...  5.27 us

profile of v7, /device:TPU:0, one launch (start us, length us, event | category | flops | bytes accessed | tf_op | source)
XLA Modules:
  0.0 63.2 jit_solution(5395099285299209360)
XLA Ops:
  1.3 0.0 copy-start.1
  1.3 0.0 copy-start.2
  1.3 0.0 copy-start.3
  1.3 0.0 copy-start.4
  1.3 0.0 copy-start.7
  1.3 0.0 copy-start.8
  1.3 0.8 %shard_map.149 = (bf16[32,8,128]{2,1,0:T(8,128)(2,1)S(1)}, s32[8,128]{1,0:T(8,128)S(1)}) custom-call(s32[1]{0:T(128)S(6)} %copy.16.length_ref, bf16[1,8,128]{2,1,0:T(8,128)(2,1)} %q_ref.1), custom_call_target="tpu_custom_call" | custom-call | flops 10000000000 | bytes 1048576 | tf_op jit(solution)/shard_map/pallas_call | solution.py:50
  2.2 14.5 %all_to_all.25.arrived_ref = bf16[32,8,128]{2,1,0:T(8,128)(2,1)S(1)} all-to-all(bf16[32,8,128]{2,1,0:T(8,128)(2,1)S(1)} %get-tuple-element.10), channel_id=1, replica_groups=mesh['ctx'=8,'head'=4] {'ctx','head'}, dimensions={0} | all-to-all | bytes 131072 | tf_op jit(solution)/shard_map/all_to_all | solution.py:236
  16.8 1.1 %shard_map.150 = f32[32,4,128]{2,1,0:T(4,128)S(1)} custom-call(s32[8,128]{1,0:T(8,128)S(1)} %get-tuple-element.9.length_ref, bf16[32,8,128]{2,1,0:T(8,128)(2,1)S(1)} %all_to_all.25.arrived_ref, bf16[1,8,128]{2,1,0:T(8,128)(2,1)S(1)} %copy-done.7, bf16[1,4,128]{2,1,0:T(4,128)(2,1)S(1)} %copy-done.8, bf16[1,4,128]{2,1,0:T(4,128)(2,1)S(1)} %copy-done.9, ...), custom_call_target="tpu_custom_call" | custom-call | flops 10000000000 | bytes 1048576 | tf_op jit(solution)/shard_map/pallas_call | solution.py:117
  17.9 9.1 %all_to_all.26.part_ref = f32[32,4,128]{2,1,0:T(4,128)S(1)} all-to-all(f32[32,4,128]{2,1,0:T(4,128)S(1)} %shard_map.150), channel_id=1, replica_groups=mesh['ctx'=8,'head'=4] {'ctx','head'}, dimensions={0} | all-to-all | bytes 131072 | tf_op jit(solution)/shard_map/all_to_all | solution.py:236
  27.0 0.0 slice-start.4
  27.0 0.2 shard_map.151
  27.2 9.4 %all_to_all.27.rows_ref = bf16[32,8,128]{2,1,0:T(8,128)(2,1)S(1)} all-to-all(bf16[32,8,128]{2,1,0:T(8,128)(2,1)S(1)} %shard_map.151), channel_id=1, replica_groups=mesh['ctx'=8,'head'=4] {'ctx','head'}, dimensions={0} | all-to-all | bytes 131072 | tf_op jit(solution)/shard_map/all_to_all | solution.py:236
  36.6 0.0 slice-start.5
  36.6 0.0 copy-start.5
  36.6 0.5 shard_map.152
  37.1 10.2 %all_to_all.28.pieces_ref = bf16[32,8,168]{2,1,0:T(8,128)(2,1)S(1)} all-to-all(bf16[32,8,168]{2,1,0:T(8,128)(2,1)S(1)} %get-tuple-element.11), channel_id=1, replica_groups=mesh['ctx'=8,'head'=4] {'ctx','head'}, dimensions={0} | all-to-all | bytes 172032 | tf_op jit(solution)/shard_map/all_to_all | solution.py:236
  47.3 0.0 slice-done.1
  47.3 0.0 slice-done.3
  47.3 0.0 slice-done.5
  47.4 0.0 copy-done.5
  47.4 5.3 %shard_map.153 = (bf16[32,8,168]{2,1,0:T(8,128)(2,1)S(1)}, bf16[8,128]{1,0:T(8,128)(2,1)}) custom-call(bf16[32,8,168]{2,1,0:T(8,128)(2,1)S(1)} %all_to_all.28.pieces_ref, f32[5376]{0:T(1024)S(1)} %copy-done.5, bf16[8,128]{1,0:T(8,128)(2,1)S(1)} %get-tuple-element.12.attention_ref, bf16[672,5376]{1,0:T(8,128)(2,1)S(1)} %bitcast.10, ...), custom_call_target="tpu_custom_call" | custom-call | flops 10000000000 | bytes 1048576 | tf_op jit(solution)/shard_map/pallas_call | solution.py:219
  52.7 9.9 %all_to_all.29 = bf16[32,8,168]{2,1,0:T(8,128)(2,1)S(1)} all-to-all(bf16[32,8,168]{2,1,0:T(8,128)(2,1)S(1)} %get-tuple-element.15), channel_id=1, replica_groups=mesh['ctx'=8,'head'=4] {'ctx','head'}, dimensions={0} | all-to-all | bytes 172032 | tf_op jit(solution)/shard_map/all_to_all | solution.py:236
  62.7 0.6 add_convert_fusion
  (23 shorter events, 0.1 us)
Async XLA Ops:
  1.3 15.4 %copy-start.1 = (bf16[1024,4,128]{2,1,0:T(4,128)(2,1)S(1)}, bf16[1024,4,128]{2,1,0:T(4,128)(2,1)}, u32[]{:S(2)}) copy-start(bf16[1024,4,128]{2,1,0:T(4,128)(2,1)} %param.20) | copy-start | bytes 3145732
  1.3 15.4 %copy-start.2 = (bf16[1024,4,128]{2,1,0:T(4,128)(2,1)S(1)}, bf16[1024,4,128]{2,1,0:T(4,128)(2,1)}, u32[]{:S(2)}) copy-start(bf16[1024,4,128]{2,1,0:T(4,128)(2,1)} %param.21) | copy-start | bytes 3145732
  1.3 15.4 %copy-start.3 = (bf16[1,256,4,128]{3,2,1,0:T(4,128)(2,1)S(1)}, bf16[1,256,4,128]{3,2,1,0:T(4,128)(2,1)}, u32[]{:S(2)}) copy-start(bf16[1,256,4,128]{3,2,1,0:T(4,128)(2,1)} %param.17) | copy-start | bytes 786436
  1.3 15.4 %copy-start.4 = (bf16[1,256,4,128]{3,2,1,0:T(4,128)(2,1)S(1)}, bf16[1,256,4,128]{3,2,1,0:T(4,128)(2,1)}, u32[]{:S(2)}) copy-start(bf16[1,256,4,128]{3,2,1,0:T(4,128)(2,1)} %param.18) | copy-start | bytes 786436
  1.3 15.4 %copy-start.7 = (bf16[1,8,128]{2,1,0:T(8,128)(2,1)S(1)}, bf16[1,8,128]{2,1,0:T(8,128)(2,1)}, u32[]{:S(2)}) copy-start(bf16[1,8,128]{2,1,0:T(8,128)(2,1)} %q_ref.1) | copy-start | bytes 6148
  1.3 15.4 %copy-start.8 = (bf16[1,4,128]{2,1,0:T(4,128)(2,1)S(1)}, bf16[1,4,128]{2,1,0:T(4,128)(2,1)}, u32[]{:S(2)}) copy-start(bf16[1,4,128]{2,1,0:T(4,128)(2,1)} %kn_ref.1) | copy-start | bytes 3076
  1.3 15.4 %copy-start.9 = (bf16[1,4,128]{2,1,0:T(4,128)(2,1)S(1)}, bf16[1,4,128]{2,1,0:T(4,128)(2,1)}, u32[]{:S(2)}) copy-start(bf16[1,4,128]{2,1,0:T(4,128)(2,1)} %vn_ref.1) | copy-start | bytes 3076
  27.0 9.6 %copy-start = (bf16[4096,168]{0,1:T(8,128)(2,1)S(1)}, bf16[4096,168]{0,1:T(8,128)(2,1)}, u32[]{:S(2)}) copy-start(bf16[4096,168]{0,1:T(8,128)(2,1)} %param.22) | copy-start | bytes 4128772
  27.0 9.6 %copy-start.6 = (bf16[8,168]{1,0:T(8,128)(2,1)S(1)}, bf16[8,168]{1,0:T(8,128)(2,1)}, u32[]{:S(2)}) copy-start(bf16[8,168]{1,0:T(8,128)(2,1)} %residual_ref.1) | copy-start | bytes 8068
  27.0 20.3 %slice-start = ((s8[7225344]{0:T(1024)(128)(4,1)}), s8[4194304]{0:T(1024)(128)(4,1)S(1)}, s32[]{:S(2)}) async-start(s8[7225344]{0:T(1024)(128)(4,1)} %bitcast.8), calls=%async_computation.5 | async-start | bytes 8388608
  27.0 20.3 %slice-start.2 = ((s8[7225344]{0:T(1024)(128)(4,1)}), s8[4194304]{0:T(1024)(128)(4,1)S(1)}, s32[]{:S(2)}) async-start(s8[7225344]{0:T(1024)(128)(4,1)} %bitcast.11), calls=%async_computation.7 | async-start | bytes 8388608
  27.0 20.3 %slice-start.4 = ((s8[7225344]{0:T(1024)(128)(4,1)}), s8[4194304]{0:T(1024)(128)(4,1)S(1)}, s32[]{:S(2)}) async-start(s8[7225344]{0:T(1024)(128)(4,1)} %bitcast.14), calls=%async_computation.9 | async-start | bytes 8388608
  36.6 10.8 %slice-start.1 = ((s8[7225344]{0:T(1024)(128)(4,1)}), s8[3031040]{0:T(1024)(128)(4,1)S(1)}, s32[]{:S(2)}) async-start(s8[7225344]{0:T(1024)(128)(4,1)} %bitcast.8), calls=%async_computation.6 | async-start | bytes 6062080
  36.6 10.8 %slice-start.3 = ((s8[7225344]{0:T(1024)(128)(4,1)}), s8[3031040]{0:T(1024)(128)(4,1)S(1)}, s32[]{:S(2)}) async-start(s8[7225344]{0:T(1024)(128)(4,1)} %bitcast.11), calls=%async_computation.8 | async-start | bytes 6062080
  36.6 10.8 %slice-start.5 = ((s8[7225344]{0:T(1024)(128)(4,1)}), s8[3031040]{0:T(1024)(128)(4,1)S(1)}, s32[]{:S(2)}) async-start(s8[7225344]{0:T(1024)(128)(4,1)} %bitcast.14), calls=%async_computation.10 | async-start | bytes 6062080
  36.6 10.8 %copy-start.5 = (f32[5376]{0:T(1024)S(1)}, f32[5376]{0:T(1024)}, u32[]{:S(2)}) copy-start(f32[5376]{0:T(1024)} %gain_ref.1) | copy-start | bytes 64516

commit v8 on v6

--- a/solution.py
+++ b/solution.py
@@ -12,6 +12,8 @@
 MASKED = -1e30
 MIB = 1024 * 1024
 COST = pl.CostEstimate(flops=10**10, bytes_accessed=MIB, transcendentals=10**6)
+JOIN_LIMIT = 2 * MIB
+TERMS = 3
 BOTH = ("ctx", "head")
 
 
@@ -61,7 +63,8 @@
 
 
 def attention_kernel(
-    length_ref, arrived_ref, q_ref, kn_ref, vn_ref, ks_ref, vs_ref, kp_ref, vp_ref, part_ref
+    finish, length_ref, arrived_ref, q_ref, kn_ref, vn_ref, ks_ref, vs_ref, kp_ref, vp_ref,
+    part_ref, sum_ref, stat_ref,
 ):
     count, heads, width = arrived_ref.shape
     kv_heads = kn_ref.shape[1]
@@ -90,24 +93,53 @@
         new_weights, vn_ref[0], preferred_element_type=jnp.float32
     )
     row_sum = jnp.dot(weights, vp_ref[...], preferred_element_type=jnp.float32)
-    part_ref[:, 0] = row_sum.reshape(count, heads, width)
-    part_ref[:, 1] = stat_rows(row_max, row_total, row_sum.shape).reshape(count, heads, width)
+    sum_ref[...] = row_sum.reshape(count, heads, width)
+    stat_ref[...] = stat_rows(row_max, row_total, row_sum.shape).reshape(count, heads, width)
     me = lax.axis_index("ctx")
-    prefix_stat = part_ref[me, 1]
+    prefix_stat = stat_ref[me]
     prefix_max = prefix_stat[:, 0:1]
     joint_max = jnp.maximum(prefix_max, suffix_max)
     prefix_factor = jnp.exp(prefix_max - joint_max)
     suffix_factor = jnp.exp(suffix_max - joint_max)
     joint_total = prefix_stat[:, 1:2] * prefix_factor + suffix_total * suffix_factor
-    joint_sum = part_ref[me, 0] * prefix_factor + suffix_sum * suffix_factor
-    part_ref[me, 0] = joint_sum
-    part_ref[me, 1] = stat_rows(joint_max, joint_total, joint_sum.shape)
-
-
-def attend(lengths, arrived, *operands):
-    return pl.pallas_call(
-        attention_kernel,
-        out_shape=jax.ShapeDtypeStruct((arrived.shape[0], 2, *arrived.shape[1:]), jnp.float32),
+    joint_sum = sum_ref[me] * prefix_factor + suffix_sum * suffix_factor
+    sum_ref[me] = joint_sum
+    stat_ref[me] = stat_rows(joint_max, joint_total, joint_sum.shape)
+    finish(part_ref, sum_ref, stat_ref)
+
+
+def keep_apart(part_ref, sum_ref, stat_ref):
+    part_ref[:, 0] = sum_ref[...]
+    part_ref[:, 1] = stat_ref[...]
+
+
+def spread_shares(part_ref, sum_ref, stat_ref):
+    count, heads, width = sum_ref.shape
+    rows = count * heads
+    stats = stat_ref[...].reshape(rows, width)
+    total = stats[:, 1:2]
+    share = (sum_ref[...].reshape(rows, width) / total).astype(jnp.bfloat16)
+    share = share.reshape(count, heads, width)
+    rest = jnp.broadcast_to(stats[:, 0:1] + jnp.log(total), (rows, width))
+    lane = lax.broadcasted_iota(jnp.int32, (rows, width), 1)
+    terms = jnp.zeros((rows, width), jnp.float32)
+    for place in range(TERMS):
+        term = rest.astype(jnp.bfloat16).astype(jnp.float32)
+        terms = jnp.where(lane == place, term, terms)
+        rest = rest - term
+    if rows < width:
+        terms = jnp.concatenate([terms, jnp.zeros((width - rows, width), jnp.float32)], axis=0)
+    logs = terms.T[:heads].astype(jnp.bfloat16)
+    for place in range(part_ref.shape[0]):
+        part_ref[place, :count] = share
+        part_ref[place, count] = logs
+
+
+def attend(finish, part, lengths, arrived, *operands):
+    return pl.pallas_call(
+        functools.partial(attention_kernel, finish),
+        out_shape=part,
+        scratch_shapes=[pltpu.VMEM(arrived.shape, jnp.float32)] * 2,
         compiler_params=pltpu.CompilerParams(vmem_limit_bytes=24 * MIB),
         cost_estimate=COST,
     )(lengths, arrived, *operands)
@@ -152,6 +184,63 @@
         copies_ref[place] = hidden
 
 
+def join_project_kernel(
+    shares_ref, w_ref, residual_ref, out_ref, copies_ref, attention_ref, wide_ref
+):
+    groups, rows, width = wide_ref.shape
+    devices, tiles, heads, unused = shares_ref.shape
+    count = devices // groups
+    logs = []
+    for group in range(groups):
+        for source in range(count):
+            tile = shares_ref[source * groups + group, count].astype(jnp.float32)
+            logs.append(jnp.sum(tile[:TERMS], axis=0, keepdims=True))
+    logs = jnp.concatenate(logs, axis=0)
+    factors = []
+    for group in range(groups):
+        own = logs[group * count : (group + 1) * count]
+        weights = jnp.exp(own - jnp.max(own, axis=0, keepdims=True))
+        factors.append(weights / jnp.sum(weights, axis=0, keepdims=True))
+    if devices < width:
+        factors.append(jnp.zeros((width - devices, width), jnp.float32))
+    factors = jnp.concatenate(factors, axis=0).T
+    for group in range(groups):
+        joined = jnp.zeros((rows, width), jnp.float32)
+        for source in range(count):
+            place = group * count + source
+            share = shares_ref[source * groups + group, :count].reshape(rows, width)
+            joined = joined + share.astype(jnp.float32) * factors[:rows, place : place + 1]
+        wide_ref[group] = joined
+    pieces = [
+        wide_ref[group, pl.ds(head, count, stride=heads), :].astype(jnp.bfloat16)
+        for group in range(groups)
+        for head in range(heads)
+    ]
+    projected = dot_rows(jnp.concatenate(pieces, axis=1), w_ref[...])
+    hidden = (residual_ref[...].astype(jnp.float32) + projected).astype(jnp.bfloat16)
+    out_ref[...] = hidden
+    for place in range(copies_ref.shape[0]):
+        copies_ref[place] = hidden
+    me, mine = lax.axis_index("ctx"), lax.axis_index("head")
+    start = pl.multiple_of(me * heads, heads)
+    attention_ref[...] = wide_ref[mine, pl.ds(start, heads), :].astype(jnp.bfloat16)
+
+
+def join_project(groups, shares, w_out, residual):
+    devices, tiles, heads, width = shares.shape
+    return pl.pallas_call(
+        join_project_kernel,
+        out_shape=(
+            jax.ShapeDtypeStruct(residual.shape, jnp.bfloat16),
+            jax.ShapeDtypeStruct((devices, *residual.shape), jnp.bfloat16),
+            jax.ShapeDtypeStruct((heads, width), jnp.bfloat16),
+        ),
+        scratch_shapes=[pltpu.VMEM((groups, (tiles - 1) * heads, width), jnp.float32)],
+        compiler_params=pltpu.CompilerParams(vmem_limit_bytes=12 * MIB),
+        cost_estimate=COST,
+    )(shares, w_out, residual)
+
+
 def project(rows, w_out, residual):
     devices, heads, width = rows.shape
     return pl.pallas_call(
@@ -167,9 +256,9 @@
 
 
 def forward_kernel(
-    pieces_ref, gain_ref, copies_ref, gate_ref, up_ref, down_ref, out_ref, attention_hbm, state_ref, sem
+    pieces_ref, gain_ref, attention_ref, gate_ref, up_ref, down_ref, out_ref, attention_hbm, state_ref, sem
 ):
-    keep = pltpu.make_async_copy(copies_ref.at[0], attention_hbm, sem)
+    keep = pltpu.make_async_copy(attention_ref, attention_hbm, sem)
     keep.start()
     devices, completions, columns = pieces_ref.shape
     for place in range(devices):
@@ -178,22 +267,22 @@
     mean_square = jnp.mean(state * state, axis=-1, keepdims=True)
     gain = gain_ref[...].reshape(1, devices * columns)
     normed = (state * lax.rsqrt(mean_square + NORM_EPSILON) * gain).astype(jnp.bfloat16)
-    gate_values = dot_rows(normed, gate_ref[...])
-    up_values = dot_rows(normed, up_ref[...])
-    activated = (jax.nn.gelu(gate_values, approximate=True) * up_values).astype(jnp.bfloat16)
+    gate_values = dot_rows(gate_ref[...], normed)
+    up_values = dot_rows(up_ref[...], normed)
+    activated = (jax.nn.gelu(gate_values, approximate=True) * up_values).T.astype(jnp.bfloat16)
     share = jnp.dot(activated, down_ref[...], preferred_element_type=jnp.float32)
     for place in range(devices):
         out_ref[place] = share[:, place * columns : (place + 1) * columns].astype(jnp.bfloat16)
     keep.wait()
 
 
-def forward(pieces, gain, copies, *weights):
+def forward(pieces, gain, attention, *weights):
     devices, completions, columns = pieces.shape
     return pl.pallas_call(
         forward_kernel,
         out_shape=(
             jax.ShapeDtypeStruct(pieces.shape, jnp.bfloat16),
-            jax.ShapeDtypeStruct(copies.shape[1:], jnp.bfloat16),
+            jax.ShapeDtypeStruct(attention.shape, jnp.bfloat16),
         ),
         out_specs=(pl.BlockSpec(memory_space=pltpu.VMEM), pl.BlockSpec(memory_space=pl.ANY)),
         scratch_shapes=[
@@ -202,7 +291,7 @@
         ],
         compiler_params=pltpu.CompilerParams(vmem_limit_bytes=8 * MIB),
         cost_estimate=COST,
-    )(pieces, gain, copies, *weights)
+    )(pieces, gain, attention, *weights)
 
 
 def exchange(copies, axes=BOTH):
@@ -225,19 +314,25 @@
     w_up,
     w_down,
 ):
-    ctx_count = lax.axis_size("ctx")
-    devices = ctx_count * lax.axis_size("head")
+    ctx_count, groups = lax.axis_size("ctx"), lax.axis_size("head")
+    devices = ctx_count * groups
+    unused, heads, width = queries.shape
     copies, own_length = spread(lengths, queries, ctx_count)
     arrived = exchange(copies, "ctx")
     rows_of = lambda values: values.reshape(-1, values.shape[-1])
-    parts = attend(
-        own_length, arrived, queries, k_new, v_new, *map(rows_of, (k_suffix, v_suffix, k_prefix, v_prefix))
-    )
-    copies = join_partials(exchange(parts, "ctx"), devices)
-    hidden_part, hidden_copies = project(exchange(copies), w_out.T, residual)
-    shares, attention = forward(
-        exchange(hidden_copies), norm_gain, copies, w_gate.T, w_up.T, w_down
-    )
+    cached = map(rows_of, (k_suffix, v_suffix, k_prefix, v_prefix))
+    operands = (own_length, arrived, queries, k_new, v_new, *cached)
+    joint = jax.ShapeDtypeStruct((devices, ctx_count + 1, heads, width), jnp.bfloat16)
+    if 2 * joint.size <= JOIN_LIMIT and ctx_count * heads <= width:
+        shares = exchange(attend(spread_shares, joint, *operands))
+        hidden_part, copies, attention = join_project(groups, shares, w_out.T, residual)
+    else:
+        apart = jax.ShapeDtypeStruct((ctx_count, 2, heads, width), jnp.float32)
+        parts = exchange(attend(keep_apart, apart, *operands), "ctx")
+        copies = join_partials(parts, devices)
+        attention = copies[0]
+        hidden_part, copies = project(exchange(copies), w_out.T, residual)
+    shares, attention = forward(exchange(copies), norm_gain, attention, w_gate.T, w_up.T, w_down)
     summed = jnp.sum(exchange(shares).astype(jnp.float32), axis=0)
     next_hidden = (hidden_part.astype(jnp.float32) + summed).astype(jnp.bfloat16)
     return (attention[None], next_hidden)

time: 63 us -> 64.4 us (1.022)
  blocking collectives: 52.4 us -> 53.6 us
    all_to_all x5 -> x4, blocking collectives: 52.4 us -> 53.6 us  [exchange(): return lax.all_to_all(copies, axes, split_axis=0, concat_axis=0, tiled=True)]
    pallas_call x3 -> x2, Pallas kernels: 1.88 us -> 2.12 us  [the longest x1 1.34 us: attend(): pl.pallas_call(functools.partial(attention_kernel, finish), out_shape=par...]
where the time goes in v8:
time: 64.4 us; the launch traced here: 64.1 us
  blocking collectives  53.6 us (83%)
  Pallas kernels  8.24 us (13%)
  between operations  1.52 us (2%)
    all_to_all x4, blocking collectives, exchange(): return lax.all_to_all(copies, axes, split_axis=0, concat_axis=0, tiled=True)  53.6 us
    pallas_call x1, Pallas kernels, forward(): pl.pallas_call(forward_kernel, out_shape=(jax.ShapeDtypeStruct(pieces.sha...  5.27 us
    pallas_call x1, Pallas kernels, attend(): pl.pallas_call(functools.partial(attention_kernel, finish), out_shape=par...  1.34 us

profile of v8, /device:TPU:0, one launch (start us, length us, event | category | flops | bytes accessed | tf_op | source)
XLA Modules:
  0.0 64.1 jit_solution(4925065982658748517)
XLA Ops:
  1.3 0.0 copy-start.1
  1.3 0.0 copy-start.2
  1.3 0.8 %shard_map.149 = (bf16[8,8,128]{2,1,0:T(8,128)(2,1)S(1)}, s32[8,128]{1,0:T(8,128)S(1)}) custom-call(s32[1]{0:T(128)S(6)} %copy.16.length_ref, bf16[1,8,128]{2,1,0:T(8,128)(2,1)} %q_ref.1), custom_call_target="tpu_custom_call" | custom-call | flops 10000000000 | bytes 1048576 | tf_op jit(solution)/shard_map/pallas_call | solution.py:52
  2.2 13.7 %all_to_all.20.arrived_ref = bf16[8,8,128]{2,1,0:T(8,128)(2,1)S(1)} all-to-all(bf16[8,8,128]{2,1,0:T(8,128)(2,1)S(1)} %get-tuple-element.10), channel_id=1, replica_groups=mesh['ctx'=8,'head'=4] {'ctx'}, dimensions={0} | all-to-all | bytes 32768 | tf_op jit(solution)/shard_map/all_to_all | solution.py:298
  15.9 0.0 copy-done.3
  15.9 0.0 copy-done.4
  15.9 0.0 copy-done.7
  15.9 0.0 copy-done.8
  15.9 0.0 copy-done.9
  15.9 0.0 copy-start
  15.9 0.0 copy-start.6
  15.9 1.3 %shard_map.150 = bf16[32,9,8,128]{3,2,1,0:T(8,128)(2,1)S(1)} custom-call(s32[8,128]{1,0:T(8,128)S(1)} %get-tuple-element.9.length_ref, bf16[8,8,128]{2,1,0:T(8,128)(2,1)S(1)} %all_to_all.20.arrived_ref, bf16[1,8,128]{2,1,0:T(8,128)(2,1)S(1)} %copy-done.7, bf16[1,4,128]{2,1,0:T(4,128)(2,1)S(1)} %copy-done.8, bf16[1,4,128]{2,1,0:T(4,128)(2,1)S(1)} %copy-done.9, ...), custom_call_target="tpu_custom_call" | custom-call | flops 10000000000 | bytes 1048576 | tf_op jit(solution)/shard_map/pallas_call | solution.py:139
  17.3 0.0 slice-start
  17.3 0.0 slice-start.2
  17.3 0.0 slice-start.4
  17.3 18.7 %all_to_all.21.shares_ref = bf16[32,9,8,128]{3,2,1,0:T(8,128)(2,1)S(1)} all-to-all(bf16[32,9,8,128]{3,2,1,0:T(8,128)(2,1)S(1)} %shard_map.150), channel_id=1, replica_groups=mesh['ctx'=8,'head'=4] {'ctx','head'}, dimensions={0} | all-to-all | bytes 1179648 | tf_op jit(solution)/shard_map/all_to_all | solution.py:298
  36.0 0.0 copy-done
  36.0 0.0 slice-start.5
  36.1 0.0 copy-start.5
  36.1 0.8 %shard_map.151 = (bf16[8,168]{1,0:T(8,128)(2,1)S(1)}, bf16[32,8,168]{2,1,0:T(8,128)(2,1)S(1)}, bf16[8,128]{1,0:T(8,128)(2,1)S(1)}) custom-call(bf16[32,9,8,128]{3,2,1,0:T(8,128)(2,1)S(1)} %all_to_all.21.shares_ref, bf16[168,4096]{1,0:T(8,128)(2,1)S(1)} %bitcast.16, bf16[8,168]{1,0:T(8,128)(2,1)S(1)} %copy-done.6), custom_call_target="tpu_custom_call" | custom-call | flops 10000000000 | bytes 1048576 | tf_op jit(solution)/shard_map/pallas_call | solution.py:231
  36.9 11.2 %all_to_all.22.pieces_ref = bf16[32,8,168]{2,1,0:T(8,128)(2,1)S(1)} all-to-all(bf16[32,8,168]{2,1,0:T(8,128)(2,1)S(1)} %get-tuple-element.11), channel_id=1, replica_groups=mesh['ctx'=8,'head'=4] {'ctx','head'}, dimensions={0} | all-to-all | bytes 172032 | tf_op jit(solution)/shard_map/all_to_all | solution.py:298
  48.2 5.3 %shard_map.152 = (bf16[32,8,168]{2,1,0:T(8,128)(2,1)S(1)}, bf16[8,128]{1,0:T(8,128)(2,1)}) custom-call(bf16[32,8,168]{2,1,0:T(8,128)(2,1)S(1)} %all_to_all.22.pieces_ref, f32[5376]{0:T(1024)S(1)} %copy-done.5, bf16[8,128]{1,0:T(8,128)(2,1)S(1)} %get-tuple-element.12.attention_ref, bf16[672,5376]{1,0:T(8,128)(2,1)S(1)} %bitcast.10, ...), custom_call_target="tpu_custom_call" | custom-call | flops 10000000000 | bytes 1048576 | tf_op jit(solution)/shard_map/pallas_call | solution.py:281
  53.4 10.0 %all_to_all.23 = bf16[32,8,168]{2,1,0:T(8,128)(2,1)S(1)} all-to-all(bf16[32,8,168]{2,1,0:T(8,128)(2,1)S(1)} %get-tuple-element.15), channel_id=1, replica_groups=mesh['ctx'=8,'head'=4] {'ctx','head'}, dimensions={0} | all-to-all | bytes 172032 | tf_op jit(solution)/shard_map/all_to_all | solution.py:298
  63.5 0.6 add_convert_fusion
  (21 shorter events, 0.1 us)
Async XLA Ops:
  1.3 14.6 %copy-start.1 = (bf16[1024,4,128]{2,1,0:T(4,128)(2,1)S(1)}, bf16[1024,4,128]{2,1,0:T(4,128)(2,1)}, u32[]{:S(2)}) copy-start(bf16[1024,4,128]{2,1,0:T(4,128)(2,1)} %param.20) | copy-start | bytes 3145732
  1.3 14.6 %copy-start.2 = (bf16[1024,4,128]{2,1,0:T(4,128)(2,1)S(1)}, bf16[1024,4,128]{2,1,0:T(4,128)(2,1)}, u32[]{:S(2)}) copy-start(bf16[1024,4,128]{2,1,0:T(4,128)(2,1)} %param.21) | copy-start | bytes 3145732
  1.3 14.6 %copy-start.3 = (bf16[1,256,4,128]{3,2,1,0:T(4,128)(2,1)S(1)}, bf16[1,256,4,128]{3,2,1,0:T(4,128)(2,1)}, u32[]{:S(2)}) copy-start(bf16[1,256,4,128]{3,2,1,0:T(4,128)(2,1)} %param.17) | copy-start | bytes 786436
  1.3 14.6 %copy-start.4 = (bf16[1,256,4,128]{3,2,1,0:T(4,128)(2,1)S(1)}, bf16[1,256,4,128]{3,2,1,0:T(4,128)(2,1)}, u32[]{:S(2)}) copy-start(bf16[1,256,4,128]{3,2,1,0:T(4,128)(2,1)} %param.18) | copy-start | bytes 786436
  1.3 14.6 %copy-start.7 = (bf16[1,8,128]{2,1,0:T(8,128)(2,1)S(1)}, bf16[1,8,128]{2,1,0:T(8,128)(2,1)}, u32[]{:S(2)}) copy-start(bf16[1,8,128]{2,1,0:T(8,128)(2,1)} %q_ref.1) | copy-start | bytes 6148
  1.3 14.6 %copy-start.8 = (bf16[1,4,128]{2,1,0:T(4,128)(2,1)S(1)}, bf16[1,4,128]{2,1,0:T(4,128)(2,1)}, u32[]{:S(2)}) copy-start(bf16[1,4,128]{2,1,0:T(4,128)(2,1)} %kn_ref.1) | copy-start | bytes 3076
  1.3 14.6 %copy-start.9 = (bf16[1,4,128]{2,1,0:T(4,128)(2,1)S(1)}, bf16[1,4,128]{2,1,0:T(4,128)(2,1)}, u32[]{:S(2)}) copy-start(bf16[1,4,128]{2,1,0:T(4,128)(2,1)} %vn_ref.1) | copy-start | bytes 3076
  15.9 20.1 %copy-start = (bf16[4096,168]{0,1:T(8,128)(2,1)S(1)}, bf16[4096,168]{0,1:T(8,128)(2,1)}, u32[]{:S(2)}) copy-start(bf16[4096,168]{0,1:T(8,128)(2,1)} %param.22) | copy-start | bytes 4128772
  15.9 20.1 %copy-start.6 = (bf16[8,168]{1,0:T(8,128)(2,1)S(1)}, bf16[8,168]{1,0:T(8,128)(2,1)}, u32[]{:S(2)}) copy-start(bf16[8,168]{1,0:T(8,128)(2,1)} %residual_ref.1) | copy-start | bytes 8068
  17.3 30.8 %slice-start = ((s8[7225344]{0:T(1024)(128)(4,1)}), s8[4194304]{0:T(1024)(128)(4,1)S(1)}, s32[]{:S(2)}) async-start(s8[7225344]{0:T(1024)(128)(4,1)} %bitcast.8), calls=%async_computation.4 | async-start | bytes 8388608
  17.3 30.8 %slice-start.2 = ((s8[7225344]{0:T(1024)(128)(4,1)}), s8[4194304]{0:T(1024)(128)(4,1)S(1)}, s32[]{:S(2)}) async-start(s8[7225344]{0:T(1024)(128)(4,1)} %bitcast.11), calls=%async_computation.6 | async-start | bytes 8388608
  17.3 30.8 %slice-start.4 = ((s8[7225344]{0:T(1024)(128)(4,1)}), s8[4194304]{0:T(1024)(128)(4,1)S(1)}, s32[]{:S(2)}) async-start(s8[7225344]{0:T(1024)(128)(4,1)} %bitcast.14), calls=%async_computation.8 | async-start | bytes 8388608
  36.0 12.1 %slice-start.1 = ((s8[7225344]{0:T(1024)(128)(4,1)}), s8[3031040]{0:T(1024)(128)(4,1)S(1)}, s32[]{:S(2)}) async-start(s8[7225344]{0:T(1024)(128)(4,1)} %bitcast.8), calls=%async_computation.5 | async-start | bytes 6062080
  36.0 12.1 %slice-start.3 = ((s8[7225344]{0:T(1024)(128)(4,1)}), s8[3031040]{0:T(1024)(128)(4,1)S(1)}, s32[]{:S(2)}) async-start(s8[7225344]{0:T(1024)(128)(4,1)} %bitcast.11), calls=%async_computation.7 | async-start | bytes 6062080
  36.0 12.1 %slice-start.5 = ((s8[7225344]{0:T(1024)(128)(4,1)}), s8[3031040]{0:T(1024)(128)(4,1)S(1)}, s32[]{:S(2)}) async-start(s8[7225344]{0:T(1024)(128)(4,1)} %bitcast.14), calls=%async_computation.9 | async-start | bytes 6062080
  36.1 12.1 %copy-start.5 = (f32[5376]{0:T(1024)S(1)}, f32[5376]{0:T(1024)}, u32[]{:S(2)}) copy-start(f32[5376]{0:T(1024)} %gain_ref.1) | copy-start | bytes 64516

commit v9 on v6

--- a/solution.py
+++ b/solution.py
@@ -12,6 +12,9 @@
 MASKED = -1e30
 MIB = 1024 * 1024
 COST = pl.CostEstimate(flops=10**10, bytes_accessed=MIB, transcendentals=10**6)
+TERMS = 3
+LANES = 128
+HALF = LANES // 2
 BOTH = ("ctx", "head")
 
 
@@ -35,6 +38,33 @@
 def stat_rows(row_max, row_total, shape):
     lane = lax.broadcasted_iota(jnp.int32, shape, 1)
     return jnp.where(lane == 0, row_max, row_total)
+
+
+def slot(rows, columns):
+    if rows == 8 and LANES < columns <= LANES + HALF:
+        return 3, 4, LANES
+    return rows, columns
+
+
+def put(ref, places, value):
+    if ref.ndim == 3:
+        for place in places:
+            ref[place] = value.astype(ref.dtype)
+        return
+    rows, columns = value.shape
+    rest = value[:, LANES:]
+    if columns < LANES + HALF:
+        rest = jnp.concatenate([rest, jnp.zeros((rows, LANES + HALF - columns), value.dtype)], axis=1)
+    rest = jnp.concatenate([rest[:4], rest[4:]], axis=1)
+    pieces = [piece.astype(ref.dtype) for piece in (value[:4, :LANES], value[4:, :LANES], rest)]
+    for place in places:
+        for part, piece in enumerate(pieces):
+            ref[place, part] = piece
+
+
+def unpacked(first, second, rest, columns):
+    rest = jnp.concatenate([rest[:, : columns - LANES], rest[:, HALF : HALF + columns - LANES]], axis=0)
+    return jnp.concatenate([first, second], axis=0), rest
 
 
 def spread_kernel(length_ref, source_hbm, copies_ref, lengths_ref, source_ref, sem):
@@ -61,7 +91,8 @@
 
 
 def attention_kernel(
-    length_ref, arrived_ref, q_ref, kn_ref, vn_ref, ks_ref, vs_ref, kp_ref, vp_ref, part_ref
+    length_ref, arrived_ref, q_ref, kn_ref, vn_ref, ks_ref, vs_ref, kp_ref, vp_ref, part_ref,
+    sum_ref, stat_ref,
 ):
     count, heads, width = arrived_ref.shape
     kv_heads = kn_ref.shape[1]
@@ -90,50 +121,60 @@
         new_weights, vn_ref[0], preferred_element_type=jnp.float32
     )
     row_sum = jnp.dot(weights, vp_ref[...], preferred_element_type=jnp.float32)
-    part_ref[:, 0] = row_sum.reshape(count, heads, width)
-    part_ref[:, 1] = stat_rows(row_max, row_total, row_sum.shape).reshape(count, heads, width)
+    sum_ref[...] = row_sum.reshape(count, heads, width)
+    stat_ref[...] = stat_rows(row_max, row_total, row_sum.shape).reshape(count, heads, width)
     me = lax.axis_index("ctx")
-    prefix_stat = part_ref[me, 1]
+    prefix_stat = stat_ref[me]
     prefix_max = prefix_stat[:, 0:1]
     joint_max = jnp.maximum(prefix_max, suffix_max)
     prefix_factor = jnp.exp(prefix_max - joint_max)
     suffix_factor = jnp.exp(suffix_max - joint_max)
     joint_total = prefix_stat[:, 1:2] * prefix_factor + suffix_total * suffix_factor
-    joint_sum = part_ref[me, 0] * prefix_factor + suffix_sum * suffix_factor
-    part_ref[me, 0] = joint_sum
-    part_ref[me, 1] = stat_rows(joint_max, joint_total, joint_sum.shape)
+    joint_sum = sum_ref[me] * prefix_factor + suffix_sum * suffix_factor
+    sum_ref[me] = joint_sum
+    stat_ref[me] = stat_rows(joint_max, joint_total, joint_sum.shape)
+    lane = lax.broadcasted_iota(jnp.int32, (heads, HALF), 1)
+    for place in range(count):
+        total = stat_ref[place, :, 1:2]
+        rest = jnp.broadcast_to(stat_ref[place, :, 0:1] + jnp.log(total), (heads, HALF))
+        terms = jnp.zeros((heads, HALF), jnp.float32)
+        for term in range(TERMS):
+            rounded = rest.astype(jnp.bfloat16).astype(jnp.float32)
+            terms = jnp.where(lane == term, rounded, terms)
+            rest = rest - rounded
+        put(part_ref, (place,), jnp.concatenate([sum_ref[place] / total, terms], axis=1))
 
 
 def attend(lengths, arrived, *operands):
+    count, heads, width = arrived.shape
     return pl.pallas_call(
         attention_kernel,
-        out_shape=jax.ShapeDtypeStruct((arrived.shape[0], 2, *arrived.shape[1:]), jnp.float32),
+        out_shape=jax.ShapeDtypeStruct((count, *slot(heads, width + HALF)), jnp.bfloat16),
+        scratch_shapes=[pltpu.VMEM(arrived.shape, jnp.float32)] * 2,
         compiler_params=pltpu.CompilerParams(vmem_limit_bytes=24 * MIB),
         cost_estimate=COST,
     )(lengths, arrived, *operands)
 
 
 def join_kernel(part_ref, copies_ref):
-    sources = part_ref.shape[0]
-    joint_max = functools.reduce(
-        jnp.maximum, [part_ref[source, 1, :, 0:1] for source in range(sources)]
-    )
-    total = jnp.zeros_like(joint_max)
-    summed = jnp.zeros(part_ref.shape[2:], jnp.float32)
-    for source in range(sources):
-        factor = jnp.exp(part_ref[source, 1, :, 0:1] - joint_max)
-        total = total + part_ref[source, 1, :, 1:2] * factor
-        summed = summed + part_ref[source, 0] * factor
-    attention = (summed / total).astype(jnp.bfloat16)
+    logs, shares = [], []
+    for source in range(part_ref.shape[0]):
+        pieces = [part_ref[source, part].astype(jnp.float32) for part in range(part_ref.shape[1])]
+        share, terms = unpacked(*pieces, LANES + HALF)
+        shares.append(share)
+        logs.append(jnp.sum(terms[:, :TERMS], axis=1, keepdims=True))
+    largest = functools.reduce(jnp.maximum, logs)
+    factors = [jnp.exp(log - largest) for log in logs]
+    summed = sum(share * factor for share, factor in zip(shares, factors))
+    attention = (summed / sum(factors)).astype(jnp.bfloat16)
     for place in range(copies_ref.shape[0]):
         copies_ref[place] = attention
 
 
-def join_partials(parts, devices):
-    shape = parts.shape[2:]
+def join_partials(parts, shape):
     return pl.pallas_call(
         join_kernel,
-        out_shape=jax.ShapeDtypeStruct((devices, *shape), jnp.bfloat16),
+        out_shape=jax.ShapeDtypeStruct(shape, jnp.bfloat16),
         compiler_params=pltpu.CompilerParams(vmem_limit_bytes=8 * MIB),
         cost_estimate=COST,
     )(parts)
@@ -148,8 +189,7 @@
     rows = jnp.concatenate([row.astype(jnp.bfloat16) for row in rows], axis=1)
     hidden = (residual_ref[...].astype(jnp.float32) + dot_rows(rows, w_ref[...])).astype(jnp.bfloat16)
     out_ref[...] = hidden
-    for place in range(copies_ref.shape[0]):
-        copies_ref[place] = hidden
+    put(copies_ref, range(copies_ref.shape[0]), hidden.astype(jnp.float32))
 
 
 def project(rows, w_out, residual):
@@ -158,7 +198,7 @@
         project_kernel,
         out_shape=(
             jax.ShapeDtypeStruct(residual.shape, jnp.bfloat16),
-            jax.ShapeDtypeStruct((devices, *residual.shape), jnp.bfloat16),
+            jax.ShapeDtypeStruct((devices, *slot(*residual.shape)), jnp.bfloat16),
         ),
         scratch_shapes=[pltpu.VMEM((devices * heads, width), jnp.float32)],
         compiler_params=pltpu.CompilerParams(vmem_limit_bytes=12 * MIB),
@@ -171,9 +211,17 @@
 ):
     keep = pltpu.make_async_copy(copies_ref.at[0], attention_hbm, sem)
     keep.start()
-    devices, completions, columns = pieces_ref.shape
+    devices = pieces_ref.shape[0]
+    columns = state_ref.shape[1] // devices
     for place in range(devices):
-        state_ref[:, place * columns : (place + 1) * columns] = pieces_ref[place].astype(jnp.float32)
+        start = place * columns
+        if pieces_ref.ndim == 3:
+            state_ref[:, start : start + columns] = pieces_ref[place].astype(jnp.float32)
+        else:
+            pieces = [pieces_ref[place, part].astype(jnp.float32) for part in range(3)]
+            first, rest = unpacked(*pieces, columns)
+            state_ref[:, start : start + LANES] = first
+            state_ref[:, start + LANES : start + columns] = rest
     state = state_ref[...]
     mean_square = jnp.mean(state * state, axis=-1, keepdims=True)
     gain = gain_ref[...].reshape(1, devices * columns)
@@ -183,12 +231,11 @@
     activated = (jax.nn.gelu(gate_values, approximate=True) * up_values).astype(jnp.bfloat16)
     share = jnp.dot(activated, down_ref[...], preferred_element_type=jnp.float32)
     for place in range(devices):
-        out_ref[place] = share[:, place * columns : (place + 1) * columns].astype(jnp.bfloat16)
+        put(out_ref, (place,), share[:, place * columns : (place + 1) * columns])
     keep.wait()
 
 
-def forward(pieces, gain, copies, *weights):
-    devices, completions, columns = pieces.shape
+def forward(pieces, completions, gain, copies, *weights):
     return pl.pallas_call(
         forward_kernel,
         out_shape=(
@@ -197,12 +244,27 @@
         ),
         out_specs=(pl.BlockSpec(memory_space=pltpu.VMEM), pl.BlockSpec(memory_space=pl.ANY)),
         scratch_shapes=[
-            pltpu.VMEM((completions, devices * columns), jnp.float32),
+            pltpu.VMEM((completions, gain.shape[0]), jnp.float32),
             pltpu.SemaphoreType.DMA,
         ],
         compiler_params=pltpu.CompilerParams(vmem_limit_bytes=8 * MIB),
         cost_estimate=COST,
     )(pieces, gain, copies, *weights)
+
+
+def total_kernel(shares_ref, hidden_ref, out_ref):
+    summed = jnp.sum(shares_ref[...].astype(jnp.float32), axis=0)
+    if shares_ref.ndim == 4:
+        summed = jnp.concatenate(unpacked(*summed, hidden_ref.shape[1]), axis=1)
+    out_ref[...] = (hidden_ref[...].astype(jnp.float32) + summed).astype(jnp.bfloat16)
+
+
+def total(shares, hidden):
+    return pl.pallas_call(
+        total_kernel,
+        out_shape=jax.ShapeDtypeStruct(hidden.shape, jnp.bfloat16),
+        compiler_params=pltpu.CompilerParams(vmem_limit_bytes=16 * MIB),
+    )(shares, hidden)
 
 
 def exchange(copies, axes=BOTH):
@@ -233,14 +295,12 @@
     parts = attend(
         own_length, arrived, queries, k_new, v_new, *map(rows_of, (k_suffix, v_suffix, k_prefix, v_prefix))
     )
-    copies = join_partials(exchange(parts, "ctx"), devices)
+    copies = join_partials(exchange(parts, "ctx"), (devices, *queries.shape[1:]))
     hidden_part, hidden_copies = project(exchange(copies), w_out.T, residual)
     shares, attention = forward(
-        exchange(hidden_copies), norm_gain, copies, w_gate.T, w_up.T, w_down
-    )
-    summed = jnp.sum(exchange(shares).astype(jnp.float32), axis=0)
-    next_hidden = (hidden_part.astype(jnp.float32) + summed).astype(jnp.bfloat16)
-    return (attention[None], next_hidden)
+        exchange(hidden_copies), residual.shape[0], norm_gain, copies, w_gate.T, w_up.T, w_down
+    )
+    return (attention[None], total(exchange(shares), hidden_part))
 
 
 def solution(mesh):

time: 63 us -> 62.7 us (level)
  Pallas kernels: 8 us -> 9.55 us
  blocking collectives: 52.4 us -> 51.3 us
  other arithmetic: 0.64 us -> 0.01 us
    all_to_all x5, blocking collectives: 52.4 us -> 51.3 us  [exchange(): return lax.all_to_all(copies, axes, split_axis=0, concat_axis=0, tiled=True)]
    pallas_call x2 -> x3, Pallas kernels: 1.38 us -> 2.22 us  [the longest x1 1.34 us: attend(): pl.pallas_call(attention_kernel, out_shape=jax.ShapeDtypeStruct((count, *...]
    pallas_call x1, Pallas kernels: 5.28 us -> 5.91 us  [forward(): pl.pallas_call(forward_kernel, out_shape=(jax.ShapeDtypeStruct(pieces.sha...]
where the time goes in v9:
time: 62.7 us; the launch traced here: 62.4 us
  blocking collectives  51.3 us (82%)
  Pallas kernels  9.55 us (15%)
  between operations  1.5 us (2%)
    all_to_all x5, blocking collectives, exchange(): return lax.all_to_all(copies, axes, split_axis=0, concat_axis=0, tiled=True)  51.3 us
    pallas_call x1, Pallas kernels, forward(): pl.pallas_call(forward_kernel, out_shape=(jax.ShapeDtypeStruct(pieces.sha...  5.91 us
    pallas_call x1, Pallas kernels, attend(): pl.pallas_call(attention_kernel, out_shape=jax.ShapeDtypeStruct((count, *...  1.34 us

profile of v9, /device:TPU:0, one launch (start us, length us, event | category | flops | bytes accessed | tf_op | source)
XLA Modules:
  0.0 62.4 jit_solution(10350037085043094817)
XLA Ops:
  1.3 0.0 copy-start.1
  1.3 0.0 copy-start.2
  1.3 0.0 copy-start.3
  1.3 0.0 copy-start.4
  1.3 0.8 %shard_map.149 = (bf16[8,8,128]{2,1,0:T(8,128)(2,1)S(1)}, s32[8,128]{1,0:T(8,128)S(1)}) custom-call(s32[1]{0:T(128)S(6)} %copy.16.length_ref, bf16[1,8,128]{2,1,0:T(8,128)(2,1)} %q_ref.1), custom_call_target="tpu_custom_call" | custom-call | flops 10000000000 | bytes 1048576 | tf_op jit(solution)/shard_map/pallas_call | solution.py:80
  2.2 13.7 %all_to_all.25.arrived_ref = bf16[8,8,128]{2,1,0:T(8,128)(2,1)S(1)} all-to-all(bf16[8,8,128]{2,1,0:T(8,128)(2,1)S(1)} %get-tuple-element.9), channel_id=1, replica_groups=mesh['ctx'=8,'head'=4] {'ctx'}, dimensions={0} | all-to-all | bytes 32768 | tf_op jit(solution)/shard_map/all_to_all | solution.py:271
  15.9 0.0 copy-done.3
  15.9 0.0 copy-done.4
  15.9 0.0 copy-done.7
  15.9 0.0 copy-done.8
  15.9 0.0 copy-done.9
  15.9 1.3 %shard_map.150 = bf16[8,3,4,128]{3,2,1,0:T(4,128)(2,1)S(1)} custom-call(s32[8,128]{1,0:T(8,128)S(1)} %get-tuple-element.8.length_ref, bf16[8,8,128]{2,1,0:T(8,128)(2,1)S(1)} %all_to_all.25.arrived_ref, bf16[1,8,128]{2,1,0:T(8,128)(2,1)S(1)} %copy-done.7, bf16[1,4,128]{2,1,0:T(4,128)(2,1)S(1)} %copy-done.8, bf16[1,4,128]{2,1,0:T(4,128)(2,1)S(1)} %copy-done.9, ...), custom_call_target="tpu_custom_call" | custom-call | flops 10000000000 | bytes 1048576 | tf_op jit(solution)/shard_map/pallas_call | solution.py:150
  17.2 9.0 %all_to_all.26.part_ref = bf16[8,3,4,128]{3,2,1,0:T(4,128)(2,1)S(1)} all-to-all(bf16[8,3,4,128]{3,2,1,0:T(4,128)(2,1)S(1)} %shard_map.150), channel_id=1, replica_groups=mesh['ctx'=8,'head'=4] {'ctx'}, dimensions={0} | all-to-all | bytes 49152 | tf_op jit(solution)/shard_map/all_to_all | solution.py:271
  26.2 0.0 slice-start.4
  26.3 0.2 shard_map.151.copies_ref
  26.4 9.4 %all_to_all.27.rows_ref = bf16[32,8,128]{2,1,0:T(8,128)(2,1)S(1)} all-to-all(bf16[32,8,128]{2,1,0:T(8,128)(2,1)S(1)} %shard_map.151.copies_ref), channel_id=1, replica_groups=mesh['ctx'=8,'head'=4] {'ctx','head'}, dimensions={0} | all-to-all | bytes 131072 | tf_op jit(solution)/shard_map/all_to_all | solution.py:271
  35.8 0.0 slice-start.5
  35.8 0.0 copy-start.5
  35.9 0.6 shard_map.152
  36.4 9.8 %all_to_all.28.pieces_ref = bf16[32,3,4,128]{3,2,1,0:T(4,128)(2,1)S(1)} all-to-all(bf16[32,3,4,128]{3,2,1,0:T(4,128)(2,1)S(1)} %get-tuple-element.10), channel_id=1, replica_groups=mesh['ctx'=8,'head'=4] {'ctx','head'}, dimensions={0} | all-to-all | bytes 196608 | tf_op jit(solution)/shard_map/all_to_all | solution.py:271
  46.2 0.0 slice-done.2
  46.3 5.9 %shard_map.153 = (bf16[32,3,4,128]{3,2,1,0:T(4,128)(2,1)S(1)}, bf16[8,128]{1,0:T(8,128)(2,1)}) custom-call(bf16[32,3,4,128]{3,2,1,0:T(4,128)(2,1)S(1)} %all_to_all.28.pieces_ref, f32[5376]{0:T(1024)S(1)} %copy-done.5, bf16[32,8,128]{2,1,0:T(8,128)(2,1)S(1)} %shard_map.151.copies_ref, bf16[672,5376]{1,0:T(8,128)(2,1)S(1)} %bitcast.10, ...), custom_call_target="tpu_custom_call" | custom-call | flops 10000000000 | bytes 1048576 | tf_op jit(solution)/shard_map/pallas_call | solution.py:239
  52.2 9.5 %all_to_all.29.shares_ref = bf16[32,3,4,128]{3,2,1,0:T(4,128)(2,1)S(1)} all-to-all(bf16[32,3,4,128]{3,2,1,0:T(4,128)(2,1)S(1)} %get-tuple-element.12), channel_id=1, replica_groups=mesh['ctx'=8,'head'=4] {'ctx','head'}, dimensions={0} | all-to-all | bytes 196608 | tf_op jit(solution)/shard_map/all_to_all | solution.py:271
  61.7 0.7 %shard_map.154 = bf16[8,168]{1,0:T(8,128)(2,1)} custom-call(bf16[32,3,4,128]{3,2,1,0:T(4,128)(2,1)S(1)} %all_to_all.29.shares_ref, bf16[8,168]{1,0:T(8,128)(2,1)S(1)} %get-tuple-element.13.hidden_ref), custom_call_target="tpu_custom_call" | custom-call | tf_op jit(solution)/shard_map/pallas_call | solution.py:263
  (22 shorter events, 0.0 us)
Async XLA Ops:
  1.3 14.6 %copy-start.1 = (bf16[1024,4,128]{2,1,0:T(4,128)(2,1)S(1)}, bf16[1024,4,128]{2,1,0:T(4,128)(2,1)}, u32[]{:S(2)}) copy-start(bf16[1024,4,128]{2,1,0:T(4,128)(2,1)} %param.20) | copy-start | bytes 3145732
  1.3 14.6 %copy-start.2 = (bf16[1024,4,128]{2,1,0:T(4,128)(2,1)S(1)}, bf16[1024,4,128]{2,1,0:T(4,128)(2,1)}, u32[]{:S(2)}) copy-start(bf16[1024,4,128]{2,1,0:T(4,128)(2,1)} %param.21) | copy-start | bytes 3145732
  1.3 14.6 %copy-start.3 = (bf16[1,256,4,128]{3,2,1,0:T(4,128)(2,1)S(1)}, bf16[1,256,4,128]{3,2,1,0:T(4,128)(2,1)}, u32[]{:S(2)}) copy-start(bf16[1,256,4,128]{3,2,1,0:T(4,128)(2,1)} %param.17) | copy-start | bytes 786436
  1.3 14.6 %copy-start.4 = (bf16[1,256,4,128]{3,2,1,0:T(4,128)(2,1)S(1)}, bf16[1,256,4,128]{3,2,1,0:T(4,128)(2,1)}, u32[]{:S(2)}) copy-start(bf16[1,256,4,128]{3,2,1,0:T(4,128)(2,1)} %param.18) | copy-start | bytes 786436
  1.3 14.6 %copy-start.7 = (bf16[1,8,128]{2,1,0:T(8,128)(2,1)S(1)}, bf16[1,8,128]{2,1,0:T(8,128)(2,1)}, u32[]{:S(2)}) copy-start(bf16[1,8,128]{2,1,0:T(8,128)(2,1)} %q_ref.1) | copy-start | bytes 6148
  1.3 14.6 %copy-start.8 = (bf16[1,4,128]{2,1,0:T(4,128)(2,1)S(1)}, bf16[1,4,128]{2,1,0:T(4,128)(2,1)}, u32[]{:S(2)}) copy-start(bf16[1,4,128]{2,1,0:T(4,128)(2,1)} %kn_ref.1) | copy-start | bytes 3076
  1.3 14.6 %copy-start.9 = (bf16[1,4,128]{2,1,0:T(4,128)(2,1)S(1)}, bf16[1,4,128]{2,1,0:T(4,128)(2,1)}, u32[]{:S(2)}) copy-start(bf16[1,4,128]{2,1,0:T(4,128)(2,1)} %vn_ref.1) | copy-start | bytes 3076
  26.2 9.6 %copy-start = (bf16[4096,168]{0,1:T(8,128)(2,1)S(1)}, bf16[4096,168]{0,1:T(8,128)(2,1)}, u32[]{:S(2)}) copy-start(bf16[4096,168]{0,1:T(8,128)(2,1)} %param.22) | copy-start | bytes 4128772
  26.2 9.6 %copy-start.6 = (bf16[8,168]{1,0:T(8,128)(2,1)S(1)}, bf16[8,168]{1,0:T(8,128)(2,1)}, u32[]{:S(2)}) copy-start(bf16[8,168]{1,0:T(8,128)(2,1)} %residual_ref.1) | copy-start | bytes 8068
  26.2 20.0 %slice-start = ((s8[7225344]{0:T(1024)(128)(4,1)}), s8[4194304]{0:T(1024)(128)(4,1)S(1)}, s32[]{:S(2)}) async-start(s8[7225344]{0:T(1024)(128)(4,1)} %bitcast.8), calls=%async_computation.5 | async-start | bytes 8388608
  26.2 20.0 %slice-start.2 = ((s8[7225344]{0:T(1024)(128)(4,1)}), s8[4194304]{0:T(1024)(128)(4,1)S(1)}, s32[]{:S(2)}) async-start(s8[7225344]{0:T(1024)(128)(4,1)} %bitcast.11), calls=%async_computation.7 | async-start | bytes 8388608
  26.2 20.0 %slice-start.4 = ((s8[7225344]{0:T(1024)(128)(4,1)}), s8[4194304]{0:T(1024)(128)(4,1)S(1)}, s32[]{:S(2)}) async-start(s8[7225344]{0:T(1024)(128)(4,1)} %bitcast.14), calls=%async_computation.9 | async-start | bytes 8388608
  35.8 10.4 %slice-start.1 = ((s8[7225344]{0:T(1024)(128)(4,1)}), s8[3031040]{0:T(1024)(128)(4,1)S(1)}, s32[]{:S(2)}) async-start(s8[7225344]{0:T(1024)(128)(4,1)} %bitcast.8), calls=%async_computation.6 | async-start | bytes 6062080
  35.8 10.4 %slice-start.3 = ((s8[7225344]{0:T(1024)(128)(4,1)}), s8[3031040]{0:T(1024)(128)(4,1)S(1)}, s32[]{:S(2)}) async-start(s8[7225344]{0:T(1024)(128)(4,1)} %bitcast.11), calls=%async_computation.8 | async-start | bytes 6062080
  35.8 10.4 %slice-start.5 = ((s8[7225344]{0:T(1024)(128)(4,1)}), s8[3031040]{0:T(1024)(128)(4,1)S(1)}, s32[]{:S(2)}) async-start(s8[7225344]{0:T(1024)(128)(4,1)} %bitcast.14), calls=%async_computation.10 | async-start | bytes 6062080
  35.8 10.4 %copy-start.5 = (f32[5376]{0:T(1024)S(1)}, f32[5376]{0:T(1024)}, u32[]{:S(2)}) copy-start(f32[5376]{0:T(1024)} %gain_ref.1) | copy-start | bytes 64516

commit v10 on v9

--- a/solution.py
+++ b/solution.py
@@ -62,9 +62,61 @@
             ref[place, part] = piece
 
 
-def unpacked(first, second, rest, columns):
-    rest = jnp.concatenate([rest[:, : columns - LANES], rest[:, HALF : HALF + columns - LANES]], axis=0)
-    return jnp.concatenate([first, second], axis=0), rest
+def joined(first, second, rest):
+    low = jnp.concatenate([first, second], axis=0).astype(jnp.float32)
+    rest = rest.astype(jnp.float32)
+    return low, jnp.concatenate([rest, pltpu.roll(rest, HALF, 1)], axis=0)
+
+
+def turn(value, columns, back=False):
+    device = lax.axis_index("ctx") * lax.axis_size("head") + lax.axis_index("head")
+    offset = lax.rem(device * columns, LANES)
+    return pltpu.roll(value, lax.rem(LANES - offset, LANES) if back else offset, 1)
+
+
+def put_turned(ref, value):
+    rows, columns = value.shape
+    rest = jnp.concatenate(
+        [value[:, LANES:], jnp.zeros((rows, 2 * LANES - columns), value.dtype)], axis=1
+    )
+    low, rest = turn(value[:, :LANES], columns), turn(rest, columns)
+    rest = rest[:4] + pltpu.roll(rest, HALF, 1)[4:]
+    pieces = [piece.astype(ref.dtype) for piece in (low[:4], low[4:], rest)]
+    for place in range(ref.shape[0]):
+        for part, piece in enumerate(pieces):
+            ref[place, part] = piece
+
+
+def whole_state(pieces_ref, order, columns):
+    lane = lax.broadcasted_iota(jnp.int32, (8, LANES), 1)
+    tiles = {}
+    for device in range(len(order)):
+        place = order.index(device)
+        low, rest = joined(*(pieces_ref[place, part] for part in range(3)))
+        first, offset = divmod(device * columns, LANES)
+        tiles[first] = jnp.where(lane >= offset, low, tiles[first]) if offset else low
+        tiles[first + 1] = jnp.where(lane < offset, low, rest)
+        if offset + columns - LANES > LANES:
+            tiles[first + 2] = rest
+    return jnp.concatenate([tiles[place] for place in range(len(order) * columns // LANES)], axis=1)
+
+
+def put_columns(ref, order, share, columns):
+    lane = lax.broadcasted_iota(jnp.int32, (8, LANES), 1)
+    tile = lambda place: share[:, place * LANES : (place + 1) * LANES]
+    for device in range(len(order)):
+        first, offset = divmod(device * columns, LANES)
+        end = offset + columns - LANES
+        low = jnp.where(lane >= offset, tile(first), tile(first + 1)) if offset else tile(first)
+        rest = tile(first + 1)
+        own = (lane >= offset) & (lane < end)
+        if end > LANES:
+            rest = jnp.where(lane >= offset, rest, tile(first + 2))
+            own = (lane >= offset) | (lane < end - LANES)
+        rest = jnp.where(own[:4], rest[:4], pltpu.roll(rest, HALF, 1)[4:])
+        place = order.index(device)
+        for part, piece in enumerate((low[:4], low[4:], rest)):
+            ref[place, part] = piece.astype(ref.dtype)
 
 
 def spread_kernel(length_ref, source_hbm, copies_ref, lengths_ref, source_ref, sem):
@@ -159,8 +211,7 @@
 def join_kernel(part_ref, copies_ref):
     logs, shares = [], []
     for source in range(part_ref.shape[0]):
-        pieces = [part_ref[source, part].astype(jnp.float32) for part in range(part_ref.shape[1])]
-        share, terms = unpacked(*pieces, LANES + HALF)
+        share, terms = joined(*(part_ref[source, part] for part in range(3)))
         shares.append(share)
         logs.append(jnp.sum(terms[:, :TERMS], axis=1, keepdims=True))
     largest = functools.reduce(jnp.maximum, logs)
@@ -180,22 +231,26 @@
     )(parts)
 
 
-def project_kernel(rows_ref, w_ref, residual_ref, out_ref, copies_ref, wide_ref):
+def project_kernel(order, rows_ref, w_ref, residual_ref, out_ref, copies_ref, wide_ref):
     devices, heads, width = rows_ref.shape
     completions = residual_ref.shape[0]
     all_heads = devices * heads // completions
-    wide_ref[...] = rows_ref[...].reshape(devices * heads, width).astype(jnp.float32)
+    for place, device in enumerate(order):
+        wide_ref[device * heads : (device + 1) * heads] = rows_ref[place].astype(jnp.float32)
     rows = [wide_ref[pl.ds(head, completions, stride=all_heads), :] for head in range(all_heads)]
     rows = jnp.concatenate([row.astype(jnp.bfloat16) for row in rows], axis=1)
     hidden = (residual_ref[...].astype(jnp.float32) + dot_rows(rows, w_ref[...])).astype(jnp.bfloat16)
     out_ref[...] = hidden
-    put(copies_ref, range(copies_ref.shape[0]), hidden.astype(jnp.float32))
-
-
-def project(rows, w_out, residual):
+    if copies_ref.ndim == 4:
+        put_turned(copies_ref, hidden.astype(jnp.float32))
+    else:
+        put(copies_ref, range(copies_ref.shape[0]), hidden)
+
+
+def project(order, rows, w_out, residual):
     devices, heads, width = rows.shape
     return pl.pallas_call(
-        project_kernel,
+        functools.partial(project_kernel, order),
         out_shape=(
             jax.ShapeDtypeStruct(residual.shape, jnp.bfloat16),
             jax.ShapeDtypeStruct((devices, *slot(*residual.shape)), jnp.bfloat16),
@@ -207,22 +262,19 @@
 
 
 def forward_kernel(
-    pieces_ref, gain_ref, copies_ref, gate_ref, up_ref, down_ref, out_ref, attention_hbm, state_ref, sem
+    order, pieces_ref, gain_ref, copies_ref, gate_ref, up_ref, down_ref, out_ref, attention_hbm, state_ref, sem
 ):
     keep = pltpu.make_async_copy(copies_ref.at[0], attention_hbm, sem)
     keep.start()
     devices = pieces_ref.shape[0]
-    columns = state_ref.shape[1] // devices
-    for place in range(devices):
-        start = place * columns
-        if pieces_ref.ndim == 3:
-            state_ref[:, start : start + columns] = pieces_ref[place].astype(jnp.float32)
-        else:
-            pieces = [pieces_ref[place, part].astype(jnp.float32) for part in range(3)]
-            first, rest = unpacked(*pieces, columns)
-            state_ref[:, start : start + LANES] = first
-            state_ref[:, start + LANES : start + columns] = rest
-    state = state_ref[...]
+    columns = gain_ref.shape[0] // devices
+    if pieces_ref.ndim == 4:
+        state = whole_state(pieces_ref, order, columns)
+    else:
+        for place, device in enumerate(order):
+            columns_of = slice(device * columns, (device + 1) * columns)
+            state_ref[:, columns_of] = pieces_ref[place].astype(jnp.float32)
+        state = state_ref[...]
     mean_square = jnp.mean(state * state, axis=-1, keepdims=True)
     gain = gain_ref[...].reshape(1, devices * columns)
     normed = (state * lax.rsqrt(mean_square + NORM_EPSILON) * gain).astype(jnp.bfloat16)
@@ -230,14 +282,17 @@
     up_values = dot_rows(normed, up_ref[...])
     activated = (jax.nn.gelu(gate_values, approximate=True) * up_values).astype(jnp.bfloat16)
     share = jnp.dot(activated, down_ref[...], preferred_element_type=jnp.float32)
-    for place in range(devices):
-        put(out_ref, (place,), share[:, place * columns : (place + 1) * columns])
+    if pieces_ref.ndim == 4:
+        put_columns(out_ref, order, share, columns)
+    else:
+        for place, device in enumerate(order):
+            put(out_ref, (place,), share[:, device * columns : (device + 1) * columns])
     keep.wait()
 
 
-def forward(pieces, completions, gain, copies, *weights):
-    return pl.pallas_call(
-        forward_kernel,
+def forward(order, pieces, completions, gain, copies, *weights):
+    return pl.pallas_call(
+        functools.partial(forward_kernel, order),
         out_shape=(
             jax.ShapeDtypeStruct(pieces.shape, jnp.bfloat16),
             jax.ShapeDtypeStruct(copies.shape[1:], jnp.bfloat16),
@@ -255,7 +310,9 @@
 def total_kernel(shares_ref, hidden_ref, out_ref):
     summed = jnp.sum(shares_ref[...].astype(jnp.float32), axis=0)
     if shares_ref.ndim == 4:
-        summed = jnp.concatenate(unpacked(*summed, hidden_ref.shape[1]), axis=1)
+        columns = hidden_ref.shape[1]
+        low, rest = (turn(part, columns, back=True) for part in joined(*summed))
+        summed = jnp.concatenate([low, rest[:, : columns - LANES]], axis=1)
     out_ref[...] = (hidden_ref[...].astype(jnp.float32) + summed).astype(jnp.bfloat16)
 
 
@@ -267,8 +324,18 @@
     )(shares, hidden)
 
 
+def listed(ctx_count, groups):
+    order = (0, 1, 4, 5, 6, 7, 2, 3) if ctx_count == 8 else range(ctx_count)
+    return [ctx * groups + group for ctx in order for group in range(groups)]
+
+
 def exchange(copies, axes=BOTH):
-    return lax.all_to_all(copies, axes, split_axis=0, concat_axis=0, tiled=True)
+    groups = None
+    if axes == BOTH:
+        groups = [listed(lax.axis_size("ctx"), lax.axis_size("head"))]
+    return lax.all_to_all(
+        copies, axes, split_axis=0, concat_axis=0, tiled=True, axis_index_groups=groups
+    )
 
 
 def body(
@@ -296,9 +363,10 @@
         own_length, arrived, queries, k_new, v_new, *map(rows_of, (k_suffix, v_suffix, k_prefix, v_prefix))
     )
     copies = join_partials(exchange(parts, "ctx"), (devices, *queries.shape[1:]))
-    hidden_part, hidden_copies = project(exchange(copies), w_out.T, residual)
+    order = listed(ctx_count, devices // ctx_count)
+    hidden_part, hidden_copies = project(order, exchange(copies), w_out.T, residual)
     shares, attention = forward(
-        exchange(hidden_copies), residual.shape[0], norm_gain, copies, w_gate.T, w_up.T, w_down
+        order, exchange(hidden_copies), residual.shape[0], norm_gain, copies, w_gate.T, w_up.T, w_down
     )
     return (attention[None], total(exchange(shares), hidden_part))
 

time: 62.7 us -> 62.7 us (level)
  no operation moved by 1% of the time
where the time goes in v10:
time: 62.7 us; the launch traced here: 62.4 us
  blocking collectives  51.5 us (82%)
  Pallas kernels  9.4 us (15%)
  between operations  1.5 us (2%)
    all_to_all x5, blocking collectives, exchange(): lax.all_to_all(copies, axes, split_axis=0, concat_axis=0, tiled=True, axi...  51.5 us
    pallas_call x1, Pallas kernels, forward(): pl.pallas_call(functools.partial(forward_kernel, order), out_shape=(jax.S...  5.62 us
    pallas_call x1, Pallas kernels, attend(): pl.pallas_call(attention_kernel, out_shape=jax.ShapeDtypeStruct((count, *...  1.34 us

profile of v10, /device:TPU:0, one launch (start us, length us, event | category | flops | bytes accessed | tf_op | source)
XLA Modules:
  0.0 62.4 jit_solution(44911314778255952)
XLA Ops:
  1.3 0.0 copy-start.1
  1.3 0.0 copy-start.2
  1.3 0.0 copy-start.3
  1.3 0.0 copy-start.4
  1.3 0.0 copy-start.7
  1.3 0.8 %shard_map.149 = (bf16[8,8,128]{2,1,0:T(8,128)(2,1)S(1)}, s32[8,128]{1,0:T(8,128)S(1)}) custom-call(s32[1]{0:T(128)S(6)} %copy.16.length_ref, bf16[1,8,128]{2,1,0:T(8,128)(2,1)} %q_ref.1), custom_call_target="tpu_custom_call" | custom-call | flops 10000000000 | bytes 1048576 | tf_op jit(solution)/shard_map/pallas_call | solution.py:132
  2.2 13.7 %all_to_all.25.arrived_ref = bf16[8,8,128]{2,1,0:T(8,128)(2,1)S(1)} all-to-all(bf16[8,8,128]{2,1,0:T(8,128)(2,1)S(1)} %get-tuple-element.9), channel_id=1, replica_groups=mesh['ctx'=8,'head'=4] {'ctx'}, dimensions={0} | all-to-all | bytes 32768 | tf_op jit(solution)/shard_map/all_to_all | solution.py:336
  15.9 0.0 copy-done.3
  15.9 0.0 copy-done.4
  15.9 0.0 copy-done.7
  15.9 0.0 copy-done.8
  15.9 0.0 copy-done.9
  15.9 1.3 %shard_map.150 = bf16[8,3,4,128]{3,2,1,0:T(4,128)(2,1)S(1)} custom-call(s32[8,128]{1,0:T(8,128)S(1)} %get-tuple-element.8.length_ref, bf16[8,8,128]{2,1,0:T(8,128)(2,1)S(1)} %all_to_all.25.arrived_ref, bf16[1,8,128]{2,1,0:T(8,128)(2,1)S(1)} %copy-done.7, bf16[1,4,128]{2,1,0:T(4,128)(2,1)S(1)} %copy-done.8, bf16[1,4,128]{2,1,0:T(4,128)(2,1)S(1)} %copy-done.9, ...), custom_call_target="tpu_custom_call" | custom-call | flops 10000000000 | bytes 1048576 | tf_op jit(solution)/shard_map/pallas_call | solution.py:202
  17.2 9.0 %all_to_all.26.part_ref = bf16[8,3,4,128]{3,2,1,0:T(4,128)(2,1)S(1)} all-to-all(bf16[8,3,4,128]{3,2,1,0:T(4,128)(2,1)S(1)} %shard_map.150), channel_id=1, replica_groups=mesh['ctx'=8,'head'=4] {'ctx'}, dimensions={0} | all-to-all | bytes 49152 | tf_op jit(solution)/shard_map/all_to_all | solution.py:336
  26.2 0.0 slice-start.4
  26.3 0.2 shard_map.151.copies_ref
  26.4 9.4 %all_to_all.27.rows_ref = bf16[32,8,128]{2,1,0:T(8,128)(2,1)S(1)} all-to-all(bf16[32,8,128]{2,1,0:T(8,128)(2,1)S(1)} %shard_map.151.copies_ref), channel_id=1, replica_groups={{0,1,2,3,4,5,6,7,16,17,18,19,20,21,22,23,24,25,26,27,28,29,30,31,8,9,10..., dimensions={0} | all-to-all | bytes 131072 | tf_op jit(solution)/shard_map/all_to_all | solution.py:336
  35.9 0.0 slice-start.5
  35.9 0.0 copy-start.5
  35.9 0.6 %shard_map.152 = (bf16[8,168]{1,0:T(8,128)(2,1)S(1)}, bf16[32,3,4,128]{3,2,1,0:T(4,128)(2,1)S(1)}) custom-call(bf16[32,8,128]{2,1,0:T(8,128)(2,1)S(1)} %all_to_all.27.rows_ref, bf16[168,4096]{1,0:T(8,128)(2,1)S(1)} %bitcast.16, bf16[8,168]{1,0:T(8,128)(2,1)S(1)} %copy-done.6), custom_call_target="tpu_custom_call" | custom-call | flops 10000000000 | bytes 1048576 | tf_op jit(solution)/shard_map/pallas_call | solution.py:252
  36.6 9.8 %all_to_all.28.pieces_ref = bf16[32,3,4,128]{3,2,1,0:T(4,128)(2,1)S(1)} all-to-all(bf16[32,3,4,128]{3,2,1,0:T(4,128)(2,1)S(1)} %get-tuple-element.10), channel_id=1, replica_groups={{0,1,2,3,4,5,6,7,16,17,18,19,20,21,22,23,24,25,26,27,28,29,30,31,8,9,10..., dimensions={0} | all-to-all | bytes 196608 | tf_op jit(solution)/shard_map/all_to_all | solution.py:336
  46.5 5.6 %shard_map.153 = (bf16[32,3,4,128]{3,2,1,0:T(4,128)(2,1)S(1)}, bf16[8,128]{1,0:T(8,128)(2,1)}) custom-call(bf16[32,3,4,128]{3,2,1,0:T(4,128)(2,1)S(1)} %all_to_all.28.pieces_ref, f32[5376]{0:T(1024)S(1)} %copy-done.5, bf16[32,8,128]{2,1,0:T(8,128)(2,1)S(1)} %shard_map.151.copies_ref, bf16[672,5376]{1,0:T(8,128)(2,1)S(1)} %bitcast.10, ...), custom_call_target="tpu_custom_call" | custom-call | flops 10000000000 | bytes 1048576 | tf_op jit(solution)/shard_map/pallas_call | solution.py:294
  52.1 9.6 %all_to_all.29.shares_ref = bf16[32,3,4,128]{3,2,1,0:T(4,128)(2,1)S(1)} all-to-all(bf16[32,3,4,128]{3,2,1,0:T(4,128)(2,1)S(1)} %get-tuple-element.12), channel_id=1, replica_groups={{0,1,2,3,4,5,6,7,16,17,18,19,20,21,22,23,24,25,26,27,28,29,30,31,8,9,10..., dimensions={0} | all-to-all | bytes 196608 | tf_op jit(solution)/shard_map/all_to_all | solution.py:336
  61.7 0.8 %shard_map.154 = bf16[8,168]{1,0:T(8,128)(2,1)} custom-call(bf16[32,3,4,128]{3,2,1,0:T(4,128)(2,1)S(1)} %all_to_all.29.shares_ref, bf16[8,168]{1,0:T(8,128)(2,1)S(1)} %get-tuple-element.13.hidden_ref), custom_call_target="tpu_custom_call" | custom-call | tf_op jit(solution)/shard_map/pallas_call | solution.py:320
  (22 shorter events, 0.0 us)
Async XLA Ops:
  1.3 14.6 %copy-start.1 = (bf16[1024,4,128]{2,1,0:T(4,128)(2,1)S(1)}, bf16[1024,4,128]{2,1,0:T(4,128)(2,1)}, u32[]{:S(2)}) copy-start(bf16[1024,4,128]{2,1,0:T(4,128)(2,1)} %param.20) | copy-start | bytes 3145732
  1.3 14.6 %copy-start.2 = (bf16[1024,4,128]{2,1,0:T(4,128)(2,1)S(1)}, bf16[1024,4,128]{2,1,0:T(4,128)(2,1)}, u32[]{:S(2)}) copy-start(bf16[1024,4,128]{2,1,0:T(4,128)(2,1)} %param.21) | copy-start | bytes 3145732
  1.3 14.6 %copy-start.3 = (bf16[1,256,4,128]{3,2,1,0:T(4,128)(2,1)S(1)}, bf16[1,256,4,128]{3,2,1,0:T(4,128)(2,1)}, u32[]{:S(2)}) copy-start(bf16[1,256,4,128]{3,2,1,0:T(4,128)(2,1)} %param.17) | copy-start | bytes 786436
  1.3 14.6 %copy-start.4 = (bf16[1,256,4,128]{3,2,1,0:T(4,128)(2,1)S(1)}, bf16[1,256,4,128]{3,2,1,0:T(4,128)(2,1)}, u32[]{:S(2)}) copy-start(bf16[1,256,4,128]{3,2,1,0:T(4,128)(2,1)} %param.18) | copy-start | bytes 786436
  1.3 14.6 %copy-start.7 = (bf16[1,8,128]{2,1,0:T(8,128)(2,1)S(1)}, bf16[1,8,128]{2,1,0:T(8,128)(2,1)}, u32[]{:S(2)}) copy-start(bf16[1,8,128]{2,1,0:T(8,128)(2,1)} %q_ref.1) | copy-start | bytes 6148
  1.3 14.6 %copy-start.8 = (bf16[1,4,128]{2,1,0:T(4,128)(2,1)S(1)}, bf16[1,4,128]{2,1,0:T(4,128)(2,1)}, u32[]{:S(2)}) copy-start(bf16[1,4,128]{2,1,0:T(4,128)(2,1)} %kn_ref.1) | copy-start | bytes 3076
  1.3 14.6 %copy-start.9 = (bf16[1,4,128]{2,1,0:T(4,128)(2,1)S(1)}, bf16[1,4,128]{2,1,0:T(4,128)(2,1)}, u32[]{:S(2)}) copy-start(bf16[1,4,128]{2,1,0:T(4,128)(2,1)} %vn_ref.1) | copy-start | bytes 3076
  26.2 9.6 %copy-start = (bf16[4096,168]{0,1:T(8,128)(2,1)S(1)}, bf16[4096,168]{0,1:T(8,128)(2,1)}, u32[]{:S(2)}) copy-start(bf16[4096,168]{0,1:T(8,128)(2,1)} %param.22) | copy-start | bytes 4128772
  26.2 9.6 %copy-start.6 = (bf16[8,168]{1,0:T(8,128)(2,1)S(1)}, bf16[8,168]{1,0:T(8,128)(2,1)}, u32[]{:S(2)}) copy-start(bf16[8,168]{1,0:T(8,128)(2,1)} %residual_ref.1) | copy-start | bytes 8068
  26.2 20.1 %slice-start = ((s8[7225344]{0:T(1024)(128)(4,1)}), s8[4194304]{0:T(1024)(128)(4,1)S(1)}, s32[]{:S(2)}) async-start(s8[7225344]{0:T(1024)(128)(4,1)} %bitcast.8), calls=%async_computation.5 | async-start | bytes 8388608
  26.2 20.2 %slice-start.2 = ((s8[7225344]{0:T(1024)(128)(4,1)}), s8[4194304]{0:T(1024)(128)(4,1)S(1)}, s32[]{:S(2)}) async-start(s8[7225344]{0:T(1024)(128)(4,1)} %bitcast.11), calls=%async_computation.7 | async-start | bytes 8388608
  26.2 20.1 %slice-start.4 = ((s8[7225344]{0:T(1024)(128)(4,1)}), s8[4194304]{0:T(1024)(128)(4,1)S(1)}, s32[]{:S(2)}) async-start(s8[7225344]{0:T(1024)(128)(4,1)} %bitcast.14), calls=%async_computation.9 | async-start | bytes 8388608
  35.9 10.5 %slice-start.1 = ((s8[7225344]{0:T(1024)(128)(4,1)}), s8[3031040]{0:T(1024)(128)(4,1)S(1)}, s32[]{:S(2)}) async-start(s8[7225344]{0:T(1024)(128)(4,1)} %bitcast.8), calls=%async_computation.6 | async-start | bytes 6062080
  35.9 10.5 %slice-start.3 = ((s8[7225344]{0:T(1024)(128)(4,1)}), s8[3031040]{0:T(1024)(128)(4,1)S(1)}, s32[]{:S(2)}) async-start(s8[7225344]{0:T(1024)(128)(4,1)} %bitcast.11), calls=%async_computation.8 | async-start | bytes 6062080
  35.9 10.5 %slice-start.5 = ((s8[7225344]{0:T(1024)(128)(4,1)}), s8[3031040]{0:T(1024)(128)(4,1)S(1)}, s32[]{:S(2)}) async-start(s8[7225344]{0:T(1024)(128)(4,1)} %bitcast.14), calls=%async_computation.10 | async-start | bytes 6062080
  35.9 10.5 %copy-start.5 = (f32[5376]{0:T(1024)S(1)}, f32[5376]{0:T(1024)}, u32[]{:S(2)}) copy-start(f32[5376]{0:T(1024)} %gain_ref.1) | copy-start | bytes 64516

commit v11 on v10

--- a/solution.py
+++ b/solution.py
@@ -143,48 +143,34 @@
 
 
 def attention_kernel(
-    length_ref, arrived_ref, q_ref, kn_ref, vn_ref, ks_ref, vs_ref, kp_ref, vp_ref, part_ref,
-    sum_ref, stat_ref,
+    length_ref, arrived_ref, kn_ref, vn_ref, ks_ref, vs_ref, kp_ref, vp_ref, part_ref, sum_ref, stat_ref
 ):
     count, heads, width = arrived_ref.shape
     kv_heads = kn_ref.shape[1]
-    queries = arrived_ref[...].reshape(count * heads, width)
-    scores = SCORE_SCALE * dot_rows(queries, kp_ref[...])
-    scores = scores + head_bias(*scores.shape, heads, kv_heads)
-    row_max = jnp.max(scores, axis=1, keepdims=True)
-    weights = jnp.exp(scores - row_max).astype(jnp.bfloat16)
-    row_total = jnp.sum(weights.astype(jnp.float32), axis=1, keepdims=True)
-    own = q_ref[0]
-    own_scores = SCORE_SCALE * dot_rows(own, ks_ref[...])
-    new_scores = SCORE_SCALE * dot_rows(own, kn_ref[0])
-    slot = lax.broadcasted_iota(jnp.int32, own_scores.shape, 1) // kv_heads
-    own_scores = own_scores + head_bias(*own_scores.shape, heads, kv_heads)
-    own_scores = jnp.where(slot < length_ref[:, 0:1], own_scores, MASKED)
-    new_scores = new_scores + head_bias(heads, 128, heads, kv_heads)[:, :kv_heads]
-    suffix_max = jnp.maximum(
-        jnp.max(own_scores, axis=1, keepdims=True), jnp.max(new_scores, axis=1, keepdims=True)
-    )
-    own_weights = jnp.exp(own_scores - suffix_max).astype(jnp.bfloat16)
-    new_weights = jnp.exp(new_scores - suffix_max).astype(jnp.bfloat16)
-    suffix_total = jnp.sum(own_weights.astype(jnp.float32), axis=1, keepdims=True) + jnp.sum(
-        new_weights.astype(jnp.float32), axis=1, keepdims=True
-    )
-    suffix_sum = jnp.dot(own_weights, vs_ref[...], preferred_element_type=jnp.float32) + jnp.dot(
-        new_weights, vn_ref[0], preferred_element_type=jnp.float32
-    )
-    row_sum = jnp.dot(weights, vp_ref[...], preferred_element_type=jnp.float32)
+    rows = count * heads
+    queries = arrived_ref[...].reshape(rows, width)
+    row = lax.broadcasted_iota(jnp.int32, (rows, LANES), 0)
+    own = jnp.where(row // heads == lax.axis_index("ctx"), 0.0, MASKED)
+    prompt_scores = SCORE_SCALE * dot_rows(queries, kp_ref[...])
+    prompt_scores = prompt_scores + head_bias(*prompt_scores.shape, heads, kv_heads)
+    cached_scores = SCORE_SCALE * dot_rows(queries, ks_ref[...])
+    column = lax.broadcasted_iota(jnp.int32, (heads, cached_scores.shape[1]), 1)
+    unused = jnp.where(column // kv_heads < length_ref[:, 0:1], 0.0, MASKED)
+    bias = head_bias(heads, cached_scores.shape[1], heads, kv_heads) + unused
+    bias = jnp.tile(bias, (count, 1)) + own[:, 0:1]
+    cached_scores = cached_scores + bias
+    new_scores = SCORE_SCALE * dot_rows(queries, kn_ref[0])
+    new_scores = new_scores + head_bias(rows, LANES, heads, kv_heads)[:, :kv_heads] + own[:, :kv_heads]
+    scores = (prompt_scores, cached_scores, new_scores)
+    row_max = functools.reduce(jnp.maximum, [jnp.max(part, axis=1, keepdims=True) for part in scores])
+    weights = [jnp.exp(part - row_max).astype(jnp.bfloat16) for part in scores]
+    row_total = sum(jnp.sum(part.astype(jnp.float32), axis=1, keepdims=True) for part in weights)
+    row_sum = sum(
+        jnp.dot(part, values, preferred_element_type=jnp.float32)
+        for part, values in zip(weights, (vp_ref[...], vs_ref[...], vn_ref[0]))
+    )
     sum_ref[...] = row_sum.reshape(count, heads, width)
     stat_ref[...] = stat_rows(row_max, row_total, row_sum.shape).reshape(count, heads, width)
-    me = lax.axis_index("ctx")
-    prefix_stat = stat_ref[me]
-    prefix_max = prefix_stat[:, 0:1]
-    joint_max = jnp.maximum(prefix_max, suffix_max)
-    prefix_factor = jnp.exp(prefix_max - joint_max)
-    suffix_factor = jnp.exp(suffix_max - joint_max)
-    joint_total = prefix_stat[:, 1:2] * prefix_factor + suffix_total * suffix_factor
-    joint_sum = sum_ref[me] * prefix_factor + suffix_sum * suffix_factor
-    sum_ref[me] = joint_sum
-    stat_ref[me] = stat_rows(joint_max, joint_total, joint_sum.shape)
     lane = lax.broadcasted_iota(jnp.int32, (heads, HALF), 1)
     for place in range(count):
         total = stat_ref[place, :, 1:2]
@@ -278,7 +264,7 @@
     mean_square = jnp.mean(state * state, axis=-1, keepdims=True)
     gain = gain_ref[...].reshape(1, devices * columns)
     normed = (state * lax.rsqrt(mean_square + NORM_EPSILON) * gain).astype(jnp.bfloat16)
-    gate_values = dot_rows(normed, gate_ref[...])
+    gate_values = dot_rows(gate_ref[...], normed).T
     up_values = dot_rows(normed, up_ref[...])
     activated = (jax.nn.gelu(gate_values, approximate=True) * up_values).astype(jnp.bfloat16)
     share = jnp.dot(activated, down_ref[...], preferred_element_type=jnp.float32)
@@ -360,7 +346,7 @@
     arrived = exchange(copies, "ctx")
     rows_of = lambda values: values.reshape(-1, values.shape[-1])
     parts = attend(
-        own_length, arrived, queries, k_new, v_new, *map(rows_of, (k_suffix, v_suffix, k_prefix, v_prefix))
+        own_length, arrived, k_new, v_new, *map(rows_of, (k_suffix, v_suffix, k_prefix, v_prefix))
     )
     copies = join_partials(exchange(parts, "ctx"), (devices, *queries.shape[1:]))
     order = listed(ctx_count, devices // ctx_count)

time: 62.7 us -> 62.3 us (level)
  no operation moved by 1% of the time
where the time goes in v11:
time: 62.3 us; the launch traced here: 62 us
  blocking collectives  51.5 us (83%)
  Pallas kernels  8.97 us (14%)
  between operations  1.48 us (2%)
    all_to_all x5, blocking collectives, exchange(): lax.all_to_all(copies, axes, split_axis=0, concat_axis=0, tiled=True, axi...  51.5 us
    pallas_call x1, Pallas kernels, forward(): pl.pallas_call(functools.partial(forward_kernel, order), out_shape=(jax.S...  5.23 us
    pallas_call x1, Pallas kernels, attend(): pl.pallas_call(attention_kernel, out_shape=jax.ShapeDtypeStruct((count, *...  1.31 us

profile of v11, /device:TPU:0, one launch (start us, length us, event | category | flops | bytes accessed | tf_op | source)
XLA Modules:
  0.0 62.0 jit_solution(2333424580855633502)
XLA Ops:
  1.3 0.8 %shard_map.149 = (bf16[8,8,128]{2,1,0:T(8,128)(2,1)S(1)}, s32[8,128]{1,0:T(8,128)S(1)}) custom-call(s32[1]{0:T(128)S(6)} %copy.16.length_ref, bf16[1,8,128]{2,1,0:T(8,128)(2,1)} %source_hbm.1), custom_call_target="tpu_custom_call" | custom-call | flops 10000000000 | bytes 1048576 | tf_op jit(solution)/shard_map/pallas_call | solution.py:132
  2.2 13.7 %all_to_all.25.arrived_ref = bf16[8,8,128]{2,1,0:T(8,128)(2,1)S(1)} all-to-all(bf16[8,8,128]{2,1,0:T(8,128)(2,1)S(1)} %get-tuple-element.9), channel_id=1, replica_groups=mesh['ctx'=8,'head'=4] {'ctx'}, dimensions={0} | all-to-all | bytes 32768 | tf_op jit(solution)/shard_map/all_to_all | solution.py:322
  15.8 0.0 copy-done.3
  15.9 0.0 copy-done.4
  15.9 0.0 copy-done.7
  15.9 0.0 copy-done.8
  15.9 1.3 %shard_map.150 = bf16[8,3,4,128]{3,2,1,0:T(4,128)(2,1)S(1)} custom-call(s32[8,128]{1,0:T(8,128)S(1)} %get-tuple-element.8.length_ref, bf16[8,8,128]{2,1,0:T(8,128)(2,1)S(1)} %all_to_all.25.arrived_ref, bf16[1,4,128]{2,1,0:T(4,128)(2,1)S(1)} %copy-done.7, bf16[1,4,128]{2,1,0:T(4,128)(2,1)S(1)} %copy-done.8, bf16[1024,128]{1,0:T(8,128)(2,1)S(1)} %bitcast.19, ...), custom_call_target="tpu_custom_call" | custom-call | flops 10000000000 | bytes 1048576 | tf_op jit(solution)/shard_map/pallas_call | solution.py:188
  17.2 9.0 %all_to_all.26.part_ref = bf16[8,3,4,128]{3,2,1,0:T(4,128)(2,1)S(1)} all-to-all(bf16[8,3,4,128]{3,2,1,0:T(4,128)(2,1)S(1)} %shard_map.150), channel_id=1, replica_groups=mesh['ctx'=8,'head'=4] {'ctx'}, dimensions={0} | all-to-all | bytes 49152 | tf_op jit(solution)/shard_map/all_to_all | solution.py:322
  26.2 0.0 slice-start.4
  26.2 0.2 shard_map.151.copies_ref
  26.4 9.4 %all_to_all.27.rows_ref = bf16[32,8,128]{2,1,0:T(8,128)(2,1)S(1)} all-to-all(bf16[32,8,128]{2,1,0:T(8,128)(2,1)S(1)} %shard_map.151.copies_ref), channel_id=1, replica_groups={{0,1,2,3,4,5,6,7,16,17,18,19,20,21,22,23,24,25,26,27,28,29,30,31,8,9,10..., dimensions={0} | all-to-all | bytes 131072 | tf_op jit(solution)/shard_map/all_to_all | solution.py:322
  35.8 0.0 copy-done.6
  35.8 0.0 slice-start.5
  35.8 0.0 copy-start.5
  35.8 0.6 %shard_map.152 = (bf16[8,168]{1,0:T(8,128)(2,1)S(1)}, bf16[32,3,4,128]{3,2,1,0:T(4,128)(2,1)S(1)}) custom-call(bf16[32,8,128]{2,1,0:T(8,128)(2,1)S(1)} %all_to_all.27.rows_ref, bf16[168,4096]{1,0:T(8,128)(2,1)S(1)} %bitcast.16, bf16[8,168]{1,0:T(8,128)(2,1)S(1)} %copy-done.6), custom_call_target="tpu_custom_call" | custom-call | flops 10000000000 | bytes 1048576 | tf_op jit(solution)/shard_map/pallas_call | solution.py:238
  36.5 9.8 %all_to_all.28.pieces_ref = bf16[32,3,4,128]{3,2,1,0:T(4,128)(2,1)S(1)} all-to-all(bf16[32,3,4,128]{3,2,1,0:T(4,128)(2,1)S(1)} %get-tuple-element.10), channel_id=1, replica_groups={{0,1,2,3,4,5,6,7,16,17,18,19,20,21,22,23,24,25,26,27,28,29,30,31,8,9,10..., dimensions={0} | all-to-all | bytes 196608 | tf_op jit(solution)/shard_map/all_to_all | solution.py:322
  46.3 0.0 slice-done.4
  46.3 0.0 slice-done.1
  46.4 0.0 slice-done.3
  46.4 0.0 slice-done.5
  46.4 0.0 copy-done.5
  46.4 5.2 %shard_map.153 = (bf16[32,3,4,128]{3,2,1,0:T(4,128)(2,1)S(1)}, bf16[8,128]{1,0:T(8,128)(2,1)}) custom-call(bf16[32,3,4,128]{3,2,1,0:T(4,128)(2,1)S(1)} %all_to_all.28.pieces_ref, f32[5376]{0:T(1024)S(1)} %copy-done.5, bf16[32,8,128]{2,1,0:T(8,128)(2,1)S(1)} %shard_map.151.copies_ref, bf16[672,5376]{1,0:T(8,128)(2,1)S(1)} %bitcast.10, ...), custom_call_target="tpu_custom_call" | custom-call | flops 10000000000 | bytes 1048576 | tf_op jit(solution)/shard_map/pallas_call | solution.py:280
  51.6 9.6 %all_to_all.29.shares_ref = bf16[32,3,4,128]{3,2,1,0:T(4,128)(2,1)S(1)} all-to-all(bf16[32,3,4,128]{3,2,1,0:T(4,128)(2,1)S(1)} %get-tuple-element.12), channel_id=1, replica_groups={{0,1,2,3,4,5,6,7,16,17,18,19,20,21,22,23,24,25,26,27,28,29,30,31,8,9,10..., dimensions={0} | all-to-all | bytes 196608 | tf_op jit(solution)/shard_map/all_to_all | solution.py:322
  61.2 0.8 %shard_map.154 = bf16[8,168]{1,0:T(8,128)(2,1)} custom-call(bf16[32,3,4,128]{3,2,1,0:T(4,128)(2,1)S(1)} %all_to_all.29.shares_ref, bf16[8,168]{1,0:T(8,128)(2,1)S(1)} %get-tuple-element.13.hidden_ref), custom_call_target="tpu_custom_call" | custom-call | tf_op jit(solution)/shard_map/pallas_call | solution.py:306
  (20 shorter events, 0.0 us)
Async XLA Ops:
  1.3 14.6 %copy-start.1 = (bf16[1024,4,128]{2,1,0:T(4,128)(2,1)S(1)}, bf16[1024,4,128]{2,1,0:T(4,128)(2,1)}, u32[]{:S(2)}) copy-start(bf16[1024,4,128]{2,1,0:T(4,128)(2,1)} %param.20) | copy-start | bytes 3145732
  1.3 14.6 %copy-start.2 = (bf16[1024,4,128]{2,1,0:T(4,128)(2,1)S(1)}, bf16[1024,4,128]{2,1,0:T(4,128)(2,1)}, u32[]{:S(2)}) copy-start(bf16[1024,4,128]{2,1,0:T(4,128)(2,1)} %param.21) | copy-start | bytes 3145732
  1.3 14.6 %copy-start.3 = (bf16[1,256,4,128]{3,2,1,0:T(4,128)(2,1)S(1)}, bf16[1,256,4,128]{3,2,1,0:T(4,128)(2,1)}, u32[]{:S(2)}) copy-start(bf16[1,256,4,128]{3,2,1,0:T(4,128)(2,1)} %param.17) | copy-start | bytes 786436
  1.3 14.5 %copy-start.4 = (bf16[1,256,4,128]{3,2,1,0:T(4,128)(2,1)S(1)}, bf16[1,256,4,128]{3,2,1,0:T(4,128)(2,1)}, u32[]{:S(2)}) copy-start(bf16[1,256,4,128]{3,2,1,0:T(4,128)(2,1)} %param.18) | copy-start | bytes 786436
  1.3 14.5 %copy-start.7 = (bf16[1,4,128]{2,1,0:T(4,128)(2,1)S(1)}, bf16[1,4,128]{2,1,0:T(4,128)(2,1)}, u32[]{:S(2)}) copy-start(bf16[1,4,128]{2,1,0:T(4,128)(2,1)} %kn_ref.1) | copy-start | bytes 3076
  1.3 14.5 %copy-start.8 = (bf16[1,4,128]{2,1,0:T(4,128)(2,1)S(1)}, bf16[1,4,128]{2,1,0:T(4,128)(2,1)}, u32[]{:S(2)}) copy-start(bf16[1,4,128]{2,1,0:T(4,128)(2,1)} %vn_ref.1) | copy-start | bytes 3076
  26.2 9.6 %copy-start = (bf16[4096,168]{0,1:T(8,128)(2,1)S(1)}, bf16[4096,168]{0,1:T(8,128)(2,1)}, u32[]{:S(2)}) copy-start(bf16[4096,168]{0,1:T(8,128)(2,1)} %param.22) | copy-start | bytes 4128772
  26.2 9.6 %copy-start.6 = (bf16[8,168]{1,0:T(8,128)(2,1)S(1)}, bf16[8,168]{1,0:T(8,128)(2,1)}, u32[]{:S(2)}) copy-start(bf16[8,168]{1,0:T(8,128)(2,1)} %residual_ref.1) | copy-start | bytes 8068
  26.2 20.1 %slice-start = ((s8[7225344]{0:T(1024)(128)(4,1)}), s8[4194304]{0:T(1024)(128)(4,1)S(1)}, s32[]{:S(2)}) async-start(s8[7225344]{0:T(1024)(128)(4,1)} %bitcast.8), calls=%async_computation.5 | async-start | bytes 8388608
  26.2 20.2 %slice-start.2 = ((s8[7225344]{0:T(1024)(128)(4,1)}), s8[4194304]{0:T(1024)(128)(4,1)S(1)}, s32[]{:S(2)}) async-start(s8[7225344]{0:T(1024)(128)(4,1)} %bitcast.11), calls=%async_computation.7 | async-start | bytes 8388608
  26.2 20.1 %slice-start.4 = ((s8[7225344]{0:T(1024)(128)(4,1)}), s8[4194304]{0:T(1024)(128)(4,1)S(1)}, s32[]{:S(2)}) async-start(s8[7225344]{0:T(1024)(128)(4,1)} %bitcast.14), calls=%async_computation.9 | async-start | bytes 8388608
  35.8 10.5 %slice-start.1 = ((s8[7225344]{0:T(1024)(128)(4,1)}), s8[3031040]{0:T(1024)(128)(4,1)S(1)}, s32[]{:S(2)}) async-start(s8[7225344]{0:T(1024)(128)(4,1)} %bitcast.8), calls=%async_computation.6 | async-start | bytes 6062080
  35.8 10.5 %slice-start.3 = ((s8[7225344]{0:T(1024)(128)(4,1)}), s8[3031040]{0:T(1024)(128)(4,1)S(1)}, s32[]{:S(2)}) async-start(s8[7225344]{0:T(1024)(128)(4,1)} %bitcast.11), calls=%async_computation.8 | async-start | bytes 6062080
  35.8 10.5 %slice-start.5 = ((s8[7225344]{0:T(1024)(128)(4,1)}), s8[3031040]{0:T(1024)(128)(4,1)S(1)}, s32[]{:S(2)}) async-start(s8[7225344]{0:T(1024)(128)(4,1)} %bitcast.14), calls=%async_computation.10 | async-start | bytes 6062080
  35.8 10.5 %copy-start.5 = (f32[5376]{0:T(1024)S(1)}, f32[5376]{0:T(1024)}, u32[]{:S(2)}) copy-start(f32[5376]{0:T(1024)} %gain_ref.1) | copy-start | bytes 64516

commit v12 on v11

--- a/solution.py
+++ b/solution.py
@@ -225,7 +225,8 @@
         wide_ref[device * heads : (device + 1) * heads] = rows_ref[place].astype(jnp.float32)
     rows = [wide_ref[pl.ds(head, completions, stride=all_heads), :] for head in range(all_heads)]
     rows = jnp.concatenate([row.astype(jnp.bfloat16) for row in rows], axis=1)
-    hidden = (residual_ref[...].astype(jnp.float32) + dot_rows(rows, w_ref[...])).astype(jnp.bfloat16)
+    projected = dot_rows(w_ref[...], rows).T
+    hidden = (residual_ref[...].astype(jnp.float32) + projected).astype(jnp.bfloat16)
     out_ref[...] = hidden
     if copies_ref.ndim == 4:
         put_turned(copies_ref, hidden.astype(jnp.float32))
@@ -265,7 +266,7 @@
     gain = gain_ref[...].reshape(1, devices * columns)
     normed = (state * lax.rsqrt(mean_square + NORM_EPSILON) * gain).astype(jnp.bfloat16)
     gate_values = dot_rows(gate_ref[...], normed).T
-    up_values = dot_rows(normed, up_ref[...])
+    up_values = dot_rows(up_ref[...], normed).T
     activated = (jax.nn.gelu(gate_values, approximate=True) * up_values).astype(jnp.bfloat16)
     share = jnp.dot(activated, down_ref[...], preferred_element_type=jnp.float32)
     if pieces_ref.ndim == 4:

time: 62.3 us -> 63 us (1.011)
  Pallas kernels: 8.97 us -> 9.66 us
where the time goes in v12:
time: 63 us; the launch traced here: 62.7 us
  blocking collectives  51.5 us (82%)
  Pallas kernels  9.66 us (15%)
  between operations  1.48 us (2%)
    all_to_all x5, blocking collectives, exchange(): lax.all_to_all(copies, axes, split_axis=0, concat_axis=0, tiled=True, axi...  51.5 us
    pallas_call x1, Pallas kernels, forward(): pl.pallas_call(functools.partial(forward_kernel, order), out_shape=(jax.S...  5.78 us
    pallas_call x1, Pallas kernels, attend(): pl.pallas_call(attention_kernel, out_shape=jax.ShapeDtypeStruct((count, *...  1.31 us

profile of v12, /device:TPU:0, one launch (start us, length us, event | category | flops | bytes accessed | tf_op | source)
XLA Modules:
  0.0 62.7 jit_solution(16289785007561102506)
XLA Ops:
  1.3 0.0 copy-start.1
  1.3 0.0 copy-start.2
  1.3 0.0 copy-start.3
  1.3 0.0 copy-start.4
  1.3 0.8 %shard_map.149 = (bf16[8,8,128]{2,1,0:T(8,128)(2,1)S(1)}, s32[8,128]{1,0:T(8,128)S(1)}) custom-call(s32[1]{0:T(128)S(6)} %copy.16.length_ref, bf16[1,8,128]{2,1,0:T(8,128)(2,1)} %source_hbm.1), custom_call_target="tpu_custom_call" | custom-call | flops 10000000000 | bytes 1048576 | tf_op jit(solution)/shard_map/pallas_call | solution.py:132
  2.2 13.7 %all_to_all.25.arrived_ref = bf16[8,8,128]{2,1,0:T(8,128)(2,1)S(1)} all-to-all(bf16[8,8,128]{2,1,0:T(8,128)(2,1)S(1)} %get-tuple-element.9), channel_id=1, replica_groups=mesh['ctx'=8,'head'=4] {'ctx'}, dimensions={0} | all-to-all | bytes 32768 | tf_op jit(solution)/shard_map/all_to_all | solution.py:323
  15.8 0.0 copy-done.3
  15.9 0.0 copy-done.4
  15.9 0.0 copy-done.7
  15.9 0.0 copy-done.8
  15.9 1.3 %shard_map.150 = bf16[8,3,4,128]{3,2,1,0:T(4,128)(2,1)S(1)} custom-call(s32[8,128]{1,0:T(8,128)S(1)} %get-tuple-element.8.length_ref, bf16[8,8,128]{2,1,0:T(8,128)(2,1)S(1)} %all_to_all.25.arrived_ref, bf16[1,4,128]{2,1,0:T(4,128)(2,1)S(1)} %copy-done.7, bf16[1,4,128]{2,1,0:T(4,128)(2,1)S(1)} %copy-done.8, bf16[1024,128]{1,0:T(8,128)(2,1)S(1)} %bitcast.19, ...), custom_call_target="tpu_custom_call" | custom-call | flops 10000000000 | bytes 1048576 | tf_op jit(solution)/shard_map/pallas_call | solution.py:188
  17.2 9.0 %all_to_all.26.part_ref = bf16[8,3,4,128]{3,2,1,0:T(4,128)(2,1)S(1)} all-to-all(bf16[8,3,4,128]{3,2,1,0:T(4,128)(2,1)S(1)} %shard_map.150), channel_id=1, replica_groups=mesh['ctx'=8,'head'=4] {'ctx'}, dimensions={0} | all-to-all | bytes 49152 | tf_op jit(solution)/shard_map/all_to_all | solution.py:323
  26.2 0.0 slice-start.4
  26.2 0.2 shard_map.151.copies_ref
  26.4 9.4 %all_to_all.27.rows_ref = bf16[32,8,128]{2,1,0:T(8,128)(2,1)S(1)} all-to-all(bf16[32,8,128]{2,1,0:T(8,128)(2,1)S(1)} %shard_map.151.copies_ref), channel_id=1, replica_groups={{0,1,2,3,4,5,6,7,16,17,18,19,20,21,22,23,24,25,26,27,28,29,30,31,8,9,10..., dimensions={0} | all-to-all | bytes 131072 | tf_op jit(solution)/shard_map/all_to_all | solution.py:323
  35.8 0.0 copy-done.6
  35.8 0.0 slice-start.5
  35.8 0.0 copy-start.5
  35.8 0.8 %shard_map.152 = (bf16[8,168]{1,0:T(8,128)(2,1)S(1)}, bf16[32,3,4,128]{3,2,1,0:T(4,128)(2,1)S(1)}) custom-call(bf16[32,8,128]{2,1,0:T(8,128)(2,1)S(1)} %all_to_all.27.rows_ref, bf16[168,4096]{1,0:T(8,128)(2,1)S(1)} %bitcast.16, bf16[8,168]{1,0:T(8,128)(2,1)S(1)} %copy-done.6), custom_call_target="tpu_custom_call" | custom-call | flops 10000000000 | bytes 1048576 | tf_op jit(solution)/shard_map/pallas_call | solution.py:239
  36.6 9.8 %all_to_all.28.pieces_ref = bf16[32,3,4,128]{3,2,1,0:T(4,128)(2,1)S(1)} all-to-all(bf16[32,3,4,128]{3,2,1,0:T(4,128)(2,1)S(1)} %get-tuple-element.10), channel_id=1, replica_groups={{0,1,2,3,4,5,6,7,16,17,18,19,20,21,22,23,24,25,26,27,28,29,30,31,8,9,10..., dimensions={0} | all-to-all | bytes 196608 | tf_op jit(solution)/shard_map/all_to_all | solution.py:323
  46.5 0.0 slice-done.2
  46.6 5.8 %shard_map.153 = (bf16[32,3,4,128]{3,2,1,0:T(4,128)(2,1)S(1)}, bf16[8,128]{1,0:T(8,128)(2,1)}) custom-call(bf16[32,3,4,128]{3,2,1,0:T(4,128)(2,1)S(1)} %all_to_all.28.pieces_ref, f32[5376]{0:T(1024)S(1)} %copy-done.5, bf16[32,8,128]{2,1,0:T(8,128)(2,1)S(1)} %shard_map.151.copies_ref, bf16[672,5376]{1,0:T(8,128)(2,1)S(1)} %bitcast.10, ...), custom_call_target="tpu_custom_call" | custom-call | flops 10000000000 | bytes 1048576 | tf_op jit(solution)/shard_map/pallas_call | solution.py:281
  52.3 9.6 %all_to_all.29.shares_ref = bf16[32,3,4,128]{3,2,1,0:T(4,128)(2,1)S(1)} all-to-all(bf16[32,3,4,128]{3,2,1,0:T(4,128)(2,1)S(1)} %get-tuple-element.12), channel_id=1, replica_groups={{0,1,2,3,4,5,6,7,16,17,18,19,20,21,22,23,24,25,26,27,28,29,30,31,8,9,10..., dimensions={0} | all-to-all | bytes 196608 | tf_op jit(solution)/shard_map/all_to_all | solution.py:323
  61.9 0.8 %shard_map.154 = bf16[8,168]{1,0:T(8,128)(2,1)} custom-call(bf16[32,3,4,128]{3,2,1,0:T(4,128)(2,1)S(1)} %all_to_all.29.shares_ref, bf16[8,168]{1,0:T(8,128)(2,1)S(1)} %get-tuple-element.13.hidden_ref), custom_call_target="tpu_custom_call" | custom-call | tf_op jit(solution)/shard_map/pallas_call | solution.py:307
  (20 shorter events, 0.0 us)
Async XLA Ops:
  1.3 14.6 %copy-start.1 = (bf16[1024,4,128]{2,1,0:T(4,128)(2,1)S(1)}, bf16[1024,4,128]{2,1,0:T(4,128)(2,1)}, u32[]{:S(2)}) copy-start(bf16[1024,4,128]{2,1,0:T(4,128)(2,1)} %param.20) | copy-start | bytes 3145732
  1.3 14.6 %copy-start.2 = (bf16[1024,4,128]{2,1,0:T(4,128)(2,1)S(1)}, bf16[1024,4,128]{2,1,0:T(4,128)(2,1)}, u32[]{:S(2)}) copy-start(bf16[1024,4,128]{2,1,0:T(4,128)(2,1)} %param.21) | copy-start | bytes 3145732
  1.3 14.6 %copy-start.3 = (bf16[1,256,4,128]{3,2,1,0:T(4,128)(2,1)S(1)}, bf16[1,256,4,128]{3,2,1,0:T(4,128)(2,1)}, u32[]{:S(2)}) copy-start(bf16[1,256,4,128]{3,2,1,0:T(4,128)(2,1)} %param.17) | copy-start | bytes 786436
  1.3 14.5 %copy-start.4 = (bf16[1,256,4,128]{3,2,1,0:T(4,128)(2,1)S(1)}, bf16[1,256,4,128]{3,2,1,0:T(4,128)(2,1)}, u32[]{:S(2)}) copy-start(bf16[1,256,4,128]{3,2,1,0:T(4,128)(2,1)} %param.18) | copy-start | bytes 786436
  1.3 14.5 %copy-start.7 = (bf16[1,4,128]{2,1,0:T(4,128)(2,1)S(1)}, bf16[1,4,128]{2,1,0:T(4,128)(2,1)}, u32[]{:S(2)}) copy-start(bf16[1,4,128]{2,1,0:T(4,128)(2,1)} %kn_ref.1) | copy-start | bytes 3076
  1.3 14.5 %copy-start.8 = (bf16[1,4,128]{2,1,0:T(4,128)(2,1)S(1)}, bf16[1,4,128]{2,1,0:T(4,128)(2,1)}, u32[]{:S(2)}) copy-start(bf16[1,4,128]{2,1,0:T(4,128)(2,1)} %vn_ref.1) | copy-start | bytes 3076
  26.2 9.6 %copy-start = (bf16[4096,168]{0,1:T(8,128)(2,1)S(1)}, bf16[4096,168]{0,1:T(8,128)(2,1)}, u32[]{:S(2)}) copy-start(bf16[4096,168]{0,1:T(8,128)(2,1)} %param.22) | copy-start | bytes 4128772
  26.2 9.6 %copy-start.6 = (bf16[8,168]{1,0:T(8,128)(2,1)S(1)}, bf16[8,168]{1,0:T(8,128)(2,1)}, u32[]{:S(2)}) copy-start(bf16[8,168]{1,0:T(8,128)(2,1)} %residual_ref.1) | copy-start | bytes 8068
  26.2 20.3 %slice-start = ((s8[7225344]{0:T(1024)(128)(4,1)}), s8[4194304]{0:T(1024)(128)(4,1)S(1)}, s32[]{:S(2)}) async-start(s8[7225344]{0:T(1024)(128)(4,1)} %bitcast.8), calls=%async_computation.5 | async-start | bytes 8388608
  26.2 20.3 %slice-start.2 = ((s8[7225344]{0:T(1024)(128)(4,1)}), s8[4194304]{0:T(1024)(128)(4,1)S(1)}, s32[]{:S(2)}) async-start(s8[7225344]{0:T(1024)(128)(4,1)} %bitcast.11), calls=%async_computation.7 | async-start | bytes 8388608
  26.2 20.3 %slice-start.4 = ((s8[7225344]{0:T(1024)(128)(4,1)}), s8[4194304]{0:T(1024)(128)(4,1)S(1)}, s32[]{:S(2)}) async-start(s8[7225344]{0:T(1024)(128)(4,1)} %bitcast.14), calls=%async_computation.9 | async-start | bytes 8388608
  35.8 10.7 %slice-start.1 = ((s8[7225344]{0:T(1024)(128)(4,1)}), s8[3031040]{0:T(1024)(128)(4,1)S(1)}, s32[]{:S(2)}) async-start(s8[7225344]{0:T(1024)(128)(4,1)} %bitcast.8), calls=%async_computation.6 | async-start | bytes 6062080
  35.8 10.7 %slice-start.3 = ((s8[7225344]{0:T(1024)(128)(4,1)}), s8[3031040]{0:T(1024)(128)(4,1)S(1)}, s32[]{:S(2)}) async-start(s8[7225344]{0:T(1024)(128)(4,1)} %bitcast.11), calls=%async_computation.8 | async-start | bytes 6062080
  35.8 10.7 %slice-start.5 = ((s8[7225344]{0:T(1024)(128)(4,1)}), s8[3031040]{0:T(1024)(128)(4,1)S(1)}, s32[]{:S(2)}) async-start(s8[7225344]{0:T(1024)(128)(4,1)} %bitcast.14), calls=%async_computation.10 | async-start | bytes 6062080
  35.8 10.7 %copy-start.5 = (f32[5376]{0:T(1024)S(1)}, f32[5376]{0:T(1024)}, u32[]{:S(2)}) copy-start(f32[5376]{0:T(1024)} %gain_ref.1) | copy-start | bytes 64516

commit v13 on v11

--- a/solution.py
+++ b/solution.py
@@ -13,6 +13,7 @@
 MIB = 1024 * 1024
 COST = pl.CostEstimate(flops=10**10, bytes_accessed=MIB, transcendentals=10**6)
 TERMS = 3
+CHUNKS = 3
 LANES = 128
 HALF = LANES // 2
 BOTH = ("ctx", "head")
@@ -264,10 +265,22 @@
     mean_square = jnp.mean(state * state, axis=-1, keepdims=True)
     gain = gain_ref[...].reshape(1, devices * columns)
     normed = (state * lax.rsqrt(mean_square + NORM_EPSILON) * gain).astype(jnp.bfloat16)
-    gate_values = dot_rows(gate_ref[...], normed).T
-    up_values = dot_rows(normed, up_ref[...])
-    activated = (jax.nn.gelu(gate_values, approximate=True) * up_values).astype(jnp.bfloat16)
-    share = jnp.dot(activated, down_ref[...], preferred_element_type=jnp.float32)
+    units = gate_ref.shape[0]
+    count = CHUNKS if units % (16 * CHUNKS) == 0 else 1
+    size = units // count
+    share = jnp.zeros((normed.shape[0], down_ref.shape[1]), jnp.float32)
+    ready = None
+    for chunk in range(count + 1):
+        if chunk < count:
+            rows = slice(chunk * size, (chunk + 1) * size)
+            gate_values = dot_rows(gate_ref[rows], normed)
+            up_values = dot_rows(normed, up_ref[rows])
+        if ready is not None:
+            activated, held = ready
+            share += jnp.dot(activated, down_ref[held], preferred_element_type=jnp.float32)
+        if chunk < count:
+            activated = jax.nn.gelu(gate_values.T, approximate=True) * up_values
+            ready = activated.astype(jnp.bfloat16), rows
     if pieces_ref.ndim == 4:
         put_columns(out_ref, order, share, columns)
     else:

time: 62.3 us -> 62.1 us (level)
  no operation moved by 1% of the time
where the time goes in v13:
time: 62.1 us; the launch traced here: 61.8 us
  blocking collectives  51.5 us (83%)
  Pallas kernels  8.8 us (14%)
  between operations  1.48 us (2%)
    all_to_all x5, blocking collectives, exchange(): lax.all_to_all(copies, axes, split_axis=0, concat_axis=0, tiled=True, axi...  51.5 us
    pallas_call x1, Pallas kernels, forward(): pl.pallas_call(functools.partial(forward_kernel, order), out_shape=(jax.S...  5.06 us
    pallas_call x1, Pallas kernels, attend(): pl.pallas_call(attention_kernel, out_shape=jax.ShapeDtypeStruct((count, *...  1.31 us

profile of v13, /device:TPU:0, one launch (start us, length us, event | category | flops | bytes accessed | tf_op | source)
XLA Modules:
  0.0 61.8 jit_solution(12075522171123701523)
XLA Ops:
  1.3 0.8 %shard_map.149 = (bf16[8,8,128]{2,1,0:T(8,128)(2,1)S(1)}, s32[8,128]{1,0:T(8,128)S(1)}) custom-call(s32[1]{0:T(128)S(6)} %copy.16.length_ref, bf16[1,8,128]{2,1,0:T(8,128)(2,1)} %source_hbm.1), custom_call_target="tpu_custom_call" | custom-call | flops 10000000000 | bytes 1048576 | tf_op jit(solution)/shard_map/pallas_call | solution.py:133
  2.2 13.7 %all_to_all.25.arrived_ref = bf16[8,8,128]{2,1,0:T(8,128)(2,1)S(1)} all-to-all(bf16[8,8,128]{2,1,0:T(8,128)(2,1)S(1)} %get-tuple-element.9), channel_id=1, replica_groups=mesh['ctx'=8,'head'=4] {'ctx'}, dimensions={0} | all-to-all | bytes 32768 | tf_op jit(solution)/shard_map/all_to_all | solution.py:335
  15.8 0.0 copy-done.3
  15.9 0.0 copy-done.4
  15.9 0.0 copy-done.7
  15.9 0.0 copy-done.8
  15.9 1.3 %shard_map.150 = bf16[8,3,4,128]{3,2,1,0:T(4,128)(2,1)S(1)} custom-call(s32[8,128]{1,0:T(8,128)S(1)} %get-tuple-element.8.length_ref, bf16[8,8,128]{2,1,0:T(8,128)(2,1)S(1)} %all_to_all.25.arrived_ref, bf16[1,4,128]{2,1,0:T(4,128)(2,1)S(1)} %copy-done.7, bf16[1,4,128]{2,1,0:T(4,128)(2,1)S(1)} %copy-done.8, bf16[1024,128]{1,0:T(8,128)(2,1)S(1)} %bitcast.19, ...), custom_call_target="tpu_custom_call" | custom-call | flops 10000000000 | bytes 1048576 | tf_op jit(solution)/shard_map/pallas_call | solution.py:189
  17.2 9.0 %all_to_all.26.part_ref = bf16[8,3,4,128]{3,2,1,0:T(4,128)(2,1)S(1)} all-to-all(bf16[8,3,4,128]{3,2,1,0:T(4,128)(2,1)S(1)} %shard_map.150), channel_id=1, replica_groups=mesh['ctx'=8,'head'=4] {'ctx'}, dimensions={0} | all-to-all | bytes 49152 | tf_op jit(solution)/shard_map/all_to_all | solution.py:335
  26.2 0.0 slice-start.4
  26.2 0.2 shard_map.151.copies_ref
  26.4 9.4 %all_to_all.27.rows_ref = bf16[32,8,128]{2,1,0:T(8,128)(2,1)S(1)} all-to-all(bf16[32,8,128]{2,1,0:T(8,128)(2,1)S(1)} %shard_map.151.copies_ref), channel_id=1, replica_groups={{0,1,2,3,4,5,6,7,16,17,18,19,20,21,22,23,24,25,26,27,28,29,30,31,8,9,10..., dimensions={0} | all-to-all | bytes 131072 | tf_op jit(solution)/shard_map/all_to_all | solution.py:335
  35.8 0.0 copy-done.6
  35.8 0.0 slice-start.5
  35.8 0.0 copy-start.5
  35.8 0.6 %shard_map.152 = (bf16[8,168]{1,0:T(8,128)(2,1)S(1)}, bf16[32,3,4,128]{3,2,1,0:T(4,128)(2,1)S(1)}) custom-call(bf16[32,8,128]{2,1,0:T(8,128)(2,1)S(1)} %all_to_all.27.rows_ref, bf16[168,4096]{1,0:T(8,128)(2,1)S(1)} %bitcast.16, bf16[8,168]{1,0:T(8,128)(2,1)S(1)} %copy-done.6), custom_call_target="tpu_custom_call" | custom-call | flops 10000000000 | bytes 1048576 | tf_op jit(solution)/shard_map/pallas_call | solution.py:239
  36.5 9.8 %all_to_all.28.pieces_ref = bf16[32,3,4,128]{3,2,1,0:T(4,128)(2,1)S(1)} all-to-all(bf16[32,3,4,128]{3,2,1,0:T(4,128)(2,1)S(1)} %get-tuple-element.10), channel_id=1, replica_groups={{0,1,2,3,4,5,6,7,16,17,18,19,20,21,22,23,24,25,26,27,28,29,30,31,8,9,10..., dimensions={0} | all-to-all | bytes 196608 | tf_op jit(solution)/shard_map/all_to_all | solution.py:335
  46.3 0.0 slice-done.4
  46.3 0.0 slice-done.1
  46.4 0.0 slice-done.3
  46.4 0.0 slice-done.5
  46.4 0.0 copy-done.5
  46.4 5.1 %shard_map.153 = (bf16[32,3,4,128]{3,2,1,0:T(4,128)(2,1)S(1)}, bf16[8,128]{1,0:T(8,128)(2,1)}) custom-call(bf16[32,3,4,128]{3,2,1,0:T(4,128)(2,1)S(1)} %all_to_all.28.pieces_ref, f32[5376]{0:T(1024)S(1)} %copy-done.5, bf16[32,8,128]{2,1,0:T(8,128)(2,1)S(1)} %shard_map.151.copies_ref, bf16[672,5376]{1,0:T(8,128)(2,1)S(1)} %bitcast.10, ...), custom_call_target="tpu_custom_call" | custom-call | flops 10000000000 | bytes 1048576 | tf_op jit(solution)/shard_map/pallas_call | solution.py:293
  51.5 9.6 %all_to_all.29.shares_ref = bf16[32,3,4,128]{3,2,1,0:T(4,128)(2,1)S(1)} all-to-all(bf16[32,3,4,128]{3,2,1,0:T(4,128)(2,1)S(1)} %get-tuple-element.12), channel_id=1, replica_groups={{0,1,2,3,4,5,6,7,16,17,18,19,20,21,22,23,24,25,26,27,28,29,30,31,8,9,10..., dimensions={0} | all-to-all | bytes 196608 | tf_op jit(solution)/shard_map/all_to_all | solution.py:335
  61.1 0.8 %shard_map.154 = bf16[8,168]{1,0:T(8,128)(2,1)} custom-call(bf16[32,3,4,128]{3,2,1,0:T(4,128)(2,1)S(1)} %all_to_all.29.shares_ref, bf16[8,168]{1,0:T(8,128)(2,1)S(1)} %get-tuple-element.13.hidden_ref), custom_call_target="tpu_custom_call" | custom-call | tf_op jit(solution)/shard_map/pallas_call | solution.py:319
  (20 shorter events, 0.0 us)
Async XLA Ops:
  1.3 14.6 %copy-start.1 = (bf16[1024,4,128]{2,1,0:T(4,128)(2,1)S(1)}, bf16[1024,4,128]{2,1,0:T(4,128)(2,1)}, u32[]{:S(2)}) copy-start(bf16[1024,4,128]{2,1,0:T(4,128)(2,1)} %param.20) | copy-start | bytes 3145732
  1.3 14.6 %copy-start.2 = (bf16[1024,4,128]{2,1,0:T(4,128)(2,1)S(1)}, bf16[1024,4,128]{2,1,0:T(4,128)(2,1)}, u32[]{:S(2)}) copy-start(bf16[1024,4,128]{2,1,0:T(4,128)(2,1)} %param.21) | copy-start | bytes 3145732
  1.3 14.6 %copy-start.3 = (bf16[1,256,4,128]{3,2,1,0:T(4,128)(2,1)S(1)}, bf16[1,256,4,128]{3,2,1,0:T(4,128)(2,1)}, u32[]{:S(2)}) copy-start(bf16[1,256,4,128]{3,2,1,0:T(4,128)(2,1)} %param.17) | copy-start | bytes 786436
  1.3 14.5 %copy-start.4 = (bf16[1,256,4,128]{3,2,1,0:T(4,128)(2,1)S(1)}, bf16[1,256,4,128]{3,2,1,0:T(4,128)(2,1)}, u32[]{:S(2)}) copy-start(bf16[1,256,4,128]{3,2,1,0:T(4,128)(2,1)} %param.18) | copy-start | bytes 786436
  1.3 14.5 %copy-start.7 = (bf16[1,4,128]{2,1,0:T(4,128)(2,1)S(1)}, bf16[1,4,128]{2,1,0:T(4,128)(2,1)}, u32[]{:S(2)}) copy-start(bf16[1,4,128]{2,1,0:T(4,128)(2,1)} %kn_ref.1) | copy-start | bytes 3076
  1.3 14.5 %copy-start.8 = (bf16[1,4,128]{2,1,0:T(4,128)(2,1)S(1)}, bf16[1,4,128]{2,1,0:T(4,128)(2,1)}, u32[]{:S(2)}) copy-start(bf16[1,4,128]{2,1,0:T(4,128)(2,1)} %vn_ref.1) | copy-start | bytes 3076
  26.2 9.6 %copy-start = (bf16[4096,168]{0,1:T(8,128)(2,1)S(1)}, bf16[4096,168]{0,1:T(8,128)(2,1)}, u32[]{:S(2)}) copy-start(bf16[4096,168]{0,1:T(8,128)(2,1)} %param.22) | copy-start | bytes 4128772
  26.2 9.6 %copy-start.6 = (bf16[8,168]{1,0:T(8,128)(2,1)S(1)}, bf16[8,168]{1,0:T(8,128)(2,1)}, u32[]{:S(2)}) copy-start(bf16[8,168]{1,0:T(8,128)(2,1)} %residual_ref.1) | copy-start | bytes 8068
  26.2 20.1 %slice-start = ((s8[7225344]{0:T(1024)(128)(4,1)}), s8[4194304]{0:T(1024)(128)(4,1)S(1)}, s32[]{:S(2)}) async-start(s8[7225344]{0:T(1024)(128)(4,1)} %bitcast.8), calls=%async_computation.5 | async-start | bytes 8388608
  26.2 20.2 %slice-start.2 = ((s8[7225344]{0:T(1024)(128)(4,1)}), s8[4194304]{0:T(1024)(128)(4,1)S(1)}, s32[]{:S(2)}) async-start(s8[7225344]{0:T(1024)(128)(4,1)} %bitcast.11), calls=%async_computation.7 | async-start | bytes 8388608
  26.2 20.1 %slice-start.4 = ((s8[7225344]{0:T(1024)(128)(4,1)}), s8[4194304]{0:T(1024)(128)(4,1)S(1)}, s32[]{:S(2)}) async-start(s8[7225344]{0:T(1024)(128)(4,1)} %bitcast.14), calls=%async_computation.9 | async-start | bytes 8388608
  35.8 10.5 %slice-start.1 = ((s8[7225344]{0:T(1024)(128)(4,1)}), s8[3031040]{0:T(1024)(128)(4,1)S(1)}, s32[]{:S(2)}) async-start(s8[7225344]{0:T(1024)(128)(4,1)} %bitcast.8), calls=%async_computation.6 | async-start | bytes 6062080
  35.8 10.5 %slice-start.3 = ((s8[7225344]{0:T(1024)(128)(4,1)}), s8[3031040]{0:T(1024)(128)(4,1)S(1)}, s32[]{:S(2)}) async-start(s8[7225344]{0:T(1024)(128)(4,1)} %bitcast.11), calls=%async_computation.8 | async-start | bytes 6062080
  35.8 10.5 %slice-start.5 = ((s8[7225344]{0:T(1024)(128)(4,1)}), s8[3031040]{0:T(1024)(128)(4,1)S(1)}, s32[]{:S(2)}) async-start(s8[7225344]{0:T(1024)(128)(4,1)} %bitcast.14), calls=%async_computation.10 | async-start | bytes 6062080
  35.8 10.5 %copy-start.5 = (f32[5376]{0:T(1024)S(1)}, f32[5376]{0:T(1024)}, u32[]{:S(2)}) copy-start(f32[5376]{0:T(1024)} %gain_ref.1) | copy-start | bytes 64516

commit v14 on v13

--- a/solution.py
+++ b/solution.py
@@ -14,6 +14,7 @@
 COST = pl.CostEstimate(flops=10**10, bytes_accessed=MIB, transcendentals=10**6)
 TERMS = 3
 CHUNKS = 3
+PARTS = 7
 LANES = 128
 HALF = LANES // 2
 BOTH = ("ctx", "head")
@@ -268,19 +269,27 @@
     units = gate_ref.shape[0]
     count = CHUNKS if units % (16 * CHUNKS) == 0 else 1
     size = units // count
-    share = jnp.zeros((normed.shape[0], down_ref.shape[1]), jnp.float32)
+    features = normed.shape[1]
+    parts = PARTS if features % (LANES * PARTS) == 0 else 1
+    cuts = [slice(part * (features // parts), (part + 1) * (features // parts)) for part in range(parts)]
+    shares = [0.0] * parts
     ready = None
     for chunk in range(count + 1):
-        if chunk < count:
-            rows = slice(chunk * size, (chunk + 1) * size)
-            gate_values = dot_rows(gate_ref[rows], normed)
-            up_values = dot_rows(normed, up_ref[rows])
-        if ready is not None:
-            activated, held = ready
-            share += jnp.dot(activated, down_ref[held], preferred_element_type=jnp.float32)
+        rows = slice(chunk * size, (chunk + 1) * size)
+        gate_values = up_values = 0.0
+        for part, cut in enumerate(cuts):
+            if chunk < count:
+                up_values += dot_rows(normed[:, cut], up_ref[rows, cut])
+                gate_values += dot_rows(gate_ref[rows, cut], normed[:, cut])
+            if ready is not None:
+                activated, held = ready
+                shares[part] += jnp.dot(
+                    activated, down_ref[held, cut], preferred_element_type=jnp.float32
+                )
         if chunk < count:
             activated = jax.nn.gelu(gate_values.T, approximate=True) * up_values
             ready = activated.astype(jnp.bfloat16), rows
+    share = jnp.concatenate(shares, axis=1)
     if pieces_ref.ndim == 4:
         put_columns(out_ref, order, share, columns)
     else:

time: 62.1 us -> 62.2 us (level)
  no operation moved by 1% of the time
where the time goes in v14:
time: 62.2 us; the launch traced here: 61.9 us
  blocking collectives  51.5 us (83%)
  Pallas kernels  8.87 us (14%)
  between operations  1.48 us (2%)
    all_to_all x5, blocking collectives, exchange(): lax.all_to_all(copies, axes, split_axis=0, concat_axis=0, tiled=True, axi...  51.5 us
    pallas_call x1, Pallas kernels, forward(): pl.pallas_call(functools.partial(forward_kernel, order), out_shape=(jax.S...  5.13 us
    pallas_call x1, Pallas kernels, attend(): pl.pallas_call(attention_kernel, out_shape=jax.ShapeDtypeStruct((count, *...  1.31 us

profile of v14, /device:TPU:0, one launch (start us, length us, event | category | flops | bytes accessed | tf_op | source)
XLA Modules:
  0.0 61.9 jit_solution(16138642101813164476)
XLA Ops:
  1.3 0.8 %shard_map.149 = (bf16[8,8,128]{2,1,0:T(8,128)(2,1)S(1)}, s32[8,128]{1,0:T(8,128)S(1)}) custom-call(s32[1]{0:T(128)S(6)} %copy.16.length_ref, bf16[1,8,128]{2,1,0:T(8,128)(2,1)} %source_hbm.1), custom_call_target="tpu_custom_call" | custom-call | flops 10000000000 | bytes 1048576 | tf_op jit(solution)/shard_map/pallas_call | solution.py:134
  2.2 13.7 %all_to_all.25.arrived_ref = bf16[8,8,128]{2,1,0:T(8,128)(2,1)S(1)} all-to-all(bf16[8,8,128]{2,1,0:T(8,128)(2,1)S(1)} %get-tuple-element.9), channel_id=1, replica_groups=mesh['ctx'=8,'head'=4] {'ctx'}, dimensions={0} | all-to-all | bytes 32768 | tf_op jit(solution)/shard_map/all_to_all | solution.py:344
  15.8 0.0 copy-done.3
  15.9 0.0 copy-done.4
  15.9 0.0 copy-done.7
  15.9 0.0 copy-done.8
  15.9 1.3 %shard_map.150 = bf16[8,3,4,128]{3,2,1,0:T(4,128)(2,1)S(1)} custom-call(s32[8,128]{1,0:T(8,128)S(1)} %get-tuple-element.8.length_ref, bf16[8,8,128]{2,1,0:T(8,128)(2,1)S(1)} %all_to_all.25.arrived_ref, bf16[1,4,128]{2,1,0:T(4,128)(2,1)S(1)} %copy-done.7, bf16[1,4,128]{2,1,0:T(4,128)(2,1)S(1)} %copy-done.8, bf16[1024,128]{1,0:T(8,128)(2,1)S(1)} %bitcast.19, ...), custom_call_target="tpu_custom_call" | custom-call | flops 10000000000 | bytes 1048576 | tf_op jit(solution)/shard_map/pallas_call | solution.py:190
  17.2 9.0 %all_to_all.26.part_ref = bf16[8,3,4,128]{3,2,1,0:T(4,128)(2,1)S(1)} all-to-all(bf16[8,3,4,128]{3,2,1,0:T(4,128)(2,1)S(1)} %shard_map.150), channel_id=1, replica_groups=mesh['ctx'=8,'head'=4] {'ctx'}, dimensions={0} | all-to-all | bytes 49152 | tf_op jit(solution)/shard_map/all_to_all | solution.py:344
  26.2 0.0 slice-start.4
  26.2 0.2 shard_map.151.copies_ref
  26.4 9.4 %all_to_all.27.rows_ref = bf16[32,8,128]{2,1,0:T(8,128)(2,1)S(1)} all-to-all(bf16[32,8,128]{2,1,0:T(8,128)(2,1)S(1)} %shard_map.151.copies_ref), channel_id=1, replica_groups={{0,1,2,3,4,5,6,7,16,17,18,19,20,21,22,23,24,25,26,27,28,29,30,31,8,9,10..., dimensions={0} | all-to-all | bytes 131072 | tf_op jit(solution)/shard_map/all_to_all | solution.py:344
  35.8 0.0 copy-done.6
  35.8 0.0 slice-start.5
  35.8 0.0 copy-start.5
  35.8 0.6 %shard_map.152 = (bf16[8,168]{1,0:T(8,128)(2,1)S(1)}, bf16[32,3,4,128]{3,2,1,0:T(4,128)(2,1)S(1)}) custom-call(bf16[32,8,128]{2,1,0:T(8,128)(2,1)S(1)} %all_to_all.27.rows_ref, bf16[168,4096]{1,0:T(8,128)(2,1)S(1)} %bitcast.16, bf16[8,168]{1,0:T(8,128)(2,1)S(1)} %copy-done.6), custom_call_target="tpu_custom_call" | custom-call | flops 10000000000 | bytes 1048576 | tf_op jit(solution)/shard_map/pallas_call | solution.py:240
  36.5 9.8 %all_to_all.28.pieces_ref = bf16[32,3,4,128]{3,2,1,0:T(4,128)(2,1)S(1)} all-to-all(bf16[32,3,4,128]{3,2,1,0:T(4,128)(2,1)S(1)} %get-tuple-element.10), channel_id=1, replica_groups={{0,1,2,3,4,5,6,7,16,17,18,19,20,21,22,23,24,25,26,27,28,29,30,31,8,9,10..., dimensions={0} | all-to-all | bytes 196608 | tf_op jit(solution)/shard_map/all_to_all | solution.py:344
  46.3 0.0 slice-done.4
  46.3 0.0 slice-done.1
  46.4 0.0 slice-done.3
  46.4 0.0 slice-done.5
  46.4 0.0 copy-done.5
  46.4 5.1 %shard_map.153 = (bf16[32,3,4,128]{3,2,1,0:T(4,128)(2,1)S(1)}, bf16[8,128]{1,0:T(8,128)(2,1)}) custom-call(bf16[32,3,4,128]{3,2,1,0:T(4,128)(2,1)S(1)} %all_to_all.28.pieces_ref, f32[5376]{0:T(1024)S(1)} %copy-done.5, bf16[32,8,128]{2,1,0:T(8,128)(2,1)S(1)} %shard_map.151.copies_ref, bf16[672,5376]{1,0:T(8,128)(2,1)S(1)} %bitcast.10, ...), custom_call_target="tpu_custom_call" | custom-call | flops 10000000000 | bytes 1048576 | tf_op jit(solution)/shard_map/pallas_call | solution.py:302
  51.5 9.6 %all_to_all.29.shares_ref = bf16[32,3,4,128]{3,2,1,0:T(4,128)(2,1)S(1)} all-to-all(bf16[32,3,4,128]{3,2,1,0:T(4,128)(2,1)S(1)} %get-tuple-element.12), channel_id=1, replica_groups={{0,1,2,3,4,5,6,7,16,17,18,19,20,21,22,23,24,25,26,27,28,29,30,31,8,9,10..., dimensions={0} | all-to-all | bytes 196608 | tf_op jit(solution)/shard_map/all_to_all | solution.py:344
  61.1 0.8 %shard_map.154 = bf16[8,168]{1,0:T(8,128)(2,1)} custom-call(bf16[32,3,4,128]{3,2,1,0:T(4,128)(2,1)S(1)} %all_to_all.29.shares_ref, bf16[8,168]{1,0:T(8,128)(2,1)S(1)} %get-tuple-element.13.hidden_ref), custom_call_target="tpu_custom_call" | custom-call | tf_op jit(solution)/shard_map/pallas_call | solution.py:328
  (20 shorter events, 0.0 us)
Async XLA Ops:
  1.3 14.6 %copy-start.1 = (bf16[1024,4,128]{2,1,0:T(4,128)(2,1)S(1)}, bf16[1024,4,128]{2,1,0:T(4,128)(2,1)}, u32[]{:S(2)}) copy-start(bf16[1024,4,128]{2,1,0:T(4,128)(2,1)} %param.20) | copy-start | bytes 3145732
  1.3 14.6 %copy-start.2 = (bf16[1024,4,128]{2,1,0:T(4,128)(2,1)S(1)}, bf16[1024,4,128]{2,1,0:T(4,128)(2,1)}, u32[]{:S(2)}) copy-start(bf16[1024,4,128]{2,1,0:T(4,128)(2,1)} %param.21) | copy-start | bytes 3145732
  1.3 14.6 %copy-start.3 = (bf16[1,256,4,128]{3,2,1,0:T(4,128)(2,1)S(1)}, bf16[1,256,4,128]{3,2,1,0:T(4,128)(2,1)}, u32[]{:S(2)}) copy-start(bf16[1,256,4,128]{3,2,1,0:T(4,128)(2,1)} %param.17) | copy-start | bytes 786436
  1.3 14.5 %copy-start.4 = (bf16[1,256,4,128]{3,2,1,0:T(4,128)(2,1)S(1)}, bf16[1,256,4,128]{3,2,1,0:T(4,128)(2,1)}, u32[]{:S(2)}) copy-start(bf16[1,256,4,128]{3,2,1,0:T(4,128)(2,1)} %param.18) | copy-start | bytes 786436
  1.3 14.5 %copy-start.7 = (bf16[1,4,128]{2,1,0:T(4,128)(2,1)S(1)}, bf16[1,4,128]{2,1,0:T(4,128)(2,1)}, u32[]{:S(2)}) copy-start(bf16[1,4,128]{2,1,0:T(4,128)(2,1)} %kn_ref.1) | copy-start | bytes 3076
  1.3 14.5 %copy-start.8 = (bf16[1,4,128]{2,1,0:T(4,128)(2,1)S(1)}, bf16[1,4,128]{2,1,0:T(4,128)(2,1)}, u32[]{:S(2)}) copy-start(bf16[1,4,128]{2,1,0:T(4,128)(2,1)} %vn_ref.1) | copy-start | bytes 3076
  26.2 9.6 %copy-start = (bf16[4096,168]{0,1:T(8,128)(2,1)S(1)}, bf16[4096,168]{0,1:T(8,128)(2,1)}, u32[]{:S(2)}) copy-start(bf16[4096,168]{0,1:T(8,128)(2,1)} %param.22) | copy-start | bytes 4128772
  26.2 9.6 %copy-start.6 = (bf16[8,168]{1,0:T(8,128)(2,1)S(1)}, bf16[8,168]{1,0:T(8,128)(2,1)}, u32[]{:S(2)}) copy-start(bf16[8,168]{1,0:T(8,128)(2,1)} %residual_ref.1) | copy-start | bytes 8068
  26.2 20.1 %slice-start = ((s8[7225344]{0:T(1024)(128)(4,1)}), s8[4194304]{0:T(1024)(128)(4,1)S(1)}, s32[]{:S(2)}) async-start(s8[7225344]{0:T(1024)(128)(4,1)} %bitcast.8), calls=%async_computation.5 | async-start | bytes 8388608
  26.2 20.2 %slice-start.2 = ((s8[7225344]{0:T(1024)(128)(4,1)}), s8[4194304]{0:T(1024)(128)(4,1)S(1)}, s32[]{:S(2)}) async-start(s8[7225344]{0:T(1024)(128)(4,1)} %bitcast.11), calls=%async_computation.7 | async-start | bytes 8388608
  26.2 20.1 %slice-start.4 = ((s8[7225344]{0:T(1024)(128)(4,1)}), s8[4194304]{0:T(1024)(128)(4,1)S(1)}, s32[]{:S(2)}) async-start(s8[7225344]{0:T(1024)(128)(4,1)} %bitcast.14), calls=%async_computation.9 | async-start | bytes 8388608
  35.8 10.5 %slice-start.1 = ((s8[7225344]{0:T(1024)(128)(4,1)}), s8[3031040]{0:T(1024)(128)(4,1)S(1)}, s32[]{:S(2)}) async-start(s8[7225344]{0:T(1024)(128)(4,1)} %bitcast.8), calls=%async_computation.6 | async-start | bytes 6062080
  35.8 10.5 %slice-start.3 = ((s8[7225344]{0:T(1024)(128)(4,1)}), s8[3031040]{0:T(1024)(128)(4,1)S(1)}, s32[]{:S(2)}) async-start(s8[7225344]{0:T(1024)(128)(4,1)} %bitcast.11), calls=%async_computation.8 | async-start | bytes 6062080
  35.8 10.5 %slice-start.5 = ((s8[7225344]{0:T(1024)(128)(4,1)}), s8[3031040]{0:T(1024)(128)(4,1)S(1)}, s32[]{:S(2)}) async-start(s8[7225344]{0:T(1024)(128)(4,1)} %bitcast.14), calls=%async_computation.10 | async-start | bytes 6062080
  35.8 10.5 %copy-start.5 = (f32[5376]{0:T(1024)S(1)}, f32[5376]{0:T(1024)}, u32[]{:S(2)}) copy-start(f32[5376]{0:T(1024)} %gain_ref.1) | copy-start | bytes 64516

commit v15 on v13

--- a/solution.py
+++ b/solution.py
@@ -14,6 +14,7 @@
 COST = pl.CostEstimate(flops=10**10, bytes_accessed=MIB, transcendentals=10**6)
 TERMS = 3
 CHUNKS = 3
+BLOCK_ROWS = 1024
 LANES = 128
 HALF = LANES // 2
 BOTH = ("ctx", "head")
@@ -152,8 +153,14 @@
     queries = arrived_ref[...].reshape(rows, width)
     row = lax.broadcasted_iota(jnp.int32, (rows, LANES), 0)
     own = jnp.where(row // heads == lax.axis_index("ctx"), 0.0, MASKED)
-    prompt_scores = SCORE_SCALE * dot_rows(queries, kp_ref[...])
-    prompt_scores = prompt_scores + head_bias(*prompt_scores.shape, heads, kv_heads)
+    prompt_rows = kp_ref.shape[0]
+    size = BLOCK_ROWS if prompt_rows % BLOCK_ROWS == 0 else prompt_rows
+    prompt_bias = head_bias(rows, size, heads, kv_heads)
+    blocks = []
+    for start in range(0, prompt_rows, size):
+        block = slice(start, start + size)
+        scores = SCORE_SCALE * dot_rows(queries, kp_ref[block]) + prompt_bias
+        blocks.append((scores, vp_ref[block], None, None))
     cached_scores = SCORE_SCALE * dot_rows(queries, ks_ref[...])
     column = lax.broadcasted_iota(jnp.int32, (heads, cached_scores.shape[1]), 1)
     unused = jnp.where(column // kv_heads < length_ref[:, 0:1], 0.0, MASKED)
@@ -162,14 +169,24 @@
     cached_scores = cached_scores + bias
     new_scores = SCORE_SCALE * dot_rows(queries, kn_ref[0])
     new_scores = new_scores + head_bias(rows, LANES, heads, kv_heads)[:, :kv_heads] + own[:, :kv_heads]
-    scores = (prompt_scores, cached_scores, new_scores)
-    row_max = functools.reduce(jnp.maximum, [jnp.max(part, axis=1, keepdims=True) for part in scores])
-    weights = [jnp.exp(part - row_max).astype(jnp.bfloat16) for part in scores]
-    row_total = sum(jnp.sum(part.astype(jnp.float32), axis=1, keepdims=True) for part in weights)
-    row_sum = sum(
-        jnp.dot(part, values, preferred_element_type=jnp.float32)
-        for part, values in zip(weights, (vp_ref[...], vs_ref[...], vn_ref[0]))
-    )
+    blocks.append((cached_scores, vs_ref[...], new_scores, vn_ref[0]))
+    parts = []
+    for block_scores, values, more_scores, more_values in blocks:
+        block_max = jnp.max(block_scores, axis=1, keepdims=True)
+        if more_scores is not None:
+            block_max = jnp.maximum(block_max, jnp.max(more_scores, axis=1, keepdims=True))
+        weights = jnp.exp(block_scores - block_max).astype(jnp.bfloat16)
+        block_total = jnp.sum(weights.astype(jnp.float32), axis=1, keepdims=True)
+        block_sum = jnp.dot(weights, values, preferred_element_type=jnp.float32)
+        if more_scores is not None:
+            weights = jnp.exp(more_scores - block_max).astype(jnp.bfloat16)
+            block_total += jnp.sum(weights.astype(jnp.float32), axis=1, keepdims=True)
+            block_sum += jnp.dot(weights, more_values, preferred_element_type=jnp.float32)
+        parts.append((block_max, block_total, block_sum))
+    row_max = functools.reduce(jnp.maximum, [part[0] for part in parts])
+    factors = [jnp.exp(part[0] - row_max) for part in parts]
+    row_total = sum(part[1] * factor for part, factor in zip(parts, factors))
+    row_sum = sum(part[2] * factor for part, factor in zip(parts, factors))
     sum_ref[...] = row_sum.reshape(count, heads, width)
     stat_ref[...] = stat_rows(row_max, row_total, row_sum.shape).reshape(count, heads, width)
     lane = lax.broadcasted_iota(jnp.int32, (heads, HALF), 1)
@@ -226,7 +243,11 @@
         wide_ref[device * heads : (device + 1) * heads] = rows_ref[place].astype(jnp.float32)
     rows = [wide_ref[pl.ds(head, completions, stride=all_heads), :] for head in range(all_heads)]
     rows = jnp.concatenate([row.astype(jnp.bfloat16) for row in rows], axis=1)
-    hidden = (residual_ref[...].astype(jnp.float32) + dot_rows(rows, w_ref[...])).astype(jnp.bfloat16)
+    held = w_ref.shape[0] // 32 * 16
+    projected = dot_rows(w_ref[held:], rows).T
+    if held:
+        projected = jnp.concatenate([dot_rows(rows, w_ref[:held]), projected], axis=1)
+    hidden = (residual_ref[...].astype(jnp.float32) + projected).astype(jnp.bfloat16)
     out_ref[...] = hidden
     if copies_ref.ndim == 4:
         put_turned(copies_ref, hidden.astype(jnp.float32))

time: 62.1 us -> 62.1 us (level)
  no operation moved by 1% of the time
where the time goes in v15:
time: 62.1 us; the launch traced here: 61.8 us
  blocking collectives  51.5 us (83%)
  Pallas kernels  8.8 us (14%)
  between operations  1.48 us (2%)
    all_to_all x5, blocking collectives, exchange(): lax.all_to_all(copies, axes, split_axis=0, concat_axis=0, tiled=True, axi...  51.5 us
    pallas_call x1, Pallas kernels, forward(): pl.pallas_call(functools.partial(forward_kernel, order), out_shape=(jax.S...  5.06 us

profile of v15, /device:TPU:0, one launch (start us, length us, event | category | flops | bytes accessed | tf_op | source)
XLA Modules:
  0.0 61.8 jit_solution(7608185147389080240)
XLA Ops:
  1.3 0.8 %shard_map.149 = (bf16[8,8,128]{2,1,0:T(8,128)(2,1)S(1)}, s32[8,128]{1,0:T(8,128)S(1)}) custom-call(s32[1]{0:T(128)S(6)} %copy.16.length_ref, bf16[1,8,128]{2,1,0:T(8,128)(2,1)} %source_hbm.1), custom_call_target="tpu_custom_call" | custom-call | flops 10000000000 | bytes 1048576 | tf_op jit(solution)/shard_map/pallas_call | solution.py:134
  2.2 13.7 %all_to_all.25.arrived_ref = bf16[8,8,128]{2,1,0:T(8,128)(2,1)S(1)} all-to-all(bf16[8,8,128]{2,1,0:T(8,128)(2,1)S(1)} %get-tuple-element.9), channel_id=1, replica_groups=mesh['ctx'=8,'head'=4] {'ctx'}, dimensions={0} | all-to-all | bytes 32768 | tf_op jit(solution)/shard_map/all_to_all | solution.py:356
  15.8 0.0 copy-done.3
  15.9 0.0 copy-done.4
  15.9 0.0 copy-done.7
  15.9 0.0 copy-done.8
  15.9 1.2 %shard_map.150 = bf16[8,3,4,128]{3,2,1,0:T(4,128)(2,1)S(1)} custom-call(s32[8,128]{1,0:T(8,128)S(1)} %get-tuple-element.8.length_ref, bf16[8,8,128]{2,1,0:T(8,128)(2,1)S(1)} %all_to_all.25.arrived_ref, bf16[1,4,128]{2,1,0:T(4,128)(2,1)S(1)} %copy-done.7, bf16[1,4,128]{2,1,0:T(4,128)(2,1)S(1)} %copy-done.8, bf16[1024,128]{1,0:T(8,128)(2,1)S(1)} %bitcast.19, ...), custom_call_target="tpu_custom_call" | custom-call | flops 10000000000 | bytes 1048576 | tf_op jit(solution)/shard_map/pallas_call | solution.py:206
  17.1 9.0 %all_to_all.26.part_ref = bf16[8,3,4,128]{3,2,1,0:T(4,128)(2,1)S(1)} all-to-all(bf16[8,3,4,128]{3,2,1,0:T(4,128)(2,1)S(1)} %shard_map.150), channel_id=1, replica_groups=mesh['ctx'=8,'head'=4] {'ctx'}, dimensions={0} | all-to-all | bytes 49152 | tf_op jit(solution)/shard_map/all_to_all | solution.py:356
  26.1 0.0 slice-start.4
  26.1 0.2 shard_map.151.copies_ref
  26.3 9.4 %all_to_all.27.rows_ref = bf16[32,8,128]{2,1,0:T(8,128)(2,1)S(1)} all-to-all(bf16[32,8,128]{2,1,0:T(8,128)(2,1)S(1)} %shard_map.151.copies_ref), channel_id=1, replica_groups={{0,1,2,3,4,5,6,7,16,17,18,19,20,21,22,23,24,25,26,27,28,29,30,31,8,9,10..., dimensions={0} | all-to-all | bytes 131072 | tf_op jit(solution)/shard_map/all_to_all | solution.py:356
  35.7 0.0 copy-done.6
  35.7 0.0 slice-start.5
  35.7 0.0 copy-start.5
  35.7 0.8 %shard_map.152 = (bf16[8,168]{1,0:T(8,128)(2,1)S(1)}, bf16[32,3,4,128]{3,2,1,0:T(4,128)(2,1)S(1)}) custom-call(bf16[32,8,128]{2,1,0:T(8,128)(2,1)S(1)} %all_to_all.27.rows_ref, bf16[168,4096]{1,0:T(8,128)(2,1)S(1)} %bitcast.16, bf16[8,168]{1,0:T(8,128)(2,1)S(1)} %copy-done.6), custom_call_target="tpu_custom_call" | custom-call | flops 10000000000 | bytes 1048576 | tf_op jit(solution)/shard_map/pallas_call | solution.py:260
  36.5 9.8 %all_to_all.28.pieces_ref = bf16[32,3,4,128]{3,2,1,0:T(4,128)(2,1)S(1)} all-to-all(bf16[32,3,4,128]{3,2,1,0:T(4,128)(2,1)S(1)} %get-tuple-element.10), channel_id=1, replica_groups={{0,1,2,3,4,5,6,7,16,17,18,19,20,21,22,23,24,25,26,27,28,29,30,31,8,9,10..., dimensions={0} | all-to-all | bytes 196608 | tf_op jit(solution)/shard_map/all_to_all | solution.py:356
  46.3 0.0 slice-done.4
  46.3 0.0 slice-done.1
  46.4 0.0 slice-done.3
  46.4 0.0 slice-done.5
  46.4 0.0 copy-done.5
  46.4 5.1 %shard_map.153 = (bf16[32,3,4,128]{3,2,1,0:T(4,128)(2,1)S(1)}, bf16[8,128]{1,0:T(8,128)(2,1)}) custom-call(bf16[32,3,4,128]{3,2,1,0:T(4,128)(2,1)S(1)} %all_to_all.28.pieces_ref, f32[5376]{0:T(1024)S(1)} %copy-done.5, bf16[32,8,128]{2,1,0:T(8,128)(2,1)S(1)} %shard_map.151.copies_ref, bf16[672,5376]{1,0:T(8,128)(2,1)S(1)} %bitcast.10, ...), custom_call_target="tpu_custom_call" | custom-call | flops 10000000000 | bytes 1048576 | tf_op jit(solution)/shard_map/pallas_call | solution.py:314
  51.5 9.6 %all_to_all.29.shares_ref = bf16[32,3,4,128]{3,2,1,0:T(4,128)(2,1)S(1)} all-to-all(bf16[32,3,4,128]{3,2,1,0:T(4,128)(2,1)S(1)} %get-tuple-element.12), channel_id=1, replica_groups={{0,1,2,3,4,5,6,7,16,17,18,19,20,21,22,23,24,25,26,27,28,29,30,31,8,9,10..., dimensions={0} | all-to-all | bytes 196608 | tf_op jit(solution)/shard_map/all_to_all | solution.py:356
  61.1 0.8 %shard_map.154 = bf16[8,168]{1,0:T(8,128)(2,1)} custom-call(bf16[32,3,4,128]{3,2,1,0:T(4,128)(2,1)S(1)} %all_to_all.29.shares_ref, bf16[8,168]{1,0:T(8,128)(2,1)S(1)} %get-tuple-element.13.hidden_ref), custom_call_target="tpu_custom_call" | custom-call | tf_op jit(solution)/shard_map/pallas_call | solution.py:340
  (20 shorter events, 0.0 us)
Async XLA Ops:
  1.3 14.6 %copy-start.1 = (bf16[1024,4,128]{2,1,0:T(4,128)(2,1)S(1)}, bf16[1024,4,128]{2,1,0:T(4,128)(2,1)}, u32[]{:S(2)}) copy-start(bf16[1024,4,128]{2,1,0:T(4,128)(2,1)} %param.20) | copy-start | bytes 3145732
  1.3 14.6 %copy-start.2 = (bf16[1024,4,128]{2,1,0:T(4,128)(2,1)S(1)}, bf16[1024,4,128]{2,1,0:T(4,128)(2,1)}, u32[]{:S(2)}) copy-start(bf16[1024,4,128]{2,1,0:T(4,128)(2,1)} %param.21) | copy-start | bytes 3145732
  1.3 14.6 %copy-start.3 = (bf16[1,256,4,128]{3,2,1,0:T(4,128)(2,1)S(1)}, bf16[1,256,4,128]{3,2,1,0:T(4,128)(2,1)}, u32[]{:S(2)}) copy-start(bf16[1,256,4,128]{3,2,1,0:T(4,128)(2,1)} %param.17) | copy-start | bytes 786436
  1.3 14.5 %copy-start.4 = (bf16[1,256,4,128]{3,2,1,0:T(4,128)(2,1)S(1)}, bf16[1,256,4,128]{3,2,1,0:T(4,128)(2,1)}, u32[]{:S(2)}) copy-start(bf16[1,256,4,128]{3,2,1,0:T(4,128)(2,1)} %param.18) | copy-start | bytes 786436
  1.3 14.5 %copy-start.7 = (bf16[1,4,128]{2,1,0:T(4,128)(2,1)S(1)}, bf16[1,4,128]{2,1,0:T(4,128)(2,1)}, u32[]{:S(2)}) copy-start(bf16[1,4,128]{2,1,0:T(4,128)(2,1)} %kn_ref.1) | copy-start | bytes 3076
  1.3 14.5 %copy-start.8 = (bf16[1,4,128]{2,1,0:T(4,128)(2,1)S(1)}, bf16[1,4,128]{2,1,0:T(4,128)(2,1)}, u32[]{:S(2)}) copy-start(bf16[1,4,128]{2,1,0:T(4,128)(2,1)} %vn_ref.1) | copy-start | bytes 3076
  26.0 9.6 %copy-start = (bf16[4096,168]{0,1:T(8,128)(2,1)S(1)}, bf16[4096,168]{0,1:T(8,128)(2,1)}, u32[]{:S(2)}) copy-start(bf16[4096,168]{0,1:T(8,128)(2,1)} %param.22) | copy-start | bytes 4128772
  26.0 9.6 %copy-start.6 = (bf16[8,168]{1,0:T(8,128)(2,1)S(1)}, bf16[8,168]{1,0:T(8,128)(2,1)}, u32[]{:S(2)}) copy-start(bf16[8,168]{1,0:T(8,128)(2,1)} %residual_ref.1) | copy-start | bytes 8068
  26.1 20.3 %slice-start = ((s8[7225344]{0:T(1024)(128)(4,1)}), s8[4194304]{0:T(1024)(128)(4,1)S(1)}, s32[]{:S(2)}) async-start(s8[7225344]{0:T(1024)(128)(4,1)} %bitcast.8), calls=%async_computation.5 | async-start | bytes 8388608
  26.1 20.3 %slice-start.2 = ((s8[7225344]{0:T(1024)(128)(4,1)}), s8[4194304]{0:T(1024)(128)(4,1)S(1)}, s32[]{:S(2)}) async-start(s8[7225344]{0:T(1024)(128)(4,1)} %bitcast.11), calls=%async_computation.7 | async-start | bytes 8388608
  26.1 20.3 %slice-start.4 = ((s8[7225344]{0:T(1024)(128)(4,1)}), s8[4194304]{0:T(1024)(128)(4,1)S(1)}, s32[]{:S(2)}) async-start(s8[7225344]{0:T(1024)(128)(4,1)} %bitcast.14), calls=%async_computation.9 | async-start | bytes 8388608
  35.7 10.7 %slice-start.1 = ((s8[7225344]{0:T(1024)(128)(4,1)}), s8[3031040]{0:T(1024)(128)(4,1)S(1)}, s32[]{:S(2)}) async-start(s8[7225344]{0:T(1024)(128)(4,1)} %bitcast.8), calls=%async_computation.6 | async-start | bytes 6062080
  35.7 10.7 %slice-start.3 = ((s8[7225344]{0:T(1024)(128)(4,1)}), s8[3031040]{0:T(1024)(128)(4,1)S(1)}, s32[]{:S(2)}) async-start(s8[7225344]{0:T(1024)(128)(4,1)} %bitcast.11), calls=%async_computation.8 | async-start | bytes 6062080
  35.7 10.7 %slice-start.5 = ((s8[7225344]{0:T(1024)(128)(4,1)}), s8[3031040]{0:T(1024)(128)(4,1)S(1)}, s32[]{:S(2)}) async-start(s8[7225344]{0:T(1024)(128)(4,1)} %bitcast.14), calls=%async_computation.10 | async-start | bytes 6062080
  35.7 10.7 %copy-start.5 = (f32[5376]{0:T(1024)S(1)}, f32[5376]{0:T(1024)}, u32[]{:S(2)}) copy-start(f32[5376]{0:T(1024)} %gain_ref.1) | copy-start | bytes 64516

commit v16 on v15

--- a/solution.py
+++ b/solution.py
@@ -243,10 +243,7 @@
         wide_ref[device * heads : (device + 1) * heads] = rows_ref[place].astype(jnp.float32)
     rows = [wide_ref[pl.ds(head, completions, stride=all_heads), :] for head in range(all_heads)]
     rows = jnp.concatenate([row.astype(jnp.bfloat16) for row in rows], axis=1)
-    held = w_ref.shape[0] // 32 * 16
-    projected = dot_rows(w_ref[held:], rows).T
-    if held:
-        projected = jnp.concatenate([dot_rows(rows, w_ref[:held]), projected], axis=1)
+    projected = dot_rows(rows, w_ref[...])
     hidden = (residual_ref[...].astype(jnp.float32) + projected).astype(jnp.bfloat16)
     out_ref[...] = hidden
     if copies_ref.ndim == 4:
@@ -295,7 +292,10 @@
         if chunk < count:
             rows = slice(chunk * size, (chunk + 1) * size)
             gate_values = dot_rows(gate_ref[rows], normed)
-            up_values = dot_rows(normed, up_ref[rows])
+            if chunk % 2:
+                up_values = dot_rows(up_ref[rows], normed).T
+            else:
+                up_values = dot_rows(normed, up_ref[rows])
         if ready is not None:
             activated, held = ready
             share += jnp.dot(activated, down_ref[held], preferred_element_type=jnp.float32)

time: 62.1 us -> 61.9 us (level)
  no operation moved by 1% of the time
where the time goes in v16:
time: 61.9 us; the launch traced here: 61.6 us
  blocking collectives  51.5 us (83%)
  Pallas kernels  8.62 us (14%)
  between operations  1.48 us (2%)
    all_to_all x5, blocking collectives, exchange(): lax.all_to_all(copies, axes, split_axis=0, concat_axis=0, tiled=True, axi...  51.5 us
    pallas_call x1, Pallas kernels, forward(): pl.pallas_call(functools.partial(forward_kernel, order), out_shape=(jax.S...  5.02 us

profile of v16, /device:TPU:0, one launch (start us, length us, event | category | flops | bytes accessed | tf_op | source)
XLA Modules:
  0.0 61.6 jit_solution(9662233741971982317)
XLA Ops:
  1.3 0.0 copy-start.1
  1.3 0.0 copy-start.2
  1.3 0.0 copy-start.3
  1.3 0.8 %shard_map.149 = (bf16[8,8,128]{2,1,0:T(8,128)(2,1)S(1)}, s32[8,128]{1,0:T(8,128)S(1)}) custom-call(s32[1]{0:T(128)S(6)} %copy.16.length_ref, bf16[1,8,128]{2,1,0:T(8,128)(2,1)} %source_hbm.1), custom_call_target="tpu_custom_call" | custom-call | flops 10000000000 | bytes 1048576 | tf_op jit(solution)/shard_map/pallas_call | solution.py:134
  2.2 13.7 %all_to_all.25.arrived_ref = bf16[8,8,128]{2,1,0:T(8,128)(2,1)S(1)} all-to-all(bf16[8,8,128]{2,1,0:T(8,128)(2,1)S(1)} %get-tuple-element.9), channel_id=1, replica_groups=mesh['ctx'=8,'head'=4] {'ctx'}, dimensions={0} | all-to-all | bytes 32768 | tf_op jit(solution)/shard_map/all_to_all | solution.py:356
  15.8 0.0 copy-done.3
  15.9 0.0 copy-done.4
  15.9 0.0 copy-done.7
  15.9 0.0 copy-done.8
  15.9 1.2 %shard_map.150 = bf16[8,3,4,128]{3,2,1,0:T(4,128)(2,1)S(1)} custom-call(s32[8,128]{1,0:T(8,128)S(1)} %get-tuple-element.8.length_ref, bf16[8,8,128]{2,1,0:T(8,128)(2,1)S(1)} %all_to_all.25.arrived_ref, bf16[1,4,128]{2,1,0:T(4,128)(2,1)S(1)} %copy-done.7, bf16[1,4,128]{2,1,0:T(4,128)(2,1)S(1)} %copy-done.8, bf16[1024,128]{1,0:T(8,128)(2,1)S(1)} %bitcast.19, ...), custom_call_target="tpu_custom_call" | custom-call | flops 10000000000 | bytes 1048576 | tf_op jit(solution)/shard_map/pallas_call | solution.py:206
  17.1 9.0 %all_to_all.26.part_ref = bf16[8,3,4,128]{3,2,1,0:T(4,128)(2,1)S(1)} all-to-all(bf16[8,3,4,128]{3,2,1,0:T(4,128)(2,1)S(1)} %shard_map.150), channel_id=1, replica_groups=mesh['ctx'=8,'head'=4] {'ctx'}, dimensions={0} | all-to-all | bytes 49152 | tf_op jit(solution)/shard_map/all_to_all | solution.py:356
  26.1 0.0 slice-start.4
  26.1 0.2 shard_map.151.copies_ref
  26.3 9.4 %all_to_all.27.rows_ref = bf16[32,8,128]{2,1,0:T(8,128)(2,1)S(1)} all-to-all(bf16[32,8,128]{2,1,0:T(8,128)(2,1)S(1)} %shard_map.151.copies_ref), channel_id=1, replica_groups={{0,1,2,3,4,5,6,7,16,17,18,19,20,21,22,23,24,25,26,27,28,29,30,31,8,9,10..., dimensions={0} | all-to-all | bytes 131072 | tf_op jit(solution)/shard_map/all_to_all | solution.py:356
  35.7 0.0 copy-done.6
  35.7 0.0 slice-start.5
  35.7 0.0 copy-start.5
  35.7 0.6 %shard_map.152 = (bf16[8,168]{1,0:T(8,128)(2,1)S(1)}, bf16[32,3,4,128]{3,2,1,0:T(4,128)(2,1)S(1)}) custom-call(bf16[32,8,128]{2,1,0:T(8,128)(2,1)S(1)} %all_to_all.27.rows_ref, bf16[168,4096]{1,0:T(8,128)(2,1)S(1)} %bitcast.16, bf16[8,168]{1,0:T(8,128)(2,1)S(1)} %copy-done.6), custom_call_target="tpu_custom_call" | custom-call | flops 10000000000 | bytes 1048576 | tf_op jit(solution)/shard_map/pallas_call | solution.py:257
  36.4 9.8 %all_to_all.28.pieces_ref = bf16[32,3,4,128]{3,2,1,0:T(4,128)(2,1)S(1)} all-to-all(bf16[32,3,4,128]{3,2,1,0:T(4,128)(2,1)S(1)} %get-tuple-element.10), channel_id=1, replica_groups={{0,1,2,3,4,5,6,7,16,17,18,19,20,21,22,23,24,25,26,27,28,29,30,31,8,9,10..., dimensions={0} | all-to-all | bytes 196608 | tf_op jit(solution)/shard_map/all_to_all | solution.py:356
  46.2 0.0 slice-done
  46.2 0.0 slice-done.4
  46.3 5.0 %shard_map.153 = (bf16[32,3,4,128]{3,2,1,0:T(4,128)(2,1)S(1)}, bf16[8,128]{1,0:T(8,128)(2,1)}) custom-call(bf16[32,3,4,128]{3,2,1,0:T(4,128)(2,1)S(1)} %all_to_all.28.pieces_ref, f32[5376]{0:T(1024)S(1)} %copy-done.5, bf16[32,8,128]{2,1,0:T(8,128)(2,1)S(1)} %shard_map.151.copies_ref, bf16[672,5376]{1,0:T(8,128)(2,1)S(1)} %bitcast.10, ...), custom_call_target="tpu_custom_call" | custom-call | flops 10000000000 | bytes 1048576 | tf_op jit(solution)/shard_map/pallas_call | solution.py:314
  51.3 9.6 %all_to_all.29.shares_ref = bf16[32,3,4,128]{3,2,1,0:T(4,128)(2,1)S(1)} all-to-all(bf16[32,3,4,128]{3,2,1,0:T(4,128)(2,1)S(1)} %get-tuple-element.12), channel_id=1, replica_groups={{0,1,2,3,4,5,6,7,16,17,18,19,20,21,22,23,24,25,26,27,28,29,30,31,8,9,10..., dimensions={0} | all-to-all | bytes 196608 | tf_op jit(solution)/shard_map/all_to_all | solution.py:356
  60.9 0.8 %shard_map.154 = bf16[8,168]{1,0:T(8,128)(2,1)} custom-call(bf16[32,3,4,128]{3,2,1,0:T(4,128)(2,1)S(1)} %all_to_all.29.shares_ref, bf16[8,168]{1,0:T(8,128)(2,1)S(1)} %get-tuple-element.13.hidden_ref), custom_call_target="tpu_custom_call" | custom-call | tf_op jit(solution)/shard_map/pallas_call | solution.py:340
  (20 shorter events, 0.0 us)
Async XLA Ops:
  1.3 14.6 %copy-start.1 = (bf16[1024,4,128]{2,1,0:T(4,128)(2,1)S(1)}, bf16[1024,4,128]{2,1,0:T(4,128)(2,1)}, u32[]{:S(2)}) copy-start(bf16[1024,4,128]{2,1,0:T(4,128)(2,1)} %param.20) | copy-start | bytes 3145732
  1.3 14.6 %copy-start.2 = (bf16[1024,4,128]{2,1,0:T(4,128)(2,1)S(1)}, bf16[1024,4,128]{2,1,0:T(4,128)(2,1)}, u32[]{:S(2)}) copy-start(bf16[1024,4,128]{2,1,0:T(4,128)(2,1)} %param.21) | copy-start | bytes 3145732
  1.3 14.6 %copy-start.3 = (bf16[1,256,4,128]{3,2,1,0:T(4,128)(2,1)S(1)}, bf16[1,256,4,128]{3,2,1,0:T(4,128)(2,1)}, u32[]{:S(2)}) copy-start(bf16[1,256,4,128]{3,2,1,0:T(4,128)(2,1)} %param.17) | copy-start | bytes 786436
  1.3 14.5 %copy-start.4 = (bf16[1,256,4,128]{3,2,1,0:T(4,128)(2,1)S(1)}, bf16[1,256,4,128]{3,2,1,0:T(4,128)(2,1)}, u32[]{:S(2)}) copy-start(bf16[1,256,4,128]{3,2,1,0:T(4,128)(2,1)} %param.18) | copy-start | bytes 786436
  1.3 14.5 %copy-start.7 = (bf16[1,4,128]{2,1,0:T(4,128)(2,1)S(1)}, bf16[1,4,128]{2,1,0:T(4,128)(2,1)}, u32[]{:S(2)}) copy-start(bf16[1,4,128]{2,1,0:T(4,128)(2,1)} %kn_ref.1) | copy-start | bytes 3076
  1.3 14.5 %copy-start.8 = (bf16[1,4,128]{2,1,0:T(4,128)(2,1)S(1)}, bf16[1,4,128]{2,1,0:T(4,128)(2,1)}, u32[]{:S(2)}) copy-start(bf16[1,4,128]{2,1,0:T(4,128)(2,1)} %vn_ref.1) | copy-start | bytes 3076
  26.0 9.6 %copy-start = (bf16[4096,168]{0,1:T(8,128)(2,1)S(1)}, bf16[4096,168]{0,1:T(8,128)(2,1)}, u32[]{:S(2)}) copy-start(bf16[4096,168]{0,1:T(8,128)(2,1)} %param.22) | copy-start | bytes 4128772
  26.0 9.6 %copy-start.6 = (bf16[8,168]{1,0:T(8,128)(2,1)S(1)}, bf16[8,168]{1,0:T(8,128)(2,1)}, u32[]{:S(2)}) copy-start(bf16[8,168]{1,0:T(8,128)(2,1)} %residual_ref.1) | copy-start | bytes 8068
  26.1 20.1 %slice-start = ((s8[7225344]{0:T(1024)(128)(4,1)}), s8[4194304]{0:T(1024)(128)(4,1)S(1)}, s32[]{:S(2)}) async-start(s8[7225344]{0:T(1024)(128)(4,1)} %bitcast.8), calls=%async_computation.5 | async-start | bytes 8388608
  26.1 20.2 %slice-start.2 = ((s8[7225344]{0:T(1024)(128)(4,1)}), s8[4194304]{0:T(1024)(128)(4,1)S(1)}, s32[]{:S(2)}) async-start(s8[7225344]{0:T(1024)(128)(4,1)} %bitcast.11), calls=%async_computation.7 | async-start | bytes 8388608
  26.1 20.1 %slice-start.4 = ((s8[7225344]{0:T(1024)(128)(4,1)}), s8[4194304]{0:T(1024)(128)(4,1)S(1)}, s32[]{:S(2)}) async-start(s8[7225344]{0:T(1024)(128)(4,1)} %bitcast.14), calls=%async_computation.9 | async-start | bytes 8388608
  35.7 10.5 %slice-start.1 = ((s8[7225344]{0:T(1024)(128)(4,1)}), s8[3031040]{0:T(1024)(128)(4,1)S(1)}, s32[]{:S(2)}) async-start(s8[7225344]{0:T(1024)(128)(4,1)} %bitcast.8), calls=%async_computation.6 | async-start | bytes 6062080
  35.7 10.5 %slice-start.3 = ((s8[7225344]{0:T(1024)(128)(4,1)}), s8[3031040]{0:T(1024)(128)(4,1)S(1)}, s32[]{:S(2)}) async-start(s8[7225344]{0:T(1024)(128)(4,1)} %bitcast.11), calls=%async_computation.8 | async-start | bytes 6062080
  35.7 10.5 %slice-start.5 = ((s8[7225344]{0:T(1024)(128)(4,1)}), s8[3031040]{0:T(1024)(128)(4,1)S(1)}, s32[]{:S(2)}) async-start(s8[7225344]{0:T(1024)(128)(4,1)} %bitcast.14), calls=%async_computation.10 | async-start | bytes 6062080
  35.7 10.5 %copy-start.5 = (f32[5376]{0:T(1024)S(1)}, f32[5376]{0:T(1024)}, u32[]{:S(2)}) copy-start(f32[5376]{0:T(1024)} %gain_ref.1) | copy-start | bytes 64516

commit v17 on v16

--- a/solution.py
+++ b/solution.py
@@ -65,7 +65,7 @@
 
 
 def joined(first, second, rest):
-    low = jnp.concatenate([first, second], axis=0).astype(jnp.float32)
+    low = jnp.concatenate([first.astype(jnp.float32), second.astype(jnp.float32)], axis=0)
     rest = rest.astype(jnp.float32)
     return low, jnp.concatenate([rest, pltpu.roll(rest, HALF, 1)], axis=0)
 
@@ -282,25 +282,23 @@
         state = state_ref[...]
     mean_square = jnp.mean(state * state, axis=-1, keepdims=True)
     gain = gain_ref[...].reshape(1, devices * columns)
-    normed = (state * lax.rsqrt(mean_square + NORM_EPSILON) * gain).astype(jnp.bfloat16)
+    scale = lax.rsqrt(mean_square + NORM_EPSILON)
+    scaled = (state * gain).astype(jnp.bfloat16)
     units = gate_ref.shape[0]
     count = CHUNKS if units % (16 * CHUNKS) == 0 else 1
     size = units // count
-    share = jnp.zeros((normed.shape[0], down_ref.shape[1]), jnp.float32)
+    share = jnp.zeros((scaled.shape[0], down_ref.shape[1]), jnp.float32)
     ready = None
     for chunk in range(count + 1):
         if chunk < count:
             rows = slice(chunk * size, (chunk + 1) * size)
-            gate_values = dot_rows(gate_ref[rows], normed)
-            if chunk % 2:
-                up_values = dot_rows(up_ref[rows], normed).T
-            else:
-                up_values = dot_rows(normed, up_ref[rows])
+            gate_values = dot_rows(gate_ref[rows], scaled)
+            up_values = dot_rows(scaled, up_ref[rows]) * scale
         if ready is not None:
             activated, held = ready
             share += jnp.dot(activated, down_ref[held], preferred_element_type=jnp.float32)
         if chunk < count:
-            activated = jax.nn.gelu(gate_values.T, approximate=True) * up_values
+            activated = jax.nn.gelu(gate_values.T * scale, approximate=True) * up_values
             ready = activated.astype(jnp.bfloat16), rows
     if pieces_ref.ndim == 4:
         put_columns(out_ref, order, share, columns)

time: 61.9 us -> 61.8 us (level)
  no operation moved by 1% of the time
where the time goes in v17:
time: 61.8 us; the launch traced here: 61.5 us
  blocking collectives  51.5 us (83%)
  Pallas kernels  8.52 us (14%)
  between operations  1.48 us (2%)
    all_to_all x5, blocking collectives, exchange(): lax.all_to_all(copies, axes, split_axis=0, concat_axis=0, tiled=True, axi...  51.5 us
    pallas_call x1, Pallas kernels, forward(): pl.pallas_call(functools.partial(forward_kernel, order), out_shape=(jax.S...  4.92 us

profile of v17, /device:TPU:0, one launch (start us, length us, event | category | flops | bytes accessed | tf_op | source)
XLA Modules:
  0.0 61.5 jit_solution(10111786978660652760)
XLA Ops:
  1.3 0.0 copy-start.1
  1.3 0.0 copy-start.2
  1.3 0.0 copy-start.3
  1.3 0.8 %shard_map.149 = (bf16[8,8,128]{2,1,0:T(8,128)(2,1)S(1)}, s32[8,128]{1,0:T(8,128)S(1)}) custom-call(s32[1]{0:T(128)S(6)} %copy.16.length_ref, bf16[1,8,128]{2,1,0:T(8,128)(2,1)} %source_hbm.1), custom_call_target="tpu_custom_call" | custom-call | flops 10000000000 | bytes 1048576 | tf_op jit(solution)/shard_map/pallas_call | solution.py:134
  2.2 13.7 %all_to_all.25.arrived_ref = bf16[8,8,128]{2,1,0:T(8,128)(2,1)S(1)} all-to-all(bf16[8,8,128]{2,1,0:T(8,128)(2,1)S(1)} %get-tuple-element.9), channel_id=1, replica_groups=mesh['ctx'=8,'head'=4] {'ctx'}, dimensions={0} | all-to-all | bytes 32768 | tf_op jit(solution)/shard_map/all_to_all | solution.py:354
  15.8 0.0 copy-done.3
  15.9 0.0 copy-done.4
  15.9 0.0 copy-done.7
  15.9 0.0 copy-done.8
  15.9 1.2 %shard_map.150 = bf16[8,3,4,128]{3,2,1,0:T(4,128)(2,1)S(1)} custom-call(s32[8,128]{1,0:T(8,128)S(1)} %get-tuple-element.8.length_ref, bf16[8,8,128]{2,1,0:T(8,128)(2,1)S(1)} %all_to_all.25.arrived_ref, bf16[1,4,128]{2,1,0:T(4,128)(2,1)S(1)} %copy-done.7, bf16[1,4,128]{2,1,0:T(4,128)(2,1)S(1)} %copy-done.8, bf16[1024,128]{1,0:T(8,128)(2,1)S(1)} %bitcast.19, ...), custom_call_target="tpu_custom_call" | custom-call | flops 10000000000 | bytes 1048576 | tf_op jit(solution)/shard_map/pallas_call | solution.py:206
  17.1 9.0 %all_to_all.26.part_ref = bf16[8,3,4,128]{3,2,1,0:T(4,128)(2,1)S(1)} all-to-all(bf16[8,3,4,128]{3,2,1,0:T(4,128)(2,1)S(1)} %shard_map.150), channel_id=1, replica_groups=mesh['ctx'=8,'head'=4] {'ctx'}, dimensions={0} | all-to-all | bytes 49152 | tf_op jit(solution)/shard_map/all_to_all | solution.py:354
  26.1 0.0 slice-start.4
  26.1 0.2 shard_map.151.copies_ref
  26.3 9.4 %all_to_all.27.rows_ref = bf16[32,8,128]{2,1,0:T(8,128)(2,1)S(1)} all-to-all(bf16[32,8,128]{2,1,0:T(8,128)(2,1)S(1)} %shard_map.151.copies_ref), channel_id=1, replica_groups={{0,1,2,3,4,5,6,7,16,17,18,19,20,21,22,23,24,25,26,27,28,29,30,31,8,9,10..., dimensions={0} | all-to-all | bytes 131072 | tf_op jit(solution)/shard_map/all_to_all | solution.py:354
  35.7 0.0 copy-done.6
  35.7 0.0 slice-start.5
  35.7 0.0 copy-start.5
  35.7 0.6 %shard_map.152 = (bf16[8,168]{1,0:T(8,128)(2,1)S(1)}, bf16[32,3,4,128]{3,2,1,0:T(4,128)(2,1)S(1)}) custom-call(bf16[32,8,128]{2,1,0:T(8,128)(2,1)S(1)} %all_to_all.27.rows_ref, bf16[168,4096]{1,0:T(8,128)(2,1)S(1)} %bitcast.16, bf16[8,168]{1,0:T(8,128)(2,1)S(1)} %copy-done.6), custom_call_target="tpu_custom_call" | custom-call | flops 10000000000 | bytes 1048576 | tf_op jit(solution)/shard_map/pallas_call | solution.py:257
  36.4 9.8 %all_to_all.28.pieces_ref = bf16[32,3,4,128]{3,2,1,0:T(4,128)(2,1)S(1)} all-to-all(bf16[32,3,4,128]{3,2,1,0:T(4,128)(2,1)S(1)} %get-tuple-element.10), channel_id=1, replica_groups={{0,1,2,3,4,5,6,7,16,17,18,19,20,21,22,23,24,25,26,27,28,29,30,31,8,9,10..., dimensions={0} | all-to-all | bytes 196608 | tf_op jit(solution)/shard_map/all_to_all | solution.py:354
  46.2 0.0 slice-done
  46.2 0.0 slice-done.4
  46.3 4.9 %shard_map.153 = (bf16[32,3,4,128]{3,2,1,0:T(4,128)(2,1)S(1)}, bf16[8,128]{1,0:T(8,128)(2,1)}) custom-call(bf16[32,3,4,128]{3,2,1,0:T(4,128)(2,1)S(1)} %all_to_all.28.pieces_ref, f32[5376]{0:T(1024)S(1)} %copy-done.5, bf16[32,8,128]{2,1,0:T(8,128)(2,1)S(1)} %shard_map.151.copies_ref, bf16[672,5376]{1,0:T(8,128)(2,1)S(1)} %bitcast.10, ...), custom_call_target="tpu_custom_call" | custom-call | flops 10000000000 | bytes 1048576 | tf_op jit(solution)/shard_map/pallas_call | solution.py:312
  51.2 9.6 %all_to_all.29.shares_ref = bf16[32,3,4,128]{3,2,1,0:T(4,128)(2,1)S(1)} all-to-all(bf16[32,3,4,128]{3,2,1,0:T(4,128)(2,1)S(1)} %get-tuple-element.12), channel_id=1, replica_groups={{0,1,2,3,4,5,6,7,16,17,18,19,20,21,22,23,24,25,26,27,28,29,30,31,8,9,10..., dimensions={0} | all-to-all | bytes 196608 | tf_op jit(solution)/shard_map/all_to_all | solution.py:354
  60.8 0.8 %shard_map.154 = bf16[8,168]{1,0:T(8,128)(2,1)} custom-call(bf16[32,3,4,128]{3,2,1,0:T(4,128)(2,1)S(1)} %all_to_all.29.shares_ref, bf16[8,168]{1,0:T(8,128)(2,1)S(1)} %get-tuple-element.13.hidden_ref), custom_call_target="tpu_custom_call" | custom-call | tf_op jit(solution)/shard_map/pallas_call | solution.py:338
  (20 shorter events, 0.0 us)
Async XLA Ops:
  1.3 14.6 %copy-start.1 = (bf16[1024,4,128]{2,1,0:T(4,128)(2,1)S(1)}, bf16[1024,4,128]{2,1,0:T(4,128)(2,1)}, u32[]{:S(2)}) copy-start(bf16[1024,4,128]{2,1,0:T(4,128)(2,1)} %param.20) | copy-start | bytes 3145732
  1.3 14.6 %copy-start.2 = (bf16[1024,4,128]{2,1,0:T(4,128)(2,1)S(1)}, bf16[1024,4,128]{2,1,0:T(4,128)(2,1)}, u32[]{:S(2)}) copy-start(bf16[1024,4,128]{2,1,0:T(4,128)(2,1)} %param.21) | copy-start | bytes 3145732
  1.3 14.6 %copy-start.3 = (bf16[1,256,4,128]{3,2,1,0:T(4,128)(2,1)S(1)}, bf16[1,256,4,128]{3,2,1,0:T(4,128)(2,1)}, u32[]{:S(2)}) copy-start(bf16[1,256,4,128]{3,2,1,0:T(4,128)(2,1)} %param.17) | copy-start | bytes 786436
  1.3 14.5 %copy-start.4 = (bf16[1,256,4,128]{3,2,1,0:T(4,128)(2,1)S(1)}, bf16[1,256,4,128]{3,2,1,0:T(4,128)(2,1)}, u32[]{:S(2)}) copy-start(bf16[1,256,4,128]{3,2,1,0:T(4,128)(2,1)} %param.18) | copy-start | bytes 786436
  1.3 14.5 %copy-start.7 = (bf16[1,4,128]{2,1,0:T(4,128)(2,1)S(1)}, bf16[1,4,128]{2,1,0:T(4,128)(2,1)}, u32[]{:S(2)}) copy-start(bf16[1,4,128]{2,1,0:T(4,128)(2,1)} %kn_ref.1) | copy-start | bytes 3076
  1.3 14.5 %copy-start.8 = (bf16[1,4,128]{2,1,0:T(4,128)(2,1)S(1)}, bf16[1,4,128]{2,1,0:T(4,128)(2,1)}, u32[]{:S(2)}) copy-start(bf16[1,4,128]{2,1,0:T(4,128)(2,1)} %vn_ref.1) | copy-start | bytes 3076
  26.0 9.6 %copy-start = (bf16[4096,168]{0,1:T(8,128)(2,1)S(1)}, bf16[4096,168]{0,1:T(8,128)(2,1)}, u32[]{:S(2)}) copy-start(bf16[4096,168]{0,1:T(8,128)(2,1)} %param.22) | copy-start | bytes 4128772
  26.0 9.6 %copy-start.6 = (bf16[8,168]{1,0:T(8,128)(2,1)S(1)}, bf16[8,168]{1,0:T(8,128)(2,1)}, u32[]{:S(2)}) copy-start(bf16[8,168]{1,0:T(8,128)(2,1)} %residual_ref.1) | copy-start | bytes 8068
  26.1 20.1 %slice-start = ((s8[7225344]{0:T(1024)(128)(4,1)}), s8[4194304]{0:T(1024)(128)(4,1)S(1)}, s32[]{:S(2)}) async-start(s8[7225344]{0:T(1024)(128)(4,1)} %bitcast.8), calls=%async_computation.5 | async-start | bytes 8388608
  26.1 20.2 %slice-start.2 = ((s8[7225344]{0:T(1024)(128)(4,1)}), s8[4194304]{0:T(1024)(128)(4,1)S(1)}, s32[]{:S(2)}) async-start(s8[7225344]{0:T(1024)(128)(4,1)} %bitcast.11), calls=%async_computation.7 | async-start | bytes 8388608
  26.1 20.1 %slice-start.4 = ((s8[7225344]{0:T(1024)(128)(4,1)}), s8[4194304]{0:T(1024)(128)(4,1)S(1)}, s32[]{:S(2)}) async-start(s8[7225344]{0:T(1024)(128)(4,1)} %bitcast.14), calls=%async_computation.9 | async-start | bytes 8388608
  35.7 10.5 %slice-start.1 = ((s8[7225344]{0:T(1024)(128)(4,1)}), s8[3031040]{0:T(1024)(128)(4,1)S(1)}, s32[]{:S(2)}) async-start(s8[7225344]{0:T(1024)(128)(4,1)} %bitcast.8), calls=%async_computation.6 | async-start | bytes 6062080
  35.7 10.5 %slice-start.3 = ((s8[7225344]{0:T(1024)(128)(4,1)}), s8[3031040]{0:T(1024)(128)(4,1)S(1)}, s32[]{:S(2)}) async-start(s8[7225344]{0:T(1024)(128)(4,1)} %bitcast.11), calls=%async_computation.8 | async-start | bytes 6062080
  35.7 10.5 %slice-start.5 = ((s8[7225344]{0:T(1024)(128)(4,1)}), s8[3031040]{0:T(1024)(128)(4,1)S(1)}, s32[]{:S(2)}) async-start(s8[7225344]{0:T(1024)(128)(4,1)} %bitcast.14), calls=%async_computation.10 | async-start | bytes 6062080
  35.7 10.5 %copy-start.5 = (f32[5376]{0:T(1024)S(1)}, f32[5376]{0:T(1024)}, u32[]{:S(2)}) copy-start(f32[5376]{0:T(1024)} %gain_ref.1) | copy-start | bytes 64516

commit v18 on v16

--- a/solution.py
+++ b/solution.py
@@ -14,7 +14,7 @@
 COST = pl.CostEstimate(flops=10**10, bytes_accessed=MIB, transcendentals=10**6)
 TERMS = 3
 CHUNKS = 3
-BLOCK_ROWS = 1024
+BLOCK_ROWS = 2048
 LANES = 128
 HALF = LANES // 2
 BOTH = ("ctx", "head")
@@ -65,7 +65,7 @@
 
 
 def joined(first, second, rest):
-    low = jnp.concatenate([first, second], axis=0).astype(jnp.float32)
+    low = jnp.concatenate([first.astype(jnp.float32), second.astype(jnp.float32)], axis=0)
     rest = rest.astype(jnp.float32)
     return low, jnp.concatenate([rest, pltpu.roll(rest, HALF, 1)], axis=0)
 
@@ -292,10 +292,7 @@
         if chunk < count:
             rows = slice(chunk * size, (chunk + 1) * size)
             gate_values = dot_rows(gate_ref[rows], normed)
-            if chunk % 2:
-                up_values = dot_rows(up_ref[rows], normed).T
-            else:
-                up_values = dot_rows(normed, up_ref[rows])
+            up_values = dot_rows(normed, up_ref[rows])
         if ready is not None:
             activated, held = ready
             share += jnp.dot(activated, down_ref[held], preferred_element_type=jnp.float32)
@@ -328,7 +325,9 @@
 
 
 def total_kernel(shares_ref, hidden_ref, out_ref):
-    summed = jnp.sum(shares_ref[...].astype(jnp.float32), axis=0)
+    half = shares_ref.shape[0] // 2
+    pairs = shares_ref[:half].astype(jnp.float32) + shares_ref[half:].astype(jnp.float32)
+    summed = jnp.sum(pairs, axis=0)
     if shares_ref.ndim == 4:
         columns = hidden_ref.shape[1]
         low, rest = (turn(part, columns, back=True) for part in joined(*summed))

time: 61.9 us -> 62 us (level)
  no operation moved by 1% of the time
where the time goes in v18:
time: 62 us; the launch traced here: 61.7 us
  blocking collectives  51.5 us (83%)
  Pallas kernels  8.7 us (14%)
  between operations  1.48 us (2%)
    all_to_all x5, blocking collectives, exchange(): lax.all_to_all(copies, axes, split_axis=0, concat_axis=0, tiled=True, axi...  51.5 us
    pallas_call x1, Pallas kernels, forward(): pl.pallas_call(functools.partial(forward_kernel, order), out_shape=(jax.S...  5.04 us

profile of v18, /device:TPU:0, one launch (start us, length us, event | category | flops | bytes accessed | tf_op | source)
XLA Modules:
  0.0 61.7 jit_solution(11096418930665140221)
XLA Ops:
  1.3 0.0 copy-start.1
  1.3 0.0 copy-start.2
  1.3 0.0 copy-start.3
  1.3 0.8 %shard_map.149 = (bf16[8,8,128]{2,1,0:T(8,128)(2,1)S(1)}, s32[8,128]{1,0:T(8,128)S(1)}) custom-call(s32[1]{0:T(128)S(6)} %copy.16.length_ref, bf16[1,8,128]{2,1,0:T(8,128)(2,1)} %source_hbm.1), custom_call_target="tpu_custom_call" | custom-call | flops 10000000000 | bytes 1048576 | tf_op jit(solution)/shard_map/pallas_call | solution.py:134
  2.2 13.7 %all_to_all.25.arrived_ref = bf16[8,8,128]{2,1,0:T(8,128)(2,1)S(1)} all-to-all(bf16[8,8,128]{2,1,0:T(8,128)(2,1)S(1)} %get-tuple-element.9), channel_id=1, replica_groups=mesh['ctx'=8,'head'=4] {'ctx'}, dimensions={0} | all-to-all | bytes 32768 | tf_op jit(solution)/shard_map/all_to_all | solution.py:355
  15.8 0.0 copy-done.3
  15.9 0.0 copy-done.4
  15.9 0.0 copy-done.7
  15.9 0.0 copy-done.8
  15.9 1.2 %shard_map.150 = bf16[8,3,4,128]{3,2,1,0:T(4,128)(2,1)S(1)} custom-call(s32[8,128]{1,0:T(8,128)S(1)} %get-tuple-element.8.length_ref, bf16[8,8,128]{2,1,0:T(8,128)(2,1)S(1)} %all_to_all.25.arrived_ref, bf16[1,4,128]{2,1,0:T(4,128)(2,1)S(1)} %copy-done.7, bf16[1,4,128]{2,1,0:T(4,128)(2,1)S(1)} %copy-done.8, bf16[1024,128]{1,0:T(8,128)(2,1)S(1)} %bitcast.19, ...), custom_call_target="tpu_custom_call" | custom-call | flops 10000000000 | bytes 1048576 | tf_op jit(solution)/shard_map/pallas_call | solution.py:206
  17.1 9.0 %all_to_all.26.part_ref = bf16[8,3,4,128]{3,2,1,0:T(4,128)(2,1)S(1)} all-to-all(bf16[8,3,4,128]{3,2,1,0:T(4,128)(2,1)S(1)} %shard_map.150), channel_id=1, replica_groups=mesh['ctx'=8,'head'=4] {'ctx'}, dimensions={0} | all-to-all | bytes 49152 | tf_op jit(solution)/shard_map/all_to_all | solution.py:355
  26.1 0.0 slice-start.4
  26.1 0.2 shard_map.151.copies_ref
  26.3 9.4 %all_to_all.27.rows_ref = bf16[32,8,128]{2,1,0:T(8,128)(2,1)S(1)} all-to-all(bf16[32,8,128]{2,1,0:T(8,128)(2,1)S(1)} %shard_map.151.copies_ref), channel_id=1, replica_groups={{0,1,2,3,4,5,6,7,16,17,18,19,20,21,22,23,24,25,26,27,28,29,30,31,8,9,10..., dimensions={0} | all-to-all | bytes 131072 | tf_op jit(solution)/shard_map/all_to_all | solution.py:355
  35.7 0.0 copy-done.6
  35.7 0.0 slice-start.5
  35.8 0.0 copy-start.5
  35.8 0.6 %shard_map.152 = (bf16[8,168]{1,0:T(8,128)(2,1)S(1)}, bf16[32,3,4,128]{3,2,1,0:T(4,128)(2,1)S(1)}) custom-call(bf16[32,8,128]{2,1,0:T(8,128)(2,1)S(1)} %all_to_all.27.rows_ref, bf16[168,4096]{1,0:T(8,128)(2,1)S(1)} %bitcast.16, bf16[8,168]{1,0:T(8,128)(2,1)S(1)} %copy-done.6), custom_call_target="tpu_custom_call" | custom-call | flops 10000000000 | bytes 1048576 | tf_op jit(solution)/shard_map/pallas_call | solution.py:257
  36.4 9.8 %all_to_all.28.pieces_ref = bf16[32,3,4,128]{3,2,1,0:T(4,128)(2,1)S(1)} all-to-all(bf16[32,3,4,128]{3,2,1,0:T(4,128)(2,1)S(1)} %get-tuple-element.10), channel_id=1, replica_groups={{0,1,2,3,4,5,6,7,16,17,18,19,20,21,22,23,24,25,26,27,28,29,30,31,8,9,10..., dimensions={0} | all-to-all | bytes 196608 | tf_op jit(solution)/shard_map/all_to_all | solution.py:355
  46.3 0.0 slice-done
  46.3 0.0 slice-done.4
  46.3 5.0 %shard_map.153 = (bf16[32,3,4,128]{3,2,1,0:T(4,128)(2,1)S(1)}, bf16[8,128]{1,0:T(8,128)(2,1)}) custom-call(bf16[32,3,4,128]{3,2,1,0:T(4,128)(2,1)S(1)} %all_to_all.28.pieces_ref, f32[5376]{0:T(1024)S(1)} %copy-done.5, bf16[32,8,128]{2,1,0:T(8,128)(2,1)S(1)} %shard_map.151.copies_ref, bf16[672,5376]{1,0:T(8,128)(2,1)S(1)} %bitcast.10, ...), custom_call_target="tpu_custom_call" | custom-call | flops 10000000000 | bytes 1048576 | tf_op jit(solution)/shard_map/pallas_call | solution.py:311
  51.4 9.6 %all_to_all.29.shares_ref = bf16[32,3,4,128]{3,2,1,0:T(4,128)(2,1)S(1)} all-to-all(bf16[32,3,4,128]{3,2,1,0:T(4,128)(2,1)S(1)} %get-tuple-element.12), channel_id=1, replica_groups={{0,1,2,3,4,5,6,7,16,17,18,19,20,21,22,23,24,25,26,27,28,29,30,31,8,9,10..., dimensions={0} | all-to-all | bytes 196608 | tf_op jit(solution)/shard_map/all_to_all | solution.py:355
  61.0 0.8 %shard_map.154 = bf16[8,168]{1,0:T(8,128)(2,1)} custom-call(bf16[32,3,4,128]{3,2,1,0:T(4,128)(2,1)S(1)} %all_to_all.29.shares_ref, bf16[8,168]{1,0:T(8,128)(2,1)S(1)} %get-tuple-element.13.hidden_ref), custom_call_target="tpu_custom_call" | custom-call | tf_op jit(solution)/shard_map/pallas_call | solution.py:339
  (20 shorter events, 0.0 us)
Async XLA Ops:
  1.3 14.6 %copy-start.1 = (bf16[1024,4,128]{2,1,0:T(4,128)(2,1)S(1)}, bf16[1024,4,128]{2,1,0:T(4,128)(2,1)}, u32[]{:S(2)}) copy-start(bf16[1024,4,128]{2,1,0:T(4,128)(2,1)} %param.20) | copy-start | bytes 3145732
  1.3 14.6 %copy-start.2 = (bf16[1024,4,128]{2,1,0:T(4,128)(2,1)S(1)}, bf16[1024,4,128]{2,1,0:T(4,128)(2,1)}, u32[]{:S(2)}) copy-start(bf16[1024,4,128]{2,1,0:T(4,128)(2,1)} %param.21) | copy-start | bytes 3145732
  1.3 14.6 %copy-start.3 = (bf16[1,256,4,128]{3,2,1,0:T(4,128)(2,1)S(1)}, bf16[1,256,4,128]{3,2,1,0:T(4,128)(2,1)}, u32[]{:S(2)}) copy-start(bf16[1,256,4,128]{3,2,1,0:T(4,128)(2,1)} %param.17) | copy-start | bytes 786436
  1.3 14.5 %copy-start.4 = (bf16[1,256,4,128]{3,2,1,0:T(4,128)(2,1)S(1)}, bf16[1,256,4,128]{3,2,1,0:T(4,128)(2,1)}, u32[]{:S(2)}) copy-start(bf16[1,256,4,128]{3,2,1,0:T(4,128)(2,1)} %param.18) | copy-start | bytes 786436
  1.3 14.5 %copy-start.7 = (bf16[1,4,128]{2,1,0:T(4,128)(2,1)S(1)}, bf16[1,4,128]{2,1,0:T(4,128)(2,1)}, u32[]{:S(2)}) copy-start(bf16[1,4,128]{2,1,0:T(4,128)(2,1)} %kn_ref.1) | copy-start | bytes 3076
  1.3 14.5 %copy-start.8 = (bf16[1,4,128]{2,1,0:T(4,128)(2,1)S(1)}, bf16[1,4,128]{2,1,0:T(4,128)(2,1)}, u32[]{:S(2)}) copy-start(bf16[1,4,128]{2,1,0:T(4,128)(2,1)} %vn_ref.1) | copy-start | bytes 3076
  26.1 9.6 %copy-start = (bf16[4096,168]{0,1:T(8,128)(2,1)S(1)}, bf16[4096,168]{0,1:T(8,128)(2,1)}, u32[]{:S(2)}) copy-start(bf16[4096,168]{0,1:T(8,128)(2,1)} %param.22) | copy-start | bytes 4128772
  26.1 9.6 %copy-start.6 = (bf16[8,168]{1,0:T(8,128)(2,1)S(1)}, bf16[8,168]{1,0:T(8,128)(2,1)}, u32[]{:S(2)}) copy-start(bf16[8,168]{1,0:T(8,128)(2,1)} %residual_ref.1) | copy-start | bytes 8068
  26.1 20.1 %slice-start = ((s8[7225344]{0:T(1024)(128)(4,1)}), s8[4194304]{0:T(1024)(128)(4,1)S(1)}, s32[]{:S(2)}) async-start(s8[7225344]{0:T(1024)(128)(4,1)} %bitcast.8), calls=%async_computation.5 | async-start | bytes 8388608
  26.1 20.2 %slice-start.2 = ((s8[7225344]{0:T(1024)(128)(4,1)}), s8[4194304]{0:T(1024)(128)(4,1)S(1)}, s32[]{:S(2)}) async-start(s8[7225344]{0:T(1024)(128)(4,1)} %bitcast.11), calls=%async_computation.7 | async-start | bytes 8388608
  26.1 20.1 %slice-start.4 = ((s8[7225344]{0:T(1024)(128)(4,1)}), s8[4194304]{0:T(1024)(128)(4,1)S(1)}, s32[]{:S(2)}) async-start(s8[7225344]{0:T(1024)(128)(4,1)} %bitcast.14), calls=%async_computation.9 | async-start | bytes 8388608
  35.7 10.5 %slice-start.1 = ((s8[7225344]{0:T(1024)(128)(4,1)}), s8[3031040]{0:T(1024)(128)(4,1)S(1)}, s32[]{:S(2)}) async-start(s8[7225344]{0:T(1024)(128)(4,1)} %bitcast.8), calls=%async_computation.6 | async-start | bytes 6062080
  35.7 10.5 %slice-start.3 = ((s8[7225344]{0:T(1024)(128)(4,1)}), s8[3031040]{0:T(1024)(128)(4,1)S(1)}, s32[]{:S(2)}) async-start(s8[7225344]{0:T(1024)(128)(4,1)} %bitcast.11), calls=%async_computation.8 | async-start | bytes 6062080
  35.7 10.5 %slice-start.5 = ((s8[7225344]{0:T(1024)(128)(4,1)}), s8[3031040]{0:T(1024)(128)(4,1)S(1)}, s32[]{:S(2)}) async-start(s8[7225344]{0:T(1024)(128)(4,1)} %bitcast.14), calls=%async_computation.10 | async-start | bytes 6062080
  35.8 10.5 %copy-start.5 = (f32[5376]{0:T(1024)S(1)}, f32[5376]{0:T(1024)}, u32[]{:S(2)}) copy-start(f32[5376]{0:T(1024)} %gain_ref.1) | copy-start | bytes 64516

commit v19 on v18

--- a/solution.py
+++ b/solution.py
@@ -14,7 +14,7 @@
 COST = pl.CostEstimate(flops=10**10, bytes_accessed=MIB, transcendentals=10**6)
 TERMS = 3
 CHUNKS = 3
-BLOCK_ROWS = 2048
+BLOCK_ROWS = 1024
 LANES = 128
 HALF = LANES // 2
 BOTH = ("ctx", "head")

time: 62 us -> 61.9 us (level)
  no operation moved by 1% of the time
where the time goes in v19:
time: 61.9 us; the launch traced here: 61.7 us
  blocking collectives  51.5 us (83%)
  Pallas kernels  8.64 us (14%)
  between operations  1.48 us (2%)
    all_to_all x5, blocking collectives, exchange(): lax.all_to_all(copies, axes, split_axis=0, concat_axis=0, tiled=True, axi...  51.5 us
    pallas_call x1, Pallas kernels, forward(): pl.pallas_call(functools.partial(forward_kernel, order), out_shape=(jax.S...  5.04 us

profile of v19, /device:TPU:0, one launch (start us, length us, event | category | flops | bytes accessed | tf_op | source)
XLA Modules:
  0.0 61.7 jit_solution(10024942438042696278)
XLA Ops:
  1.3 0.0 copy-start.1
  1.3 0.0 copy-start.2
  1.3 0.0 copy-start.3
  1.3 0.8 %shard_map.149 = (bf16[8,8,128]{2,1,0:T(8,128)(2,1)S(1)}, s32[8,128]{1,0:T(8,128)S(1)}) custom-call(s32[1]{0:T(128)S(6)} %copy.16.length_ref, bf16[1,8,128]{2,1,0:T(8,128)(2,1)} %source_hbm.1), custom_call_target="tpu_custom_call" | custom-call | flops 10000000000 | bytes 1048576 | tf_op jit(solution)/shard_map/pallas_call | solution.py:134
  2.2 13.7 %all_to_all.25.arrived_ref = bf16[8,8,128]{2,1,0:T(8,128)(2,1)S(1)} all-to-all(bf16[8,8,128]{2,1,0:T(8,128)(2,1)S(1)} %get-tuple-element.9), channel_id=1, replica_groups=mesh['ctx'=8,'head'=4] {'ctx'}, dimensions={0} | all-to-all | bytes 32768 | tf_op jit(solution)/shard_map/all_to_all | solution.py:355
  15.8 0.0 copy-done.3
  15.9 0.0 copy-done.4
  15.9 0.0 copy-done.7
  15.9 0.0 copy-done.8
  15.9 1.2 %shard_map.150 = bf16[8,3,4,128]{3,2,1,0:T(4,128)(2,1)S(1)} custom-call(s32[8,128]{1,0:T(8,128)S(1)} %get-tuple-element.8.length_ref, bf16[8,8,128]{2,1,0:T(8,128)(2,1)S(1)} %all_to_all.25.arrived_ref, bf16[1,4,128]{2,1,0:T(4,128)(2,1)S(1)} %copy-done.7, bf16[1,4,128]{2,1,0:T(4,128)(2,1)S(1)} %copy-done.8, bf16[1024,128]{1,0:T(8,128)(2,1)S(1)} %bitcast.19, ...), custom_call_target="tpu_custom_call" | custom-call | flops 10000000000 | bytes 1048576 | tf_op jit(solution)/shard_map/pallas_call | solution.py:206
  17.1 9.0 %all_to_all.26.part_ref = bf16[8,3,4,128]{3,2,1,0:T(4,128)(2,1)S(1)} all-to-all(bf16[8,3,4,128]{3,2,1,0:T(4,128)(2,1)S(1)} %shard_map.150), channel_id=1, replica_groups=mesh['ctx'=8,'head'=4] {'ctx'}, dimensions={0} | all-to-all | bytes 49152 | tf_op jit(solution)/shard_map/all_to_all | solution.py:355
  26.1 0.0 slice-start.4
  26.1 0.2 shard_map.151.copies_ref
  26.3 9.4 %all_to_all.27.rows_ref = bf16[32,8,128]{2,1,0:T(8,128)(2,1)S(1)} all-to-all(bf16[32,8,128]{2,1,0:T(8,128)(2,1)S(1)} %shard_map.151.copies_ref), channel_id=1, replica_groups={{0,1,2,3,4,5,6,7,16,17,18,19,20,21,22,23,24,25,26,27,28,29,30,31,8,9,10..., dimensions={0} | all-to-all | bytes 131072 | tf_op jit(solution)/shard_map/all_to_all | solution.py:355
  35.7 0.0 copy-done.6
  35.7 0.0 slice-start.5
  35.7 0.0 copy-start.5
  35.7 0.6 %shard_map.152 = (bf16[8,168]{1,0:T(8,128)(2,1)S(1)}, bf16[32,3,4,128]{3,2,1,0:T(4,128)(2,1)S(1)}) custom-call(bf16[32,8,128]{2,1,0:T(8,128)(2,1)S(1)} %all_to_all.27.rows_ref, bf16[168,4096]{1,0:T(8,128)(2,1)S(1)} %bitcast.16, bf16[8,168]{1,0:T(8,128)(2,1)S(1)} %copy-done.6), custom_call_target="tpu_custom_call" | custom-call | flops 10000000000 | bytes 1048576 | tf_op jit(solution)/shard_map/pallas_call | solution.py:257
  36.4 9.8 %all_to_all.28.pieces_ref = bf16[32,3,4,128]{3,2,1,0:T(4,128)(2,1)S(1)} all-to-all(bf16[32,3,4,128]{3,2,1,0:T(4,128)(2,1)S(1)} %get-tuple-element.10), channel_id=1, replica_groups={{0,1,2,3,4,5,6,7,16,17,18,19,20,21,22,23,24,25,26,27,28,29,30,31,8,9,10..., dimensions={0} | all-to-all | bytes 196608 | tf_op jit(solution)/shard_map/all_to_all | solution.py:355
  46.2 0.0 slice-done
  46.2 0.0 slice-done.4
  46.3 5.0 %shard_map.153 = (bf16[32,3,4,128]{3,2,1,0:T(4,128)(2,1)S(1)}, bf16[8,128]{1,0:T(8,128)(2,1)}) custom-call(bf16[32,3,4,128]{3,2,1,0:T(4,128)(2,1)S(1)} %all_to_all.28.pieces_ref, f32[5376]{0:T(1024)S(1)} %copy-done.5, bf16[32,8,128]{2,1,0:T(8,128)(2,1)S(1)} %shard_map.151.copies_ref, bf16[672,5376]{1,0:T(8,128)(2,1)S(1)} %bitcast.10, ...), custom_call_target="tpu_custom_call" | custom-call | flops 10000000000 | bytes 1048576 | tf_op jit(solution)/shard_map/pallas_call | solution.py:311
  51.3 9.6 %all_to_all.29.shares_ref = bf16[32,3,4,128]{3,2,1,0:T(4,128)(2,1)S(1)} all-to-all(bf16[32,3,4,128]{3,2,1,0:T(4,128)(2,1)S(1)} %get-tuple-element.12), channel_id=1, replica_groups={{0,1,2,3,4,5,6,7,16,17,18,19,20,21,22,23,24,25,26,27,28,29,30,31,8,9,10..., dimensions={0} | all-to-all | bytes 196608 | tf_op jit(solution)/shard_map/all_to_all | solution.py:355
  60.9 0.8 %shard_map.154 = bf16[8,168]{1,0:T(8,128)(2,1)} custom-call(bf16[32,3,4,128]{3,2,1,0:T(4,128)(2,1)S(1)} %all_to_all.29.shares_ref, bf16[8,168]{1,0:T(8,128)(2,1)S(1)} %get-tuple-element.13.hidden_ref), custom_call_target="tpu_custom_call" | custom-call | tf_op jit(solution)/shard_map/pallas_call | solution.py:339
  (20 shorter events, 0.0 us)
Async XLA Ops:
  1.3 14.6 %copy-start.1 = (bf16[1024,4,128]{2,1,0:T(4,128)(2,1)S(1)}, bf16[1024,4,128]{2,1,0:T(4,128)(2,1)}, u32[]{:S(2)}) copy-start(bf16[1024,4,128]{2,1,0:T(4,128)(2,1)} %param.20) | copy-start | bytes 3145732
  1.3 14.6 %copy-start.2 = (bf16[1024,4,128]{2,1,0:T(4,128)(2,1)S(1)}, bf16[1024,4,128]{2,1,0:T(4,128)(2,1)}, u32[]{:S(2)}) copy-start(bf16[1024,4,128]{2,1,0:T(4,128)(2,1)} %param.21) | copy-start | bytes 3145732
  1.3 14.6 %copy-start.3 = (bf16[1,256,4,128]{3,2,1,0:T(4,128)(2,1)S(1)}, bf16[1,256,4,128]{3,2,1,0:T(4,128)(2,1)}, u32[]{:S(2)}) copy-start(bf16[1,256,4,128]{3,2,1,0:T(4,128)(2,1)} %param.17) | copy-start | bytes 786436
  1.3 14.5 %copy-start.4 = (bf16[1,256,4,128]{3,2,1,0:T(4,128)(2,1)S(1)}, bf16[1,256,4,128]{3,2,1,0:T(4,128)(2,1)}, u32[]{:S(2)}) copy-start(bf16[1,256,4,128]{3,2,1,0:T(4,128)(2,1)} %param.18) | copy-start | bytes 786436
  1.3 14.5 %copy-start.7 = (bf16[1,4,128]{2,1,0:T(4,128)(2,1)S(1)}, bf16[1,4,128]{2,1,0:T(4,128)(2,1)}, u32[]{:S(2)}) copy-start(bf16[1,4,128]{2,1,0:T(4,128)(2,1)} %kn_ref.1) | copy-start | bytes 3076
  1.3 14.5 %copy-start.8 = (bf16[1,4,128]{2,1,0:T(4,128)(2,1)S(1)}, bf16[1,4,128]{2,1,0:T(4,128)(2,1)}, u32[]{:S(2)}) copy-start(bf16[1,4,128]{2,1,0:T(4,128)(2,1)} %vn_ref.1) | copy-start | bytes 3076
  26.0 9.6 %copy-start = (bf16[4096,168]{0,1:T(8,128)(2,1)S(1)}, bf16[4096,168]{0,1:T(8,128)(2,1)}, u32[]{:S(2)}) copy-start(bf16[4096,168]{0,1:T(8,128)(2,1)} %param.22) | copy-start | bytes 4128772
  26.0 9.6 %copy-start.6 = (bf16[8,168]{1,0:T(8,128)(2,1)S(1)}, bf16[8,168]{1,0:T(8,128)(2,1)}, u32[]{:S(2)}) copy-start(bf16[8,168]{1,0:T(8,128)(2,1)} %residual_ref.1) | copy-start | bytes 8068
  26.1 20.1 %slice-start = ((s8[7225344]{0:T(1024)(128)(4,1)}), s8[4194304]{0:T(1024)(128)(4,1)S(1)}, s32[]{:S(2)}) async-start(s8[7225344]{0:T(1024)(128)(4,1)} %bitcast.8), calls=%async_computation.5 | async-start | bytes 8388608
  26.1 20.2 %slice-start.2 = ((s8[7225344]{0:T(1024)(128)(4,1)}), s8[4194304]{0:T(1024)(128)(4,1)S(1)}, s32[]{:S(2)}) async-start(s8[7225344]{0:T(1024)(128)(4,1)} %bitcast.11), calls=%async_computation.7 | async-start | bytes 8388608
  26.1 20.1 %slice-start.4 = ((s8[7225344]{0:T(1024)(128)(4,1)}), s8[4194304]{0:T(1024)(128)(4,1)S(1)}, s32[]{:S(2)}) async-start(s8[7225344]{0:T(1024)(128)(4,1)} %bitcast.14), calls=%async_computation.9 | async-start | bytes 8388608
  35.7 10.5 %slice-start.1 = ((s8[7225344]{0:T(1024)(128)(4,1)}), s8[3031040]{0:T(1024)(128)(4,1)S(1)}, s32[]{:S(2)}) async-start(s8[7225344]{0:T(1024)(128)(4,1)} %bitcast.8), calls=%async_computation.6 | async-start | bytes 6062080
  35.7 10.5 %slice-start.3 = ((s8[7225344]{0:T(1024)(128)(4,1)}), s8[3031040]{0:T(1024)(128)(4,1)S(1)}, s32[]{:S(2)}) async-start(s8[7225344]{0:T(1024)(128)(4,1)} %bitcast.11), calls=%async_computation.8 | async-start | bytes 6062080
  35.7 10.5 %slice-start.5 = ((s8[7225344]{0:T(1024)(128)(4,1)}), s8[3031040]{0:T(1024)(128)(4,1)S(1)}, s32[]{:S(2)}) async-start(s8[7225344]{0:T(1024)(128)(4,1)} %bitcast.14), calls=%async_computation.10 | async-start | bytes 6062080
  35.7 10.5 %copy-start.5 = (f32[5376]{0:T(1024)S(1)}, f32[5376]{0:T(1024)}, u32[]{:S(2)}) copy-start(f32[5376]{0:T(1024)} %gain_ref.1) | copy-start | bytes 64516

commit v20 on v19

--- a/solution.py
+++ b/solution.py
@@ -14,6 +14,7 @@
 COST = pl.CostEstimate(flops=10**10, bytes_accessed=MIB, transcendentals=10**6)
 TERMS = 3
 CHUNKS = 3
+PARTS = 7
 BLOCK_ROWS = 1024
 LANES = 128
 HALF = LANES // 2
@@ -286,7 +287,10 @@
     units = gate_ref.shape[0]
     count = CHUNKS if units % (16 * CHUNKS) == 0 else 1
     size = units // count
-    share = jnp.zeros((normed.shape[0], down_ref.shape[1]), jnp.float32)
+    features = down_ref.shape[1]
+    parts = PARTS if features % (LANES * PARTS) == 0 else 1
+    cuts = [slice(part * (features // parts), (part + 1) * (features // parts)) for part in range(parts)]
+    shares = [0.0] * parts
     ready = None
     for chunk in range(count + 1):
         if chunk < count:
@@ -295,10 +299,14 @@
             up_values = dot_rows(normed, up_ref[rows])
         if ready is not None:
             activated, held = ready
-            share += jnp.dot(activated, down_ref[held], preferred_element_type=jnp.float32)
+            for part, cut in enumerate(cuts):
+                shares[part] += jnp.dot(
+                    activated, down_ref[held, cut], preferred_element_type=jnp.float32
+                )
         if chunk < count:
             activated = jax.nn.gelu(gate_values.T, approximate=True) * up_values
             ready = activated.astype(jnp.bfloat16), rows
+    share = jnp.concatenate(shares, axis=1)
     if pieces_ref.ndim == 4:
         put_columns(out_ref, order, share, columns)
     else:

time: 61.9 us -> 61.9 us (level)
  no operation moved by 1% of the time
where the time goes in v20:
time: 61.9 us; the launch traced here: 61.7 us
  blocking collectives  51.5 us (83%)
  Pallas kernels  8.64 us (14%)
  between operations  1.48 us (2%)
    all_to_all x5, blocking collectives, exchange(): lax.all_to_all(copies, axes, split_axis=0, concat_axis=0, tiled=True, axi...  51.5 us
    pallas_call x1, Pallas kernels, forward(): pl.pallas_call(functools.partial(forward_kernel, order), out_shape=(jax.S...  5.05 us

profile of v20, /device:TPU:0, one launch (start us, length us, event | category | flops | bytes accessed | tf_op | source)
XLA Modules:
  0.0 61.7 jit_solution(2682676702090632275)
XLA Ops:
  1.3 0.0 copy-start.1
  1.3 0.0 copy-start.2
  1.3 0.0 copy-start.3
  1.3 0.8 %shard_map.149 = (bf16[8,8,128]{2,1,0:T(8,128)(2,1)S(1)}, s32[8,128]{1,0:T(8,128)S(1)}) custom-call(s32[1]{0:T(128)S(6)} %copy.16.length_ref, bf16[1,8,128]{2,1,0:T(8,128)(2,1)} %source_hbm.1), custom_call_target="tpu_custom_call" | custom-call | flops 10000000000 | bytes 1048576 | tf_op jit(solution)/shard_map/pallas_call | solution.py:135
  2.2 13.7 %all_to_all.25.arrived_ref = bf16[8,8,128]{2,1,0:T(8,128)(2,1)S(1)} all-to-all(bf16[8,8,128]{2,1,0:T(8,128)(2,1)S(1)} %get-tuple-element.9), channel_id=1, replica_groups=mesh['ctx'=8,'head'=4] {'ctx'}, dimensions={0} | all-to-all | bytes 32768 | tf_op jit(solution)/shard_map/all_to_all | solution.py:363
  15.8 0.0 copy-done.3
  15.9 0.0 copy-done.4
  15.9 0.0 copy-done.7
  15.9 0.0 copy-done.8
  15.9 1.2 %shard_map.150 = bf16[8,3,4,128]{3,2,1,0:T(4,128)(2,1)S(1)} custom-call(s32[8,128]{1,0:T(8,128)S(1)} %get-tuple-element.8.length_ref, bf16[8,8,128]{2,1,0:T(8,128)(2,1)S(1)} %all_to_all.25.arrived_ref, bf16[1,4,128]{2,1,0:T(4,128)(2,1)S(1)} %copy-done.7, bf16[1,4,128]{2,1,0:T(4,128)(2,1)S(1)} %copy-done.8, bf16[1024,128]{1,0:T(8,128)(2,1)S(1)} %bitcast.19, ...), custom_call_target="tpu_custom_call" | custom-call | flops 10000000000 | bytes 1048576 | tf_op jit(solution)/shard_map/pallas_call | solution.py:207
  17.1 9.0 %all_to_all.26.part_ref = bf16[8,3,4,128]{3,2,1,0:T(4,128)(2,1)S(1)} all-to-all(bf16[8,3,4,128]{3,2,1,0:T(4,128)(2,1)S(1)} %shard_map.150), channel_id=1, replica_groups=mesh['ctx'=8,'head'=4] {'ctx'}, dimensions={0} | all-to-all | bytes 49152 | tf_op jit(solution)/shard_map/all_to_all | solution.py:363
  26.1 0.0 slice-start.4
  26.1 0.2 shard_map.151.copies_ref
  26.3 9.4 %all_to_all.27.rows_ref = bf16[32,8,128]{2,1,0:T(8,128)(2,1)S(1)} all-to-all(bf16[32,8,128]{2,1,0:T(8,128)(2,1)S(1)} %shard_map.151.copies_ref), channel_id=1, replica_groups={{0,1,2,3,4,5,6,7,16,17,18,19,20,21,22,23,24,25,26,27,28,29,30,31,8,9,10..., dimensions={0} | all-to-all | bytes 131072 | tf_op jit(solution)/shard_map/all_to_all | solution.py:363
  35.7 0.0 copy-done.6
  35.7 0.0 slice-start.5
  35.7 0.0 copy-start.5
  35.7 0.6 %shard_map.152 = (bf16[8,168]{1,0:T(8,128)(2,1)S(1)}, bf16[32,3,4,128]{3,2,1,0:T(4,128)(2,1)S(1)}) custom-call(bf16[32,8,128]{2,1,0:T(8,128)(2,1)S(1)} %all_to_all.27.rows_ref, bf16[168,4096]{1,0:T(8,128)(2,1)S(1)} %bitcast.16, bf16[8,168]{1,0:T(8,128)(2,1)S(1)} %copy-done.6), custom_call_target="tpu_custom_call" | custom-call | flops 10000000000 | bytes 1048576 | tf_op jit(solution)/shard_map/pallas_call | solution.py:258
  36.4 9.8 %all_to_all.28.pieces_ref = bf16[32,3,4,128]{3,2,1,0:T(4,128)(2,1)S(1)} all-to-all(bf16[32,3,4,128]{3,2,1,0:T(4,128)(2,1)S(1)} %get-tuple-element.10), channel_id=1, replica_groups={{0,1,2,3,4,5,6,7,16,17,18,19,20,21,22,23,24,25,26,27,28,29,30,31,8,9,10..., dimensions={0} | all-to-all | bytes 196608 | tf_op jit(solution)/shard_map/all_to_all | solution.py:363
  46.2 0.0 slice-done
  46.2 0.0 slice-done.4
  46.3 5.0 %shard_map.153 = (bf16[32,3,4,128]{3,2,1,0:T(4,128)(2,1)S(1)}, bf16[8,128]{1,0:T(8,128)(2,1)}) custom-call(bf16[32,3,4,128]{3,2,1,0:T(4,128)(2,1)S(1)} %all_to_all.28.pieces_ref, f32[5376]{0:T(1024)S(1)} %copy-done.5, bf16[32,8,128]{2,1,0:T(8,128)(2,1)S(1)} %shard_map.151.copies_ref, bf16[672,5376]{1,0:T(8,128)(2,1)S(1)} %bitcast.10, ...), custom_call_target="tpu_custom_call" | custom-call | flops 10000000000 | bytes 1048576 | tf_op jit(solution)/shard_map/pallas_call | solution.py:319
  51.3 9.6 %all_to_all.29.shares_ref = bf16[32,3,4,128]{3,2,1,0:T(4,128)(2,1)S(1)} all-to-all(bf16[32,3,4,128]{3,2,1,0:T(4,128)(2,1)S(1)} %get-tuple-element.12), channel_id=1, replica_groups={{0,1,2,3,4,5,6,7,16,17,18,19,20,21,22,23,24,25,26,27,28,29,30,31,8,9,10..., dimensions={0} | all-to-all | bytes 196608 | tf_op jit(solution)/shard_map/all_to_all | solution.py:363
  60.9 0.8 %shard_map.154 = bf16[8,168]{1,0:T(8,128)(2,1)} custom-call(bf16[32,3,4,128]{3,2,1,0:T(4,128)(2,1)S(1)} %all_to_all.29.shares_ref, bf16[8,168]{1,0:T(8,128)(2,1)S(1)} %get-tuple-element.13.hidden_ref), custom_call_target="tpu_custom_call" | custom-call | tf_op jit(solution)/shard_map/pallas_call | solution.py:347
  (20 shorter events, 0.0 us)
Async XLA Ops:
  1.3 14.6 %copy-start.1 = (bf16[1024,4,128]{2,1,0:T(4,128)(2,1)S(1)}, bf16[1024,4,128]{2,1,0:T(4,128)(2,1)}, u32[]{:S(2)}) copy-start(bf16[1024,4,128]{2,1,0:T(4,128)(2,1)} %param.20) | copy-start | bytes 3145732
  1.3 14.6 %copy-start.2 = (bf16[1024,4,128]{2,1,0:T(4,128)(2,1)S(1)}, bf16[1024,4,128]{2,1,0:T(4,128)(2,1)}, u32[]{:S(2)}) copy-start(bf16[1024,4,128]{2,1,0:T(4,128)(2,1)} %param.21) | copy-start | bytes 3145732
  1.3 14.6 %copy-start.3 = (bf16[1,256,4,128]{3,2,1,0:T(4,128)(2,1)S(1)}, bf16[1,256,4,128]{3,2,1,0:T(4,128)(2,1)}, u32[]{:S(2)}) copy-start(bf16[1,256,4,128]{3,2,1,0:T(4,128)(2,1)} %param.17) | copy-start | bytes 786436
  1.3 14.5 %copy-start.4 = (bf16[1,256,4,128]{3,2,1,0:T(4,128)(2,1)S(1)}, bf16[1,256,4,128]{3,2,1,0:T(4,128)(2,1)}, u32[]{:S(2)}) copy-start(bf16[1,256,4,128]{3,2,1,0:T(4,128)(2,1)} %param.18) | copy-start | bytes 786436
  1.3 14.5 %copy-start.7 = (bf16[1,4,128]{2,1,0:T(4,128)(2,1)S(1)}, bf16[1,4,128]{2,1,0:T(4,128)(2,1)}, u32[]{:S(2)}) copy-start(bf16[1,4,128]{2,1,0:T(4,128)(2,1)} %kn_ref.1) | copy-start | bytes 3076
  1.3 14.5 %copy-start.8 = (bf16[1,4,128]{2,1,0:T(4,128)(2,1)S(1)}, bf16[1,4,128]{2,1,0:T(4,128)(2,1)}, u32[]{:S(2)}) copy-start(bf16[1,4,128]{2,1,0:T(4,128)(2,1)} %vn_ref.1) | copy-start | bytes 3076
  26.0 9.6 %copy-start = (bf16[4096,168]{0,1:T(8,128)(2,1)S(1)}, bf16[4096,168]{0,1:T(8,128)(2,1)}, u32[]{:S(2)}) copy-start(bf16[4096,168]{0,1:T(8,128)(2,1)} %param.22) | copy-start | bytes 4128772
  26.0 9.6 %copy-start.6 = (bf16[8,168]{1,0:T(8,128)(2,1)S(1)}, bf16[8,168]{1,0:T(8,128)(2,1)}, u32[]{:S(2)}) copy-start(bf16[8,168]{1,0:T(8,128)(2,1)} %residual_ref.1) | copy-start | bytes 8068
  26.1 20.1 %slice-start = ((s8[7225344]{0:T(1024)(128)(4,1)}), s8[4194304]{0:T(1024)(128)(4,1)S(1)}, s32[]{:S(2)}) async-start(s8[7225344]{0:T(1024)(128)(4,1)} %bitcast.8), calls=%async_computation.5 | async-start | bytes 8388608
  26.1 20.2 %slice-start.2 = ((s8[7225344]{0:T(1024)(128)(4,1)}), s8[4194304]{0:T(1024)(128)(4,1)S(1)}, s32[]{:S(2)}) async-start(s8[7225344]{0:T(1024)(128)(4,1)} %bitcast.11), calls=%async_computation.7 | async-start | bytes 8388608
  26.1 20.1 %slice-start.4 = ((s8[7225344]{0:T(1024)(128)(4,1)}), s8[4194304]{0:T(1024)(128)(4,1)S(1)}, s32[]{:S(2)}) async-start(s8[7225344]{0:T(1024)(128)(4,1)} %bitcast.14), calls=%async_computation.9 | async-start | bytes 8388608
  35.7 10.5 %slice-start.1 = ((s8[7225344]{0:T(1024)(128)(4,1)}), s8[3031040]{0:T(1024)(128)(4,1)S(1)}, s32[]{:S(2)}) async-start(s8[7225344]{0:T(1024)(128)(4,1)} %bitcast.8), calls=%async_computation.6 | async-start | bytes 6062080
  35.7 10.5 %slice-start.3 = ((s8[7225344]{0:T(1024)(128)(4,1)}), s8[3031040]{0:T(1024)(128)(4,1)S(1)}, s32[]{:S(2)}) async-start(s8[7225344]{0:T(1024)(128)(4,1)} %bitcast.11), calls=%async_computation.8 | async-start | bytes 6062080
  35.7 10.5 %slice-start.5 = ((s8[7225344]{0:T(1024)(128)(4,1)}), s8[3031040]{0:T(1024)(128)(4,1)S(1)}, s32[]{:S(2)}) async-start(s8[7225344]{0:T(1024)(128)(4,1)} %bitcast.14), calls=%async_computation.10 | async-start | bytes 6062080
  35.7 10.5 %copy-start.5 = (f32[5376]{0:T(1024)S(1)}, f32[5376]{0:T(1024)}, u32[]{:S(2)}) copy-start(f32[5376]{0:T(1024)} %gain_ref.1) | copy-start | bytes 64516

commit v21 on v19

--- a/solution.py
+++ b/solution.py
@@ -14,6 +14,7 @@
 COST = pl.CostEstimate(flops=10**10, bytes_accessed=MIB, transcendentals=10**6)
 TERMS = 3
 CHUNKS = 3
+QUARTERS = 4
 BLOCK_ROWS = 1024
 LANES = 128
 HALF = LANES // 2
@@ -169,7 +170,7 @@
     cached_scores = cached_scores + bias
     new_scores = SCORE_SCALE * dot_rows(queries, kn_ref[0])
     new_scores = new_scores + head_bias(rows, LANES, heads, kv_heads)[:, :kv_heads] + own[:, :kv_heads]
-    blocks.append((cached_scores, vs_ref[...], new_scores, vn_ref[0]))
+    blocks.insert(0, (cached_scores, vs_ref[...], new_scores, vn_ref[0]))
     parts = []
     for block_scores, values, more_scores, more_values in blocks:
         block_max = jnp.max(block_scores, axis=1, keepdims=True)
@@ -241,9 +242,15 @@
     all_heads = devices * heads // completions
     for place, device in enumerate(order):
         wide_ref[device * heads : (device + 1) * heads] = rows_ref[place].astype(jnp.float32)
-    rows = [wide_ref[pl.ds(head, completions, stride=all_heads), :] for head in range(all_heads)]
-    rows = jnp.concatenate([row.astype(jnp.bfloat16) for row in rows], axis=1)
-    projected = dot_rows(rows, w_ref[...])
+    quarter = all_heads // QUARTERS
+    projected = 0.0
+    for first in range(0, all_heads, quarter):
+        rows = [
+            wide_ref[pl.ds(head, completions, stride=all_heads), :].astype(jnp.bfloat16)
+            for head in range(first, first + quarter)
+        ]
+        cut = slice(first * width, (first + quarter) * width)
+        projected += dot_rows(jnp.concatenate(rows, axis=1), w_ref[:, cut])
     hidden = (residual_ref[...].astype(jnp.float32) + projected).astype(jnp.bfloat16)
     out_ref[...] = hidden
     if copies_ref.ndim == 4:
@@ -291,8 +298,8 @@
     for chunk in range(count + 1):
         if chunk < count:
             rows = slice(chunk * size, (chunk + 1) * size)
+            up_values = dot_rows(normed, up_ref[rows])
             gate_values = dot_rows(gate_ref[rows], normed)
-            up_values = dot_rows(normed, up_ref[rows])
         if ready is not None:
             activated, held = ready
             share += jnp.dot(activated, down_ref[held], preferred_element_type=jnp.float32)

time: 61.9 us -> 62.5 us (level)
  no operation moved by 1% of the time
where the time goes in v21:
time: 62.5 us; the launch traced here: 62.2 us
  blocking collectives  51.5 us (82%)
  Pallas kernels  9.2 us (15%)
  between operations  1.48 us (2%)
    all_to_all x5, blocking collectives, exchange(): lax.all_to_all(copies, axes, split_axis=0, concat_axis=0, tiled=True, axi...  51.5 us
    pallas_call x1, Pallas kernels, forward(): pl.pallas_call(functools.partial(forward_kernel, order), out_shape=(jax.S...  5.5 us
    pallas_call x1, Pallas kernels, attend(): pl.pallas_call(attention_kernel, out_shape=jax.ShapeDtypeStruct((count, *...  1.28 us

profile of v21, /device:TPU:0, one launch (start us, length us, event | category | flops | bytes accessed | tf_op | source)
XLA Modules:
  0.0 62.2 jit_solution(18187596588513989852)
XLA Ops:
  1.3 0.0 copy-start.1
  1.3 0.0 copy-start.2
  1.3 0.0 copy-start.3
  1.3 0.0 copy-start.4
  1.3 0.0 copy-start.7
  1.3 0.8 %shard_map.149 = (bf16[8,8,128]{2,1,0:T(8,128)(2,1)S(1)}, s32[8,128]{1,0:T(8,128)S(1)}) custom-call(s32[1]{0:T(128)S(6)} %copy.16.length_ref, bf16[1,8,128]{2,1,0:T(8,128)(2,1)} %source_hbm.1), custom_call_target="tpu_custom_call" | custom-call | flops 10000000000 | bytes 1048576 | tf_op jit(solution)/shard_map/pallas_call | solution.py:135
  2.2 13.7 %all_to_all.25.arrived_ref = bf16[8,8,128]{2,1,0:T(8,128)(2,1)S(1)} all-to-all(bf16[8,8,128]{2,1,0:T(8,128)(2,1)S(1)} %get-tuple-element.9), channel_id=1, replica_groups=mesh['ctx'=8,'head'=4] {'ctx'}, dimensions={0} | all-to-all | bytes 32768 | tf_op jit(solution)/shard_map/all_to_all | solution.py:362
  15.8 0.0 copy-done.3
  15.9 0.0 copy-done.4
  15.9 0.0 copy-done.7
  15.9 0.0 copy-done.8
  15.9 1.3 %shard_map.150 = bf16[8,3,4,128]{3,2,1,0:T(4,128)(2,1)S(1)} custom-call(s32[8,128]{1,0:T(8,128)S(1)} %get-tuple-element.8.length_ref, bf16[8,8,128]{2,1,0:T(8,128)(2,1)S(1)} %all_to_all.25.arrived_ref, bf16[1,4,128]{2,1,0:T(4,128)(2,1)S(1)} %copy-done.7, bf16[1,4,128]{2,1,0:T(4,128)(2,1)S(1)} %copy-done.8, bf16[1024,128]{1,0:T(8,128)(2,1)S(1)} %bitcast.19, ...), custom_call_target="tpu_custom_call" | custom-call | flops 10000000000 | bytes 1048576 | tf_op jit(solution)/shard_map/pallas_call | solution.py:207
  17.2 9.0 %all_to_all.26.part_ref = bf16[8,3,4,128]{3,2,1,0:T(4,128)(2,1)S(1)} all-to-all(bf16[8,3,4,128]{3,2,1,0:T(4,128)(2,1)S(1)} %shard_map.150), channel_id=1, replica_groups=mesh['ctx'=8,'head'=4] {'ctx'}, dimensions={0} | all-to-all | bytes 49152 | tf_op jit(solution)/shard_map/all_to_all | solution.py:362
  26.2 0.0 slice-start.4
  26.2 0.2 shard_map.151.copies_ref
  26.4 9.4 %all_to_all.27.rows_ref = bf16[32,8,128]{2,1,0:T(8,128)(2,1)S(1)} all-to-all(bf16[32,8,128]{2,1,0:T(8,128)(2,1)S(1)} %shard_map.151.copies_ref), channel_id=1, replica_groups={{0,1,2,3,4,5,6,7,16,17,18,19,20,21,22,23,24,25,26,27,28,29,30,31,8,9,10..., dimensions={0} | all-to-all | bytes 131072 | tf_op jit(solution)/shard_map/all_to_all | solution.py:362
  35.8 0.0 copy-done
  35.8 0.0 slice-start.5
  35.8 0.0 copy-start.5
  35.8 0.6 %shard_map.152 = (bf16[8,168]{1,0:T(8,128)(2,1)S(1)}, bf16[32,3,4,128]{3,2,1,0:T(4,128)(2,1)S(1)}) custom-call(bf16[32,8,128]{2,1,0:T(8,128)(2,1)S(1)} %all_to_all.27.rows_ref, bf16[168,4096]{1,0:T(8,128)(2,1)S(1)} %bitcast.16, bf16[8,168]{1,0:T(8,128)(2,1)S(1)} %copy-done.6), custom_call_target="tpu_custom_call" | custom-call | flops 10000000000 | bytes 1048576 | tf_op jit(solution)/shard_map/pallas_call | solution.py:264
  36.5 9.8 %all_to_all.28.pieces_ref = bf16[32,3,4,128]{3,2,1,0:T(4,128)(2,1)S(1)} all-to-all(bf16[32,3,4,128]{3,2,1,0:T(4,128)(2,1)S(1)} %get-tuple-element.10), channel_id=1, replica_groups={{0,1,2,3,4,5,6,7,16,17,18,19,20,21,22,23,24,25,26,27,28,29,30,31,8,9,10..., dimensions={0} | all-to-all | bytes 196608 | tf_op jit(solution)/shard_map/all_to_all | solution.py:362
  46.4 5.5 %shard_map.153 = (bf16[32,3,4,128]{3,2,1,0:T(4,128)(2,1)S(1)}, bf16[8,128]{1,0:T(8,128)(2,1)}) custom-call(bf16[32,3,4,128]{3,2,1,0:T(4,128)(2,1)S(1)} %all_to_all.28.pieces_ref, f32[5376]{0:T(1024)S(1)} %copy-done.5, bf16[32,8,128]{2,1,0:T(8,128)(2,1)S(1)} %shard_map.151.copies_ref, bf16[672,5376]{1,0:T(8,128)(2,1)S(1)} %bitcast.10, ...), custom_call_target="tpu_custom_call" | custom-call | flops 10000000000 | bytes 1048576 | tf_op jit(solution)/shard_map/pallas_call | solution.py:318
  51.9 9.6 %all_to_all.29.shares_ref = bf16[32,3,4,128]{3,2,1,0:T(4,128)(2,1)S(1)} all-to-all(bf16[32,3,4,128]{3,2,1,0:T(4,128)(2,1)S(1)} %get-tuple-element.12), channel_id=1, replica_groups={{0,1,2,3,4,5,6,7,16,17,18,19,20,21,22,23,24,25,26,27,28,29,30,31,8,9,10..., dimensions={0} | all-to-all | bytes 196608 | tf_op jit(solution)/shard_map/all_to_all | solution.py:362
  61.5 0.8 %shard_map.154 = bf16[8,168]{1,0:T(8,128)(2,1)} custom-call(bf16[32,3,4,128]{3,2,1,0:T(4,128)(2,1)S(1)} %all_to_all.29.shares_ref, bf16[8,168]{1,0:T(8,128)(2,1)S(1)} %get-tuple-element.13.hidden_ref), custom_call_target="tpu_custom_call" | custom-call | tf_op jit(solution)/shard_map/pallas_call | solution.py:346
  (20 shorter events, 0.0 us)
Async XLA Ops:
  1.3 14.6 %copy-start.1 = (bf16[1024,4,128]{2,1,0:T(4,128)(2,1)S(1)}, bf16[1024,4,128]{2,1,0:T(4,128)(2,1)}, u32[]{:S(2)}) copy-start(bf16[1024,4,128]{2,1,0:T(4,128)(2,1)} %param.20) | copy-start | bytes 3145732
  1.3 14.6 %copy-start.2 = (bf16[1024,4,128]{2,1,0:T(4,128)(2,1)S(1)}, bf16[1024,4,128]{2,1,0:T(4,128)(2,1)}, u32[]{:S(2)}) copy-start(bf16[1024,4,128]{2,1,0:T(4,128)(2,1)} %param.21) | copy-start | bytes 3145732
  1.3 14.6 %copy-start.3 = (bf16[1,256,4,128]{3,2,1,0:T(4,128)(2,1)S(1)}, bf16[1,256,4,128]{3,2,1,0:T(4,128)(2,1)}, u32[]{:S(2)}) copy-start(bf16[1,256,4,128]{3,2,1,0:T(4,128)(2,1)} %param.17) | copy-start | bytes 786436
  1.3 14.5 %copy-start.4 = (bf16[1,256,4,128]{3,2,1,0:T(4,128)(2,1)S(1)}, bf16[1,256,4,128]{3,2,1,0:T(4,128)(2,1)}, u32[]{:S(2)}) copy-start(bf16[1,256,4,128]{3,2,1,0:T(4,128)(2,1)} %param.18) | copy-start | bytes 786436
  1.3 14.5 %copy-start.7 = (bf16[1,4,128]{2,1,0:T(4,128)(2,1)S(1)}, bf16[1,4,128]{2,1,0:T(4,128)(2,1)}, u32[]{:S(2)}) copy-start(bf16[1,4,128]{2,1,0:T(4,128)(2,1)} %kn_ref.1) | copy-start | bytes 3076
  1.3 14.5 %copy-start.8 = (bf16[1,4,128]{2,1,0:T(4,128)(2,1)S(1)}, bf16[1,4,128]{2,1,0:T(4,128)(2,1)}, u32[]{:S(2)}) copy-start(bf16[1,4,128]{2,1,0:T(4,128)(2,1)} %vn_ref.1) | copy-start | bytes 3076
  26.2 9.6 %copy-start = (bf16[4096,168]{0,1:T(8,128)(2,1)S(1)}, bf16[4096,168]{0,1:T(8,128)(2,1)}, u32[]{:S(2)}) copy-start(bf16[4096,168]{0,1:T(8,128)(2,1)} %param.22) | copy-start | bytes 4128772
  26.2 9.6 %copy-start.6 = (bf16[8,168]{1,0:T(8,128)(2,1)S(1)}, bf16[8,168]{1,0:T(8,128)(2,1)}, u32[]{:S(2)}) copy-start(bf16[8,168]{1,0:T(8,128)(2,1)} %residual_ref.1) | copy-start | bytes 8068
  26.2 20.2 %slice-start = ((s8[7225344]{0:T(1024)(128)(4,1)}), s8[4194304]{0:T(1024)(128)(4,1)S(1)}, s32[]{:S(2)}) async-start(s8[7225344]{0:T(1024)(128)(4,1)} %bitcast.8), calls=%async_computation.5 | async-start | bytes 8388608
  26.2 20.2 %slice-start.2 = ((s8[7225344]{0:T(1024)(128)(4,1)}), s8[4194304]{0:T(1024)(128)(4,1)S(1)}, s32[]{:S(2)}) async-start(s8[7225344]{0:T(1024)(128)(4,1)} %bitcast.11), calls=%async_computation.7 | async-start | bytes 8388608
  26.2 20.1 %slice-start.4 = ((s8[7225344]{0:T(1024)(128)(4,1)}), s8[4194304]{0:T(1024)(128)(4,1)S(1)}, s32[]{:S(2)}) async-start(s8[7225344]{0:T(1024)(128)(4,1)} %bitcast.14), calls=%async_computation.9 | async-start | bytes 8388608
  35.8 10.5 %slice-start.1 = ((s8[7225344]{0:T(1024)(128)(4,1)}), s8[3031040]{0:T(1024)(128)(4,1)S(1)}, s32[]{:S(2)}) async-start(s8[7225344]{0:T(1024)(128)(4,1)} %bitcast.8), calls=%async_computation.6 | async-start | bytes 6062080
  35.8 10.5 %slice-start.3 = ((s8[7225344]{0:T(1024)(128)(4,1)}), s8[3031040]{0:T(1024)(128)(4,1)S(1)}, s32[]{:S(2)}) async-start(s8[7225344]{0:T(1024)(128)(4,1)} %bitcast.11), calls=%async_computation.8 | async-start | bytes 6062080
  35.8 10.5 %slice-start.5 = ((s8[7225344]{0:T(1024)(128)(4,1)}), s8[3031040]{0:T(1024)(128)(4,1)S(1)}, s32[]{:S(2)}) async-start(s8[7225344]{0:T(1024)(128)(4,1)} %bitcast.14), calls=%async_computation.10 | async-start | bytes 6062080
  35.8 10.5 %copy-start.5 = (f32[5376]{0:T(1024)S(1)}, f32[5376]{0:T(1024)}, u32[]{:S(2)}) copy-start(f32[5376]{0:T(1024)} %gain_ref.1) | copy-start | bytes 64516

commit v22 on v19

--- a/solution.py
+++ b/solution.py
@@ -292,11 +292,11 @@
         if chunk < count:
             rows = slice(chunk * size, (chunk + 1) * size)
             gate_values = dot_rows(gate_ref[rows], normed)
-            up_values = dot_rows(normed, up_ref[rows])
         if ready is not None:
             activated, held = ready
             share += jnp.dot(activated, down_ref[held], preferred_element_type=jnp.float32)
         if chunk < count:
+            up_values = dot_rows(normed, up_ref[rows])
             activated = jax.nn.gelu(gate_values.T, approximate=True) * up_values
             ready = activated.astype(jnp.bfloat16), rows
     if pieces_ref.ndim == 4:

time: 61.9 us -> 63.1 us (1.019)
  Pallas kernels: 8.64 us -> 9.79 us
    pallas_call x1, Pallas kernels: 5.04 us -> 6.2 us  [forward(): pl.pallas_call(functools.partial(forward_kernel, order), out_shape=(jax.S...]
where the time goes in v22:
time: 63.1 us; the launch traced here: 62.8 us
  blocking collectives  51.5 us (82%)
  Pallas kernels  9.79 us (16%)
  between operations  1.48 us (2%)
    all_to_all x5, blocking collectives, exchange(): lax.all_to_all(copies, axes, split_axis=0, concat_axis=0, tiled=True, axi...  51.5 us
    pallas_call x1, Pallas kernels, forward(): pl.pallas_call(functools.partial(forward_kernel, order), out_shape=(jax.S...  6.2 us

profile of v22, /device:TPU:0, one launch (start us, length us, event | category | flops | bytes accessed | tf_op | source)
XLA Modules:
  0.0 62.8 jit_solution(17005851452202668613)
XLA Ops:
  1.3 0.0 copy-start.1
  1.3 0.0 copy-start.2
  1.3 0.0 copy-start.3
  1.3 0.8 %shard_map.149 = (bf16[8,8,128]{2,1,0:T(8,128)(2,1)S(1)}, s32[8,128]{1,0:T(8,128)S(1)}) custom-call(s32[1]{0:T(128)S(6)} %copy.16.length_ref, bf16[1,8,128]{2,1,0:T(8,128)(2,1)} %source_hbm.1), custom_call_target="tpu_custom_call" | custom-call | flops 10000000000 | bytes 1048576 | tf_op jit(solution)/shard_map/pallas_call | solution.py:134
  2.2 13.7 %all_to_all.25.arrived_ref = bf16[8,8,128]{2,1,0:T(8,128)(2,1)S(1)} all-to-all(bf16[8,8,128]{2,1,0:T(8,128)(2,1)S(1)} %get-tuple-element.9), channel_id=1, replica_groups=mesh['ctx'=8,'head'=4] {'ctx'}, dimensions={0} | all-to-all | bytes 32768 | tf_op jit(solution)/shard_map/all_to_all | solution.py:355
  15.8 0.0 copy-done.3
  15.9 0.0 copy-done.4
  15.9 0.0 copy-done.7
  15.9 0.0 copy-done.8
  15.9 1.2 %shard_map.150 = bf16[8,3,4,128]{3,2,1,0:T(4,128)(2,1)S(1)} custom-call(s32[8,128]{1,0:T(8,128)S(1)} %get-tuple-element.8.length_ref, bf16[8,8,128]{2,1,0:T(8,128)(2,1)S(1)} %all_to_all.25.arrived_ref, bf16[1,4,128]{2,1,0:T(4,128)(2,1)S(1)} %copy-done.7, bf16[1,4,128]{2,1,0:T(4,128)(2,1)S(1)} %copy-done.8, bf16[1024,128]{1,0:T(8,128)(2,1)S(1)} %bitcast.19, ...), custom_call_target="tpu_custom_call" | custom-call | flops 10000000000 | bytes 1048576 | tf_op jit(solution)/shard_map/pallas_call | solution.py:206
  17.1 9.0 %all_to_all.26.part_ref = bf16[8,3,4,128]{3,2,1,0:T(4,128)(2,1)S(1)} all-to-all(bf16[8,3,4,128]{3,2,1,0:T(4,128)(2,1)S(1)} %shard_map.150), channel_id=1, replica_groups=mesh['ctx'=8,'head'=4] {'ctx'}, dimensions={0} | all-to-all | bytes 49152 | tf_op jit(solution)/shard_map/all_to_all | solution.py:355
  26.1 0.0 slice-start.4
  26.1 0.2 shard_map.151.copies_ref
  26.3 9.4 %all_to_all.27.rows_ref = bf16[32,8,128]{2,1,0:T(8,128)(2,1)S(1)} all-to-all(bf16[32,8,128]{2,1,0:T(8,128)(2,1)S(1)} %shard_map.151.copies_ref), channel_id=1, replica_groups={{0,1,2,3,4,5,6,7,16,17,18,19,20,21,22,23,24,25,26,27,28,29,30,31,8,9,10..., dimensions={0} | all-to-all | bytes 131072 | tf_op jit(solution)/shard_map/all_to_all | solution.py:355
  35.7 0.0 copy-done.6
  35.7 0.0 slice-start.5
  35.7 0.0 copy-start.5
  35.7 0.6 %shard_map.152 = (bf16[8,168]{1,0:T(8,128)(2,1)S(1)}, bf16[32,3,4,128]{3,2,1,0:T(4,128)(2,1)S(1)}) custom-call(bf16[32,8,128]{2,1,0:T(8,128)(2,1)S(1)} %all_to_all.27.rows_ref, bf16[168,4096]{1,0:T(8,128)(2,1)S(1)} %bitcast.16, bf16[8,168]{1,0:T(8,128)(2,1)S(1)} %copy-done.6), custom_call_target="tpu_custom_call" | custom-call | flops 10000000000 | bytes 1048576 | tf_op jit(solution)/shard_map/pallas_call | solution.py:257
  36.4 9.8 %all_to_all.28.pieces_ref = bf16[32,3,4,128]{3,2,1,0:T(4,128)(2,1)S(1)} all-to-all(bf16[32,3,4,128]{3,2,1,0:T(4,128)(2,1)S(1)} %get-tuple-element.10), channel_id=1, replica_groups={{0,1,2,3,4,5,6,7,16,17,18,19,20,21,22,23,24,25,26,27,28,29,30,31,8,9,10..., dimensions={0} | all-to-all | bytes 196608 | tf_op jit(solution)/shard_map/all_to_all | solution.py:355
  46.2 0.0 slice-done
  46.2 0.0 slice-done.4
  46.3 6.2 %shard_map.153 = (bf16[32,3,4,128]{3,2,1,0:T(4,128)(2,1)S(1)}, bf16[8,128]{1,0:T(8,128)(2,1)}) custom-call(bf16[32,3,4,128]{3,2,1,0:T(4,128)(2,1)S(1)} %all_to_all.28.pieces_ref, f32[5376]{0:T(1024)S(1)} %copy-done.5, bf16[32,8,128]{2,1,0:T(8,128)(2,1)S(1)} %shard_map.151.copies_ref, bf16[672,5376]{1,0:T(8,128)(2,1)S(1)} %bitcast.10, ...), custom_call_target="tpu_custom_call" | custom-call | flops 10000000000 | bytes 1048576 | tf_op jit(solution)/shard_map/pallas_call | solution.py:311
  52.5 9.6 %all_to_all.29.shares_ref = bf16[32,3,4,128]{3,2,1,0:T(4,128)(2,1)S(1)} all-to-all(bf16[32,3,4,128]{3,2,1,0:T(4,128)(2,1)S(1)} %get-tuple-element.12), channel_id=1, replica_groups={{0,1,2,3,4,5,6,7,16,17,18,19,20,21,22,23,24,25,26,27,28,29,30,31,8,9,10..., dimensions={0} | all-to-all | bytes 196608 | tf_op jit(solution)/shard_map/all_to_all | solution.py:355
  62.1 0.8 %shard_map.154 = bf16[8,168]{1,0:T(8,128)(2,1)} custom-call(bf16[32,3,4,128]{3,2,1,0:T(4,128)(2,1)S(1)} %all_to_all.29.shares_ref, bf16[8,168]{1,0:T(8,128)(2,1)S(1)} %get-tuple-element.13.hidden_ref), custom_call_target="tpu_custom_call" | custom-call | tf_op jit(solution)/shard_map/pallas_call | solution.py:339
  (20 shorter events, 0.0 us)
Async XLA Ops:
  1.3 14.6 %copy-start.1 = (bf16[1024,4,128]{2,1,0:T(4,128)(2,1)S(1)}, bf16[1024,4,128]{2,1,0:T(4,128)(2,1)}, u32[]{:S(2)}) copy-start(bf16[1024,4,128]{2,1,0:T(4,128)(2,1)} %param.20) | copy-start | bytes 3145732
  1.3 14.6 %copy-start.2 = (bf16[1024,4,128]{2,1,0:T(4,128)(2,1)S(1)}, bf16[1024,4,128]{2,1,0:T(4,128)(2,1)}, u32[]{:S(2)}) copy-start(bf16[1024,4,128]{2,1,0:T(4,128)(2,1)} %param.21) | copy-start | bytes 3145732
  1.3 14.6 %copy-start.3 = (bf16[1,256,4,128]{3,2,1,0:T(4,128)(2,1)S(1)}, bf16[1,256,4,128]{3,2,1,0:T(4,128)(2,1)}, u32[]{:S(2)}) copy-start(bf16[1,256,4,128]{3,2,1,0:T(4,128)(2,1)} %param.17) | copy-start | bytes 786436
  1.3 14.5 %copy-start.4 = (bf16[1,256,4,128]{3,2,1,0:T(4,128)(2,1)S(1)}, bf16[1,256,4,128]{3,2,1,0:T(4,128)(2,1)}, u32[]{:S(2)}) copy-start(bf16[1,256,4,128]{3,2,1,0:T(4,128)(2,1)} %param.18) | copy-start | bytes 786436
  1.3 14.5 %copy-start.7 = (bf16[1,4,128]{2,1,0:T(4,128)(2,1)S(1)}, bf16[1,4,128]{2,1,0:T(4,128)(2,1)}, u32[]{:S(2)}) copy-start(bf16[1,4,128]{2,1,0:T(4,128)(2,1)} %kn_ref.1) | copy-start | bytes 3076
  1.3 14.5 %copy-start.8 = (bf16[1,4,128]{2,1,0:T(4,128)(2,1)S(1)}, bf16[1,4,128]{2,1,0:T(4,128)(2,1)}, u32[]{:S(2)}) copy-start(bf16[1,4,128]{2,1,0:T(4,128)(2,1)} %vn_ref.1) | copy-start | bytes 3076
  26.0 9.6 %copy-start = (bf16[4096,168]{0,1:T(8,128)(2,1)S(1)}, bf16[4096,168]{0,1:T(8,128)(2,1)}, u32[]{:S(2)}) copy-start(bf16[4096,168]{0,1:T(8,128)(2,1)} %param.22) | copy-start | bytes 4128772
  26.0 9.6 %copy-start.6 = (bf16[8,168]{1,0:T(8,128)(2,1)S(1)}, bf16[8,168]{1,0:T(8,128)(2,1)}, u32[]{:S(2)}) copy-start(bf16[8,168]{1,0:T(8,128)(2,1)} %residual_ref.1) | copy-start | bytes 8068
  26.1 20.1 %slice-start = ((s8[7225344]{0:T(1024)(128)(4,1)}), s8[4194304]{0:T(1024)(128)(4,1)S(1)}, s32[]{:S(2)}) async-start(s8[7225344]{0:T(1024)(128)(4,1)} %bitcast.8), calls=%async_computation.5 | async-start | bytes 8388608
  26.1 20.2 %slice-start.2 = ((s8[7225344]{0:T(1024)(128)(4,1)}), s8[4194304]{0:T(1024)(128)(4,1)S(1)}, s32[]{:S(2)}) async-start(s8[7225344]{0:T(1024)(128)(4,1)} %bitcast.11), calls=%async_computation.7 | async-start | bytes 8388608
  26.1 20.1 %slice-start.4 = ((s8[7225344]{0:T(1024)(128)(4,1)}), s8[4194304]{0:T(1024)(128)(4,1)S(1)}, s32[]{:S(2)}) async-start(s8[7225344]{0:T(1024)(128)(4,1)} %bitcast.14), calls=%async_computation.9 | async-start | bytes 8388608
  35.7 10.5 %slice-start.1 = ((s8[7225344]{0:T(1024)(128)(4,1)}), s8[3031040]{0:T(1024)(128)(4,1)S(1)}, s32[]{:S(2)}) async-start(s8[7225344]{0:T(1024)(128)(4,1)} %bitcast.8), calls=%async_computation.6 | async-start | bytes 6062080
  35.7 10.5 %slice-start.3 = ((s8[7225344]{0:T(1024)(128)(4,1)}), s8[3031040]{0:T(1024)(128)(4,1)S(1)}, s32[]{:S(2)}) async-start(s8[7225344]{0:T(1024)(128)(4,1)} %bitcast.11), calls=%async_computation.8 | async-start | bytes 6062080
  35.7 10.5 %slice-start.5 = ((s8[7225344]{0:T(1024)(128)(4,1)}), s8[3031040]{0:T(1024)(128)(4,1)S(1)}, s32[]{:S(2)}) async-start(s8[7225344]{0:T(1024)(128)(4,1)} %bitcast.14), calls=%async_computation.10 | async-start | bytes 6062080
  35.7 10.5 %copy-start.5 = (f32[5376]{0:T(1024)S(1)}, f32[5376]{0:T(1024)}, u32[]{:S(2)}) copy-start(f32[5376]{0:T(1024)} %gain_ref.1) | copy-start | bytes 64516

commit v23 on v19

--- a/solution.py
+++ b/solution.py
@@ -14,7 +14,7 @@
 COST = pl.CostEstimate(flops=10**10, bytes_accessed=MIB, transcendentals=10**6)
 TERMS = 3
 CHUNKS = 3
-BLOCK_ROWS = 1024
+BLOCK_ROWS = 512
 LANES = 128
 HALF = LANES // 2
 BOTH = ("ctx", "head")

time: 61.9 us -> 61.9 us (level)
  no operation moved by 1% of the time
where the time goes in v23:
time: 61.9 us; the launch traced here: 61.6 us
  blocking collectives  51.5 us (83%)
  Pallas kernels  8.63 us (14%)
  between operations  1.48 us (2%)
    all_to_all x5, blocking collectives, exchange(): lax.all_to_all(copies, axes, split_axis=0, concat_axis=0, tiled=True, axi...  51.5 us
    pallas_call x1, Pallas kernels, forward(): pl.pallas_call(functools.partial(forward_kernel, order), out_shape=(jax.S...  5.05 us

profile of v23, /device:TPU:0, one launch (start us, length us, event | category | flops | bytes accessed | tf_op | source)
XLA Modules:
  0.0 61.6 jit_solution(14966532901069449607)
XLA Ops:
  1.3 0.0 copy-start.1
  1.3 0.0 copy-start.2
  1.3 0.0 copy-start.3
  1.3 0.0 copy-start.4
  1.3 0.0 copy-start.7
  1.3 0.8 %shard_map.149 = (bf16[8,8,128]{2,1,0:T(8,128)(2,1)S(1)}, s32[8,128]{1,0:T(8,128)S(1)}) custom-call(s32[1]{0:T(128)S(6)} %copy.16.length_ref, bf16[1,8,128]{2,1,0:T(8,128)(2,1)} %source_hbm.1), custom_call_target="tpu_custom_call" | custom-call | flops 10000000000 | bytes 1048576 | tf_op jit(solution)/shard_map/pallas_call | solution.py:134
  2.2 13.7 %all_to_all.25.arrived_ref = bf16[8,8,128]{2,1,0:T(8,128)(2,1)S(1)} all-to-all(bf16[8,8,128]{2,1,0:T(8,128)(2,1)S(1)} %get-tuple-element.9), channel_id=1, replica_groups=mesh['ctx'=8,'head'=4] {'ctx'}, dimensions={0} | all-to-all | bytes 32768 | tf_op jit(solution)/shard_map/all_to_all | solution.py:355
  15.8 0.0 copy-done.3
  15.9 0.0 copy-done.4
  15.9 0.0 copy-done.7
  15.9 0.0 copy-done.8
  15.9 1.2 %shard_map.150 = bf16[8,3,4,128]{3,2,1,0:T(4,128)(2,1)S(1)} custom-call(s32[8,128]{1,0:T(8,128)S(1)} %get-tuple-element.8.length_ref, bf16[8,8,128]{2,1,0:T(8,128)(2,1)S(1)} %all_to_all.25.arrived_ref, bf16[1,4,128]{2,1,0:T(4,128)(2,1)S(1)} %copy-done.7, bf16[1,4,128]{2,1,0:T(4,128)(2,1)S(1)} %copy-done.8, bf16[1024,128]{1,0:T(8,128)(2,1)S(1)} %bitcast.19, ...), custom_call_target="tpu_custom_call" | custom-call | flops 10000000000 | bytes 1048576 | tf_op jit(solution)/shard_map/pallas_call | solution.py:206
  17.0 9.0 %all_to_all.26.part_ref = bf16[8,3,4,128]{3,2,1,0:T(4,128)(2,1)S(1)} all-to-all(bf16[8,3,4,128]{3,2,1,0:T(4,128)(2,1)S(1)} %shard_map.150), channel_id=1, replica_groups=mesh['ctx'=8,'head'=4] {'ctx'}, dimensions={0} | all-to-all | bytes 49152 | tf_op jit(solution)/shard_map/all_to_all | solution.py:355
  26.0 0.0 slice-start.4
  26.1 0.2 shard_map.151.copies_ref
  26.2 9.4 %all_to_all.27.rows_ref = bf16[32,8,128]{2,1,0:T(8,128)(2,1)S(1)} all-to-all(bf16[32,8,128]{2,1,0:T(8,128)(2,1)S(1)} %shard_map.151.copies_ref), channel_id=1, replica_groups={{0,1,2,3,4,5,6,7,16,17,18,19,20,21,22,23,24,25,26,27,28,29,30,31,8,9,10..., dimensions={0} | all-to-all | bytes 131072 | tf_op jit(solution)/shard_map/all_to_all | solution.py:355
  35.7 0.0 slice-start.5
  35.7 0.0 copy-start.5
  35.7 0.6 %shard_map.152 = (bf16[8,168]{1,0:T(8,128)(2,1)S(1)}, bf16[32,3,4,128]{3,2,1,0:T(4,128)(2,1)S(1)}) custom-call(bf16[32,8,128]{2,1,0:T(8,128)(2,1)S(1)} %all_to_all.27.rows_ref, bf16[168,4096]{1,0:T(8,128)(2,1)S(1)} %bitcast.16, bf16[8,168]{1,0:T(8,128)(2,1)S(1)} %copy-done.6), custom_call_target="tpu_custom_call" | custom-call | flops 10000000000 | bytes 1048576 | tf_op jit(solution)/shard_map/pallas_call | solution.py:257
  36.4 9.8 %all_to_all.28.pieces_ref = bf16[32,3,4,128]{3,2,1,0:T(4,128)(2,1)S(1)} all-to-all(bf16[32,3,4,128]{3,2,1,0:T(4,128)(2,1)S(1)} %get-tuple-element.10), channel_id=1, replica_groups={{0,1,2,3,4,5,6,7,16,17,18,19,20,21,22,23,24,25,26,27,28,29,30,31,8,9,10..., dimensions={0} | all-to-all | bytes 196608 | tf_op jit(solution)/shard_map/all_to_all | solution.py:355
  46.2 0.0 slice-done.2
  46.3 5.0 %shard_map.153 = (bf16[32,3,4,128]{3,2,1,0:T(4,128)(2,1)S(1)}, bf16[8,128]{1,0:T(8,128)(2,1)}) custom-call(bf16[32,3,4,128]{3,2,1,0:T(4,128)(2,1)S(1)} %all_to_all.28.pieces_ref, f32[5376]{0:T(1024)S(1)} %copy-done.5, bf16[32,8,128]{2,1,0:T(8,128)(2,1)S(1)} %shard_map.151.copies_ref, bf16[672,5376]{1,0:T(8,128)(2,1)S(1)} %bitcast.10, ...), custom_call_target="tpu_custom_call" | custom-call | flops 10000000000 | bytes 1048576 | tf_op jit(solution)/shard_map/pallas_call | solution.py:311
  51.3 9.6 %all_to_all.29.shares_ref = bf16[32,3,4,128]{3,2,1,0:T(4,128)(2,1)S(1)} all-to-all(bf16[32,3,4,128]{3,2,1,0:T(4,128)(2,1)S(1)} %get-tuple-element.12), channel_id=1, replica_groups={{0,1,2,3,4,5,6,7,16,17,18,19,20,21,22,23,24,25,26,27,28,29,30,31,8,9,10..., dimensions={0} | all-to-all | bytes 196608 | tf_op jit(solution)/shard_map/all_to_all | solution.py:355
  60.9 0.8 %shard_map.154 = bf16[8,168]{1,0:T(8,128)(2,1)} custom-call(bf16[32,3,4,128]{3,2,1,0:T(4,128)(2,1)S(1)} %all_to_all.29.shares_ref, bf16[8,168]{1,0:T(8,128)(2,1)S(1)} %get-tuple-element.13.hidden_ref), custom_call_target="tpu_custom_call" | custom-call | tf_op jit(solution)/shard_map/pallas_call | solution.py:339
  (20 shorter events, 0.0 us)
Async XLA Ops:
  1.3 14.6 %copy-start.1 = (bf16[1024,4,128]{2,1,0:T(4,128)(2,1)S(1)}, bf16[1024,4,128]{2,1,0:T(4,128)(2,1)}, u32[]{:S(2)}) copy-start(bf16[1024,4,128]{2,1,0:T(4,128)(2,1)} %param.20) | copy-start | bytes 3145732
  1.3 14.6 %copy-start.2 = (bf16[1024,4,128]{2,1,0:T(4,128)(2,1)S(1)}, bf16[1024,4,128]{2,1,0:T(4,128)(2,1)}, u32[]{:S(2)}) copy-start(bf16[1024,4,128]{2,1,0:T(4,128)(2,1)} %param.21) | copy-start | bytes 3145732
  1.3 14.6 %copy-start.3 = (bf16[1,256,4,128]{3,2,1,0:T(4,128)(2,1)S(1)}, bf16[1,256,4,128]{3,2,1,0:T(4,128)(2,1)}, u32[]{:S(2)}) copy-start(bf16[1,256,4,128]{3,2,1,0:T(4,128)(2,1)} %param.17) | copy-start | bytes 786436
  1.3 14.5 %copy-start.4 = (bf16[1,256,4,128]{3,2,1,0:T(4,128)(2,1)S(1)}, bf16[1,256,4,128]{3,2,1,0:T(4,128)(2,1)}, u32[]{:S(2)}) copy-start(bf16[1,256,4,128]{3,2,1,0:T(4,128)(2,1)} %param.18) | copy-start | bytes 786436
  1.3 14.5 %copy-start.7 = (bf16[1,4,128]{2,1,0:T(4,128)(2,1)S(1)}, bf16[1,4,128]{2,1,0:T(4,128)(2,1)}, u32[]{:S(2)}) copy-start(bf16[1,4,128]{2,1,0:T(4,128)(2,1)} %kn_ref.1) | copy-start | bytes 3076
  1.3 14.5 %copy-start.8 = (bf16[1,4,128]{2,1,0:T(4,128)(2,1)S(1)}, bf16[1,4,128]{2,1,0:T(4,128)(2,1)}, u32[]{:S(2)}) copy-start(bf16[1,4,128]{2,1,0:T(4,128)(2,1)} %vn_ref.1) | copy-start | bytes 3076
  26.0 9.6 %copy-start = (bf16[4096,168]{0,1:T(8,128)(2,1)S(1)}, bf16[4096,168]{0,1:T(8,128)(2,1)}, u32[]{:S(2)}) copy-start(bf16[4096,168]{0,1:T(8,128)(2,1)} %param.22) | copy-start | bytes 4128772
  26.0 9.6 %copy-start.6 = (bf16[8,168]{1,0:T(8,128)(2,1)S(1)}, bf16[8,168]{1,0:T(8,128)(2,1)}, u32[]{:S(2)}) copy-start(bf16[8,168]{1,0:T(8,128)(2,1)} %residual_ref.1) | copy-start | bytes 8068
  26.0 20.1 %slice-start = ((s8[7225344]{0:T(1024)(128)(4,1)}), s8[4194304]{0:T(1024)(128)(4,1)S(1)}, s32[]{:S(2)}) async-start(s8[7225344]{0:T(1024)(128)(4,1)} %bitcast.8), calls=%async_computation.5 | async-start | bytes 8388608
  26.0 20.2 %slice-start.2 = ((s8[7225344]{0:T(1024)(128)(4,1)}), s8[4194304]{0:T(1024)(128)(4,1)S(1)}, s32[]{:S(2)}) async-start(s8[7225344]{0:T(1024)(128)(4,1)} %bitcast.11), calls=%async_computation.7 | async-start | bytes 8388608
  26.0 20.1 %slice-start.4 = ((s8[7225344]{0:T(1024)(128)(4,1)}), s8[4194304]{0:T(1024)(128)(4,1)S(1)}, s32[]{:S(2)}) async-start(s8[7225344]{0:T(1024)(128)(4,1)} %bitcast.14), calls=%async_computation.9 | async-start | bytes 8388608
  35.7 10.5 %slice-start.1 = ((s8[7225344]{0:T(1024)(128)(4,1)}), s8[3031040]{0:T(1024)(128)(4,1)S(1)}, s32[]{:S(2)}) async-start(s8[7225344]{0:T(1024)(128)(4,1)} %bitcast.8), calls=%async_computation.6 | async-start | bytes 6062080
  35.7 10.5 %slice-start.3 = ((s8[7225344]{0:T(1024)(128)(4,1)}), s8[3031040]{0:T(1024)(128)(4,1)S(1)}, s32[]{:S(2)}) async-start(s8[7225344]{0:T(1024)(128)(4,1)} %bitcast.11), calls=%async_computation.8 | async-start | bytes 6062080
  35.7 10.5 %slice-start.5 = ((s8[7225344]{0:T(1024)(128)(4,1)}), s8[3031040]{0:T(1024)(128)(4,1)S(1)}, s32[]{:S(2)}) async-start(s8[7225344]{0:T(1024)(128)(4,1)} %bitcast.14), calls=%async_computation.10 | async-start | bytes 6062080
  35.7 10.5 %copy-start.5 = (f32[5376]{0:T(1024)S(1)}, f32[5376]{0:T(1024)}, u32[]{:S(2)}) copy-start(f32[5376]{0:T(1024)} %gain_ref.1) | copy-start | bytes 64516
